TPU v7x, 32 devices: a whole 2x2x4 slice. The times are simulated.
32 devices in a mesh: adjust: 2 (over y), hid: 16 (over z, x, core).
Axes of the slice: x: 2, y: 2, z: 4, core: 2. Of those that a mesh axis runs over, the one named last changes fastest.
Arguments:
- tokens: bfloat16 [1024, 4096], P(('adjust', 'hid')), parts along dimension 0, may hold values from -6 to 6
- grad_out: bfloat16 [1024, 4096], P(('adjust', 'hid')), parts along dimension 0, may hold values from -3 to 3
- gate_weight: bfloat16 [8192, 28672], P('adjust', 'hid'), parts along dimension 0, may hold values from -0.09375 to 0.09375
- up_weight: bfloat16 [8192, 28672], P('adjust', 'hid'), parts along dimension 0, may hold values from -0.09375 to 0.09375
- down_weight: bfloat16 [57344, 4096], P(('adjust', 'hid')), parts along dimension 0, may hold values from -0.03125 to 0.03125
Outputs:
- fisher_gate: bfloat16 [8192, 28672], P('adjust', 'hid'), parts along dimension 0
- fisher_up: bfloat16 [8192, 28672], P('adjust', 'hid'), parts along dimension 0
- input_grad: bfloat16 [1024, 4096], P(('adjust', 'hid')), parts along dimension 0
There are 2 independent parts, one for each index of `adjust`. A program takes and returns all parts, laid end to end along the dimension named above; each array names one. Nothing has to cross between parts.
All inputs are finite; a program needn't handle non-finite values.
Results may differ from a plain program's by a relative error of at most 0.0058.
Values may be sent and summed in bfloat16 or wider, within the bound.
No kernel may reach another device: no remote copies, remote signals or barrier semaphores. Data moves between devices by JAX's collectives and lax.ppermute only.
A program may use at most 192 MiB of HBM per device.

v0:
```python
import jax
import jax.numpy as jnp
from jax import lax
from jax.sharding import PartitionSpec as P

SEQ_LEN = 256


def project_back(upstream, down_weight):
    return lax.dot_general(
        upstream, down_weight, (((1,), (1,)), ((), ())), preferred_element_type=jnp.float32
    )


def term_rows(grads, weight):
    return lax.dot_general(
        grads, weight, (((1,), (1,)), ((), ())), preferred_element_type=jnp.float32
    )


def per_device(tokens, grad_out, gate_weight, up_weight, down_weight):
    whole, upstream = (
        lax.all_gather(tokens, "hid", axis=0, tiled=True),
        lax.all_gather(grad_out, "hid", axis=0, tiled=True),
    )
    gate = jnp.dot(whole, gate_weight, preferred_element_type=jnp.float32)
    up = jnp.dot(whole, up_weight, preferred_element_type=jnp.float32)
    hidden_grad = project_back(upstream, down_weight)
    sigma = jax.nn.sigmoid(gate)
    grad_gate = (hidden_grad * up * sigma * (1.0 + gate * (1.0 - sigma))).astype(jnp.bfloat16)
    grad_up = (hidden_grad * gate * sigma).astype(jnp.bfloat16)
    input_grad = lax.psum_scatter(
        term_rows(grad_gate, gate_weight) + term_rows(grad_up, up_weight),
        "hid",
        scatter_dimension=0,
        tiled=True,
    )
    count = whole.shape[0] // SEQ_LEN
    fisher_gate = jnp.zeros(gate_weight.shape, jnp.bfloat16)
    fisher_up = jnp.zeros(up_weight.shape, jnp.bfloat16)
    for index in range(count):
        rows = whole[index * SEQ_LEN : (index + 1) * SEQ_LEN]
        seq_gate = lax.dot_general(
            rows,
            grad_gate[index * SEQ_LEN : (index + 1) * SEQ_LEN],
            (((0,), (0,)), ((), ())),
            preferred_element_type=jnp.float32,
        )
        seq_up = lax.dot_general(
            rows,
            grad_up[index * SEQ_LEN : (index + 1) * SEQ_LEN],
            (((0,), (0,)), ((), ())),
            preferred_element_type=jnp.float32,
        )
        fisher_gate = (
            fisher_gate.astype(jnp.float32) + seq_gate * seq_gate * (1.0 / count)
        ).astype(jnp.bfloat16)
        fisher_up = (fisher_up.astype(jnp.float32) + seq_up * seq_up * (1.0 / count)).astype(
            jnp.bfloat16
        )
    return (fisher_gate, fisher_up, input_grad.astype(jnp.bfloat16))


def solution(mesh):
    in_specs = (
        P(("adjust", "hid"), None),
        P(("adjust", "hid"), None),
        P("adjust", "hid"),
        P("adjust", "hid"),
        P(("adjust", "hid"), None),
    )
    out_specs = (P("adjust", "hid"), P("adjust", "hid"), P(("adjust", "hid"), None))
    return jax.shard_map(
        per_device, mesh=mesh, in_specs=in_specs, out_specs=out_specs, check_vma=False
    )
```

profile of v0, /device:TPU:0, one launch (start us, length us, event | category | flops | bytes accessed | tf_op | source)
XLA Modules:
  0.0 297.9 jit_solution(4527272235071040959)
XLA Ops:
  7.2 0.0 all-gather.5.cloned.1.call-start
  7.2 0.7 all-gather.5.cloned.1.call-update
  7.9 0.0 all-gather.3.cloned.1.call-start
  7.9 0.7 all-gather.3.cloned.1.call-update
  8.6 0.0 reduce-scatter.2.cloned.1.call-start
  8.7 54.8 %all-gather.5.cloned.1.call-done = bf16[512,4096]{1,0:T(8,128)(2,1)} async-done(((bf16[32,4096]{1,0:T(8,128)(2,1)}), bf16[512,4096]{1,0:T(8,128)(2,1)}) %all-gather.5.cloned.1.call-update) | async-done | bytes 4194320 | tf_op jit(solution)/shard_map/all_gather | solution.py:23
  63.4 14.5 %fusion.10 = f32[512,1792]{1,0:T(8,128)} fusion(bf16[512,4096]{1,0:T(8,128)(2,1)} %all-gather.5.cloned.1.call-done, bf16[4096,1792]{1,0:T(8,128)(2,1)} %param.7), kind=kOutput, calls=%fused_computation.18 | convolution fusion | flops 7516192768 | bytes 22544384 | tf_op jit(solution)/shard_map/dot_general | solution.py:26
  78.0 36.7 %all-gather.3.cloned.1.call-done = bf16[512,4096]{1,0:T(8,128)(2,1)} async-done(((bf16[32,4096]{1,0:T(8,128)(2,1)}), bf16[512,4096]{1,0:T(8,128)(2,1)}) %all-gather.3.cloned.1.call-update) | async-done | bytes 4194320 | tf_op jit(solution)/shard_map/all_gather | solution.py:24
  114.7 15.8 %multiply_convert_fusion.2 = (bf16[512,1792]{1,0:T(8,128)(2,1)S(1)}, f32[512,1792]{1,0:T(8,128)}) fusion(f32[512,1792]{1,0:T(8,128)} %fusion.10, bf16[512,4096]{1,0:T(8,128)(2,1)} %all-gather.3.cloned.1.call-done, bf16[1792,4096]{1,0:T(8,128)(2,1)} %param.9), kind=kOutput, calls=%fused_computation.7 | convolution fusion | flops 7521697792 | bytes 28049408 | tf_op jit(solution)/shard_map/dot_general | solution.py:10
  130.5 15.6 %multiply_convert_fusion.3 = bf16[512,1792]{1,0:T(8,128)(2,1)S(1)} fusion(f32[512,1792]{1,0:T(8,128)} %fusion.10, f32[512,1792]{1,0:T(8,128)} %get-tuple-element.7, bf16[512,4096]{1,0:T(8,128)(2,1)} %all-gather.5.cloned.1.call-done, bf16[4096,1792]{1,0:T(8,128)(2,1)} %param.8), kind=kOutput, calls=%fused_computation.8 | convolution fusion | flops 7525367808 | bytes 28049408 | tf_op jit(solution)/shard_map/dot_general | solution.py:27
  146.1 0.0 copy-start.2
  146.1 13.7 %fusion.11 = f32[512,4096]{1,0:T(8,128)} fusion(bf16[512,1792]{1,0:T(8,128)(2,1)S(1)} %multiply_convert_fusion.3, bf16[4096,1792]{1,0:T(8,128)(2,1)} %param.7), kind=kOutput, calls=%fused_computation.19 | convolution fusion | flops 7516192768 | bytes 24903680 | tf_op jit(solution)/shard_map/dot_general | solution.py:16
  159.8 26.4 %convolution_add_fusion = f32[512,4096]{1,0:T(8,128)} fusion(f32[512,4096]{1,0:T(8,128)} %fusion.11, bf16[512,1792]{1,0:T(8,128)(2,1)S(1)} %get-tuple-element.6, bf16[4096,1792]{1,0:T(8,128)(2,1)} %param.8), kind=kOutput, calls=%fused_computation.6 | convolution fusion | flops 7518289920 | bytes 33292288 | tf_op jit(solution)/shard_map/dot_general | solution.py:16
  186.2 0.0 reduce-scatter.2.cloned.1.call-update
  186.3 0.0 copy-start
  186.3 12.5 %multiply_convert_fusion.1 = bf16[1792,4096]{1,0:T(8,128)(2,1)} fusion(bf16[512,4096]{1,0:T(8,128)(2,1)} %all-gather.5.cloned.1.call-done, bf16[512,1792]{1,0:T(8,128)(2,1)} %copy-done.2), kind=kOutput, calls=%fused_computation.3 | convolution fusion | flops 3780116480 | bytes 17694720 | tf_op jit(solution)/shard_map/dot_general | solution.py:43
  198.8 0.0 copy-done
  198.8 12.5 %fusion = bf16[4096,1792]{0,1:T(8,128)(2,1)} fusion(bf16[1792,4096]{1,0:T(8,128)(2,1)} %multiply_convert_fusion.1, bf16[512,4096]{1,0:T(8,128)(2,1)S(1)} %copy-done, bf16[512,1792]{1,0:T(8,128)(2,1)} %copy-done.2), kind=kOutput, calls=%fused_computation.4 | convolution fusion | flops 3794796544 | bytes 32374784 | tf_op jit(solution)/shard_map/dot_general | solution.py:43
  211.3 18.7 %copy.8 = bf16[4096,1792]{1,0:T(8,128)(2,1)} copy(bf16[4096,1792]{0,1:T(8,128)(2,1)} %fusion) | data formatting | bytes 29360128
  230.0 9.3 %multiply_convert_fusion = bf16[1792,4096]{1,0:T(8,128)(2,1)} fusion(bf16[512,4096]{1,0:T(8,128)(2,1)} %all-gather.5.cloned.1.call-done, bf16[512,1792]{1,0:T(8,128)(2,1)S(1)} %get-tuple-element.6), kind=kOutput, calls=%fused_computation.2 | convolution fusion | flops 3780116480 | bytes 17694720 | tf_op jit(solution)/shard_map/dot_general | solution.py:49
  239.3 11.2 %fusion.1 = bf16[4096,1792]{0,1:T(8,128)(2,1)} fusion(bf16[1792,4096]{1,0:T(8,128)(2,1)} %multiply_convert_fusion, bf16[512,4096]{1,0:T(8,128)(2,1)S(1)} %copy-done.1, bf16[512,1792]{1,0:T(8,128)(2,1)S(1)} %get-tuple-element.6), kind=kOutput, calls=%fused_computation.5 | convolution fusion | flops 3794796544 | bytes 32374784 | tf_op jit(solution)/shard_map/dot_general | solution.py:49
  250.5 18.7 %copy.9 = bf16[4096,1792]{1,0:T(8,128)(2,1)} copy(bf16[4096,1792]{0,1:T(8,128)(2,1)} %fusion.1) | data formatting | bytes 29360128
  269.2 20.4 %reduce-scatter.2.cloned.1.call-done = f32[32,4096]{1,0:T(8,128)} async-done(((f32[512,4096]{1,0:T(8,128)}), f32[32,4096]{1,0:T(8,128)}) %reduce-scatter.2.cloned.1.call-update) | async-done | bytes 524304 | tf_op jit(solution)/shard_map/reduce_scatter | solution.py:32
  289.6 1.8 convert_element_type.48
  (3 shorter events, 0.0 us)
Async XLA Ops:
  7.2 56.3 %all-gather.5.cloned.1.call-start = ((), (), s32[]{:S(2)}) async-start(), calls=%async_computation.2 | async-start | bytes 4456448 | tf_op jit(solution)/shard_map/all_gather | solution.py:23
  7.9 106.8 %all-gather.3.cloned.1.call-start = ((), (), s32[]{:S(2)}) async-start(), calls=%async_computation.1 | async-start | bytes 4456448 | tf_op jit(solution)/shard_map/all_gather | solution.py:24
  8.6 281.0 %reduce-scatter.2.cloned.1.call-start = ((), (), s32[]{:S(2)}) async-start(), calls=%async_computation.3 | async-start | bytes 8912896 | tf_op jit(solution)/shard_map/reduce_scatter | solution.py:32
  146.1 13.8 %copy-start.2 = (bf16[512,1792]{1,0:T(8,128)(2,1)}, bf16[512,1792]{1,0:T(8,128)(2,1)S(1)}, u32[]{:S(2)}) copy-start(bf16[512,1792]{1,0:T(8,128)(2,1)S(1)} %multiply_convert_fusion.3) | copy-start | bytes 5505028
  186.3 12.6 %copy-start = (bf16[512,4096]{1,0:T(8,128)(2,1)S(1)}, bf16[512,4096]{1,0:T(8,128)(2,1)}, u32[]{:S(2)}) copy-start(bf16[512,4096]{1,0:T(8,128)(2,1)} %all-gather.5.cloned.1.call-done) | copy-start | bytes 12582916
  230.0 9.3 %copy-start.1 = (bf16[512,4096]{1,0:T(8,128)(2,1)S(1)}, bf16[512,4096]{1,0:T(8,128)(2,1)}, u32[]{:S(2)}) copy-start(bf16[512,4096]{1,0:T(8,128)(2,1)} %all-gather.5.cloned.1.call-done) | copy-start | bytes 12582916
Sparse Core Ops, SparseCore 0:
  10.2 53.2 all-gather.4
  65.6 49.0 all-gather.2
  186.4 103.1 reduce-scatter.1
where the time goes:
time: 299 us; the launch traced here: 298 us
  matrix products  132 us (44%)
  waiting for transfers between devices  113 us (38%)
  local copies, waits for them, and re-layouts  37.5 us (13%)
  between operations  13.8 us (5%)
    all_gather x1, waiting for transfers between devices, per_device(): lax.all_gather(tokens, 'hid', axis=0, tiled=True)  54.8 us
    dot_general x2, matrix products, term_rows(): lax.dot_general(grads, weight, (((1,), (1,)), ((), ())), preferred_elemen...  40.1 us
    unnamed x8, local copies, waits for them, and re-layouts  37.5 us
    all_gather x1, waiting for transfers between devices, per_device(): lax.all_gather(grad_out, 'hid', axis=0, tiled=True)  36.7 us
    dot_general x2, matrix products, per_device(): lax.dot_general(rows, grad_gate[index * SEQ_LEN:(index + 1) * SEQ_LEN], (...  25 us
    dot_general x2, matrix products, per_device(): lax.dot_general(rows, grad_up[index * SEQ_LEN:(index + 1) * SEQ_LEN], (((...  20.5 us
    reduce_scatter x1, waiting for transfers between devices, per_device(): lax.psum_scatter(term_rows(grad_gate, gate_weight) + term_rows(grad_up, u...  20.4 us
    dot_general x1, matrix products, project_back(): lax.dot_general(upstream, down_weight, (((1,), (1,)), ((), ())), preferre...  15.8 us
  transfers between devices with their start and end apart: 3, of which 3 were waited for; matrix products, arithmetic and copies ran while one was open for 33% of the time, Pallas kernels for 0%

commit v1 on v0

v1 whole, which is shorter than its diff:
```python
import functools

import jax
import jax.numpy as jnp
from jax import lax
from jax.experimental import pallas as pl
from jax.experimental.pallas import tpu as pltpu
from jax.sharding import PartitionSpec as P

SEQS = 2
MIB = 1 << 20
NT = (((1,), (1,)), ((), ()))
TN = (((0,), (0,)), ((), ()))


def tile(size, want):
    return want if size % want == 0 else size


def params(mib):
    return pltpu.CompilerParams(vmem_limit_bytes=mib * MIB)


def cost(flops, read):
    return pl.CostEstimate(flops=flops, bytes_accessed=read, transcendentals=0)


def forward_kernel(x_ref, wg_ref, wu_ref, gate_ref, up_ref):
    x = x_ref[...]
    gate_ref[...] = jnp.dot(x, wg_ref[...], preferred_element_type=jnp.float32)
    up_ref[...] = jnp.dot(x, wu_ref[...], preferred_element_type=jnp.float32)


def forward(x, wg, wu):
    rows, depth = x.shape
    width = wg.shape[1]
    step = tile(width, 256)
    return pl.pallas_call(
        forward_kernel,
        grid=(width // step,),
        in_specs=[
            pl.BlockSpec((rows, depth), lambda j: (0, 0)),
            pl.BlockSpec((depth, step), lambda j: (0, j)),
            pl.BlockSpec((depth, step), lambda j: (0, j)),
        ],
        out_specs=[pl.BlockSpec((rows, step), lambda j: (0, j))] * 2,
        out_shape=[jax.ShapeDtypeStruct((rows, width), jnp.float32)] * 2,
        compiler_params=params(40),
        cost_estimate=cost(4 * rows * depth * width, 4 * depth * width),
        name="gate_up",
    )(x, wg, wu)


def back_kernel(parts, dy_ref, wd_ref, gate_ref, up_ref, gg_ref, gu_ref):
    rows = dy_ref.shape[0] // parts
    for p in range(parts):
        at = pl.ds(p * rows, rows)
        hidden = lax.dot_general(dy_ref[at, :], wd_ref[...], NT, preferred_element_type=jnp.float32)
        gate = gate_ref[at, :]
        sigma = jax.nn.sigmoid(gate)
        both = hidden * sigma
        gg_ref[at, :] = (both * up_ref[at, :] * (1.0 + gate * (1.0 - sigma))).astype(jnp.bfloat16)
        gu_ref[at, :] = (both * gate).astype(jnp.bfloat16)


def back(dy, wd, gate, up):
    rows, depth = dy.shape
    width = wd.shape[0]
    step = tile(width, 256)
    column = pl.BlockSpec((rows, step), lambda j: (0, j))
    return pl.pallas_call(
        functools.partial(back_kernel, 2),
        grid=(width // step,),
        in_specs=[
            pl.BlockSpec((rows, depth), lambda j: (0, 0)),
            pl.BlockSpec((step, depth), lambda j: (j, 0)),
            column,
            column,
        ],
        out_specs=[column, column],
        out_shape=[jax.ShapeDtypeStruct((rows, width), jnp.bfloat16)] * 2,
        compiler_params=params(40),
        cost_estimate=cost(2 * rows * depth * width, 2 * depth * width),
        name="hidden_back",
    )(dy, wd, gate, up)


def input_kernel(gg_ref, gu_ref, wg_ref, wu_ref, out_ref):
    total = lax.dot_general(gg_ref[...], wg_ref[...], NT, preferred_element_type=jnp.float32)
    total += lax.dot_general(gu_ref[...], wu_ref[...], NT, preferred_element_type=jnp.float32)
    out_ref[...] = total.astype(jnp.bfloat16)


def input_terms(gg, gu, wg, wu):
    rows, width = gg.shape
    depth = wg.shape[0]
    step = 512
    held = pl.BlockSpec((rows, width), lambda j: (0, 0))
    return pl.pallas_call(
        input_kernel,
        grid=(depth // step,),
        in_specs=[
            held,
            held,
            pl.BlockSpec((step, width), lambda j: (j, 0)),
            pl.BlockSpec((step, width), lambda j: (j, 0)),
        ],
        out_specs=pl.BlockSpec((rows, step), lambda j: (0, j)),
        out_shape=jax.ShapeDtypeStruct((rows, depth), jnp.bfloat16),
        compiler_params=params(40),
        cost_estimate=cost(4 * rows * depth * width, 4 * depth * width),
        name="input_terms",
    )(gg, gu, wg, wu)


def fisher_kernel(step, x_ref, gg_ref, gu_ref, fg_ref, fu_ref):
    half = x_ref.shape[0] // 2
    span = half // SEQS
    width = gg_ref.shape[1]

    def rows(ref, q, at):
        near = ref[pl.ds(q * span, span), at]
        far = ref[pl.ds(half + q * span, span), at]
        return jnp.concatenate([near, far], axis=0)

    xs = [rows(x_ref, q, slice(None)).T for q in range(SEQS)]
    for g_ref, f_ref in ((gg_ref, fg_ref), (gu_ref, fu_ref)):
        for c in range(width // step):
            at = pl.ds(c * step, step)
            total = None
            for q in range(SEQS):
                seq = jnp.dot(xs[q], rows(g_ref, q, at), preferred_element_type=jnp.float32)
                total = seq * seq if total is None else total + seq * seq
            f_ref[:, at] = (total * (1.0 / SEQS)).astype(jnp.bfloat16)


def fisher(x, gg, gu):
    rows, depth = x.shape
    width = gg.shape[1]
    step = 512
    held = pl.BlockSpec((rows, width), lambda j: (0, 0))
    block = pl.BlockSpec((step, width), lambda j: (j, 0))
    return pl.pallas_call(
        functools.partial(fisher_kernel, tile(width, 256)),
        grid=(depth // step,),
        in_specs=[pl.BlockSpec((rows, step), lambda j: (0, j)), held, held],
        out_specs=[block, block],
        out_shape=[jax.ShapeDtypeStruct((depth, width), jnp.bfloat16)] * 2,
        compiler_params=params(40),
        cost_estimate=cost(4 * rows * depth * width, 4 * depth * width),
        name="fisher",
    )(x, gg, gu)


def per_device(size, tokens, grad_out, wg, wu, wd):
    chips = size // 2
    across = [[2 * i + c for i in range(chips)] for c in range(2)]
    pairs = [[2 * i, 2 * i + 1] for i in range(chips)]
    block, depth = tokens.shape

    def gather(rows):
        near = lax.all_gather(rows, "hid", axis=0, tiled=True, axis_index_groups=across)
        return lax.all_gather(near, "hid", axis=0, tiled=False, axis_index_groups=pairs)

    x = gather(tokens).reshape(-1, depth)
    dy = gather(grad_out).reshape(-1, depth)
    gate, up = forward(x, wg, wu)
    gg, gu = back(dy, wd, gate, up)
    terms = input_terms(gg, gu, wg, wu).reshape(2, -1, depth)
    mine = lax.psum_scatter(
        terms, "hid", scatter_dimension=0, tiled=False, axis_index_groups=pairs
    )
    mine = lax.psum_scatter(
        mine, "hid", scatter_dimension=0, tiled=True, axis_index_groups=across
    )
    fg, fu = fisher(x, gg, gu)
    return fg, fu, mine


def solution(mesh):
    rows = P(("adjust", "hid"), None)
    weights = P("adjust", "hid")
    return jax.shard_map(
        functools.partial(per_device, mesh.shape["hid"]),
        mesh=mesh,
        in_specs=(rows, rows, weights, weights, rows),
        out_specs=(weights, weights, rows),
        check_vma=False,
    )
```

time: 299 us -> 285 us (0.953)
  matrix products: 132 us -> 0 us
  Pallas kernels: 0 us -> 71.5 us
  waiting for transfers between devices: 113 us -> 183 us
  local copies, waits for them, and re-layouts: 37.5 us -> 15.6 us
    dot_general x9 -> x0, matrix products: 132 us -> none  [the longest x2 40.1 us: term_rows(): lax.dot_general(grads, weight, (((1,), (1,)), ((), ())), preferred_elemen...]
    pallas_call x0 -> x4, Pallas kernels: none -> 71.5 us  [the longest x1 19.8 us: forward(): pl.pallas_call(forward_kernel, grid=(width // step,), in_specs=[pl.BlockS...]
    reduce_scatter x1 -> x2, waiting for transfers between devices: 20.4 us -> 64.4 us  [the longest x1 51.1 us: per_device(): lax.psum_scatter(mine, 'hid', scatter_dimension=0, tiled=True, axis_index...]
    all_gather x2 -> x4, waiting for transfers between devices: 91.5 us -> 117 us  [the longest x2 103 us: gather(): lax.all_gather(rows, 'hid', axis=0, tiled=True, axis_index_groups=across)]
    unnamed x8 -> x18, local copies, waits for them, and re-layouts: 37.5 us -> 15.6 us
  transfers between devices with their start and end apart: 3 -> 6, of which waited for: 3 -> 5; matrix products, arithmetic and copies ran while one was open for 33% -> 0% of each run, Pallas kernels for 0% -> 14%
where the time goes in v1:
time: 285 us; the launch traced here: 284 us
  waiting for transfers between devices  183 us (64%)
  Pallas kernels  71.5 us (25%)
  local copies, waits for them, and re-layouts  15.6 us (5%)
  between operations  14.2 us (5%)
    all_gather x2, waiting for transfers between devices, gather(): lax.all_gather(rows, 'hid', axis=0, tiled=True, axis_index_groups=across)  103 us
    reduce_scatter x1, waiting for transfers between devices, per_device(): lax.psum_scatter(mine, 'hid', scatter_dimension=0, tiled=True, axis_index...  51.1 us
    pallas_call x1, Pallas kernels, forward(): pl.pallas_call(forward_kernel, grid=(width // step,), in_specs=[pl.BlockS...  19.8 us
    pallas_call x1, Pallas kernels, input_terms(): pl.pallas_call(input_kernel, grid=(depth // step,), in_specs=[held, held,...  19.7 us
    pallas_call x1, Pallas kernels, fisher(): pl.pallas_call(functools.partial(fisher_kernel, tile(width, 256)), grid=(...  18.7 us
    unnamed x18, local copies, waits for them, and re-layouts  15.6 us
    all_gather x2, waiting for transfers between devices, gather(): lax.all_gather(near, 'hid', axis=0, tiled=False, axis_index_groups=pairs)  13.7 us
    pallas_call x1, Pallas kernels, back(): pl.pallas_call(functools.partial(back_kernel, 2), grid=(width // step,),...  13.3 us
  transfers between devices with their start and end apart: 6, of which 5 were waited for; matrix products, arithmetic and copies ran while one was open for 0% of the time, Pallas kernels for 14%

profile of v1, /device:TPU:0, one launch (start us, length us, event | category | flops | bytes accessed | tf_op | source)
XLA Modules:
  0.0 284.4 jit_solution(6012304434567959375)
XLA Ops:
  7.2 0.7 all-gather.7.cloned.1.call-update
  7.9 0.0 all-gather.9.cloned.1.call-start
  7.9 0.7 all-gather.9.cloned.1.call-update
  8.6 0.0 all-gather.11.cloned.1.call-start
  8.7 53.4 %all-gather.7.cloned.1.call-done = bf16[256,4096]{1,0:T(8,128)(2,1)} async-done(((bf16[32,4096]{1,0:T(8,128)(2,1)}), bf16[256,4096]{1,0:T(8,128)(2,1)}) %all-gather.7.cloned.1.call-update) | async-done | bytes 2097168 | tf_op jit(solution)/shard_map/all_gather | solution.py:162
  62.2 0.0 all-gather.13.cloned.1.call-start
  62.2 49.9 %all-gather.9.cloned.1.call-done = bf16[256,4096]{1,0:T(8,128)(2,1)} async-done(((bf16[32,4096]{1,0:T(8,128)(2,1)}), bf16[256,4096]{1,0:T(8,128)(2,1)}) %all-gather.9.cloned.1.call-update) | async-done | bytes 2097168 | tf_op jit(solution)/shard_map/all_gather | solution.py:162
  112.1 0.0 reduce-scatter.3.cloned.1.call-start
  112.1 13.7 %all-gather.11.cloned.1.call-done.x_ref = bf16[512,4096]{1,0:T(8,128)(2,1)} async-done(((bf16[256,4096]{1,0:T(8,128)(2,1)}), bf16[512,4096]{1,0:T(8,128)(2,1)}) %all-gather.11.cloned.1.call-update) | async-done | bytes 4194320 | tf_op jit(solution)/shard_map/all_gather | solution.py:163
  125.8 2.2 copy-done.1
  128.0 19.8 %gate_up.1 = (f32[512,1792]{1,0:T(8,128)S(1)}, f32[512,1792]{1,0:T(8,128)S(1)}) custom-call(bf16[512,4096]{1,0:T(8,128)(2,1)S(1)} %copy-done.1, bf16[4096,1792]{1,0:T(8,128)(2,1)} %wg_ref.3, bf16[4096,1792]{1,0:T(8,128)(2,1)} %wu_ref.3), custom_call_target="tpu_custom_call" | custom-call | flops 15032385536 | bytes 29360128 | tf_op jit(solution)/shard_map/gate_up/pallas_call | solution.py:38
  147.9 1.8 copy-done.3
  149.7 1.8 copy-done.5
  151.5 2.0 copy-done.4
  153.6 2.0 copy-done.6
  155.6 13.3 %hidden_back.1 = (bf16[512,1792]{1,0:T(8,128)(2,1)S(1)}, bf16[512,1792]{1,0:T(8,128)(2,1)S(1)}) custom-call(bf16[512,4096]{1,0:T(8,128)(2,1)} %all-gather.13.cloned.1.call-done.dy_ref, bf16[1792,4096]{1,0:T(8,128)(2,1)} %wd_ref.1, f32[512,1792]{1,0:T(8,128)S(1)} %copy-done.4, f32[512,1792]{1,0:T(8,128)S(1)} %copy-done.6), custom_call_target="tpu_custom_call" | custom-call | flops 7516192768 | bytes 14680064 | tf_op jit(solution)/shard_map/hidden_back/pallas_call | solution.py:71
  169.0 19.7 %input_terms.1 = bf16[512,4096]{1,0:T(8,128)(2,1)S(1)} custom-call(bf16[512,1792]{1,0:T(8,128)(2,1)S(1)} %get-tuple-element.11.gg_ref, bf16[512,1792]{1,0:T(8,128)(2,1)S(1)} %get-tuple-element.12.gu_ref, bf16[4096,1792]{1,0:T(8,128)(2,1)} %wg_ref.3, bf16[4096,1792]{1,0:T(8,128)(2,1)} %wu_ref.3), custom_call_target="tpu_custom_call" | custom-call | flops 15032385536 | bytes 29360128 | tf_op jit(solution)/shard_map/input_terms/pallas_call | solution.py:99
  188.7 2.0 copy-done
  190.7 0.0 reduce-scatter.5.cloned.1.call-start
  190.8 13.3 %reduce-scatter.3.cloned.1.call-done = bf16[1,256,4096]{2,1,0:T(8,128)(2,1)} async-done(((bf16[2,256,4096]{2,1,0:T(8,128)(2,1)}), bf16[1,256,4096]{2,1,0:T(8,128)(2,1)}) %reduce-scatter.3.cloned.1.call-update) | async-done | bytes 2097168 | tf_op jit(solution)/shard_map/reduce_scatter | solution.py:170
  204.1 2.2 copy-done.2
  206.3 1.5 copy-done.8
  207.8 18.7 %fisher.1 = (bf16[4096,1792]{1,0:T(8,128)(2,1)}, bf16[4096,1792]{1,0:T(8,128)(2,1)}) custom-call(bf16[512,4096]{1,0:T(8,128)(2,1)S(1)} %copy-done.2, bf16[512,1792]{1,0:T(8,128)(2,1)S(1)} %get-tuple-element.11.gg_ref, bf16[512,1792]{1,0:T(8,128)(2,1)S(1)} %copy-done.8), custom_call_target="tpu_custom_call" | custom-call | flops 15032385536 | bytes 29360128 | tf_op jit(solution)/shard_map/fisher/pallas_call | solution.py:143
  226.5 51.1 %reduce-scatter.5.cloned.1.call-done = bf16[32,4096]{1,0:T(8,128)(2,1)} async-done(((bf16[256,4096]{1,0:T(8,128)(2,1)}), bf16[32,4096]{1,0:T(8,128)(2,1)}) %reduce-scatter.5.cloned.1.call-update) | async-done | bytes 262160 | tf_op jit(solution)/shard_map/reduce_scatter | solution.py:173
  (16 shorter events, 0.1 us)
Async XLA Ops:
  7.2 55.0 %all-gather.7.cloned.1.call-start = ((), (), s32[]{:S(2)}) async-start(), calls=%async_computation.2 | async-start | bytes 2359296 | tf_op jit(solution)/shard_map/all_gather | solution.py:162
  7.9 104.2 %all-gather.9.cloned.1.call-start = ((), (), s32[]{:S(2)}) async-start(), calls=%async_computation.3 | async-start | bytes 2359296 | tf_op jit(solution)/shard_map/all_gather | solution.py:162
  8.6 117.2 %all-gather.11.cloned.1.call-start = ((), (), s32[]{:S(2)}) async-start(), calls=%async_computation.6 | async-start | bytes 6291456 | tf_op jit(solution)/shard_map/all_gather | solution.py:163
  62.2 89.4 %all-gather.13.cloned.1.call-start = ((), (), s32[]{:S(2)}) async-start(), calls=%async_computation.7 | async-start | bytes 6291456 | tf_op jit(solution)/shard_map/all_gather | solution.py:163
  112.1 92.0 %reduce-scatter.3.cloned.1.call-start = ((), (), s32[]{:S(2)}) async-start(), calls=%async_computation.4 | async-start | bytes 6291456 | tf_op jit(solution)/shard_map/reduce_scatter | solution.py:170
  125.8 2.2 copy-start.1
  147.8 1.8 copy-start.3
  149.7 1.8 copy-start.5
  151.5 2.0 copy-start.4
  153.6 2.0 copy-start.6
  169.0 19.7 %copy-start.7 = (bf16[512,1792]{1,0:T(8,128)(2,1)}, bf16[512,1792]{1,0:T(8,128)(2,1)S(1)}, u32[]{:S(2)}) copy-start(bf16[512,1792]{1,0:T(8,128)(2,1)S(1)} %get-tuple-element.12.gu_ref) | copy-start | bytes 5505028
  188.7 2.0 copy-start
  190.7 86.9 %reduce-scatter.5.cloned.1.call-start = ((), (), s32[]{:S(2)}) async-start(), calls=%async_computation.5 | async-start | bytes 2359296 | tf_op jit(solution)/shard_map/reduce_scatter | solution.py:173
  204.1 2.2 copy-start.2
  206.3 1.5 copy-start.8
Sparse Core Ops, SparseCore 0:
  10.1 51.9 all-gather.6
  64.3 47.7 all-gather.8
  113.6 12.1 all-gather.10
  127.2 14.8 all-gather.12
  190.8 13.1 reduce-scatter.2
  208.4 69.0 reduce-scatter.4

commit v2 on v1

--- a/solution.py
+++ b/solution.py
@@ -9,8 +9,10 @@
 
 SEQS = 2
 MIB = 1 << 20
+CYCLE = (0, 2, 4, 6, 7, 5, 3, 1)
 NT = (((1,), (1,)), ((), ()))
-TN = (((0,), (0,)), ((), ()))
+BF16 = jnp.bfloat16
+F32 = jnp.float32
 
 
 def tile(size, want):
@@ -25,18 +27,294 @@
     return pl.CostEstimate(flops=flops, bytes_accessed=read, transcendentals=0)
 
 
-def forward_kernel(x_ref, wg_ref, wu_ref, gate_ref, up_ref):
+def silu_grads(hidden, gate, up):
+    sigma = jax.nn.sigmoid(gate)
+    both = hidden * sigma
+    gg = both * up * (1.0 + gate * (1.0 - sigma))
+    return gg.astype(BF16), (both * gate).astype(BF16)
+
+
+def forward_kernel(near_ref, far_ref, wg_ref, wu_ref, wd_ref, *rest):
+    gg_ref, gu_ref = rest[-2:]
+    half = near_ref.shape[0] // 2
+    x = jnp.concatenate([near_ref[:half, :], far_ref[:half, :]], axis=0)
+    dy = jnp.concatenate([near_ref[half:, :], far_ref[half:, :]], axis=0)
+    gate = jnp.dot(x, wg_ref[...], preferred_element_type=F32)
+    up = jnp.dot(x, wu_ref[...], preferred_element_type=F32)
+    hidden = lax.dot_general(dy, wd_ref[...], NT, preferred_element_type=F32)
+    gg_ref[...], gu_ref[...] = silu_grads(hidden, gate, up)
+
+
+def forward(near, far, wg, wu, wd, first, count, step, held=(), after=()):
+    rows, depth = near.shape
+    width = wg.shape[1]
+    whole = pl.BlockSpec((rows, depth), lambda j: (0, 0))
+    column = pl.BlockSpec((depth, step), lambda j: (0, first + j))
+    out = pl.BlockSpec((rows, step), lambda j: (0, first + j))
+    return pl.pallas_call(
+        forward_kernel,
+        grid=(count,),
+        in_specs=[
+            whole,
+            whole,
+            column,
+            column,
+            pl.BlockSpec((step, depth), lambda j: (first + j, 0)),
+        ]
+        + [pl.BlockSpec(memory_space=pl.ANY)] * len((*held, *after)),
+        out_specs=[out, out],
+        out_shape=[jax.ShapeDtypeStruct((rows, width), BF16)] * 2,
+        input_output_aliases={5 + i: i for i in range(len(held))},
+        compiler_params=params(56),
+        cost_estimate=cost(6 * rows * depth * count * step, 6 * depth * count * step),
+        name="forward",
+    )(near, far, wg, wu, wd, *held, *after)
+
+
+def input_kernel(gg_ref, gu_ref, wg_ref, wu_ref, *rest):
+    own_ref, far_ref = rest[-2:]
+    total = lax.dot_general(gg_ref[...], wg_ref[...], NT, preferred_element_type=F32)
+    total += lax.dot_general(gu_ref[...], wu_ref[...], NT, preferred_element_type=F32)
+    half = own_ref.shape[0]
+    own_ref[...] = total[:half, :]
+    far_ref[...] = total[half:, :].astype(BF16)
+
+
+def input_terms(gg, gu, wg, wu, first, count, step, held=(), after=()):
+    rows, width = gg.shape
+    depth = wg.shape[0]
+    whole = pl.BlockSpec((rows, width), lambda j: (0, 0))
+    weight = pl.BlockSpec((step, width), lambda j: (first + j, 0))
+    out = pl.BlockSpec((rows // 2, step), lambda j: (0, first + j))
+    return pl.pallas_call(
+        input_kernel,
+        grid=(count,),
+        in_specs=[whole, whole, weight, weight]
+        + [pl.BlockSpec(memory_space=pl.ANY)] * len((*held, *after)),
+        out_specs=[out, out],
+        out_shape=[
+            jax.ShapeDtypeStruct((rows // 2, depth), F32),
+            jax.ShapeDtypeStruct((rows // 2, depth), BF16),
+        ],
+        input_output_aliases={4 + i: i for i in range(len(held))},
+        compiler_params=params(56),
+        cost_estimate=cost(4 * rows * width * count * step, 4 * width * count * step),
+        name="input_terms",
+    )(gg, gu, wg, wu, *held, *after)
+
+
+def fisher_kernel(step, row, at_ref, *refs):
+    xs, gates, ups = refs[:4], refs[4:6], refs[6:8]
+    fg_ref, fu_ref = refs[-2:]
+    spots = at_ref.shape[0] // SEQS
+    width = fg_ref.shape[1]
+
+    def pick(pieces, q, at):
+        blocks = []
+        for ref, base in pieces:
+            for i in range(spots):
+                start = pl.multiple_of(base + at_ref[q * spots + i] * row, row)
+                blocks.append(ref[pl.ds(start, row), at])
+        return jnp.concatenate(blocks, axis=0)
+
+    lots = [[(x, 0) for x in xs]]
+    for chunks in (gates, ups):
+        lots.append([(g, h * g.shape[0] // 2) for g in chunks for h in range(2)])
+    cols = [pick(lots[0], q, slice(None)).T for q in range(SEQS)]
+    for lot, f_ref in ((lots[1], fg_ref), (lots[2], fu_ref)):
+        for c in range(width // step):
+            at = pl.ds(c * step, step)
+            total = None
+            for q in range(SEQS):
+                seq = jnp.dot(cols[q], pick(lot, q, at), preferred_element_type=F32)
+                total = seq * seq if total is None else total + seq * seq
+            f_ref[:, at] = (total * (1.0 / SEQS)).astype(BF16)
+
+
+def fisher(at, xs, gates, ups, row, first, count, step, held=(), after=()):
+    rows, depth = xs[0].shape
+    held_rows, width = gates[0].shape
+    x_spec = pl.BlockSpec((rows // 2, step), lambda j, _: (0, first + j))
+    g_spec = pl.BlockSpec((held_rows, width), lambda j, _: (0, 0))
+    out = pl.BlockSpec((step, width), lambda j, _: (first + j, 0))
+    flops = 8 * held_rows * width * count * step
+    return pl.pallas_call(
+        functools.partial(fisher_kernel, tile(width, 256), row),
+        grid_spec=pltpu.PrefetchScalarGridSpec(
+            num_scalar_prefetch=1,
+            grid=(count,),
+            in_specs=[x_spec] * 4
+            + [g_spec] * 4
+            + [pl.BlockSpec(memory_space=pl.ANY)] * len((*held, *after)),
+            out_specs=[out, out],
+        ),
+        out_shape=[jax.ShapeDtypeStruct((depth, width), BF16)] * 2,
+        input_output_aliases={9 + i: i for i in range(len(held))},
+        compiler_params=params(56),
+        cost_estimate=cost(flops, 4 * width * count * step),
+        name="fisher",
+    )(at, *xs, *gates, *ups, *held, *after)
+
+
+def split_kernel(row, at, tokens_ref, grad_ref, *rest):
+    x_ref, dy_ref = rest[-2:]
+    x_ref[...] = tokens_ref[pl.ds(at, row), :]
+    dy_ref[...] = grad_ref[pl.ds(at, row), :]
+
+
+def split(tokens, grad_out, row, at, after=()):
+    whole = pl.BlockSpec(memory_space=pltpu.VMEM)
+    return pl.pallas_call(
+        functools.partial(split_kernel, row, at),
+        in_specs=[whole, whole] + [pl.BlockSpec(memory_space=pl.ANY)] * len(after),
+        out_specs=[whole, whole],
+        out_shape=[jax.ShapeDtypeStruct((row, tokens.shape[1]), BF16)] * 2,
+        compiler_params=params(32),
+        cost_estimate=cost(0, 4 * row * tokens.shape[1]),
+        name="split",
+    )(tokens, grad_out, *after)
+
+
+def pack_kernel(*refs):
+    pieces, out_ref, sems = refs[:-2], refs[-2], refs[-1]
+    row = pieces[0].shape[0]
+    copies = [
+        pltpu.make_async_copy(piece, out_ref.at[pl.ds(i * row, row), :], sems.at[i])
+        for i, piece in enumerate(pieces)
+    ]
+    for copy in copies:
+        copy.start()
+    for copy in copies:
+        copy.wait()
+
+
+def pack(pieces):
+    row, depth = pieces[0].shape
+    whole = pl.BlockSpec(memory_space=pl.ANY)
+    return pl.pallas_call(
+        pack_kernel,
+        in_specs=[whole] * len(pieces),
+        out_specs=whole,
+        out_shape=jax.ShapeDtypeStruct((row * len(pieces), depth), BF16),
+        scratch_shapes=[pltpu.SemaphoreType.DMA((len(pieces),))],
+        compiler_params=params(56),
+        cost_estimate=cost(0, 4 * row * len(pieces) * depth),
+        name="pack",
+    )(*pieces)
+
+
+def ring_part(tokens, grad_out, wg, wu, wd):
+    chips = len(CYCLE)
+    far = chips // 2
+    block, depth = tokens.shape
+    width = wg.shape[1]
+    row = block // 2
+    links = [(CYCLE[i], CYCLE[(i + 1) % chips]) for i in range(chips)]
+    to_right = [(2 * a + c, 2 * b + c) for a, b in links for c in range(2)]
+    to_left = [(b, a) for a, b in to_right]
+    across = [(2 * i + c, 2 * i + 1 - c) for i in range(chips) for c in range(2)]
+
+    def right(value):
+        return lax.ppermute(value, "hid", to_right)
+
+    def left(value):
+        return lax.ppermute(value, "hid", to_left)
+
+    def swap(value):
+        return lax.ppermute(value, "hid", across)
+
+    def gather(x, dy):
+        by = [[x] + [None] * (chips - 1), [dy] + [None] * (chips - 1)]
+        rounds = []
+        for k in range(1, far + 1):
+            got = []
+            for s in range(2):
+                if k < far or s == 0:
+                    by[s][k] = right(by[s][k - 1])
+                    got.append(by[s][k])
+                if k < far or s == 1:
+                    by[s][chips - k] = left(by[s][(chips - k + 1) % chips])
+                    got.append(by[s][chips - k])
+            rounds.append(got)
+        return by[0] + by[1], rounds
+
+    def scatter(own, near, right_far):
+        def base(p):
+            at = slice(p * row, (p + 1) * row)
+            return own[at] + near[at].astype(F32)
+
+        def plus(p, got):
+            return base(p) if got is None else base(p) + got.astype(F32)
+
+        rounds = []
+        r = l = None
+        for k in range(far, 0, -1):
+            got = []
+            if k < far or right_far:
+                r = right(plus(chips - k, r).astype(BF16))
+                got.append(r)
+            if k < far or not right_far:
+                l = left(plus(k, l).astype(BF16))
+                got.append(l)
+            rounds.append(got)
+        return plus(0, r) + l.astype(F32), rounds
+
+    step = tile(width, 256)
+    tiles = width // step
+    cuts = [0, tiles // 3, 2 * (tiles // 3), tiles] if tiles > 2 else [0, tiles]
+    lots = list(zip(cuts, cuts[1:]))
+    deep = depth // 512
+
+    def compute(near, away, waits):
+        waits = list(waits) + [()] * (len(lots) + 2 - len(waits))
+        held = ()
+        for a, b in lots:
+            held = forward(near, away, wg, wu, wd, a, b - a, step, held, waits.pop(0))
+        gg, gu = held
+        held = input_terms(gg, gu, wg, wu, 0, deep // 2, 512, (), waits.pop(0))
+        own, sent = input_terms(gg, gu, wg, wu, deep // 2, deep // 2, 512, held, waits.pop(0))
+        return gg, gu, own, swap(sent)
+
+    pieces, rounds = gather(*split(tokens, grad_out, row, 0))
+    near_a = pack(pieces)
+    pieces, waits = gather(*split(tokens, grad_out, row, row, rounds[far - 2]))
+    near_b = pack(pieces)
+    away_a = swap(near_a)
+    away_b = swap(near_b)
+    gg_a, gu_a, own, got = compute(near_a, away_a, [()] + waits[:-1] + [(near_b,)])
+    mine_a, waits = scatter(own, got, True)
+    gg_b, gu_b, own, got_b = compute(near_b, away_b, [(), (got,)] + waits[:-1])
+    mine_b, more = scatter(own, got_b, False)
+
+    spot = [0] * chips
+    for i, c in enumerate(CYCLE):
+        spot[c] = i
+    me = jnp.array(spot, jnp.int32)[lax.axis_index("hid") // 2]
+    at = (me - jnp.array(spot, jnp.int32)) % chips
+    xs = [near_a, away_a, near_b, away_b]
+    waits = [waits[-1], (got_b,)] + more[:-1]
+    held = ()
+    first = 0
+    for i, wait in enumerate(waits):
+        count = (deep - first) // (len(waits) - i)
+        held = fisher(at, xs, (gg_a, gg_b), (gu_a, gu_b), row, first, count, 512, held, wait)
+        first += count
+    mine = jnp.concatenate([mine_a, mine_b], axis=0).astype(BF16)
+    return held[0], held[1], mine
+
+
+def plain_forward_kernel(x_ref, wg_ref, wu_ref, gate_ref, up_ref):
     x = x_ref[...]
     gate_ref[...] = jnp.dot(x, wg_ref[...], preferred_element_type=jnp.float32)
     up_ref[...] = jnp.dot(x, wu_ref[...], preferred_element_type=jnp.float32)
 
 
-def forward(x, wg, wu):
+def plain_forward(x, wg, wu):
     rows, depth = x.shape
     width = wg.shape[1]
     step = tile(width, 256)
     return pl.pallas_call(
-        forward_kernel,
+        plain_forward_kernel,
         grid=(width // step,),
         in_specs=[
             pl.BlockSpec((rows, depth), lambda j: (0, 0)),
@@ -51,7 +329,7 @@
     )(x, wg, wu)
 
 
-def back_kernel(parts, dy_ref, wd_ref, gate_ref, up_ref, gg_ref, gu_ref):
+def plain_back_kernel(parts, dy_ref, wd_ref, gate_ref, up_ref, gg_ref, gu_ref):
     rows = dy_ref.shape[0] // parts
     for p in range(parts):
         at = pl.ds(p * rows, rows)
@@ -63,13 +341,13 @@
         gu_ref[at, :] = (both * gate).astype(jnp.bfloat16)
 
 
-def back(dy, wd, gate, up):
+def plain_back(dy, wd, gate, up):
     rows, depth = dy.shape
     width = wd.shape[0]
     step = tile(width, 256)
     column = pl.BlockSpec((rows, step), lambda j: (0, j))
     return pl.pallas_call(
-        functools.partial(back_kernel, 2),
+        functools.partial(plain_back_kernel, 2),
         grid=(width // step,),
         in_specs=[
             pl.BlockSpec((rows, depth), lambda j: (0, 0)),
@@ -85,19 +363,19 @@
     )(dy, wd, gate, up)
 
 
-def input_kernel(gg_ref, gu_ref, wg_ref, wu_ref, out_ref):
+def plain_input_kernel(gg_ref, gu_ref, wg_ref, wu_ref, out_ref):
     total = lax.dot_general(gg_ref[...], wg_ref[...], NT, preferred_element_type=jnp.float32)
     total += lax.dot_general(gu_ref[...], wu_ref[...], NT, preferred_element_type=jnp.float32)
     out_ref[...] = total.astype(jnp.bfloat16)
 
 
-def input_terms(gg, gu, wg, wu):
+def plain_input_terms(gg, gu, wg, wu):
     rows, width = gg.shape
     depth = wg.shape[0]
     step = 512
     held = pl.BlockSpec((rows, width), lambda j: (0, 0))
     return pl.pallas_call(
-        input_kernel,
+        plain_input_kernel,
         grid=(depth // step,),
         in_specs=[
             held,
@@ -113,7 +391,7 @@
     )(gg, gu, wg, wu)
 
 
-def fisher_kernel(step, x_ref, gg_ref, gu_ref, fg_ref, fu_ref):
+def plain_fisher_kernel(step, x_ref, gg_ref, gu_ref, fg_ref, fu_ref):
     half = x_ref.shape[0] // 2
     span = half // SEQS
     width = gg_ref.shape[1]
@@ -134,14 +412,14 @@
             f_ref[:, at] = (total * (1.0 / SEQS)).astype(jnp.bfloat16)
 
 
-def fisher(x, gg, gu):
+def plain_fisher(x, gg, gu):
     rows, depth = x.shape
     width = gg.shape[1]
     step = 512
     held = pl.BlockSpec((rows, width), lambda j: (0, 0))
     block = pl.BlockSpec((step, width), lambda j: (j, 0))
     return pl.pallas_call(
-        functools.partial(fisher_kernel, tile(width, 256)),
+        functools.partial(plain_fisher_kernel, tile(width, 256)),
         grid=(depth // step,),
         in_specs=[pl.BlockSpec((rows, step), lambda j: (0, j)), held, held],
         out_specs=[block, block],
@@ -152,7 +430,7 @@
     )(x, gg, gu)
 
 
-def per_device(size, tokens, grad_out, wg, wu, wd):
+def plain_part(size, tokens, grad_out, wg, wu, wd):
     chips = size // 2
     across = [[2 * i + c for i in range(chips)] for c in range(2)]
     pairs = [[2 * i, 2 * i + 1] for i in range(chips)]
@@ -164,17 +442,23 @@
 
     x = gather(tokens).reshape(-1, depth)
     dy = gather(grad_out).reshape(-1, depth)
-    gate, up = forward(x, wg, wu)
-    gg, gu = back(dy, wd, gate, up)
-    terms = input_terms(gg, gu, wg, wu).reshape(2, -1, depth)
+    gate, up = plain_forward(x, wg, wu)
+    gg, gu = plain_back(dy, wd, gate, up)
+    terms = plain_input_terms(gg, gu, wg, wu).reshape(2, -1, depth)
     mine = lax.psum_scatter(
         terms, "hid", scatter_dimension=0, tiled=False, axis_index_groups=pairs
     )
     mine = lax.psum_scatter(
         mine, "hid", scatter_dimension=0, tiled=True, axis_index_groups=across
     )
-    fg, fu = fisher(x, gg, gu)
+    fg, fu = plain_fisher(x, gg, gu)
     return fg, fu, mine
+
+
+def per_device(size, tokens, grad_out, wg, wu, wd):
+    if size == 2 * len(CYCLE) and tokens.shape[0] % 32 == 0:
+        return ring_part(tokens, grad_out, wg, wu, wd)
+    return plain_part(size, tokens, grad_out, wg, wu, wd)
 
 
 def solution(mesh):

time: 285 us -> 355 us (1.25)
  Pallas kernels: 71.5 us -> 268 us
  waiting for transfers between devices: 183 us -> 23.3 us
  starting transfers between devices: 0.23 us -> 45.2 us
  between operations: 14.2 us -> 1.35 us
  other arithmetic: 0 us -> 5.65 us
  local copies, waits for them, and re-layouts: 15.6 us -> 10.6 us
    pallas_call x4 -> x19, Pallas kernels: 71.5 us -> 268 us  [the longest x2 130 us: pack(): pl.pallas_call(pack_kernel, in_specs=[whole] * len(pieces), out_specs=who...]
    all_gather x4 -> x0, waiting for transfers between devices: 117 us -> none  [the longest x2 103 us: gather(): lax.all_gather(rows, 'hid', axis=0, tiled=True, axis_index_groups=across)]
    reduce_scatter x2 -> x0, waiting for transfers between devices: 64.4 us -> none  [the longest x1 51.1 us: per_device(): lax.psum_scatter(mine, 'hid', scatter_dimension=0, tiled=True, axis_index...]
    ppermute x0 -> x46, starting transfers between devices: none -> 45.2 us  [the longest x21 35 us: right(): return lax.ppermute(value, 'hid', to_right)]
    ppermute x0 -> x46, waiting for transfers between devices: none -> 23.3 us  [the longest x21 15.7 us: left(): return lax.ppermute(value, 'hid', to_left)]
    unnamed x18 -> x122, local copies, waits for them, and re-layouts: 15.6 us -> 10 us
  transfers between devices with their start and end apart: 6 -> 46, of which waited for: 5 -> 14; matrix products, arithmetic and copies ran while one was open for 0% -> 1% of each run, Pallas kernels for 14% -> 57%
where the time goes in v2:
time: 355 us; the launch traced here: 354 us
  Pallas kernels  268 us (75%)
  starting transfers between devices  45.2 us (13%)
  waiting for transfers between devices  23.3 us (7%)
  local copies, waits for them, and re-layouts  10.6 us (3%)
  other arithmetic  5.65 us (2%)
    pallas_call x2, Pallas kernels, pack(): pl.pallas_call(pack_kernel, in_specs=[whole] * len(pieces), out_specs=who...  130 us
    pallas_call x6, Pallas kernels, forward(): pl.pallas_call(forward_kernel, grid=(count,), in_specs=[whole, whole, col...  62.3 us
    pallas_call x5, Pallas kernels, fisher(): pl.pallas_call(functools.partial(fisher_kernel, tile(width, 256), row), g...  39.6 us
    pallas_call x4, Pallas kernels, input_terms(): pl.pallas_call(input_kernel, grid=(count,), in_specs=[whole, whole, weigh...  36.9 us
    ppermute x21, starting transfers between devices, right(): return lax.ppermute(value, 'hid', to_right)  35 us
    ppermute x21, waiting for transfers between devices, left(): return lax.ppermute(value, 'hid', to_left)  15.7 us
    unnamed x122, local copies, waits for them, and re-layouts  10 us
    ppermute x21, starting transfers between devices, left(): return lax.ppermute(value, 'hid', to_left)  9.57 us
  transfers between devices with their start and end apart: 46, of which 14 were waited for; matrix products, arithmetic and copies ran while one was open for 1% of the time, Pallas kernels for 57%

profile of v2, /device:TPU:0, one launch (start us, length us, event | category | flops | bytes accessed | tf_op | source)
XLA Modules:
  0.0 354.4 jit_solution(3647065775410731717)
XLA Ops:
  2.6 3.1 collective-permute-start
  9.6 2.5 collective-permute-start.1
  12.1 2.6 collective-permute-done.4.refs_7_
  18.7 2.2 collective-permute-done.5.refs_6_
  30.5 64.8 %pack.2.near_ref.refs_0_ = bf16[256,4096]{1,0:T(8,128)(2,1)} custom-call(bf16[16,4096]{1,0:T(8,128)(2,1)} %copy-done.14, bf16[16,4096]{1,0:T(8,128)(2,1)} %copy-done.47, bf16[16,4096]{1,0:T(8,128)(2,1)} %copy-done.51, bf16[16,4096]{1,0:T(8,128)(2,1)} %copy-done.4, bf16[16,4096]{1,0:T(8,128)(2,1)} %copy-done.55, bf16[16,4096]{1,0:T(8,128)(2,1)} %copy-done.8, ...), custom_call_target="tpu_custom_call" | custom-call | bytes 4194304 | tf_op jit(solution)/shard_map/pack/pallas_call | solution.py:194
  103.2 2.2 collective-permute-done.15.refs_1_.rest_2_
  113.6 2.2 collective-permute-done.20.refs_6_.rest_3_
  119.9 2.1 collective-permute-done.21.refs_5_.rest_1_
  125.3 64.8 %pack.3.near_ref.rest_2_.refs_2_ = bf16[256,4096]{1,0:T(8,128)(2,1)} custom-call(bf16[16,4096]{1,0:T(8,128)(2,1)} %copy-done.12, bf16[16,4096]{1,0:T(8,128)(2,1)} %copy-done.23, bf16[16,4096]{1,0:T(8,128)(2,1)} %copy-done.27, bf16[16,4096]{1,0:T(8,128)(2,1)} %copy-done.31, bf16[16,4096]{1,0:T(8,128)(2,1)} %copy-done.57, bf16[16,4096]{1,0:T(8,128)(2,1)} %copy-done.33, ...), custom_call_target="tpu_custom_call" | custom-call | bytes 4194304 | tf_op jit(solution)/shard_map/pack/pallas_call | solution.py:194
  191.5 9.2 %forward.6 = (bf16[256,1792]{1,0:T(8,128)(2,1)}, bf16[256,1792]{1,0:T(8,128)(2,1)}) custom-call(bf16[256,4096]{1,0:T(8,128)(2,1)} %pack.2.near_ref.refs_0_, bf16[256,4096]{1,0:T(8,128)(2,1)} %copy-done.16, bf16[4096,1792]{1,0:T(8,128)(2,1)} %wg_ref.19, bf16[4096,1792]{1,0:T(8,128)(2,1)} %wu_ref.19, bf16[1792,4096]{1,0:T(8,128)(2,1)} %wd_ref.11), custom_call_target="tpu_custom_call" | custom-call | flops 3221225472 | bytes 12582912 | tf_op jit(solution)/shard_map/forward/pallas_call | solution.py:54
  200.6 9.7 %forward.7 = (bf16[256,1792]{1,0:T(8,128)(2,1)}, bf16[256,1792]{1,0:T(8,128)(2,1)}) custom-call(bf16[256,4096]{1,0:T(8,128)(2,1)} %pack.2.near_ref.refs_0_, bf16[256,4096]{1,0:T(8,128)(2,1)} %copy-done.16, bf16[4096,1792]{1,0:T(8,128)(2,1)} %wg_ref.19, bf16[4096,1792]{1,0:T(8,128)(2,1)} %wu_ref.19, ...), custom_call_target="tpu_custom_call", output_to_operand_aliasing={{0}: (5, {}), {1}: (6, {})} | custom-call | flops 3221225472 | bytes 12582912 | tf_op jit(solution)/shard_map/forward/pallas_call | solution.py:54
  210.4 12.2 %forward.8 = (bf16[256,1792]{1,0:T(8,128)(2,1)}, bf16[256,1792]{1,0:T(8,128)(2,1)}) custom-call(bf16[256,4096]{1,0:T(8,128)(2,1)} %pack.2.near_ref.refs_0_, bf16[256,4096]{1,0:T(8,128)(2,1)} %copy-done.16, bf16[4096,1792]{1,0:T(8,128)(2,1)} %wg_ref.19, bf16[4096,1792]{1,0:T(8,128)(2,1)} %wu_ref.19, ...), custom_call_target="tpu_custom_call", output_to_operand_aliasing={{0}: (5, {}), {1}: (6, {})} | custom-call | flops 4831838208 | bytes 18874368 | tf_op jit(solution)/shard_map/forward/pallas_call | solution.py:54
  222.6 9.2 %input_terms.4 = (f32[128,4096]{1,0:T(8,128)}, bf16[128,4096]{1,0:T(8,128)(2,1)}) custom-call(bf16[256,1792]{1,0:T(8,128)(2,1)} %get-tuple-element.45.gg_ref.refs_4_, bf16[256,1792]{1,0:T(8,128)(2,1)} %get-tuple-element.48.gu_ref.refs_6_, bf16[4096,1792]{1,0:T(8,128)(2,1)} %wg_ref.19, bf16[4096,1792]{1,0:T(8,128)(2,1)} %wu_ref.19, ...), custom_call_target="tpu_custom_call" | custom-call | flops 3758096384 | bytes 14680064 | tf_op jit(solution)/shard_map/input_terms/pallas_call | solution.py:89
  231.7 9.2 %input_terms.5 = (f32[128,4096]{1,0:T(8,128)}, bf16[128,4096]{1,0:T(8,128)(2,1)}) custom-call(bf16[256,1792]{1,0:T(8,128)(2,1)} %get-tuple-element.45.gg_ref.refs_4_, bf16[256,1792]{1,0:T(8,128)(2,1)} %get-tuple-element.48.gu_ref.refs_6_, bf16[4096,1792]{1,0:T(8,128)(2,1)} %wg_ref.19, ...), custom_call_target="tpu_custom_call", output_to_operand_aliasing={{0}: (4, {}), {1}: (5, {})} | custom-call | flops 3758096384 | bytes 14680064 | tf_op jit(solution)/shard_map/input_terms/pallas_call | solution.py:89
  245.5 9.2 %forward.9 = (bf16[256,1792]{1,0:T(8,128)(2,1)}, bf16[256,1792]{1,0:T(8,128)(2,1)}) custom-call(bf16[256,4096]{1,0:T(8,128)(2,1)} %pack.3.near_ref.rest_2_.refs_2_, bf16[256,4096]{1,0:T(8,128)(2,1)} %collective-permute-done.29.far_ref.refs_3_, bf16[4096,1792]{1,0:T(8,128)(2,1)} %wg_ref.19, bf16[4096,1792]{1,0:T(8,128)(2,1)} %wu_ref.19, ...), custom_call_target="tpu_custom_call" | custom-call | flops 3221225472 | bytes 12582912 | tf_op jit(solution)/shard_map/forward/pallas_call | solution.py:54
  257.0 9.8 %forward.10 = (bf16[256,1792]{1,0:T(8,128)(2,1)}, bf16[256,1792]{1,0:T(8,128)(2,1)}) custom-call(bf16[256,4096]{1,0:T(8,128)(2,1)} %pack.3.near_ref.rest_2_.refs_2_, bf16[256,4096]{1,0:T(8,128)(2,1)} %collective-permute-done.29.far_ref.refs_3_, bf16[4096,1792]{1,0:T(8,128)(2,1)} %wg_ref.19, ...), custom_call_target="tpu_custom_call", output_to_operand_aliasing={{0}: (5, {}), {1}: (6, {})} | custom-call | flops 3221225472 | bytes 12582912 | tf_op jit(solution)/shard_map/forward/pallas_call | solution.py:54
  269.0 12.2 %forward.11 = (bf16[256,1792]{1,0:T(8,128)(2,1)}, bf16[256,1792]{1,0:T(8,128)(2,1)}) custom-call(bf16[256,4096]{1,0:T(8,128)(2,1)} %pack.3.near_ref.rest_2_.refs_2_, bf16[256,4096]{1,0:T(8,128)(2,1)} %collective-permute-done.29.far_ref.refs_3_, bf16[4096,1792]{1,0:T(8,128)(2,1)} %wg_ref.19, ...), custom_call_target="tpu_custom_call", output_to_operand_aliasing={{0}: (5, {}), {1}: (6, {})} | custom-call | flops 4831838208 | bytes 18874368 | tf_op jit(solution)/shard_map/forward/pallas_call | solution.py:54
  282.9 9.2 %input_terms.6 = (f32[128,4096]{1,0:T(8,128)}, bf16[128,4096]{1,0:T(8,128)(2,1)}) custom-call(bf16[256,1792]{1,0:T(8,128)(2,1)} %get-tuple-element.55.refs_5_.gg_ref, bf16[256,1792]{1,0:T(8,128)(2,1)} %get-tuple-element.56.refs_7_.gu_ref, bf16[4096,1792]{1,0:T(8,128)(2,1)} %wg_ref.19, bf16[4096,1792]{1,0:T(8,128)(2,1)} %wu_ref.19, ...), custom_call_target="tpu_custom_call" | custom-call | flops 3758096384 | bytes 14680064 | tf_op jit(solution)/shard_map/input_terms/pallas_call | solution.py:89
  293.7 9.3 %input_terms.7 = (f32[128,4096]{1,0:T(8,128)}, bf16[128,4096]{1,0:T(8,128)(2,1)}) custom-call(bf16[256,1792]{1,0:T(8,128)(2,1)} %get-tuple-element.55.refs_5_.gg_ref, bf16[256,1792]{1,0:T(8,128)(2,1)} %get-tuple-element.56.refs_7_.gu_ref, bf16[4096,1792]{1,0:T(8,128)(2,1)} %wg_ref.19, ...), custom_call_target="tpu_custom_call", output_to_operand_aliasing={{0}: (4, {}), {1}: (5, {})} | custom-call | flops 3758096384 | bytes 14680064 | tf_op jit(solution)/shard_map/input_terms/pallas_call | solution.py:89
  304.4 6.5 %fisher.5 = (bf16[4096,1792]{1,0:T(8,128)(2,1)}, bf16[4096,1792]{1,0:T(8,128)(2,1)}) custom-call(s32[8]{0:T(128)} %and_select_fusion.at_ref, bf16[256,4096]{1,0:T(8,128)(2,1)} %pack.2.near_ref.refs_0_, bf16[256,4096]{1,0:T(8,128)(2,1)} %copy-done.16, bf16[256,4096]{1,0:T(8,128)(2,1)} %pack.3.near_ref.rest_2_.refs_2_, ...), custom_call_target="tpu_custom_call" | custom-call | flops 1879048192 | bytes 3670016 | tf_op jit(solution)/shard_map/fisher/pallas_call | solution.py:141
  312.9 6.5 %fisher.6 = (bf16[4096,1792]{1,0:T(8,128)(2,1)}, bf16[4096,1792]{1,0:T(8,128)(2,1)}) custom-call(s32[8]{0:T(128)} %and_select_fusion.at_ref, bf16[256,4096]{1,0:T(8,128)(2,1)} %pack.2.near_ref.refs_0_, bf16[256,4096]{1,0:T(8,128)(2,1)} %copy-done.16, bf16[256,4096]{1,0:T(8,128)(2,1)} %pack.3.near_ref.rest_2_.refs_2_, ...), custom_call_target="tpu_custom_call", output_to_operand_aliasing={{0}: (9, {}), {1}: (10, {})} | custom-call | flops 1879048192 | bytes 3670016 | tf_op jit(solution)/shard_map/fisher/pallas_call | solution.py:141
  322.6 8.9 %fisher.7 = (bf16[4096,1792]{1,0:T(8,128)(2,1)}, bf16[4096,1792]{1,0:T(8,128)(2,1)}) custom-call(s32[8]{0:T(128)} %and_select_fusion.at_ref, bf16[256,4096]{1,0:T(8,128)(2,1)} %pack.2.near_ref.refs_0_, bf16[256,4096]{1,0:T(8,128)(2,1)} %copy-done.16, bf16[256,4096]{1,0:T(8,128)(2,1)} %pack.3.near_ref.rest_2_.refs_2_, ...), custom_call_target="tpu_custom_call", output_to_operand_aliasing={{0}: (9, {}), {1}: (10, {})} | custom-call | flops 3758096384 | bytes 7340032 | tf_op jit(solution)/shard_map/fisher/pallas_call | solution.py:141
  333.8 8.8 %fisher.8 = (bf16[4096,1792]{1,0:T(8,128)(2,1)}, bf16[4096,1792]{1,0:T(8,128)(2,1)}) custom-call(s32[8]{0:T(128)} %and_select_fusion.at_ref, bf16[256,4096]{1,0:T(8,128)(2,1)} %pack.2.near_ref.refs_0_, bf16[256,4096]{1,0:T(8,128)(2,1)} %copy-done.16, bf16[256,4096]{1,0:T(8,128)(2,1)} %pack.3.near_ref.rest_2_.refs_2_, ...), custom_call_target="tpu_custom_call", output_to_operand_aliasing={{0}: (9, {}), {1}: (10, {})} | custom-call | flops 3758096384 | bytes 7340032 | tf_op jit(solution)/shard_map/fisher/pallas_call | solution.py:141
  344.8 8.8 %fisher.9 = (bf16[4096,1792]{1,0:T(8,128)(2,1)}, bf16[4096,1792]{1,0:T(8,128)(2,1)}) custom-call(s32[8]{0:T(128)} %and_select_fusion.at_ref, bf16[256,4096]{1,0:T(8,128)(2,1)} %pack.2.near_ref.refs_0_, bf16[256,4096]{1,0:T(8,128)(2,1)} %copy-done.16, bf16[256,4096]{1,0:T(8,128)(2,1)} %pack.3.near_ref.rest_2_.refs_2_, ...), custom_call_target="tpu_custom_call", output_to_operand_aliasing={{0}: (9, {}), {1}: (10, {})} | custom-call | flops 3758096384 | bytes 7340032 | tf_op jit(solution)/shard_map/fisher/pallas_call | solution.py:141
  (223 shorter events, 67.9 us)
Async XLA Ops:
  2.6 7.0 %collective-permute-start = (bf16[16,4096]{1,0:T(8,128)(2,1)S(1)}, bf16[16,4096]{1,0:T(8,128)(2,1)S(1)}, u32[]{:S(2)}, u32[]{:S(2)}) collective-permute-start(bf16[16,4096]{1,0:T(8,128)(2,1)S(1)} %get-tuple-element.37.refs_0_), channel_id=1, source_target_pairs={{0,4},{1,5},{4,8},{5,9},{8,12},{9,13},{12,14},{13,15},{14,10},{15,... | collective-permute-start | bytes 393224 | tf_op jit(solution)/shard_map/ppermute | solution.py:218
  5.7 8.9 %collective-permute-start.4 = (bf16[16,4096]{1,0:T(8,128)(2,1)S(1)}, bf16[16,4096]{1,0:T(8,128)(2,1)S(1)}, u32[]{:S(2)}, u32[]{:S(2)}) collective-permute-start(bf16[16,4096]{1,0:T(8,128)(2,1)S(1)} %get-tuple-element.37.refs_0_), channel_id=1, source_target_pairs={{4,0},{5,1},{8,4},{9,5},{12,8},{13,9},{14,12},{15,13},{10,14},{11,... | collective-permute-start | bytes 393224 | tf_op jit(solution)/shard_map/ppermute | solution.py:221
  7.6 7.1 %collective-permute-start.7 = (bf16[16,4096]{1,0:T(8,128)(2,1)S(1)}, bf16[16,4096]{1,0:T(8,128)(2,1)S(1)}, u32[]{:S(2)}, u32[]{:S(2)}) collective-permute-start(bf16[16,4096]{1,0:T(8,128)(2,1)S(1)} %get-tuple-element.38.refs_8_), channel_id=1, source_target_pairs={{0,4},{1,5},{4,8},{5,9},{8,12},{9,13},{12,14},{13,15},{14,10},{15,... | collective-permute-start | bytes 393224 | tf_op jit(solution)/shard_map/ppermute | solution.py:218
  9.6 7.1 %collective-permute-start.1 = (bf16[16,4096]{1,0:T(8,128)(2,1)S(1)}, bf16[16,4096]{1,0:T(8,128)(2,1)S(1)}, u32[]{:S(2)}, u32[]{:S(2)}) collective-permute-start(bf16[16,4096]{1,0:T(8,128)(2,1)S(1)} %collective-permute-done.refs_1_), channel_id=1, source_target_pairs={{0,4},{1,5},{4,8},{5,9},{8,12},{9,13},{12,14},{13,15},{14,10},{15,... | collective-permute-start | bytes 393224 | tf_op jit(solution)/shard_map/ppermute | solution.py:218
  18.2 6.5 %collective-permute-start.12 = (bf16[16,4096]{1,0:T(8,128)(2,1)S(1)}, bf16[16,4096]{1,0:T(8,128)(2,1)S(1)}, u32[]{:S(2)}, u32[]{:S(2)}) collective-permute-start(bf16[16,4096]{1,0:T(8,128)(2,1)S(1)} %collective-permute-done.11.refs_14_), channel_id=1, source_target_pairs={{4,0},{5,1},{8,4},{9,5},{12,8},{13,9},{14,12},{15,13},{10,14},{11,... | collective-permute-start | bytes 393224 | tf_op jit(solution)/shard_map/ppermute | solution.py:221
  95.3 94.8 %collective-permute-start.14 = (bf16[256,4096]{1,0:T(8,128)(2,1)}, bf16[256,4096]{1,0:T(8,128)(2,1)S(1)}, u32[]{:S(2)}, u32[]{:S(2)}) collective-permute-start(bf16[256,4096]{1,0:T(8,128)(2,1)} %pack.2.near_ref.refs_0_), channel_id=1, source_target_pairs={{0,1},{1,0},{2,3},{3,2},{4,5},{5,4},{6,7},{7,6},{8,9},{9,8},{10,11... | collective-permute-start | bytes 6291464 | tf_op jit(solution)/shard_map/ppermute | solution.py:224
  101.1 8.4 %collective-permute-start.19 = (bf16[16,4096]{1,0:T(8,128)(2,1)S(1)}, bf16[16,4096]{1,0:T(8,128)(2,1)S(1)}, u32[]{:S(2)}, u32[]{:S(2)}) collective-permute-start(bf16[16,4096]{1,0:T(8,128)(2,1)S(1)} %get-tuple-element.39.refs_0_), channel_id=1, source_target_pairs={{4,0},{5,1},{8,4},{9,5},{12,8},{13,9},{14,12},{15,13},{10,14},{11,... | collective-permute-start | bytes 393224 | tf_op jit(solution)/shard_map/ppermute | solution.py:221
  101.6 8.4 %collective-permute-start.22 = (bf16[16,4096]{1,0:T(8,128)(2,1)S(1)}, bf16[16,4096]{1,0:T(8,128)(2,1)S(1)}, u32[]{:S(2)}, u32[]{:S(2)}) collective-permute-start(bf16[16,4096]{1,0:T(8,128)(2,1)S(1)} %get-tuple-element.40.refs_8_), channel_id=1, source_target_pairs={{0,4},{1,5},{4,8},{5,9},{8,12},{9,13},{12,14},{13,15},{14,10},{15,... | collective-permute-start | bytes 393224 | tf_op jit(solution)/shard_map/ppermute | solution.py:218
  190.0 55.5 %collective-permute-start.29 = (bf16[256,4096]{1,0:T(8,128)(2,1)}, bf16[256,4096]{1,0:T(8,128)(2,1)}, u32[]{:S(2)}, u32[]{:S(2)}) collective-permute-start(bf16[256,4096]{1,0:T(8,128)(2,1)} %pack.3.near_ref.rest_2_.refs_2_), channel_id=1, source_target_pairs={{0,1},{1,0},{2,3},{3,2},{4,5},{5,4},{6,7},{7,6},{8,9},{9,8},{10,11... | collective-permute-start | bytes 6291464 | tf_op jit(solution)/shard_map/ppermute | solution.py:224
  245.1 9.7 %collective-permute-start.35 = (bf16[16,4096]{1,0:T(8,128)(2,1)S(1)}, bf16[16,4096]{1,0:T(8,128)(2,1)S(1)}, u32[]{:S(2)}, u32[]{:S(2)}) collective-permute-start(bf16[16,4096]{1,0:T(8,128)(2,1)S(1)} %add_convert_fusion.11), channel_id=1, source_target_pairs={{4,0},{5,1},{8,4},{9,5},{12,8},{13,9},{14,12},{15,13},{10,14},{11,... | collective-permute-start | bytes 393224 | tf_op jit(solution)/shard_map/ppermute | solution.py:221
  254.9 11.9 %collective-permute-start.36 = (bf16[16,4096]{1,0:T(8,128)(2,1)S(1)}, bf16[16,4096]{1,0:T(8,128)(2,1)S(1)}, u32[]{:S(2)}, u32[]{:S(2)}) collective-permute-start(bf16[16,4096]{1,0:T(8,128)(2,1)S(1)} %get-tuple-element.79), channel_id=1, source_target_pairs={{4,0},{5,1},{8,4},{9,5},{12,8},{13,9},{14,12},{15,13},{10,14},{11,... | collective-permute-start | bytes 393224 | tf_op jit(solution)/shard_map/ppermute | solution.py:221
  255.3 11.4 %collective-permute-start.31 = (bf16[16,4096]{1,0:T(8,128)(2,1)S(1)}, bf16[16,4096]{1,0:T(8,128)(2,1)S(1)}, u32[]{:S(2)}, u32[]{:S(2)}) collective-permute-start(bf16[16,4096]{1,0:T(8,128)(2,1)S(1)} %get-tuple-element.80), channel_id=1, source_target_pairs={{0,4},{1,5},{4,8},{5,9},{8,12},{9,13},{12,14},{13,15},{14,10},{15,... | collective-permute-start | bytes 393224 | tf_op jit(solution)/shard_map/ppermute | solution.py:218
  266.9 36.1 %collective-permute-start.37 = (bf16[16,4096]{1,0:T(8,128)(2,1)S(1)}, bf16[16,4096]{1,0:T(8,128)(2,1)S(1)}, u32[]{:S(2)}, u32[]{:S(2)}) collective-permute-start(bf16[16,4096]{1,0:T(8,128)(2,1)S(1)} %get-tuple-element.77), channel_id=1, source_target_pairs={{4,0},{5,1},{8,4},{9,5},{12,8},{13,9},{14,12},{15,13},{10,14},{11,... | collective-permute-start | bytes 393224 | tf_op jit(solution)/shard_map/ppermute | solution.py:221
  267.3 13.8 %collective-permute-start.32 = (bf16[16,4096]{1,0:T(8,128)(2,1)S(1)}, bf16[16,4096]{1,0:T(8,128)(2,1)S(1)}, u32[]{:S(2)}, u32[]{:S(2)}) collective-permute-start(bf16[16,4096]{1,0:T(8,128)(2,1)S(1)} %get-tuple-element.78), channel_id=1, source_target_pairs={{0,4},{1,5},{4,8},{5,9},{8,12},{9,13},{12,14},{13,15},{14,10},{15,... | collective-permute-start | bytes 393224 | tf_op jit(solution)/shard_map/ppermute | solution.py:218
  281.2 10.9 %collective-permute-start.33 = (bf16[16,4096]{1,0:T(8,128)(2,1)S(1)}, bf16[16,4096]{1,0:T(8,128)(2,1)S(1)}, u32[]{:S(2)}, u32[]{:S(2)}) collective-permute-start(bf16[16,4096]{1,0:T(8,128)(2,1)S(1)} %add_convert_fusion.13), channel_id=1, source_target_pairs={{0,4},{1,5},{4,8},{5,9},{8,12},{9,13},{12,14},{13,15},{14,10},{15,... | collective-permute-start | bytes 393224 | tf_op jit(solution)/shard_map/ppermute | solution.py:218
  292.2 10.9 %collective-permute-start.34 = (bf16[16,4096]{1,0:T(8,128)(2,1)S(1)}, bf16[16,4096]{1,0:T(8,128)(2,1)S(1)}, u32[]{:S(2)}, u32[]{:S(2)}) collective-permute-start(bf16[16,4096]{1,0:T(8,128)(2,1)S(1)} %add_convert_fusion.12), channel_id=1, source_target_pairs={{0,4},{1,5},{4,8},{5,9},{8,12},{9,13},{12,14},{13,15},{14,10},{15,... | collective-permute-start | bytes 393224 | tf_op jit(solution)/shard_map/ppermute | solution.py:218
  303.0 8.9 %collective-permute-start.38 = (bf16[128,4096]{1,0:T(8,128)(2,1)}, bf16[128,4096]{1,0:T(8,128)(2,1)S(1)}, u32[]{:S(2)}, u32[]{:S(2)}) collective-permute-start(bf16[128,4096]{1,0:T(8,128)(2,1)} %get-tuple-element.61), channel_id=1, source_target_pairs={{0,1},{1,0},{2,3},{3,2},{4,5},{5,4},{6,7},{7,6},{8,9},{9,8},{10,11... | collective-permute-start | bytes 3145736 | tf_op jit(solution)/shard_map/ppermute | solution.py:224
  311.9 7.5 %collective-permute-start.39 = (bf16[16,4096]{1,0:T(8,128)(2,1)S(1)}, bf16[16,4096]{1,0:T(8,128)(2,1)S(1)}, u32[]{:S(2)}, u32[]{:S(2)}) collective-permute-start(bf16[16,4096]{1,0:T(8,128)(2,1)S(1)} %add_convert_fusion.8), channel_id=1, source_target_pairs={{4,0},{5,1},{8,4},{9,5},{12,8},{13,9},{14,12},{15,13},{10,14},{11,... | collective-permute-start | bytes 393224 | tf_op jit(solution)/shard_map/ppermute | solution.py:221
  320.5 11.0 %collective-permute-start.41 = (bf16[16,4096]{1,0:T(8,128)(2,1)S(1)}, bf16[16,4096]{1,0:T(8,128)(2,1)S(1)}, u32[]{:S(2)}, u32[]{:S(2)}) collective-permute-start(bf16[16,4096]{1,0:T(8,128)(2,1)S(1)} %get-tuple-element.75), channel_id=1, source_target_pairs={{4,0},{5,1},{8,4},{9,5},{12,8},{13,9},{14,12},{15,13},{10,14},{11,... | collective-permute-start | bytes 393224 | tf_op jit(solution)/shard_map/ppermute | solution.py:221
  321.1 10.5 %collective-permute-start.40 = (bf16[16,4096]{1,0:T(8,128)(2,1)S(1)}, bf16[16,4096]{1,0:T(8,128)(2,1)S(1)}, u32[]{:S(2)}, u32[]{:S(2)}) collective-permute-start(bf16[16,4096]{1,0:T(8,128)(2,1)S(1)} %get-tuple-element.76), channel_id=1, source_target_pairs={{0,4},{1,5},{4,8},{5,9},{8,12},{9,13},{12,14},{13,15},{14,10},{15,... | collective-permute-start | bytes 393224 | tf_op jit(solution)/shard_map/ppermute | solution.py:218
  331.7 10.9 %collective-permute-start.43 = (bf16[16,4096]{1,0:T(8,128)(2,1)S(1)}, bf16[16,4096]{1,0:T(8,128)(2,1)S(1)}, u32[]{:S(2)}, u32[]{:S(2)}) collective-permute-start(bf16[16,4096]{1,0:T(8,128)(2,1)S(1)} %get-tuple-element.73), channel_id=1, source_target_pairs={{4,0},{5,1},{8,4},{9,5},{12,8},{13,9},{14,12},{15,13},{10,14},{11,... | collective-permute-start | bytes 393224 | tf_op jit(solution)/shard_map/ppermute | solution.py:221
  332.3 10.3 %collective-permute-start.42 = (bf16[16,4096]{1,0:T(8,128)(2,1)S(1)}, bf16[16,4096]{1,0:T(8,128)(2,1)S(1)}, u32[]{:S(2)}, u32[]{:S(2)}) collective-permute-start(bf16[16,4096]{1,0:T(8,128)(2,1)S(1)} %get-tuple-element.74), channel_id=1, source_target_pairs={{0,4},{1,5},{4,8},{5,9},{8,12},{9,13},{12,14},{13,15},{14,10},{15,... | collective-permute-start | bytes 393224 | tf_op jit(solution)/shard_map/ppermute | solution.py:218
  342.7 10.9 %collective-permute-start.44 = (bf16[16,4096]{1,0:T(8,128)(2,1)S(1)}, bf16[16,4096]{1,0:T(8,128)(2,1)S(1)}, u32[]{:S(2)}, u32[]{:S(2)}) collective-permute-start(bf16[16,4096]{1,0:T(8,128)(2,1)S(1)} %get-tuple-element.71), channel_id=1, source_target_pairs={{0,4},{1,5},{4,8},{5,9},{8,12},{9,13},{12,14},{13,15},{14,10},{15,... | collective-permute-start | bytes 393224 | tf_op jit(solution)/shard_map/ppermute | solution.py:218
  344.1 9.5 %collective-permute-start.45 = (bf16[16,4096]{1,0:T(8,128)(2,1)S(1)}, bf16[16,4096]{1,0:T(8,128)(2,1)S(1)}, u32[]{:S(2)}, u32[]{:S(2)}) collective-permute-start(bf16[16,4096]{1,0:T(8,128)(2,1)S(1)} %get-tuple-element.72), channel_id=1, source_target_pairs={{4,0},{5,1},{8,4},{9,5},{12,8},{13,9},{14,12},{15,13},{10,14},{11,... | collective-permute-start | bytes 393224 | tf_op jit(solution)/shard_map/ppermute | solution.py:221
  (83 other events, 791.9 us)

commit v3 on v1

--- a/solution.py
+++ b/solution.py
@@ -9,8 +9,10 @@
 
 SEQS = 2
 MIB = 1 << 20
+CYCLE = (0, 2, 4, 6, 7, 5, 3, 1)
 NT = (((1,), (1,)), ((), ()))
-TN = (((0,), (0,)), ((), ()))
+BF16 = jnp.bfloat16
+F32 = jnp.float32
 
 
 def tile(size, want):
@@ -25,18 +27,214 @@
     return pl.CostEstimate(flops=flops, bytes_accessed=read, transcendentals=0)
 
 
-def forward_kernel(x_ref, wg_ref, wu_ref, gate_ref, up_ref):
+def silu_grads(hidden, gate, up):
+    sigma = jax.nn.sigmoid(gate)
+    both = hidden * sigma
+    gg = both * up * (1.0 + gate * (1.0 - sigma))
+    return gg.astype(BF16), (both * gate).astype(BF16)
+
+
+def pack_kernel(at_ref, *refs):
+    pieces, out_ref = refs[:-1], refs[-1]
+    row = pieces[0].shape[0]
+    start = 0
+    for piece in pieces:
+        part = piece.shape[0]
+        base = at_ref[start // row] * row + start % row
+        out_ref[pl.ds(pl.multiple_of(base, part), part), :] = piece[...]
+        start += part
+
+
+def pack(at, pieces):
+    depth = pieces[0].shape[1]
+    rows = sum(piece.shape[0] for piece in pieces)
+    return pl.pallas_call(
+        pack_kernel,
+        in_specs=[pl.BlockSpec(memory_space=pltpu.SMEM)]
+        + [pl.BlockSpec(memory_space=pltpu.VMEM)] * len(pieces),
+        out_specs=pl.BlockSpec(memory_space=pltpu.VMEM),
+        out_shape=jax.ShapeDtypeStruct((rows, depth), BF16),
+        compiler_params=params(16),
+        cost_estimate=cost(0, 4 * rows * depth),
+        name="pack",
+    )(at, *pieces)
+
+
+def gate_up_kernel(row, core_ref, near_ref, far_ref, wg_ref, wu_ref, gate_ref, up_ref, x_ref):
+    @pl.when(pl.program_id(0) == 0)
+    def _():
+        mine = core_ref[0]
+        for c in range(near_ref.shape[0] // row):
+            at = pl.ds(c * row, row)
+            base = 2 * c * row
+            x_ref[pl.ds(pl.multiple_of(base + mine * row, row), row), :] = near_ref[at, :]
+            x_ref[pl.ds(pl.multiple_of(base + (1 - mine) * row, row), row), :] = far_ref[at, :]
+
+    gate_ref[...] = jnp.dot(x_ref[...], wg_ref[...], preferred_element_type=F32)
+    up_ref[...] = jnp.dot(x_ref[...], wu_ref[...], preferred_element_type=F32)
+
+
+def gate_up(core, near, far, wg, wu, row):
+    rows, depth = near.shape
+    width = wg.shape[1]
+    step = tile(width, 256)
+    half = pl.BlockSpec((rows, depth), lambda j: (0, 0))
+    column = pl.BlockSpec((depth, step), lambda j: (0, j))
+    out = pl.BlockSpec((2 * rows, step), lambda j: (0, j))
+    return pl.pallas_call(
+        functools.partial(gate_up_kernel, row),
+        grid=(width // step,),
+        in_specs=[pl.BlockSpec(memory_space=pltpu.SMEM), half, half, column, column],
+        out_specs=[out, out, pl.BlockSpec((2 * rows, depth), lambda j: (0, 0))],
+        out_shape=[jax.ShapeDtypeStruct((2 * rows, width), F32)] * 2
+        + [jax.ShapeDtypeStruct((2 * rows, depth), BF16)],
+        compiler_params=params(36),
+        cost_estimate=cost(8 * rows * depth * width, 4 * depth * width),
+        name="gate_up",
+    )(core, near, far, wg, wu)
+
+
+def back_kernel(parts, dy_ref, wd_ref, gate_ref, up_ref, gg_ref, gu_ref):
+    rows = dy_ref.shape[0] // parts
+    for p in range(parts):
+        at = pl.ds(p * rows, rows)
+        hidden = lax.dot_general(dy_ref[at, :], wd_ref[...], NT, preferred_element_type=F32)
+        gg_ref[at, :], gu_ref[at, :] = silu_grads(hidden, gate_ref[at, :], up_ref[at, :])
+
+
+def back(dy, wd, gate, up):
+    rows, depth = dy.shape
+    width = wd.shape[0]
+    step = tile(width, 256)
+    column = pl.BlockSpec((rows, step), lambda j: (0, j))
+    return pl.pallas_call(
+        functools.partial(back_kernel, 2),
+        grid=(width // step,),
+        in_specs=[
+            pl.BlockSpec((rows, depth), lambda j: (0, 0)),
+            pl.BlockSpec((step, depth), lambda j: (j, 0)),
+            column,
+            column,
+        ],
+        out_specs=[column, column],
+        out_shape=[jax.ShapeDtypeStruct((rows, width), BF16)] * 2,
+        compiler_params=params(58),
+        cost_estimate=cost(2 * rows * depth * width, 2 * depth * width),
+        name="hidden_back",
+    )(dy, wd, gate, up)
+
+
+def input_kernel(gg_ref, gu_ref, wg_ref, wu_ref, *rest):
+    out_ref = rest[-1]
+    total = lax.dot_general(gg_ref[...], wg_ref[...], NT, preferred_element_type=F32)
+    total += lax.dot_general(gu_ref[...], wu_ref[...], NT, preferred_element_type=F32)
+    out_ref[...] = total.astype(BF16)
+
+
+def input_terms(gg, gu, wg, wu, first, count, step, after=()):
+    rows, width = gg.shape
+    whole = pl.BlockSpec((rows, width), lambda j: (0, 0))
+    weight = pl.BlockSpec((step, width), lambda j: (first + j, 0))
+    return pl.pallas_call(
+        input_kernel,
+        grid=(count,),
+        in_specs=[whole, whole, weight, weight]
+        + [pl.BlockSpec(memory_space=pl.ANY)] * len(after),
+        out_specs=pl.BlockSpec((rows, step), lambda j: (0, j)),
+        out_shape=jax.ShapeDtypeStruct((rows, count * step), BF16),
+        compiler_params=params(58),
+        cost_estimate=cost(4 * rows * width * count * step, 4 * width * count * step),
+        name="input_terms",
+    )(gg, gu, wg, wu, *after)
+
+
+def fisher_kernel(step, x_ref, gg_ref, gu_ref, *rest):
+    fg_ref, fu_ref = rest[-2:]
+    span = x_ref.shape[0] // SEQS
+    seqs = [pl.ds(q * span, span) for q in range(SEQS)]
+    cols = [x_ref[at, :].T for at in seqs]
+    for g_ref, f_ref in ((gg_ref, fg_ref), (gu_ref, fu_ref)):
+        for c in range(g_ref.shape[1] // step):
+            at = pl.ds(c * step, step)
+            total = None
+            for q in range(SEQS):
+                seq = jnp.dot(cols[q], g_ref[seqs[q], at], preferred_element_type=F32)
+                total = seq * seq if total is None else total + seq * seq
+            f_ref[:, at] = (total * (1.0 / SEQS)).astype(BF16)
+
+
+def fisher(x, gg, gu, step, after=()):
+    rows, depth = x.shape
+    width = gg.shape[1]
+    held = pl.BlockSpec((rows, width), lambda j: (0, 0))
+    block = pl.BlockSpec((step, width), lambda j: (j, 0))
+    return pl.pallas_call(
+        functools.partial(fisher_kernel, tile(width, 256)),
+        grid=(depth // step,),
+        in_specs=[pl.BlockSpec((rows, step), lambda j: (0, j)), held, held]
+        + [pl.BlockSpec(memory_space=pl.ANY)] * len(after),
+        out_specs=[block, block],
+        out_shape=[jax.ShapeDtypeStruct((depth, width), BF16)] * 2,
+        compiler_params=params(58),
+        cost_estimate=cost(4 * rows * depth * width, 4 * depth * width),
+        name="fisher",
+    )(x, gg, gu, *after)
+
+
+def ring_part(tokens, grad_out, wg, wu, wd):
+    chips = len(CYCLE)
+    far = chips // 2
+    row, depth = tokens.shape
+    links = [(CYCLE[i], CYCLE[(i + 1) % chips]) for i in range(chips)]
+    to_right = [(2 * a + c, 2 * b + c) for a, b in links for c in range(2)]
+    to_left = [(b, a) for a, b in to_right]
+    across = [(2 * i + c, 2 * i + 1 - c) for i in range(chips) for c in range(2)]
+
+    def right(value):
+        return lax.ppermute(value, "hid", to_right)
+
+    def left(value):
+        return lax.ppermute(value, "hid", to_left)
+
+    device = lax.axis_index("hid")
+    spot = [CYCLE.index(c) for c in range(chips)]
+    me = jnp.array(spot, jnp.int32)[device // 2]
+    at = jnp.array(CYCLE, jnp.int32)[(me - jnp.arange(chips, dtype=jnp.int32)) % chips]
+    core = (device % 2).astype(jnp.int32).reshape(1)
+
+    dy = lax.all_gather(grad_out, "hid", axis=0, tiled=True)
+    from_left, from_right = [tokens], [tokens]
+    for _ in range(1, far):
+        from_left.append(right(from_left[-1]))
+        from_right.append(left(from_right[-1]))
+    ends = [right(from_left[-1][: row // 2]), left(from_right[-1][row // 2 :])]
+    near = pack(at, from_left + ends + from_right[:0:-1])
+    apart = lax.ppermute(near, "hid", across)
+    gate, up, x = gate_up(core, near, apart, wg, wu, row)
+    gg, gu = back(dy, wd, gate, up)
+    half = depth // 512 // 2
+    low = input_terms(gg, gu, wg, wu, 0, half, 512)
+    high = input_terms(gg, gu, wg, wu, half, half, 512, (low,))
+    mine = [
+        lax.psum_scatter(terms, "hid", scatter_dimension=0, tiled=True)
+        for terms in (low, high)
+    ]
+    fg, fu = fisher(x, gg, gu, 512, (high,))
+    return fg, fu, jnp.concatenate(mine, axis=1)
+
+
+def plain_forward_kernel(x_ref, wg_ref, wu_ref, gate_ref, up_ref):
     x = x_ref[...]
     gate_ref[...] = jnp.dot(x, wg_ref[...], preferred_element_type=jnp.float32)
     up_ref[...] = jnp.dot(x, wu_ref[...], preferred_element_type=jnp.float32)
 
 
-def forward(x, wg, wu):
+def plain_forward(x, wg, wu):
     rows, depth = x.shape
     width = wg.shape[1]
     step = tile(width, 256)
     return pl.pallas_call(
-        forward_kernel,
+        plain_forward_kernel,
         grid=(width // step,),
         in_specs=[
             pl.BlockSpec((rows, depth), lambda j: (0, 0)),
@@ -51,7 +249,7 @@
     )(x, wg, wu)
 
 
-def back_kernel(parts, dy_ref, wd_ref, gate_ref, up_ref, gg_ref, gu_ref):
+def plain_back_kernel(parts, dy_ref, wd_ref, gate_ref, up_ref, gg_ref, gu_ref):
     rows = dy_ref.shape[0] // parts
     for p in range(parts):
         at = pl.ds(p * rows, rows)
@@ -63,13 +261,13 @@
         gu_ref[at, :] = (both * gate).astype(jnp.bfloat16)
 
 
-def back(dy, wd, gate, up):
+def plain_back(dy, wd, gate, up):
     rows, depth = dy.shape
     width = wd.shape[0]
     step = tile(width, 256)
     column = pl.BlockSpec((rows, step), lambda j: (0, j))
     return pl.pallas_call(
-        functools.partial(back_kernel, 2),
+        functools.partial(plain_back_kernel, 2),
         grid=(width // step,),
         in_specs=[
             pl.BlockSpec((rows, depth), lambda j: (0, 0)),
@@ -85,19 +283,19 @@
     )(dy, wd, gate, up)
 
 
-def input_kernel(gg_ref, gu_ref, wg_ref, wu_ref, out_ref):
+def plain_input_kernel(gg_ref, gu_ref, wg_ref, wu_ref, out_ref):
     total = lax.dot_general(gg_ref[...], wg_ref[...], NT, preferred_element_type=jnp.float32)
     total += lax.dot_general(gu_ref[...], wu_ref[...], NT, preferred_element_type=jnp.float32)
     out_ref[...] = total.astype(jnp.bfloat16)
 
 
-def input_terms(gg, gu, wg, wu):
+def plain_input_terms(gg, gu, wg, wu):
     rows, width = gg.shape
     depth = wg.shape[0]
     step = 512
     held = pl.BlockSpec((rows, width), lambda j: (0, 0))
     return pl.pallas_call(
-        input_kernel,
+        plain_input_kernel,
         grid=(depth // step,),
         in_specs=[
             held,
@@ -113,7 +311,7 @@
     )(gg, gu, wg, wu)
 
 
-def fisher_kernel(step, x_ref, gg_ref, gu_ref, fg_ref, fu_ref):
+def plain_fisher_kernel(step, x_ref, gg_ref, gu_ref, fg_ref, fu_ref):
     half = x_ref.shape[0] // 2
     span = half // SEQS
     width = gg_ref.shape[1]
@@ -134,14 +332,14 @@
             f_ref[:, at] = (total * (1.0 / SEQS)).astype(jnp.bfloat16)
 
 
-def fisher(x, gg, gu):
+def plain_fisher(x, gg, gu):
     rows, depth = x.shape
     width = gg.shape[1]
     step = 512
     held = pl.BlockSpec((rows, width), lambda j: (0, 0))
     block = pl.BlockSpec((step, width), lambda j: (j, 0))
     return pl.pallas_call(
-        functools.partial(fisher_kernel, tile(width, 256)),
+        functools.partial(plain_fisher_kernel, tile(width, 256)),
         grid=(depth // step,),
         in_specs=[pl.BlockSpec((rows, step), lambda j: (0, j)), held, held],
         out_specs=[block, block],
@@ -152,7 +350,7 @@
     )(x, gg, gu)
 
 
-def per_device(size, tokens, grad_out, wg, wu, wd):
+def plain_part(size, tokens, grad_out, wg, wu, wd):
     chips = size // 2
     across = [[2 * i + c for i in range(chips)] for c in range(2)]
     pairs = [[2 * i, 2 * i + 1] for i in range(chips)]
@@ -164,17 +362,23 @@
 
     x = gather(tokens).reshape(-1, depth)
     dy = gather(grad_out).reshape(-1, depth)
-    gate, up = forward(x, wg, wu)
-    gg, gu = back(dy, wd, gate, up)
-    terms = input_terms(gg, gu, wg, wu).reshape(2, -1, depth)
+    gate, up = plain_forward(x, wg, wu)
+    gg, gu = plain_back(dy, wd, gate, up)
+    terms = plain_input_terms(gg, gu, wg, wu).reshape(2, -1, depth)
     mine = lax.psum_scatter(
         terms, "hid", scatter_dimension=0, tiled=False, axis_index_groups=pairs
     )
     mine = lax.psum_scatter(
         mine, "hid", scatter_dimension=0, tiled=True, axis_index_groups=across
     )
-    fg, fu = fisher(x, gg, gu)
+    fg, fu = plain_fisher(x, gg, gu)
     return fg, fu, mine
+
+
+def per_device(size, tokens, grad_out, wg, wu, wd):
+    if size == 2 * len(CYCLE) and tokens.shape[0] % 32 == 0:
+        return ring_part(tokens, grad_out, wg, wu, wd)
+    return plain_part(size, tokens, grad_out, wg, wu, wd)
 
 
 def solution(mesh):

time: 285 us -> 252 us (0.88)
  waiting for transfers between devices: 183 us -> 130 us
  Pallas kernels: 71.5 us -> 82.9 us
  starting transfers between devices: 0.23 us -> 10.6 us
  local copies, waits for them, and re-layouts: 15.6 us -> 11.6 us
    all_gather x4 -> x1, waiting for transfers between devices: 117 us -> 0.01 us  [ring_part(): dy = lax.all_gather(grad_out, 'hid', axis=0, tiled=True)]
    ppermute x0 -> x9, waiting for transfers between devices: none -> 33.5 us  [the longest x4 20.3 us: right(): return lax.ppermute(value, 'hid', to_right)]
    reduce_scatter x2, waiting for transfers between devices: 64.4 us -> 96 us  [ring_part(): lax.psum_scatter(terms, 'hid', scatter_dimension=0, tiled=True)]
    ppermute x0 -> x9, starting transfers between devices: none -> 10.5 us  [the longest x4 10.1 us: right(): return lax.ppermute(value, 'hid', to_right)]
    pallas_call x2 -> x4, Pallas kernels: 39.5 us -> 46.1 us  [the longest x2 25.2 us: input_terms(): pl.pallas_call(input_kernel, grid=(count,), in_specs=[whole, whole, weigh...]
    unnamed x18 -> x16, local copies, waits for them, and re-layouts: 15.6 us -> 9.06 us
  transfers between devices with their start and end apart: 6 -> 12, of which waited for: 5 -> 10; matrix products, arithmetic and copies ran while one was open for 0% -> 1% of each run, Pallas kernels for 14% -> 22%
where the time goes in v3:
time: 252 us; the launch traced here: 251 us
  waiting for transfers between devices  130 us (52%)
  Pallas kernels  82.9 us (33%)
  between operations  13.8 us (5%)
  local copies, waits for them, and re-layouts  11.6 us (5%)
  starting transfers between devices  10.6 us (4%)
    reduce_scatter x2, waiting for transfers between devices, ring_part(): lax.psum_scatter(terms, 'hid', scatter_dimension=0, tiled=True)  96 us
    pallas_call x2, Pallas kernels, input_terms(): pl.pallas_call(input_kernel, grid=(count,), in_specs=[whole, whole, weigh...  25.2 us
    pallas_call x1, Pallas kernels, fisher(): pl.pallas_call(functools.partial(fisher_kernel, tile(width, 256)), grid=(...  20.8 us
    ppermute x4, waiting for transfers between devices, right(): return lax.ppermute(value, 'hid', to_right)  20.3 us
    pallas_call x1, Pallas kernels, gate_up(): pl.pallas_call(functools.partial(gate_up_kernel, row), grid=(width // ste...  20.2 us
    pallas_call x1, Pallas kernels, back(): pl.pallas_call(functools.partial(back_kernel, 2), grid=(width // step,),...  16 us
    ppermute x4, starting transfers between devices, right(): return lax.ppermute(value, 'hid', to_right)  10.1 us
    unnamed x16, local copies, waits for them, and re-layouts  9.06 us
  transfers between devices with their start and end apart: 12, of which 10 were waited for; matrix products, arithmetic and copies ran while one was open for 1% of the time, Pallas kernels for 22%

profile of v3, /device:TPU:0, one launch (start us, length us, event | category | flops | bytes accessed | tf_op | source)
XLA Modules:
  0.0 251.5 jit_solution(5794793408205652891)
XLA Ops:
  7.9 3.1 %collective-permute-start = (bf16[32,4096]{1,0:T(8,128)(2,1)}, bf16[32,4096]{1,0:T(8,128)(2,1)S(1)}, u32[]{:S(2)}, u32[]{:S(2)}) collective-permute-start(bf16[32,4096]{1,0:T(8,128)(2,1)} %refs_0_.1), channel_id=1, source_target_pairs={{0,4},{1,5},{4,8},{5,9},{8,12},{9,13},{12,14},{13,15},{14,10},{15,... | collective-permute-start | bytes 786440 | tf_op jit(solution)/shard_map/ppermute | solution.py:194
  11.0 6.4 %collective-permute-done.refs_1_ = bf16[32,4096]{1,0:T(8,128)(2,1)S(1)} collective-permute-done((bf16[32,4096]{1,0:T(8,128)(2,1)}, bf16[32,4096]{1,0:T(8,128)(2,1)S(1)}, u32[]{:S(2)}, u32[]{:S(2)}) %collective-permute-start) | collective-permute-done | bytes 262176 | tf_op jit(solution)/shard_map/ppermute | solution.py:194
  17.5 1.8 collective-permute-start.1
  19.5 10.1 %collective-permute-done.1.refs_2_ = bf16[32,4096]{1,0:T(8,128)(2,1)S(1)} collective-permute-done((bf16[32,4096]{1,0:T(8,128)(2,1)S(1)}, bf16[32,4096]{1,0:T(8,128)(2,1)S(1)}, u32[]{:S(2)}, u32[]{:S(2)}) %collective-permute-start.1) | collective-permute-done | bytes 262176 | tf_op jit(solution)/shard_map/ppermute | solution.py:194
  29.6 2.7 %collective-permute-start.2 = (bf16[32,4096]{1,0:T(8,128)(2,1)S(1)}, bf16[32,4096]{1,0:T(8,128)(2,1)S(1)}, u32[]{:S(2)}, u32[]{:S(2)}) collective-permute-start(bf16[32,4096]{1,0:T(8,128)(2,1)S(1)} %collective-permute-done.1.refs_2_), channel_id=1, source_target_pairs={{0,4},{1,5},{4,8},{5,9},{8,12},{9,13},{12,14},{13,15},{14,10},{15,... | collective-permute-start | bytes 786440 | tf_op jit(solution)/shard_map/ppermute | solution.py:194
  32.3 1.4 collective-permute-done.5.refs_7_
  33.7 1.3 dynamic_slice.3
  35.0 3.2 %collective-permute-done.2.refs_3_ = bf16[32,4096]{1,0:T(8,128)(2,1)S(1)} collective-permute-done((bf16[32,4096]{1,0:T(8,128)(2,1)S(1)}, bf16[32,4096]{1,0:T(8,128)(2,1)S(1)}, u32[]{:S(2)}, u32[]{:S(2)}) %collective-permute-start.2) | collective-permute-done | bytes 262176 | tf_op jit(solution)/shard_map/ppermute | solution.py:194
  38.2 2.5 %collective-permute-start.3 = (bf16[16,4096]{1,0:T(8,128)(2,1)S(1)}, bf16[16,4096]{1,0:T(8,128)(2,1)S(1)}, u32[]{:S(2)}, u32[]{:S(2)}) collective-permute-start(bf16[16,4096]{1,0:T(8,128)(2,1)S(1)} %slice.10), channel_id=1, source_target_pairs={{0,4},{1,5},{4,8},{5,9},{8,12},{9,13},{12,14},{13,15},{14,10},{15,... | collective-permute-start | bytes 393224 | tf_op jit(solution)/shard_map/ppermute | solution.py:194
  41.9 1.3 gather_fusion
  43.8 7.0 %collective-permute-done.7.refs_5_ = bf16[16,4096]{1,0:T(8,128)(2,1)S(1)} collective-permute-done((bf16[16,4096]{1,0:T(8,128)(2,1)S(1)}, bf16[16,4096]{1,0:T(8,128)(2,1)S(1)}, u32[]{:S(2)}, u32[]{:S(2)}) %collective-permute-start.7) | collective-permute-done | bytes 131104 | tf_op jit(solution)/shard_map/ppermute | solution.py:197
  52.4 0.9 copy-done.2
  55.1 4.3 %collective-permute-done.8.far_ref = bf16[256,4096]{1,0:T(8,128)(2,1)} collective-permute-done((bf16[256,4096]{1,0:T(8,128)(2,1)S(1)}, bf16[256,4096]{1,0:T(8,128)(2,1)}, u32[]{:S(2)}, u32[]{:S(2)}) %collective-permute-start.8) | collective-permute-done | bytes 2097184 | tf_op jit(solution)/shard_map/ppermute | solution.py:212
  59.3 20.2 %gate_up.1 = (f32[512,1792]{1,0:T(8,128)S(1)}, f32[512,1792]{1,0:T(8,128)S(1)}, bf16[512,4096]{1,0:T(8,128)(2,1)S(1)}) custom-call(s32[1]{0:T(128)} %bitcast.core_ref, bf16[256,4096]{1,0:T(8,128)(2,1)S(1)} %pack.1.near_ref, bf16[256,4096]{1,0:T(8,128)(2,1)} %collective-permute-done.8.far_ref, bf16[4096,1792]{1,0:T(8,128)(2,1)} %wg_ref.5, ...), custom_call_target="tpu_custom_call" | custom-call | flops 15032385536 | bytes 29360128 | tf_op jit(solution)/shard_map/gate_up/pallas_call | solution.py:84
  79.5 1.8 copy-done.5
  81.4 1.8 copy-done.6
  83.2 1.9 copy-done.7
  85.1 16.0 %hidden_back.1 = (bf16[512,1792]{1,0:T(8,128)(2,1)}, bf16[512,1792]{1,0:T(8,128)(2,1)}) custom-call(bf16[512,4096]{1,0:T(8,128)(2,1)} %all-gather.2.cloned.1.call-done.dy_ref, bf16[1792,4096]{1,0:T(8,128)(2,1)} %wd_ref.1, f32[512,1792]{1,0:T(8,128)} %copy-done.5, f32[512,1792]{1,0:T(8,128)} %copy-done.6), custom_call_target="tpu_custom_call" | custom-call | flops 7516192768 | bytes 14680064 | tf_op jit(solution)/shard_map/hidden_back/pallas_call | solution.py:110
  101.1 12.6 %input_terms.2.rest_0_ = bf16[512,2048]{1,0:T(8,128)(2,1)} custom-call(bf16[512,1792]{1,0:T(8,128)(2,1)} %get-tuple-element.13.gg_ref, bf16[512,1792]{1,0:T(8,128)(2,1)} %get-tuple-element.14.gu_ref, bf16[4096,1792]{1,0:T(8,128)(2,1)} %wg_ref.5, bf16[4096,1792]{1,0:T(8,128)(2,1)} %wu_ref.5), custom_call_target="tpu_custom_call" | custom-call | flops 7516192768 | bytes 14680064 | tf_op jit(solution)/shard_map/input_terms/pallas_call | solution.py:138
  113.8 12.7 %input_terms.3.rest_0_ = bf16[512,2048]{1,0:T(8,128)(2,1)} custom-call(bf16[512,1792]{1,0:T(8,128)(2,1)} %get-tuple-element.13.gg_ref, bf16[512,1792]{1,0:T(8,128)(2,1)} %get-tuple-element.14.gu_ref, bf16[4096,1792]{1,0:T(8,128)(2,1)} %wg_ref.5, bf16[4096,1792]{1,0:T(8,128)(2,1)} %wu_ref.5, bf16[512,2048]{1,0:T(8,128)(2,1)} %input_terms.2.rest_0_), custom_call_target="tpu_custom_call" | custom-call | flops 7516192768 | bytes 14680064 | tf_op jit(solution)/shard_map/input_terms/pallas_call | solution.py:138
  126.5 20.8 %fisher.1 = (bf16[4096,1792]{1,0:T(8,128)(2,1)}, bf16[4096,1792]{1,0:T(8,128)(2,1)}) custom-call(bf16[512,4096]{1,0:T(8,128)(2,1)} %copy-done.7, bf16[512,1792]{1,0:T(8,128)(2,1)} %get-tuple-element.13.gg_ref, bf16[512,1792]{1,0:T(8,128)(2,1)} %get-tuple-element.14.gu_ref, bf16[512,2048]{1,0:T(8,128)(2,1)} %input_terms.3.rest_0_), custom_call_target="tpu_custom_call" | custom-call | flops 15032385536 | bytes 29360128 | tf_op jit(solution)/shard_map/fisher/pallas_call | solution.py:171
  147.3 31.1 %reduce-scatter.3.cloned.1.call-done = bf16[32,2048]{1,0:T(8,128)(2,1)} async-done(((bf16[512,2048]{1,0:T(8,128)(2,1)}), bf16[32,2048]{1,0:T(8,128)(2,1)}) %reduce-scatter.3.cloned.1.call-update) | async-done | bytes 131088 | tf_op jit(solution)/shard_map/reduce_scatter | solution.py:219
  178.4 64.9 %reduce-scatter.5.cloned.1.call-done = bf16[32,2048]{1,0:T(8,128)(2,1)} async-done(((bf16[512,2048]{1,0:T(8,128)(2,1)}), bf16[32,2048]{1,0:T(8,128)(2,1)}) %reduce-scatter.5.cloned.1.call-update) | async-done | bytes 131088 | tf_op jit(solution)/shard_map/reduce_scatter | solution.py:219
  243.3 1.7 pad_maximum_fusion
  (32 shorter events, 6.0 us)
Async XLA Ops:
  7.2 78.0 %all-gather.2.cloned.1.call-start = ((), (), s32[]{:S(2)}) async-start(), calls=%async_computation.2 | async-start | bytes 4456448 | tf_op jit(solution)/shard_map/all_gather | solution.py:205
  7.9 170.5 %reduce-scatter.3.cloned.1.call-start = ((), (), s32[]{:S(2)}) async-start(), calls=%async_computation.3 | async-start | bytes 2228224 | tf_op jit(solution)/shard_map/reduce_scatter | solution.py:219
  7.9 9.5 %collective-permute-start = (bf16[32,4096]{1,0:T(8,128)(2,1)}, bf16[32,4096]{1,0:T(8,128)(2,1)S(1)}, u32[]{:S(2)}, u32[]{:S(2)}) collective-permute-start(bf16[32,4096]{1,0:T(8,128)(2,1)} %refs_0_.1), channel_id=1, source_target_pairs={{0,4},{1,5},{4,8},{5,9},{8,12},{9,13},{12,14},{13,15},{14,10},{15,... | collective-permute-start | bytes 786440 | tf_op jit(solution)/shard_map/ppermute | solution.py:194
  11.0 8.3 %collective-permute-start.4 = (bf16[32,4096]{1,0:T(8,128)(2,1)}, bf16[32,4096]{1,0:T(8,128)(2,1)S(1)}, u32[]{:S(2)}, u32[]{:S(2)}) collective-permute-start(bf16[32,4096]{1,0:T(8,128)(2,1)} %refs_0_.1), channel_id=1, source_target_pairs={{4,0},{5,1},{8,4},{9,5},{12,8},{13,9},{14,12},{15,13},{10,14},{11,... | collective-permute-start | bytes 786440 | tf_op jit(solution)/shard_map/ppermute | solution.py:197
  17.5 12.2 %collective-permute-start.1 = (bf16[32,4096]{1,0:T(8,128)(2,1)S(1)}, bf16[32,4096]{1,0:T(8,128)(2,1)S(1)}, u32[]{:S(2)}, u32[]{:S(2)}) collective-permute-start(bf16[32,4096]{1,0:T(8,128)(2,1)S(1)} %collective-permute-done.refs_1_), channel_id=1, source_target_pairs={{0,4},{1,5},{4,8},{5,9},{8,12},{9,13},{12,14},{13,15},{14,10},{15,... | collective-permute-start | bytes 786440 | tf_op jit(solution)/shard_map/ppermute | solution.py:194
  19.3 14.5 %collective-permute-start.5 = (bf16[32,4096]{1,0:T(8,128)(2,1)S(1)}, bf16[32,4096]{1,0:T(8,128)(2,1)S(1)}, u32[]{:S(2)}, u32[]{:S(2)}) collective-permute-start(bf16[32,4096]{1,0:T(8,128)(2,1)S(1)} %collective-permute-done.4.refs_8_), channel_id=1, source_target_pairs={{4,0},{5,1},{8,4},{9,5},{12,8},{13,9},{14,12},{15,13},{10,14},{11,... | collective-permute-start | bytes 786440 | tf_op jit(solution)/shard_map/ppermute | solution.py:197
  29.6 8.6 %collective-permute-start.2 = (bf16[32,4096]{1,0:T(8,128)(2,1)S(1)}, bf16[32,4096]{1,0:T(8,128)(2,1)S(1)}, u32[]{:S(2)}, u32[]{:S(2)}) collective-permute-start(bf16[32,4096]{1,0:T(8,128)(2,1)S(1)} %collective-permute-done.1.refs_2_), channel_id=1, source_target_pairs={{0,4},{1,5},{4,8},{5,9},{8,12},{9,13},{12,14},{13,15},{14,10},{15,... | collective-permute-start | bytes 786440 | tf_op jit(solution)/shard_map/ppermute | solution.py:194
  33.7 10.0 %copy-start.1 = (bf16[32,4096]{1,0:T(8,128)(2,1)}, bf16[32,4096]{1,0:T(8,128)(2,1)S(1)}, u32[]{:S(2)}) copy-start(bf16[32,4096]{1,0:T(8,128)(2,1)S(1)} %collective-permute-done.5.refs_7_) | copy-start | bytes 786436
  33.7 7.4 %collective-permute-start.6 = (bf16[32,4096]{1,0:T(8,128)(2,1)S(1)}, bf16[32,4096]{1,0:T(8,128)(2,1)S(1)}, u32[]{:S(2)}, u32[]{:S(2)}) collective-permute-start(bf16[32,4096]{1,0:T(8,128)(2,1)S(1)} %collective-permute-done.5.refs_7_), channel_id=1, source_target_pairs={{4,0},{5,1},{8,4},{9,5},{12,8},{13,9},{14,12},{15,13},{10,14},{11,... | collective-permute-start | bytes 786440 | tf_op jit(solution)/shard_map/ppermute | solution.py:197
  38.2 5.5 %collective-permute-start.3 = (bf16[16,4096]{1,0:T(8,128)(2,1)S(1)}, bf16[16,4096]{1,0:T(8,128)(2,1)S(1)}, u32[]{:S(2)}, u32[]{:S(2)}) collective-permute-start(bf16[16,4096]{1,0:T(8,128)(2,1)S(1)} %slice.10), channel_id=1, source_target_pairs={{0,4},{1,5},{4,8},{5,9},{8,12},{9,13},{12,14},{13,15},{14,10},{15,... | collective-permute-start | bytes 393224 | tf_op jit(solution)/shard_map/ppermute | solution.py:194
  41.2 9.6 %collective-permute-start.7 = (bf16[16,4096]{1,0:T(8,128)(2,1)S(1)}, bf16[16,4096]{1,0:T(8,128)(2,1)S(1)}, u32[]{:S(2)}, u32[]{:S(2)}) collective-permute-start(bf16[16,4096]{1,0:T(8,128)(2,1)S(1)} %slice.11), channel_id=1, source_target_pairs={{4,0},{5,1},{8,4},{9,5},{12,8},{13,9},{14,12},{15,13},{10,14},{11,... | collective-permute-start | bytes 393224 | tf_op jit(solution)/shard_map/ppermute | solution.py:197
  50.8 0.7 copy-start.3
  51.5 0.9 copy-start
  52.4 1.0 copy-start.2
  53.4 0.9 copy-start.4
  55.0 4.4 %collective-permute-start.8 = (bf16[256,4096]{1,0:T(8,128)(2,1)S(1)}, bf16[256,4096]{1,0:T(8,128)(2,1)}, u32[]{:S(2)}, u32[]{:S(2)}) collective-permute-start(bf16[256,4096]{1,0:T(8,128)(2,1)S(1)} %pack.1.near_ref), channel_id=1, source_target_pairs={{0,1},{1,0},{2,3},{3,2},{4,5},{5,4},{6,7},{7,6},{8,9},{9,8},{10,11... | collective-permute-start | bytes 6291464 | tf_op jit(solution)/shard_map/ppermute | solution.py:212
  79.5 1.8 copy-start.5
  81.4 1.8 copy-start.6
  83.2 1.9 copy-start.7
  113.7 129.5 %reduce-scatter.5.cloned.1.call-start = ((), (), s32[]{:S(2)}) async-start(), calls=%async_computation.4 | async-start | bytes 2228224 | tf_op jit(solution)/shard_map/reduce_scatter | solution.py:219
Sparse Core Ops, SparseCore 0:
  10.2 56.8 all-gather.1
  113.8 64.4 reduce-scatter.2
  182.6 60.6 reduce-scatter.4

commit v4 on v3

--- a/solution.py
+++ b/solution.py
@@ -27,54 +27,84 @@
     return pl.CostEstimate(flops=flops, bytes_accessed=read, transcendentals=0)
 
 
-def silu_grads(hidden, gate, up):
-    sigma = jax.nn.sigmoid(gate)
-    both = hidden * sigma
-    gg = both * up * (1.0 + gate * (1.0 - sigma))
-    return gg.astype(BF16), (both * gate).astype(BF16)
-
-
-def pack_kernel(at_ref, *refs):
+def any_specs(values):
+    return [pl.BlockSpec(memory_space=pl.ANY)] * len(values)
+
+
+def relay_kernel(in_ref, *rest):
+    rest[-1][...] = in_ref[...]
+
+
+def relay(value, after):
+    whole = pl.BlockSpec(memory_space=pltpu.VMEM)
+    return pl.pallas_call(
+        relay_kernel,
+        in_specs=[whole] + any_specs(after),
+        out_specs=whole,
+        out_shape=jax.ShapeDtypeStruct(value.shape, value.dtype),
+        compiler_params=params(8),
+        cost_estimate=cost(0, 4 * value.size),
+        name="relay",
+    )(value, *after)
+
+
+def pack_kernel(*refs):
     pieces, out_ref = refs[:-1], refs[-1]
-    row = pieces[0].shape[0]
     start = 0
     for piece in pieces:
-        part = piece.shape[0]
-        base = at_ref[start // row] * row + start % row
-        out_ref[pl.ds(pl.multiple_of(base, part), part), :] = piece[...]
-        start += part
-
-
-def pack(at, pieces):
+        out_ref[pl.ds(start, piece.shape[0]), :] = piece[...]
+        start += piece.shape[0]
+
+
+def pack(pieces):
     depth = pieces[0].shape[1]
     rows = sum(piece.shape[0] for piece in pieces)
+    whole = pl.BlockSpec(memory_space=pltpu.VMEM)
     return pl.pallas_call(
         pack_kernel,
-        in_specs=[pl.BlockSpec(memory_space=pltpu.SMEM)]
-        + [pl.BlockSpec(memory_space=pltpu.VMEM)] * len(pieces),
-        out_specs=pl.BlockSpec(memory_space=pltpu.VMEM),
+        in_specs=[whole] * len(pieces),
+        out_specs=whole,
         out_shape=jax.ShapeDtypeStruct((rows, depth), BF16),
-        compiler_params=params(16),
+        compiler_params=params(8),
         cost_estimate=cost(0, 4 * rows * depth),
         name="pack",
-    )(at, *pieces)
-
-
-def gate_up_kernel(row, core_ref, near_ref, far_ref, wg_ref, wu_ref, gate_ref, up_ref, x_ref):
+    )(*pieces)
+
+
+def places(chips, row):
+    span = chips // SEQS
+    for q in range(SEQS):
+        for side in range(2):
+            for k in range(span):
+                yield q * span + k, side, ((q * 2 + side) * span + k) * row
+
+
+def arrange(spot_ref, near_ref, far_ref, out_ref):
+    chips = spot_ref.shape[0]
+    row = near_ref.shape[0] // chips
+    for chip, side, place in places(chips, row):
+        start = pl.multiple_of(spot_ref[chip] * row, row)
+        out_ref[pl.ds(place, row), :] = (near_ref, far_ref)[side][pl.ds(start, row), :]
+
+
+def gate_up_kernel(parts, spot_ref, near_ref, far_ref, wg_ref, wu_ref, *rest):
+    a_ref, b_ref, x_ref = rest[-3:]
+
     @pl.when(pl.program_id(0) == 0)
     def _():
-        mine = core_ref[0]
-        for c in range(near_ref.shape[0] // row):
-            at = pl.ds(c * row, row)
-            base = 2 * c * row
-            x_ref[pl.ds(pl.multiple_of(base + mine * row, row), row), :] = near_ref[at, :]
-            x_ref[pl.ds(pl.multiple_of(base + (1 - mine) * row, row), row), :] = far_ref[at, :]
-
-    gate_ref[...] = jnp.dot(x_ref[...], wg_ref[...], preferred_element_type=F32)
-    up_ref[...] = jnp.dot(x_ref[...], wu_ref[...], preferred_element_type=F32)
-
-
-def gate_up(core, near, far, wg, wu, row):
+        arrange(spot_ref, near_ref, far_ref, x_ref)
+
+    rows = x_ref.shape[0] // parts
+    for p in range(parts):
+        at = pl.ds(p * rows, rows)
+        gate = jnp.dot(x_ref[at, :], wg_ref[...], preferred_element_type=F32)
+        up = jnp.dot(x_ref[at, :], wu_ref[...], preferred_element_type=F32)
+        sigma = jax.nn.sigmoid(gate)
+        a_ref[at, :] = up * sigma * (1.0 + gate * (1.0 - sigma))
+        b_ref[at, :] = gate * sigma
+
+
+def gate_up(spot, near, far, wg, wu, after):
     rows, depth = near.shape
     width = wg.shape[1]
     step = tile(width, 256)
@@ -82,74 +112,153 @@
     column = pl.BlockSpec((depth, step), lambda j: (0, j))
     out = pl.BlockSpec((2 * rows, step), lambda j: (0, j))
     return pl.pallas_call(
-        functools.partial(gate_up_kernel, row),
+        functools.partial(gate_up_kernel, 2),
         grid=(width // step,),
-        in_specs=[pl.BlockSpec(memory_space=pltpu.SMEM), half, half, column, column],
+        in_specs=[pl.BlockSpec(memory_space=pltpu.SMEM), half, half, column, column]
+        + any_specs(after),
         out_specs=[out, out, pl.BlockSpec((2 * rows, depth), lambda j: (0, 0))],
         out_shape=[jax.ShapeDtypeStruct((2 * rows, width), F32)] * 2
         + [jax.ShapeDtypeStruct((2 * rows, depth), BF16)],
         compiler_params=params(36),
         cost_estimate=cost(8 * rows * depth * width, 4 * depth * width),
         name="gate_up",
-    )(core, near, far, wg, wu)
-
-
-def back_kernel(parts, dy_ref, wd_ref, gate_ref, up_ref, gg_ref, gu_ref):
-    rows = dy_ref.shape[0] // parts
-    for p in range(parts):
-        at = pl.ds(p * rows, rows)
-        hidden = lax.dot_general(dy_ref[at, :], wd_ref[...], NT, preferred_element_type=F32)
-        gg_ref[at, :], gu_ref[at, :] = silu_grads(hidden, gate_ref[at, :], up_ref[at, :])
-
-
-def back(dy, wd, gate, up):
-    rows, depth = dy.shape
+    )(spot, near, far, wg, wu, *after)
+
+
+def back_kernel(
+    tiles, spot_ref, near_ref, far_ref, wd_ref, a_ref, b_ref, wg_ref, wu_ref,
+    gg_ref, gu_ref, own_ref, sent_ref, dy_ref,
+):
+    j = pl.program_id(0)
+    chips = spot_ref.shape[0]
+    row = near_ref.shape[0] // chips
+    step = wd_ref.shape[0]
+
+    @pl.when(j == 0)
+    def _():
+        arrange(spot_ref, near_ref, far_ref, dy_ref)
+
+    @pl.when(j < tiles)
+    def _():
+        hidden = lax.dot_general(dy_ref[...], wd_ref[...], NT, preferred_element_type=F32)
+        at = pl.ds(pl.multiple_of(j * step, step), step)
+        gg_ref[:, at] = (hidden * a_ref[...]).astype(BF16)
+        gu_ref[:, at] = (hidden * b_ref[...]).astype(BF16)
+
+    @pl.when(j >= tiles)
+    def _():
+        total = lax.dot_general(gg_ref[...], wg_ref[...], NT, preferred_element_type=F32)
+        total += lax.dot_general(gu_ref[...], wu_ref[...], NT, preferred_element_type=F32)
+        for chip, side, place in places(chips, row):
+            start = pl.multiple_of(spot_ref[chip] * row, row)
+            terms = total[place : place + row, :]
+            if side:
+                sent_ref[pl.ds(start, row), :] = terms.astype(BF16)
+            else:
+                own_ref[pl.ds(start, row), :] = terms
+
+
+def back(spot, near, far, wd, a, b, wg, wu):
+    rows, depth = near.shape
     width = wd.shape[0]
     step = tile(width, 256)
-    column = pl.BlockSpec((rows, step), lambda j: (0, j))
-    return pl.pallas_call(
-        functools.partial(back_kernel, 2),
-        grid=(width // step,),
+    tiles = width // step
+    deep = 256
+
+    def early(j):
+        return jnp.minimum(j, tiles - 1)
+
+    def late(j):
+        return jnp.maximum(j - tiles, 0)
+
+    half = pl.BlockSpec((rows, depth), lambda j: (0, 0))
+    column = pl.BlockSpec((2 * rows, step), lambda j: (0, early(j)))
+    weight = pl.BlockSpec((deep, width), lambda j: (late(j), 0))
+    grads = pl.BlockSpec((2 * rows, width), lambda j: (0, 0))
+    terms = pl.BlockSpec((rows, deep), lambda j: (0, late(j)))
+    return pl.pallas_call(
+        functools.partial(back_kernel, tiles),
+        grid=(tiles + depth // deep,),
         in_specs=[
-            pl.BlockSpec((rows, depth), lambda j: (0, 0)),
-            pl.BlockSpec((step, depth), lambda j: (j, 0)),
+            pl.BlockSpec(memory_space=pltpu.SMEM),
+            half,
+            half,
+            pl.BlockSpec((step, depth), lambda j: (early(j), 0)),
             column,
             column,
+            weight,
+            weight,
         ],
-        out_specs=[column, column],
-        out_shape=[jax.ShapeDtypeStruct((rows, width), BF16)] * 2,
-        compiler_params=params(58),
-        cost_estimate=cost(2 * rows * depth * width, 2 * depth * width),
+        out_specs=[grads, grads, terms, terms],
+        out_shape=[jax.ShapeDtypeStruct((2 * rows, width), BF16)] * 2
+        + [
+            jax.ShapeDtypeStruct((rows, depth), F32),
+            jax.ShapeDtypeStruct((rows, depth), BF16),
+        ],
+        scratch_shapes=[pltpu.VMEM((2 * rows, depth), BF16)],
+        compiler_params=params(34),
+        cost_estimate=cost(12 * rows * depth * width, 6 * depth * width),
         name="hidden_back",
-    )(dy, wd, gate, up)
-
-
-def input_kernel(gg_ref, gu_ref, wg_ref, wu_ref, *rest):
-    out_ref = rest[-1]
-    total = lax.dot_general(gg_ref[...], wg_ref[...], NT, preferred_element_type=F32)
-    total += lax.dot_general(gu_ref[...], wu_ref[...], NT, preferred_element_type=F32)
-    out_ref[...] = total.astype(BF16)
-
-
-def input_terms(gg, gu, wg, wu, first, count, step, after=()):
-    rows, width = gg.shape
-    whole = pl.BlockSpec((rows, width), lambda j: (0, 0))
-    weight = pl.BlockSpec((step, width), lambda j: (first + j, 0))
-    return pl.pallas_call(
-        input_kernel,
-        grid=(count,),
-        in_specs=[whole, whole, weight, weight]
-        + [pl.BlockSpec(memory_space=pl.ANY)] * len(after),
-        out_specs=pl.BlockSpec((rows, step), lambda j: (0, j)),
-        out_shape=jax.ShapeDtypeStruct((rows, count * step), BF16),
-        compiler_params=params(58),
-        cost_estimate=cost(4 * rows * width * count * step, 4 * width * count * step),
-        name="input_terms",
-    )(gg, gu, wg, wu, *after)
+    )(spot, near, far, wd, a, b, wg, wu)
+
+
+def fold_kernel(cuts, *refs):
+    count = len(cuts)
+    outs = refs[-count:]
+    for i, (at, got_at) in enumerate(cuts):
+        own_ref, near_ref, got_ref = refs[3 * i : 3 * i + 3]
+        out_ref = outs[i]
+        out_ref[...] = (own_ref[at, :] + near_ref[at, :].astype(F32)).astype(BF16)
+        if got_at is not None:
+            total = own_ref[got_at, :] + near_ref[got_at, :].astype(F32)
+            out_ref[got_at, :] = (total + got_ref[...].astype(F32)).astype(BF16)
+
+
+def fold(own, near, row, sends, after):
+    depth = own.shape[1]
+    operands, specs, shapes, cuts = [], [], [], []
+    for p, at, got_at, got in sends:
+        block = pl.BlockSpec((row, depth), lambda i, p=p: (p, 0))
+        got = near if got is None else got
+        size = got.shape[0] if got_at is not None else row
+        operands += [own, near, got]
+        specs += [block, block, pl.BlockSpec((size, depth), lambda i: (0, 0))]
+        shapes.append(jax.ShapeDtypeStruct((at.size, depth), BF16))
+        cuts.append((at, got_at))
+    return pl.pallas_call(
+        functools.partial(fold_kernel, cuts),
+        grid=(1,),
+        in_specs=specs + any_specs(after),
+        out_specs=[pl.BlockSpec(shape.shape, lambda i: (0, 0)) for shape in shapes],
+        out_shape=shapes,
+        compiler_params=params(24),
+        cost_estimate=cost(0, 16 * row * depth),
+        name="fold",
+    )(*operands, *after)
+
+
+def last_kernel(own_ref, near_ref, r_ref, l_ref, out_ref):
+    total = own_ref[...] + near_ref[...].astype(F32)
+    out_ref[...] = (total + r_ref[...].astype(F32) + l_ref[...].astype(F32)).astype(BF16)
+
+
+def last(own, near, r, l):
+    block = pl.BlockSpec(r.shape, lambda i: (0, 0))
+    return pl.pallas_call(
+        last_kernel,
+        grid=(1,),
+        in_specs=[block] * 4,
+        out_specs=block,
+        out_shape=jax.ShapeDtypeStruct(r.shape, BF16),
+        compiler_params=params(24),
+        cost_estimate=cost(0, 12 * r.size),
+        name="last",
+    )(own, near, r, l)
 
 
 def fisher_kernel(step, x_ref, gg_ref, gu_ref, *rest):
-    fg_ref, fu_ref = rest[-2:]
+    fg_ref, fu_ref, done_ref = rest[-3:]
+    done_ref[...] = jnp.zeros_like(done_ref)
     span = x_ref.shape[0] // SEQS
     seqs = [pl.ds(q * span, span) for q in range(SEQS)]
     cols = [x_ref[at, :].T for at in seqs]
@@ -163,22 +272,24 @@
             f_ref[:, at] = (total * (1.0 / SEQS)).astype(BF16)
 
 
-def fisher(x, gg, gu, step, after=()):
+def fisher(x, gg, gu, first, count, step, held, after):
     rows, depth = x.shape
     width = gg.shape[1]
-    held = pl.BlockSpec((rows, width), lambda j: (0, 0))
-    block = pl.BlockSpec((step, width), lambda j: (j, 0))
+    whole = pl.BlockSpec((rows, width), lambda j: (0, 0))
+    block = pl.BlockSpec((step, width), lambda j: (first + j, 0))
     return pl.pallas_call(
         functools.partial(fisher_kernel, tile(width, 256)),
-        grid=(depth // step,),
-        in_specs=[pl.BlockSpec((rows, step), lambda j: (0, j)), held, held]
-        + [pl.BlockSpec(memory_space=pl.ANY)] * len(after),
-        out_specs=[block, block],
-        out_shape=[jax.ShapeDtypeStruct((depth, width), BF16)] * 2,
-        compiler_params=params(58),
-        cost_estimate=cost(4 * rows * depth * width, 4 * depth * width),
+        grid=(count,),
+        in_specs=[pl.BlockSpec((rows, step), lambda j: (0, first + j)), whole, whole]
+        + any_specs((*held, *after)),
+        out_specs=[block, block, pl.BlockSpec((8, 128), lambda j: (0, 0))],
+        out_shape=[jax.ShapeDtypeStruct((depth, width), BF16)] * 2
+        + [jax.ShapeDtypeStruct((8, 128), F32)],
+        input_output_aliases={3 + i: i for i in range(len(held))},
+        compiler_params=params(40),
+        cost_estimate=cost(4 * rows * step * count * width, 4 * step * count * width),
         name="fisher",
-    )(x, gg, gu, *after)
+    )(x, gg, gu, *held, *after)
 
 
 def ring_part(tokens, grad_out, wg, wu, wd):
@@ -196,31 +307,48 @@
     def left(value):
         return lax.ppermute(value, "hid", to_left)
 
-    device = lax.axis_index("hid")
-    spot = [CYCLE.index(c) for c in range(chips)]
-    me = jnp.array(spot, jnp.int32)[device // 2]
-    at = jnp.array(CYCLE, jnp.int32)[(me - jnp.arange(chips, dtype=jnp.int32)) % chips]
-    core = (device % 2).astype(jnp.int32).reshape(1)
-
-    dy = lax.all_gather(grad_out, "hid", axis=0, tiled=True)
-    from_left, from_right = [tokens], [tokens]
-    for _ in range(1, far):
-        from_left.append(right(from_left[-1]))
-        from_right.append(left(from_right[-1]))
-    ends = [right(from_left[-1][: row // 2]), left(from_right[-1][row // 2 :])]
-    near = pack(at, from_left + ends + from_right[:0:-1])
-    apart = lax.ppermute(near, "hid", across)
-    gate, up, x = gate_up(core, near, apart, wg, wu, row)
-    gg, gu = back(dy, wd, gate, up)
-    half = depth // 512 // 2
-    low = input_terms(gg, gu, wg, wu, 0, half, 512)
-    high = input_terms(gg, gu, wg, wu, half, half, 512, (low,))
-    mine = [
-        lax.psum_scatter(terms, "hid", scatter_dimension=0, tiled=True)
-        for terms in (low, high)
-    ]
-    fg, fu = fisher(x, gg, gu, 512, (high,))
-    return fg, fu, jnp.concatenate(mine, axis=1)
+    def swap(value):
+        return lax.ppermute(value, "hid", across)
+
+    def gather(value):
+        r, l = [value], [value]
+        for _ in range(1, far):
+            r.append(right(r[-1]))
+            l.append(left(l[-1]))
+        ends = [right(r[-1][: row // 2]), left(l[-1][row // 2 :])]
+        return pack(r + ends + l[:0:-1]), (r[-1], l[-1])
+
+    cycle = jnp.array([CYCLE.index(c) for c in range(chips)], jnp.int32)
+    spot = (cycle[lax.axis_index("hid") // 2] - cycle) % chips
+
+    near_x, busy = gather(tokens)
+    far_x = swap(near_x)
+    near_dy, _ = gather(relay(grad_out, busy))
+    far_dy = swap(near_dy)
+    a, b, x = gate_up(spot, near_x, far_x, wg, wu, (near_dy,))
+    gg, gu, own, sent = back(spot, near_dy, far_dy, wd, a, b, wg, wu)
+
+    near = swap(sent)
+    full, head, tail = pl.ds(0, row), pl.ds(0, row // 2), pl.ds(row // 2, row // 2)
+    step = 512
+    counts = [2, 1, 2, 2, 1]
+    held, first = (), 0
+    r = l = None
+    ready = ()
+    for k in range(far, 0, -1):
+        *held, done = fisher(x, gg, gu, first, counts[far - k], step, held, ready)
+        first += counts[far - k]
+        if k == far:
+            sends = [(far, head, None, None), (far, tail, None, None)]
+        elif k == far - 1:
+            sends = [(chips - k, full, head, r), (k, full, tail, l)]
+        else:
+            sends = [(chips - k, full, full, r), (k, full, full, l)]
+        ready = fold(own, near, row, sends, (done,))
+        r, l = right(ready[0]), left(ready[1])
+    fg, fu, _ = fisher(x, gg, gu, first, counts[far], step, held, ready)
+    mine = last(own, near, r, l)
+    return fg, fu, mine
 
 
 def plain_forward_kernel(x_ref, wg_ref, wu_ref, gate_ref, up_ref):

time: 252 us -> 167 us (0.66)
  waiting for transfers between devices: 130 us -> 46.8 us
  starting transfers between devices: 10.6 us -> 26.4 us
  between operations: 13.8 us -> 0.73 us
  local copies, waits for them, and re-layouts: 11.6 us -> 7.04 us
    reduce_scatter x2 -> x0, waiting for transfers between devices: 96 us -> none  [ring_part(): lax.psum_scatter(terms, 'hid', scatter_dimension=0, tiled=True)]
    ppermute x4 -> x12, waiting for transfers between devices: 8.87 us -> 26.1 us  [left(): return lax.ppermute(value, 'hid', to_left)]
    ppermute x4 -> x12, starting transfers between devices: 10.1 us -> 21.5 us  [right(): return lax.ppermute(value, 'hid', to_right)]
    ppermute x1 -> x3, waiting for transfers between devices: 4.27 us -> 0.01 us  [swap(): return lax.ppermute(value, 'hid', across)]
    ppermute x4 -> x12, starting transfers between devices: 0.27 us -> 4.33 us  [left(): return lax.ppermute(value, 'hid', to_left)]
    unnamed x16 -> x10, local copies, waits for them, and re-layouts: 9.06 us -> 5.77 us
    pallas_call x1 -> x5, Pallas kernels: 20.8 us -> 23.7 us  [fisher(): pl.pallas_call(functools.partial(fisher_kernel, tile(width, 256)), grid=(...]
    pallas_call x5 -> x10, Pallas kernels: 62.1 us -> 60.3 us  [the longest x1 36.6 us: back(): pl.pallas_call(functools.partial(back_kernel, tiles), grid=(tiles + depth...]
  transfers between devices with their start and end apart: 12 -> 27, of which waited for: 10 -> 15; matrix products, arithmetic and copies ran while one was open for 1% -> 2% of each run, Pallas kernels for 22% -> 28%
where the time goes in v4:
time: 167 us; the launch traced here: 166 us
  Pallas kernels  84 us (50%)
  waiting for transfers between devices  46.8 us (28%)
  starting transfers between devices  26.4 us (16%)
  local copies, waits for them, and re-layouts  7.04 us (4%)
    pallas_call x1, Pallas kernels, back(): pl.pallas_call(functools.partial(back_kernel, tiles), grid=(tiles + depth...  36.6 us
    ppermute x12, waiting for transfers between devices, left(): return lax.ppermute(value, 'hid', to_left)  26.1 us
    pallas_call x5, Pallas kernels, fisher(): pl.pallas_call(functools.partial(fisher_kernel, tile(width, 256)), grid=(...  23.7 us
    ppermute x12, starting transfers between devices, right(): return lax.ppermute(value, 'hid', to_right)  21.5 us
    pallas_call x1, Pallas kernels, gate_up(): pl.pallas_call(functools.partial(gate_up_kernel, 2), grid=(width // step,...  20.7 us
    ppermute x12, waiting for transfers between devices, right(): return lax.ppermute(value, 'hid', to_right)  20.7 us
    unnamed x10, local copies, waits for them, and re-layouts  5.77 us
    ppermute x12, starting transfers between devices, left(): return lax.ppermute(value, 'hid', to_left)  4.33 us
  transfers between devices with their start and end apart: 27, of which 15 were waited for; matrix products, arithmetic and copies ran while one was open for 2% of the time, Pallas kernels for 28%

profile of v4, /device:TPU:0, one launch (start us, length us, event | category | flops | bytes accessed | tf_op | source)
XLA Modules:
  0.0 166.3 jit_solution(8606950424518282267)
XLA Ops:
  0.6 3.1 %collective-permute-start = (bf16[32,4096]{1,0:T(8,128)(2,1)}, bf16[32,4096]{1,0:T(8,128)(2,1)S(1)}, u32[]{:S(2)}, u32[]{:S(2)}) collective-permute-start(bf16[32,4096]{1,0:T(8,128)(2,1)} %refs_0_.1), channel_id=1, source_target_pairs={{0,4},{1,5},{4,8},{5,9},{8,12},{9,13},{12,14},{13,15},{14,10},{15,... | collective-permute-start | bytes 786440 | tf_op jit(solution)/shard_map/ppermute | solution.py:305
  3.7 6.4 %collective-permute-done.refs_1_ = bf16[32,4096]{1,0:T(8,128)(2,1)S(1)} collective-permute-done((bf16[32,4096]{1,0:T(8,128)(2,1)}, bf16[32,4096]{1,0:T(8,128)(2,1)S(1)}, u32[]{:S(2)}, u32[]{:S(2)}) %collective-permute-start) | collective-permute-done | bytes 262176 | tf_op jit(solution)/shard_map/ppermute | solution.py:305
  10.1 1.8 %collective-permute-start.1 = (bf16[32,4096]{1,0:T(8,128)(2,1)S(1)}, bf16[32,4096]{1,0:T(8,128)(2,1)S(1)}, u32[]{:S(2)}, u32[]{:S(2)}) collective-permute-start(bf16[32,4096]{1,0:T(8,128)(2,1)S(1)} %collective-permute-done.refs_1_), channel_id=1, source_target_pairs={{0,4},{1,5},{4,8},{5,9},{8,12},{9,13},{12,14},{13,15},{14,10},{15,... | collective-permute-start | bytes 786440 | tf_op jit(solution)/shard_map/ppermute | solution.py:305
  12.2 5.5 %collective-permute-done.1.refs_2_ = bf16[32,4096]{1,0:T(8,128)(2,1)S(1)} collective-permute-done((bf16[32,4096]{1,0:T(8,128)(2,1)S(1)}, bf16[32,4096]{1,0:T(8,128)(2,1)S(1)}, u32[]{:S(2)}, u32[]{:S(2)}) %collective-permute-start.1) | collective-permute-done | bytes 262176 | tf_op jit(solution)/shard_map/ppermute | solution.py:305
  19.7 4.5 %collective-permute-done.2.refs_3_.rest_0_ = bf16[32,4096]{1,0:T(8,128)(2,1)S(1)} collective-permute-done((bf16[32,4096]{1,0:T(8,128)(2,1)S(1)}, bf16[32,4096]{1,0:T(8,128)(2,1)S(1)}, u32[]{:S(2)}, u32[]{:S(2)}) %collective-permute-start.2) | collective-permute-done | bytes 262176 | tf_op jit(solution)/shard_map/ppermute | solution.py:305
  24.2 1.7 %collective-permute-start.3 = (bf16[16,4096]{1,0:T(8,128)(2,1)S(1)}, bf16[16,4096]{1,0:T(8,128)(2,1)S(1)}, u32[]{:S(2)}, u32[]{:S(2)}) collective-permute-start(bf16[16,4096]{1,0:T(8,128)(2,1)S(1)} %slice.16), channel_id=1, source_target_pairs={{0,4},{1,5},{4,8},{5,9},{8,12},{9,13},{12,14},{13,15},{14,10},{15,... | collective-permute-start | bytes 393224 | tf_op jit(solution)/shard_map/ppermute | solution.py:305
  26.4 2.9 %collective-permute-done.3.refs_4_ = bf16[16,4096]{1,0:T(8,128)(2,1)S(1)} collective-permute-done((bf16[16,4096]{1,0:T(8,128)(2,1)S(1)}, bf16[16,4096]{1,0:T(8,128)(2,1)S(1)}, u32[]{:S(2)}, u32[]{:S(2)}) %collective-permute-start.3) | collective-permute-done | bytes 131104 | tf_op jit(solution)/shard_map/ppermute | solution.py:305
  29.2 1.8 %collective-permute-done.7.refs_5_ = bf16[16,4096]{1,0:T(8,128)(2,1)S(1)} collective-permute-done((bf16[16,4096]{1,0:T(8,128)(2,1)S(1)}, bf16[16,4096]{1,0:T(8,128)(2,1)S(1)}, u32[]{:S(2)}, u32[]{:S(2)}) %collective-permute-start.7) | collective-permute-done | bytes 131104 | tf_op jit(solution)/shard_map/ppermute | solution.py:308
  35.2 6.7 %collective-permute-done.13.refs_8_ = bf16[32,4096]{1,0:T(8,128)(2,1)S(1)} collective-permute-done((bf16[32,4096]{1,0:T(8,128)(2,1)S(1)}, bf16[32,4096]{1,0:T(8,128)(2,1)S(1)}, u32[]{:S(2)}, u32[]{:S(2)}) %collective-permute-start.13) | collective-permute-done | bytes 262176 | tf_op jit(solution)/shard_map/ppermute | solution.py:308
  42.2 1.7 %collective-permute-start.10 = (bf16[32,4096]{1,0:T(8,128)(2,1)S(1)}, bf16[32,4096]{1,0:T(8,128)(2,1)S(1)}, u32[]{:S(2)}, u32[]{:S(2)}) collective-permute-start(bf16[32,4096]{1,0:T(8,128)(2,1)S(1)} %collective-permute-done.9.refs_1_), channel_id=1, source_target_pairs={{0,4},{1,5},{4,8},{5,9},{8,12},{9,13},{12,14},{13,15},{14,10},{15,... | collective-permute-start | bytes 786440 | tf_op jit(solution)/shard_map/ppermute | solution.py:305
  43.9 5.9 %collective-permute-done.14.refs_7_ = bf16[32,4096]{1,0:T(8,128)(2,1)S(1)} collective-permute-done((bf16[32,4096]{1,0:T(8,128)(2,1)S(1)}, bf16[32,4096]{1,0:T(8,128)(2,1)S(1)}, u32[]{:S(2)}, u32[]{:S(2)}) %collective-permute-start.14) | collective-permute-done | bytes 262176 | tf_op jit(solution)/shard_map/ppermute | solution.py:308
  51.8 5.0 %collective-permute-done.15.refs_6_ = bf16[32,4096]{1,0:T(8,128)(2,1)S(1)} collective-permute-done((bf16[32,4096]{1,0:T(8,128)(2,1)S(1)}, bf16[32,4096]{1,0:T(8,128)(2,1)S(1)}, u32[]{:S(2)}, u32[]{:S(2)}) %collective-permute-start.15) | collective-permute-done | bytes 262176 | tf_op jit(solution)/shard_map/ppermute | solution.py:308
  57.3 1.7 %collective-permute-start.12 = (bf16[16,4096]{1,0:T(8,128)(2,1)S(1)}, bf16[16,4096]{1,0:T(8,128)(2,1)S(1)}, u32[]{:S(2)}, u32[]{:S(2)}) collective-permute-start(bf16[16,4096]{1,0:T(8,128)(2,1)S(1)} %slice.18), channel_id=1, source_target_pairs={{0,4},{1,5},{4,8},{5,9},{8,12},{9,13},{12,14},{13,15},{14,10},{15,... | collective-permute-start | bytes 393224 | tf_op jit(solution)/shard_map/ppermute | solution.py:305
  59.0 2.9 %collective-permute-done.16.refs_5_ = bf16[16,4096]{1,0:T(8,128)(2,1)S(1)} collective-permute-done((bf16[16,4096]{1,0:T(8,128)(2,1)S(1)}, bf16[16,4096]{1,0:T(8,128)(2,1)S(1)}, u32[]{:S(2)}, u32[]{:S(2)}) %collective-permute-start.16) | collective-permute-done | bytes 131104 | tf_op jit(solution)/shard_map/ppermute | solution.py:308
  66.3 20.7 %gate_up.1 = (f32[512,1792]{1,0:T(8,128)S(1)}, f32[512,1792]{1,0:T(8,128)S(1)}, bf16[512,4096]{1,0:T(8,128)(2,1)S(1)}) custom-call(s32[8]{0:T(128)S(1)} %and_select_fusion.spot_ref, bf16[256,4096]{1,0:T(8,128)(2,1)S(1)} %pack.2.near_ref, bf16[256,4096]{1,0:T(8,128)(2,1)} %collective-permute-done.8.far_ref, bf16[4096,1792]{1,0:T(8,128)(2,1)} %wg_ref.3, ...), custom_call_target="tpu_custom_call" | custom-call | flops 15032385536 | bytes 29360128 | tf_op jit(solution)/shard_map/gate_up/pallas_call | solution.py:114
  87.0 1.8 %copy-done.3 = f32[512,1792]{1,0:T(8,128)} copy-done((f32[512,1792]{1,0:T(8,128)}, f32[512,1792]{1,0:T(8,128)S(1)}, u32[]{:S(2)}) %copy-start.3) | copy-done | bytes 3670040
  88.9 2.0 %copy-done.4 = f32[512,1792]{1,0:T(8,128)S(1)} copy-done((f32[512,1792]{1,0:T(8,128)S(1)}, f32[512,1792]{1,0:T(8,128)}, u32[]{:S(2)}) %copy-start.4) | copy-done | bytes 3670040
  90.9 36.6 %hidden_back.1 = (bf16[512,1792]{1,0:T(8,128)(2,1)S(1)}, bf16[512,1792]{1,0:T(8,128)(2,1)S(1)}, f32[256,4096]{1,0:T(8,128)}, bf16[256,4096]{1,0:T(8,128)(2,1)S(1)}) custom-call(s32[8]{0:T(128)S(1)} %and_select_fusion.spot_ref, bf16[256,4096]{1,0:T(8,128)(2,1)} %pack.3.rest_0_.near_ref, bf16[256,4096]{1,0:T(8,128)(2,1)} %collective-permute-done.17.far_ref, ...), custom_call_target="tpu_custom_call" | custom-call | flops 22548578304 | bytes 44040192 | tf_op jit(solution)/shard_map/hidden_back/pallas_call | solution.py:179
  128.0 5.6 %fisher.5 = (bf16[4096,1792]{1,0:T(8,128)(2,1)}, bf16[4096,1792]{1,0:T(8,128)(2,1)}, f32[8,128]{1,0:T(8,128)S(1)}) custom-call(bf16[512,4096]{1,0:T(8,128)(2,1)S(1)} %get-tuple-element.32.x_ref, bf16[512,1792]{1,0:T(8,128)(2,1)S(1)} %get-tuple-element.35.gg_ref, bf16[512,1792]{1,0:T(8,128)(2,1)S(1)} %get-tuple-element.36.gu_ref), custom_call_target="tpu_custom_call" | custom-call | flops 3758096384 | bytes 7340032 | tf_op jit(solution)/shard_map/fisher/pallas_call | solution.py:280
  133.7 1.7 %collective-permute-start.19 = (bf16[16,4096]{1,0:T(8,128)(2,1)S(1)}, bf16[16,4096]{1,0:T(8,128)(2,1)S(1)}, u32[]{:S(2)}, u32[]{:S(2)}) collective-permute-start(bf16[16,4096]{1,0:T(8,128)(2,1)S(1)} %get-tuple-element.42.rest_2_), channel_id=1, source_target_pairs={{0,4},{1,5},{4,8},{5,9},{8,12},{9,13},{12,14},{13,15},{14,10},{15,... | collective-permute-start | bytes 393224 | tf_op jit(solution)/shard_map/ppermute | solution.py:305
  135.8 3.4 %fisher.6 = (bf16[4096,1792]{1,0:T(8,128)(2,1)}, bf16[4096,1792]{1,0:T(8,128)(2,1)}, f32[8,128]{1,0:T(8,128)S(1)}) custom-call(bf16[512,4096]{1,0:T(8,128)(2,1)S(1)} %get-tuple-element.32.x_ref, bf16[512,1792]{1,0:T(8,128)(2,1)S(1)} %get-tuple-element.35.gg_ref, ...), custom_call_target="tpu_custom_call", output_to_operand_aliasing={{0}: (3, {}), {1}: (4, {})} | custom-call | flops 1879048192 | bytes 3670016 | tf_op jit(solution)/shard_map/fisher/pallas_call | solution.py:280
  142.8 5.6 %fisher.7 = (bf16[4096,1792]{1,0:T(8,128)(2,1)}, bf16[4096,1792]{1,0:T(8,128)(2,1)}, f32[8,128]{1,0:T(8,128)S(1)}) custom-call(bf16[512,4096]{1,0:T(8,128)(2,1)S(1)} %get-tuple-element.32.x_ref, bf16[512,1792]{1,0:T(8,128)(2,1)S(1)} %get-tuple-element.35.gg_ref, ...), custom_call_target="tpu_custom_call", output_to_operand_aliasing={{0}: (3, {}), {1}: (4, {})} | custom-call | flops 3758096384 | bytes 7340032 | tf_op jit(solution)/shard_map/fisher/pallas_call | solution.py:280
  151.4 5.6 %fisher.8 = (bf16[4096,1792]{1,0:T(8,128)(2,1)}, bf16[4096,1792]{1,0:T(8,128)(2,1)}, f32[8,128]{1,0:T(8,128)S(1)}) custom-call(bf16[512,4096]{1,0:T(8,128)(2,1)S(1)} %get-tuple-element.32.x_ref, bf16[512,1792]{1,0:T(8,128)(2,1)S(1)} %get-tuple-element.35.gg_ref, ...), custom_call_target="tpu_custom_call", output_to_operand_aliasing={{0}: (3, {}), {1}: (4, {})} | custom-call | flops 3758096384 | bytes 7340032 | tf_op jit(solution)/shard_map/fisher/pallas_call | solution.py:280
  159.6 3.4 %fisher.9 = (bf16[4096,1792]{1,0:T(8,128)(2,1)}, bf16[4096,1792]{1,0:T(8,128)(2,1)}, f32[8,128]{1,0:T(8,128)}) custom-call(bf16[512,4096]{1,0:T(8,128)(2,1)S(1)} %get-tuple-element.32.x_ref, bf16[512,1792]{1,0:T(8,128)(2,1)S(1)} %get-tuple-element.35.gg_ref, ...), custom_call_target="tpu_custom_call", output_to_operand_aliasing={{0}: (3, {}), {1}: (4, {})} | custom-call | flops 1879048192 | bytes 3670016 | tf_op jit(solution)/shard_map/fisher/pallas_call | solution.py:280
  (61 shorter events, 27.3 us)
Async XLA Ops:
  0.6 9.5 %collective-permute-start = (bf16[32,4096]{1,0:T(8,128)(2,1)}, bf16[32,4096]{1,0:T(8,128)(2,1)S(1)}, u32[]{:S(2)}, u32[]{:S(2)}) collective-permute-start(bf16[32,4096]{1,0:T(8,128)(2,1)} %refs_0_.1), channel_id=1, source_target_pairs={{0,4},{1,5},{4,8},{5,9},{8,12},{9,13},{12,14},{13,15},{14,10},{15,... | collective-permute-start | bytes 786440 | tf_op jit(solution)/shard_map/ppermute | solution.py:305
  3.7 8.3 %collective-permute-start.4 = (bf16[32,4096]{1,0:T(8,128)(2,1)}, bf16[32,4096]{1,0:T(8,128)(2,1)S(1)}, u32[]{:S(2)}, u32[]{:S(2)}) collective-permute-start(bf16[32,4096]{1,0:T(8,128)(2,1)} %refs_0_.1), channel_id=1, source_target_pairs={{4,0},{5,1},{8,4},{9,5},{12,8},{13,9},{14,12},{15,13},{10,14},{11,... | collective-permute-start | bytes 786440 | tf_op jit(solution)/shard_map/ppermute | solution.py:308
  10.1 7.5 %collective-permute-start.1 = (bf16[32,4096]{1,0:T(8,128)(2,1)S(1)}, bf16[32,4096]{1,0:T(8,128)(2,1)S(1)}, u32[]{:S(2)}, u32[]{:S(2)}) collective-permute-start(bf16[32,4096]{1,0:T(8,128)(2,1)S(1)} %collective-permute-done.refs_1_), channel_id=1, source_target_pairs={{0,4},{1,5},{4,8},{5,9},{8,12},{9,13},{12,14},{13,15},{14,10},{15,... | collective-permute-start | bytes 786440 | tf_op jit(solution)/shard_map/ppermute | solution.py:305
  12.0 7.2 %collective-permute-start.5 = (bf16[32,4096]{1,0:T(8,128)(2,1)S(1)}, bf16[32,4096]{1,0:T(8,128)(2,1)S(1)}, u32[]{:S(2)}, u32[]{:S(2)}) collective-permute-start(bf16[32,4096]{1,0:T(8,128)(2,1)S(1)} %collective-permute-done.4.refs_8_), channel_id=1, source_target_pairs={{4,0},{5,1},{8,4},{9,5},{12,8},{13,9},{14,12},{15,13},{10,14},{11,... | collective-permute-start | bytes 786440 | tf_op jit(solution)/shard_map/ppermute | solution.py:308
  17.6 6.6 %collective-permute-start.2 = (bf16[32,4096]{1,0:T(8,128)(2,1)S(1)}, bf16[32,4096]{1,0:T(8,128)(2,1)S(1)}, u32[]{:S(2)}, u32[]{:S(2)}) collective-permute-start(bf16[32,4096]{1,0:T(8,128)(2,1)S(1)} %collective-permute-done.1.refs_2_), channel_id=1, source_target_pairs={{0,4},{1,5},{4,8},{5,9},{8,12},{9,13},{12,14},{13,15},{14,10},{15,... | collective-permute-start | bytes 786440 | tf_op jit(solution)/shard_map/ppermute | solution.py:305
  19.1 6.8 %collective-permute-start.6 = (bf16[32,4096]{1,0:T(8,128)(2,1)S(1)}, bf16[32,4096]{1,0:T(8,128)(2,1)S(1)}, u32[]{:S(2)}, u32[]{:S(2)}) collective-permute-start(bf16[32,4096]{1,0:T(8,128)(2,1)S(1)} %collective-permute-done.5.refs_7_), channel_id=1, source_target_pairs={{4,0},{5,1},{8,4},{9,5},{12,8},{13,9},{14,12},{15,13},{10,14},{11,... | collective-permute-start | bytes 786440 | tf_op jit(solution)/shard_map/ppermute | solution.py:308
  24.2 5.0 %collective-permute-start.3 = (bf16[16,4096]{1,0:T(8,128)(2,1)S(1)}, bf16[16,4096]{1,0:T(8,128)(2,1)S(1)}, u32[]{:S(2)}, u32[]{:S(2)}) collective-permute-start(bf16[16,4096]{1,0:T(8,128)(2,1)S(1)} %slice.16), channel_id=1, source_target_pairs={{0,4},{1,5},{4,8},{5,9},{8,12},{9,13},{12,14},{13,15},{14,10},{15,... | collective-permute-start | bytes 393224 | tf_op jit(solution)/shard_map/ppermute | solution.py:305
  32.1 34.2 %collective-permute-start.8 = (bf16[256,4096]{1,0:T(8,128)(2,1)S(1)}, bf16[256,4096]{1,0:T(8,128)(2,1)}, u32[]{:S(2)}, u32[]{:S(2)}) collective-permute-start(bf16[256,4096]{1,0:T(8,128)(2,1)S(1)} %pack.2.near_ref), channel_id=1, source_target_pairs={{0,1},{1,0},{2,3},{3,2},{4,5},{5,4},{6,7},{7,6},{8,9},{9,8},{10,11... | collective-permute-start | bytes 6291464 | tf_op jit(solution)/shard_map/ppermute | solution.py:311
  33.1 8.8 %collective-permute-start.13 = (bf16[32,4096]{1,0:T(8,128)(2,1)S(1)}, bf16[32,4096]{1,0:T(8,128)(2,1)S(1)}, u32[]{:S(2)}, u32[]{:S(2)}) collective-permute-start(bf16[32,4096]{1,0:T(8,128)(2,1)S(1)} %relay.1.refs_0_), channel_id=1, source_target_pairs={{4,0},{5,1},{8,4},{9,5},{12,8},{13,9},{14,12},{15,13},{10,14},{11,... | collective-permute-start | bytes 786440 | tf_op jit(solution)/shard_map/ppermute | solution.py:308
  33.5 8.7 %collective-permute-start.9 = (bf16[32,4096]{1,0:T(8,128)(2,1)S(1)}, bf16[32,4096]{1,0:T(8,128)(2,1)S(1)}, u32[]{:S(2)}, u32[]{:S(2)}) collective-permute-start(bf16[32,4096]{1,0:T(8,128)(2,1)S(1)} %relay.1.refs_0_), channel_id=1, source_target_pairs={{0,4},{1,5},{4,8},{5,9},{8,12},{9,13},{12,14},{13,15},{14,10},{15,... | collective-permute-start | bytes 786440 | tf_op jit(solution)/shard_map/ppermute | solution.py:305
  41.9 7.9 %collective-permute-start.14 = (bf16[32,4096]{1,0:T(8,128)(2,1)S(1)}, bf16[32,4096]{1,0:T(8,128)(2,1)S(1)}, u32[]{:S(2)}, u32[]{:S(2)}) collective-permute-start(bf16[32,4096]{1,0:T(8,128)(2,1)S(1)} %collective-permute-done.13.refs_8_), channel_id=1, source_target_pairs={{4,0},{5,1},{8,4},{9,5},{12,8},{13,9},{14,12},{15,13},{10,14},{11,... | collective-permute-start | bytes 786440 | tf_op jit(solution)/shard_map/ppermute | solution.py:308
  42.2 7.9 %collective-permute-start.10 = (bf16[32,4096]{1,0:T(8,128)(2,1)S(1)}, bf16[32,4096]{1,0:T(8,128)(2,1)S(1)}, u32[]{:S(2)}, u32[]{:S(2)}) collective-permute-start(bf16[32,4096]{1,0:T(8,128)(2,1)S(1)} %collective-permute-done.9.refs_1_), channel_id=1, source_target_pairs={{0,4},{1,5},{4,8},{5,9},{8,12},{9,13},{12,14},{13,15},{14,10},{15,... | collective-permute-start | bytes 786440 | tf_op jit(solution)/shard_map/ppermute | solution.py:305
  49.8 7.0 %collective-permute-start.15 = (bf16[32,4096]{1,0:T(8,128)(2,1)S(1)}, bf16[32,4096]{1,0:T(8,128)(2,1)S(1)}, u32[]{:S(2)}, u32[]{:S(2)}) collective-permute-start(bf16[32,4096]{1,0:T(8,128)(2,1)S(1)} %collective-permute-done.14.refs_7_), channel_id=1, source_target_pairs={{4,0},{5,1},{8,4},{9,5},{12,8},{13,9},{14,12},{15,13},{10,14},{11,... | collective-permute-start | bytes 786440 | tf_op jit(solution)/shard_map/ppermute | solution.py:308
  50.2 7.1 %collective-permute-start.11 = (bf16[32,4096]{1,0:T(8,128)(2,1)S(1)}, bf16[32,4096]{1,0:T(8,128)(2,1)S(1)}, u32[]{:S(2)}, u32[]{:S(2)}) collective-permute-start(bf16[32,4096]{1,0:T(8,128)(2,1)S(1)} %collective-permute-done.10.refs_2_), channel_id=1, source_target_pairs={{0,4},{1,5},{4,8},{5,9},{8,12},{9,13},{12,14},{13,15},{14,10},{15,... | collective-permute-start | bytes 786440 | tf_op jit(solution)/shard_map/ppermute | solution.py:305
  63.7 25.1 %collective-permute-start.17 = (bf16[256,4096]{1,0:T(8,128)(2,1)}, bf16[256,4096]{1,0:T(8,128)(2,1)}, u32[]{:S(2)}, u32[]{:S(2)}) collective-permute-start(bf16[256,4096]{1,0:T(8,128)(2,1)} %pack.3.rest_0_.near_ref), channel_id=1, source_target_pairs={{0,1},{1,0},{2,3},{3,2},{4,5},{5,4},{6,7},{7,6},{8,9},{9,8},{10,11... | collective-permute-start | bytes 6291464 | tf_op jit(solution)/shard_map/ppermute | solution.py:311
  127.5 6.1 %collective-permute-start.18 = (bf16[256,4096]{1,0:T(8,128)(2,1)S(1)}, bf16[256,4096]{1,0:T(8,128)(2,1)S(1)}, u32[]{:S(2)}, u32[]{:S(2)}) collective-permute-start(bf16[256,4096]{1,0:T(8,128)(2,1)S(1)} %get-tuple-element.40), channel_id=1, source_target_pairs={{0,1},{1,0},{2,3},{3,2},{4,5},{5,4},{6,7},{7,6},{8,9},{9,8},{10,11... | collective-permute-start | bytes 6291464 | tf_op jit(solution)/shard_map/ppermute | solution.py:311
  133.7 5.5 %collective-permute-start.19 = (bf16[16,4096]{1,0:T(8,128)(2,1)S(1)}, bf16[16,4096]{1,0:T(8,128)(2,1)S(1)}, u32[]{:S(2)}, u32[]{:S(2)}) collective-permute-start(bf16[16,4096]{1,0:T(8,128)(2,1)S(1)} %get-tuple-element.42.rest_2_), channel_id=1, source_target_pairs={{0,4},{1,5},{4,8},{5,9},{8,12},{9,13},{12,14},{13,15},{14,10},{15,... | collective-permute-start | bytes 393224 | tf_op jit(solution)/shard_map/ppermute | solution.py:305
  135.5 5.1 %collective-permute-start.20 = (bf16[16,4096]{1,0:T(8,128)(2,1)S(1)}, bf16[16,4096]{1,0:T(8,128)(2,1)S(1)}, u32[]{:S(2)}, u32[]{:S(2)}) collective-permute-start(bf16[16,4096]{1,0:T(8,128)(2,1)S(1)} %get-tuple-element.43.rest_3_), channel_id=1, source_target_pairs={{4,0},{5,1},{8,4},{9,5},{12,8},{13,9},{14,12},{15,13},{10,14},{11,... | collective-permute-start | bytes 393224 | tf_op jit(solution)/shard_map/ppermute | solution.py:308
  140.7 7.7 %collective-permute-start.21 = (bf16[32,4096]{1,0:T(8,128)(2,1)S(1)}, bf16[32,4096]{1,0:T(8,128)(2,1)S(1)}, u32[]{:S(2)}, u32[]{:S(2)}) collective-permute-start(bf16[32,4096]{1,0:T(8,128)(2,1)S(1)} %get-tuple-element.47.rest_2_), channel_id=1, source_target_pairs={{0,4},{1,5},{4,8},{5,9},{8,12},{9,13},{12,14},{13,15},{14,10},{15,... | collective-permute-start | bytes 786440 | tf_op jit(solution)/shard_map/ppermute | solution.py:305
  142.4 6.8 %collective-permute-start.22 = (bf16[32,4096]{1,0:T(8,128)(2,1)S(1)}, bf16[32,4096]{1,0:T(8,128)(2,1)S(1)}, u32[]{:S(2)}, u32[]{:S(2)}) collective-permute-start(bf16[32,4096]{1,0:T(8,128)(2,1)S(1)} %get-tuple-element.48.rest_3_), channel_id=1, source_target_pairs={{4,0},{5,1},{8,4},{9,5},{12,8},{13,9},{14,12},{15,13},{10,14},{11,... | collective-permute-start | bytes 786440 | tf_op jit(solution)/shard_map/ppermute | solution.py:308
  149.3 7.7 %collective-permute-start.23 = (bf16[32,4096]{1,0:T(8,128)(2,1)S(1)}, bf16[32,4096]{1,0:T(8,128)(2,1)S(1)}, u32[]{:S(2)}, u32[]{:S(2)}) collective-permute-start(bf16[32,4096]{1,0:T(8,128)(2,1)S(1)} %get-tuple-element.52.rest_2_), channel_id=1, source_target_pairs={{0,4},{1,5},{4,8},{5,9},{8,12},{9,13},{12,14},{13,15},{14,10},{15,... | collective-permute-start | bytes 786440 | tf_op jit(solution)/shard_map/ppermute | solution.py:305
  150.9 6.4 %collective-permute-start.24 = (bf16[32,4096]{1,0:T(8,128)(2,1)S(1)}, bf16[32,4096]{1,0:T(8,128)(2,1)S(1)}, u32[]{:S(2)}, u32[]{:S(2)}) collective-permute-start(bf16[32,4096]{1,0:T(8,128)(2,1)S(1)} %get-tuple-element.53.rest_3_), channel_id=1, source_target_pairs={{4,0},{5,1},{8,4},{9,5},{12,8},{13,9},{14,12},{15,13},{10,14},{11,... | collective-permute-start | bytes 786440 | tf_op jit(solution)/shard_map/ppermute | solution.py:308
  157.5 6.4 %collective-permute-start.25 = (bf16[32,4096]{1,0:T(8,128)(2,1)S(1)}, bf16[32,4096]{1,0:T(8,128)(2,1)S(1)}, u32[]{:S(2)}, u32[]{:S(2)}) collective-permute-start(bf16[32,4096]{1,0:T(8,128)(2,1)S(1)} %get-tuple-element.57.rest_2_), channel_id=1, source_target_pairs={{0,4},{1,5},{4,8},{5,9},{8,12},{9,13},{12,14},{13,15},{14,10},{15,... | collective-permute-start | bytes 786440 | tf_op jit(solution)/shard_map/ppermute | solution.py:305
  159.1 6.4 %collective-permute-start.26 = (bf16[32,4096]{1,0:T(8,128)(2,1)S(1)}, bf16[32,4096]{1,0:T(8,128)(2,1)S(1)}, u32[]{:S(2)}, u32[]{:S(2)}) collective-permute-start(bf16[32,4096]{1,0:T(8,128)(2,1)S(1)} %get-tuple-element.58.rest_3_), channel_id=1, source_target_pairs={{4,0},{5,1},{8,4},{9,5},{12,8},{13,9},{14,12},{15,13},{10,14},{11,... | collective-permute-start | bytes 786440 | tf_op jit(solution)/shard_map/ppermute | solution.py:308
  (8 other events, 27.0 us)

commit v5 on v4

--- a/solution.py
+++ b/solution.py
@@ -31,44 +31,31 @@
     return [pl.BlockSpec(memory_space=pl.ANY)] * len(values)
 
 
-def relay_kernel(in_ref, *rest):
-    rest[-1][...] = in_ref[...]
-
-
-def relay(value, after):
-    whole = pl.BlockSpec(memory_space=pltpu.VMEM)
-    return pl.pallas_call(
-        relay_kernel,
-        in_specs=[whole] + any_specs(after),
-        out_specs=whole,
-        out_shape=jax.ShapeDtypeStruct(value.shape, value.dtype),
-        compiler_params=params(8),
-        cost_estimate=cost(0, 4 * value.size),
-        name="relay",
-    )(value, *after)
-
-
-def pack_kernel(*refs):
-    pieces, out_ref = refs[:-1], refs[-1]
+def held_specs(count):
+    return [pl.BlockSpec(memory_space=pltpu.VMEM)] * count
+
+
+def pack_kernel(count, *refs):
+    out_ref = refs[-1]
     start = 0
-    for piece in pieces:
+    for piece in refs[:count]:
         out_ref[pl.ds(start, piece.shape[0]), :] = piece[...]
         start += piece.shape[0]
 
 
-def pack(pieces):
+def pack(pieces, after):
     depth = pieces[0].shape[1]
     rows = sum(piece.shape[0] for piece in pieces)
     whole = pl.BlockSpec(memory_space=pltpu.VMEM)
     return pl.pallas_call(
-        pack_kernel,
-        in_specs=[whole] * len(pieces),
+        functools.partial(pack_kernel, len(pieces)),
+        in_specs=[whole] * len(pieces) + any_specs(after),
         out_specs=whole,
         out_shape=jax.ShapeDtypeStruct((rows, depth), BF16),
         compiler_params=params(8),
         cost_estimate=cost(0, 4 * rows * depth),
         name="pack",
-    )(*pieces)
+    )(*pieces, *after)
 
 
 def places(chips, row):
@@ -95,31 +82,33 @@
         arrange(spot_ref, near_ref, far_ref, x_ref)
 
     rows = x_ref.shape[0] // parts
+    step = wg_ref.shape[1]
+    to = pl.ds(pl.multiple_of(pl.program_id(0) * step, step), step)
     for p in range(parts):
         at = pl.ds(p * rows, rows)
         gate = jnp.dot(x_ref[at, :], wg_ref[...], preferred_element_type=F32)
         up = jnp.dot(x_ref[at, :], wu_ref[...], preferred_element_type=F32)
         sigma = jax.nn.sigmoid(gate)
-        a_ref[at, :] = up * sigma * (1.0 + gate * (1.0 - sigma))
-        b_ref[at, :] = gate * sigma
+        a_ref[at, to] = up * sigma * (1.0 + gate * (1.0 - sigma))
+        b_ref[at, to] = gate * sigma
 
 
 def gate_up(spot, near, far, wg, wu, after):
     rows, depth = near.shape
     width = wg.shape[1]
     step = tile(width, 256)
-    half = pl.BlockSpec((rows, depth), lambda j: (0, 0))
     column = pl.BlockSpec((depth, step), lambda j: (0, j))
-    out = pl.BlockSpec((2 * rows, step), lambda j: (0, j))
     return pl.pallas_call(
         functools.partial(gate_up_kernel, 2),
         grid=(width // step,),
-        in_specs=[pl.BlockSpec(memory_space=pltpu.SMEM), half, half, column, column]
+        in_specs=[pl.BlockSpec(memory_space=pltpu.SMEM)]
+        + held_specs(2)
+        + [column, column]
         + any_specs(after),
-        out_specs=[out, out, pl.BlockSpec((2 * rows, depth), lambda j: (0, 0))],
+        out_specs=held_specs(3),
         out_shape=[jax.ShapeDtypeStruct((2 * rows, width), F32)] * 2
         + [jax.ShapeDtypeStruct((2 * rows, depth), BF16)],
-        compiler_params=params(36),
+        compiler_params=params(34),
         cost_estimate=cost(8 * rows * depth * width, 4 * depth * width),
         name="gate_up",
     )(spot, near, far, wg, wu, *after)
@@ -142,8 +131,8 @@
     def _():
         hidden = lax.dot_general(dy_ref[...], wd_ref[...], NT, preferred_element_type=F32)
         at = pl.ds(pl.multiple_of(j * step, step), step)
-        gg_ref[:, at] = (hidden * a_ref[...]).astype(BF16)
-        gu_ref[:, at] = (hidden * b_ref[...]).astype(BF16)
+        gg_ref[:, at] = (hidden * a_ref[:, at]).astype(BF16)
+        gu_ref[:, at] = (hidden * b_ref[:, at]).astype(BF16)
 
     @pl.when(j >= tiles)
     def _():
@@ -171,25 +160,17 @@
     def late(j):
         return jnp.maximum(j - tiles, 0)
 
-    half = pl.BlockSpec((rows, depth), lambda j: (0, 0))
-    column = pl.BlockSpec((2 * rows, step), lambda j: (0, early(j)))
     weight = pl.BlockSpec((deep, width), lambda j: (late(j), 0))
-    grads = pl.BlockSpec((2 * rows, width), lambda j: (0, 0))
     terms = pl.BlockSpec((rows, deep), lambda j: (0, late(j)))
     return pl.pallas_call(
         functools.partial(back_kernel, tiles),
         grid=(tiles + depth // deep,),
-        in_specs=[
-            pl.BlockSpec(memory_space=pltpu.SMEM),
-            half,
-            half,
-            pl.BlockSpec((step, depth), lambda j: (early(j), 0)),
-            column,
-            column,
-            weight,
-            weight,
-        ],
-        out_specs=[grads, grads, terms, terms],
+        in_specs=[pl.BlockSpec(memory_space=pltpu.SMEM)]
+        + held_specs(2)
+        + [pl.BlockSpec((step, depth), lambda j: (early(j), 0))]
+        + held_specs(2)
+        + [weight, weight],
+        out_specs=held_specs(2) + [terms, terms],
         out_shape=[jax.ShapeDtypeStruct((2 * rows, width), BF16)] * 2
         + [
             jax.ShapeDtypeStruct((rows, depth), F32),
@@ -256,12 +237,14 @@
     )(own, near, r, l)
 
 
-def fisher_kernel(step, x_ref, gg_ref, gu_ref, *rest):
+def fisher_kernel(step, first, x_ref, gg_ref, gu_ref, *rest):
     fg_ref, fu_ref, done_ref = rest[-3:]
+    deep = fg_ref.shape[0]
+    here = pl.ds(pl.multiple_of((first + pl.program_id(0)) * deep, deep), deep)
     done_ref[...] = jnp.zeros_like(done_ref)
     span = x_ref.shape[0] // SEQS
     seqs = [pl.ds(q * span, span) for q in range(SEQS)]
-    cols = [x_ref[at, :].T for at in seqs]
+    cols = [x_ref[at, here].T for at in seqs]
     for g_ref, f_ref in ((gg_ref, fg_ref), (gu_ref, fu_ref)):
         for c in range(g_ref.shape[1] // step):
             at = pl.ds(c * step, step)
@@ -275,13 +258,11 @@
 def fisher(x, gg, gu, first, count, step, held, after):
     rows, depth = x.shape
     width = gg.shape[1]
-    whole = pl.BlockSpec((rows, width), lambda j: (0, 0))
     block = pl.BlockSpec((step, width), lambda j: (first + j, 0))
     return pl.pallas_call(
-        functools.partial(fisher_kernel, tile(width, 256)),
+        functools.partial(fisher_kernel, tile(width, 256), first),
         grid=(count,),
-        in_specs=[pl.BlockSpec((rows, step), lambda j: (0, first + j)), whole, whole]
-        + any_specs((*held, *after)),
+        in_specs=held_specs(3) + any_specs((*held, *after)),
         out_specs=[block, block, pl.BlockSpec((8, 128), lambda j: (0, 0))],
         out_shape=[jax.ShapeDtypeStruct((depth, width), BF16)] * 2
         + [jax.ShapeDtypeStruct((8, 128), F32)],
@@ -310,28 +291,38 @@
     def swap(value):
         return lax.ppermute(value, "hid", across)
 
-    def gather(value):
-        r, l = [value], [value]
-        for _ in range(1, far):
-            r.append(right(r[-1]))
-            l.append(left(l[-1]))
-        ends = [right(r[-1][: row // 2]), left(l[-1][row // 2 :])]
-        return pack(r + ends + l[:0:-1]), (r[-1], l[-1])
+    def gather_both(x, dy):
+        r, l = [[x], [dy]], [[x], [dy]]
+        halves = slice(None, row // 2), slice(row // 2, None)
+        busy = ()
+        for step in range(far + 1):
+            live = [(i, step - i) for i in range(2) if 0 <= step - i < far]
+            ends = [side[i][-1] for i, _ in live for side in (r, l)]
+            ends, busy = lax.optimization_barrier((ends, busy))
+            for at, (i, k) in enumerate(live):
+                to_r, to_l = ends[2 * at : 2 * at + 2]
+                if k == far - 1:
+                    to_r, to_l = to_r[halves[0]], to_l[halves[1]]
+                r[i].append(right(to_r))
+                l[i].append(left(to_l))
+            busy = [side[i][-1] for i, _ in live for side in (r, l)]
+        return [r[i] + l[i][:0:-1] for i in range(2)]
 
     cycle = jnp.array([CYCLE.index(c) for c in range(chips)], jnp.int32)
     spot = (cycle[lax.axis_index("hid") // 2] - cycle) % chips
 
-    near_x, busy = gather(tokens)
+    blocks_x, blocks_dy = gather_both(tokens, grad_out)
+    near_x = pack(blocks_x, (spot,))
     far_x = swap(near_x)
-    near_dy, _ = gather(relay(grad_out, busy))
+    near_dy = pack(blocks_dy, ())
     far_dy = swap(near_dy)
     a, b, x = gate_up(spot, near_x, far_x, wg, wu, (near_dy,))
     gg, gu, own, sent = back(spot, near_dy, far_dy, wd, a, b, wg, wu)
 
     near = swap(sent)
     full, head, tail = pl.ds(0, row), pl.ds(0, row // 2), pl.ds(row // 2, row // 2)
-    step = 512
-    counts = [2, 1, 2, 2, 1]
+    step = 256
+    counts = [4, 2, 4, 4, 2]
     held, first = (), 0
     r = l = None
     ready = ()

time: 167 us -> 156 us (0.934)
  local copies, waits for them, and re-layouts: 7.04 us -> 3.18 us
  Pallas kernels: 84 us -> 80.4 us
  waiting for transfers between devices: 46.8 us -> 43.3 us
    ppermute x12, waiting for transfers between devices: 26.1 us -> 16.7 us  [left(): return lax.ppermute(value, 'hid', to_left)]
    ppermute x12, waiting for transfers between devices: 20.7 us -> 26.6 us  [right(): return lax.ppermute(value, 'hid', to_right)]
    unnamed x10 -> x6, local copies, waits for them, and re-layouts: 5.77 us -> 1.9 us
    ppermute x12, starting transfers between devices: 21.5 us -> 19.4 us  [right(): return lax.ppermute(value, 'hid', to_right)]
    ppermute x12, starting transfers between devices: 4.33 us -> 6.36 us  [left(): return lax.ppermute(value, 'hid', to_left)]
    pallas_call x8 -> x7, Pallas kernels: 25.3 us -> 24.1 us  [the longest x5 23.8 us: fisher(): pl.pallas_call(functools.partial(fisher_kernel, tile(width, 256), first),...]
  transfers between devices with their start and end apart: 27 -> 27, of which waited for: 15 -> 21; matrix products, arithmetic and copies ran while one was open for 2% -> 2% of each run, Pallas kernels for 28% -> 28%
where the time goes in v5:
time: 156 us; the launch traced here: 155 us
  Pallas kernels  80.4 us (52%)
  waiting for transfers between devices  43.3 us (28%)
  starting transfers between devices  26.3 us (17%)
  local copies, waits for them, and re-layouts  3.18 us (2%)
    pallas_call x1, Pallas kernels, back(): pl.pallas_call(functools.partial(back_kernel, tiles), grid=(tiles + depth...  35.4 us
    ppermute x12, waiting for transfers between devices, right(): return lax.ppermute(value, 'hid', to_right)  26.6 us
    pallas_call x5, Pallas kernels, fisher(): pl.pallas_call(functools.partial(fisher_kernel, tile(width, 256), first),...  23.8 us
    pallas_call x1, Pallas kernels, gate_up(): pl.pallas_call(functools.partial(gate_up_kernel, 2), grid=(width // step,...  19.6 us
    ppermute x12, starting transfers between devices, right(): return lax.ppermute(value, 'hid', to_right)  19.4 us
    ppermute x12, waiting for transfers between devices, left(): return lax.ppermute(value, 'hid', to_left)  16.7 us
    ppermute x12, starting transfers between devices, left(): return lax.ppermute(value, 'hid', to_left)  6.36 us
  transfers between devices with their start and end apart: 27, of which 21 were waited for; matrix products, arithmetic and copies ran while one was open for 2% of the time, Pallas kernels for 28%

profile of v5, /device:TPU:0, one launch (start us, length us, event | category | flops | bytes accessed | tf_op | source)
XLA Modules:
  0.0 155.3 jit_solution(17523356482222806746)
XLA Ops:
  0.6 3.1 %collective-permute-start = (bf16[32,4096]{1,0:T(8,128)(2,1)}, bf16[32,4096]{1,0:T(8,128)(2,1)S(1)}, u32[]{:S(2)}, u32[]{:S(2)}) collective-permute-start(bf16[32,4096]{1,0:T(8,128)(2,1)} %refs_0_.2), channel_id=1, source_target_pairs={{0,4},{1,5},{4,8},{5,9},{8,12},{9,13},{12,14},{13,15},{14,10},{15,... | collective-permute-start | bytes 786440 | tf_op jit(solution)/shard_map/ppermute | solution.py:286
  3.7 6.4 %collective-permute-done.refs_1_ = bf16[32,4096]{1,0:T(8,128)(2,1)S(1)} collective-permute-done((bf16[32,4096]{1,0:T(8,128)(2,1)}, bf16[32,4096]{1,0:T(8,128)(2,1)S(1)}, u32[]{:S(2)}, u32[]{:S(2)}) %collective-permute-start) | collective-permute-done | bytes 262176 | tf_op jit(solution)/shard_map/ppermute | solution.py:286
  11.7 1.6 %collective-permute-start.2 = (bf16[32,4096]{1,0:T(8,128)(2,1)S(1)}, bf16[32,4096]{1,0:T(8,128)(2,1)S(1)}, u32[]{:S(2)}, u32[]{:S(2)}) collective-permute-start(bf16[32,4096]{1,0:T(8,128)(2,1)S(1)} %collective-permute-done.refs_1_), channel_id=1, source_target_pairs={{0,4},{1,5},{4,8},{5,9},{8,12},{9,13},{12,14},{13,15},{14,10},{15,... | collective-permute-start | bytes 786440 | tf_op jit(solution)/shard_map/ppermute | solution.py:286
  13.7 1.6 %collective-permute-start.4 = (bf16[32,4096]{1,0:T(8,128)(2,1)}, bf16[32,4096]{1,0:T(8,128)(2,1)S(1)}, u32[]{:S(2)}, u32[]{:S(2)}) collective-permute-start(bf16[32,4096]{1,0:T(8,128)(2,1)} %refs_0_.3), channel_id=1, source_target_pairs={{0,4},{1,5},{4,8},{5,9},{8,12},{9,13},{12,14},{13,15},{14,10},{15,... | collective-permute-start | bytes 786440 | tf_op jit(solution)/shard_map/ppermute | solution.py:286
  15.7 5.2 %collective-permute-done.2.refs_2_ = bf16[32,4096]{1,0:T(8,128)(2,1)S(1)} collective-permute-done((bf16[32,4096]{1,0:T(8,128)(2,1)S(1)}, bf16[32,4096]{1,0:T(8,128)(2,1)S(1)}, u32[]{:S(2)}, u32[]{:S(2)}) %collective-permute-start.2) | collective-permute-done | bytes 262176 | tf_op jit(solution)/shard_map/ppermute | solution.py:286
  20.9 1.6 %collective-permute-done.3.refs_7_ = bf16[32,4096]{1,0:T(8,128)(2,1)S(1)} collective-permute-done((bf16[32,4096]{1,0:T(8,128)(2,1)S(1)}, bf16[32,4096]{1,0:T(8,128)(2,1)S(1)}, u32[]{:S(2)}, u32[]{:S(2)}) %collective-permute-start.3) | collective-permute-done | bytes 262176 | tf_op jit(solution)/shard_map/ppermute | solution.py:289
  22.5 1.7 %collective-permute-done.4.refs_1_ = bf16[32,4096]{1,0:T(8,128)(2,1)S(1)} collective-permute-done((bf16[32,4096]{1,0:T(8,128)(2,1)}, bf16[32,4096]{1,0:T(8,128)(2,1)S(1)}, u32[]{:S(2)}, u32[]{:S(2)}) %collective-permute-start.4) | collective-permute-done | bytes 262176 | tf_op jit(solution)/shard_map/ppermute | solution.py:286
  25.5 1.6 %collective-permute-start.6 = (bf16[32,4096]{1,0:T(8,128)(2,1)S(1)}, bf16[32,4096]{1,0:T(8,128)(2,1)S(1)}, u32[]{:S(2)}, u32[]{:S(2)}) collective-permute-start(bf16[32,4096]{1,0:T(8,128)(2,1)S(1)} %collective-permute-done.2.refs_2_), channel_id=1, source_target_pairs={{0,4},{1,5},{4,8},{5,9},{8,12},{9,13},{12,14},{13,15},{14,10},{15,... | collective-permute-start | bytes 786440 | tf_op jit(solution)/shard_map/ppermute | solution.py:286
  27.5 1.6 %collective-permute-start.8 = (bf16[32,4096]{1,0:T(8,128)(2,1)S(1)}, bf16[32,4096]{1,0:T(8,128)(2,1)S(1)}, u32[]{:S(2)}, u32[]{:S(2)}) collective-permute-start(bf16[32,4096]{1,0:T(8,128)(2,1)S(1)} %collective-permute-done.4.refs_1_), channel_id=1, source_target_pairs={{0,4},{1,5},{4,8},{5,9},{8,12},{9,13},{12,14},{13,15},{14,10},{15,... | collective-permute-start | bytes 786440 | tf_op jit(solution)/shard_map/ppermute | solution.py:286
  30.7 3.2 %collective-permute-done.6.refs_3_ = bf16[32,4096]{1,0:T(8,128)(2,1)S(1)} collective-permute-done((bf16[32,4096]{1,0:T(8,128)(2,1)S(1)}, bf16[32,4096]{1,0:T(8,128)(2,1)S(1)}, u32[]{:S(2)}, u32[]{:S(2)}) %collective-permute-start.6) | collective-permute-done | bytes 262176 | tf_op jit(solution)/shard_map/ppermute | solution.py:286
  36.7 2.3 %collective-permute-done.9.refs_7_ = bf16[32,4096]{1,0:T(8,128)(2,1)S(1)} collective-permute-done((bf16[32,4096]{1,0:T(8,128)(2,1)S(1)}, bf16[32,4096]{1,0:T(8,128)(2,1)S(1)}, u32[]{:S(2)}, u32[]{:S(2)}) %collective-permute-start.9) | collective-permute-done | bytes 262176 | tf_op jit(solution)/shard_map/ppermute | solution.py:289
  39.6 1.6 %collective-permute-start.10 = (bf16[16,4096]{1,0:T(8,128)(2,1)S(1)}, bf16[16,4096]{1,0:T(8,128)(2,1)S(1)}, u32[]{:S(2)}, u32[]{:S(2)}) collective-permute-start(bf16[16,4096]{1,0:T(8,128)(2,1)S(1)} %slice.12), channel_id=1, source_target_pairs={{0,4},{1,5},{4,8},{5,9},{8,12},{9,13},{12,14},{13,15},{14,10},{15,... | collective-permute-start | bytes 393224 | tf_op jit(solution)/shard_map/ppermute | solution.py:286
  42.5 1.6 %collective-permute-done.11.refs_5_ = bf16[16,4096]{1,0:T(8,128)(2,1)S(1)} collective-permute-done((bf16[16,4096]{1,0:T(8,128)(2,1)S(1)}, bf16[16,4096]{1,0:T(8,128)(2,1)S(1)}, u32[]{:S(2)}, u32[]{:S(2)}) %collective-permute-start.11) | collective-permute-done | bytes 131104 | tf_op jit(solution)/shard_map/ppermute | solution.py:289
  45.7 1.6 %collective-permute-start.13 = (bf16[32,4096]{1,0:T(8,128)(2,1)S(1)}, bf16[32,4096]{1,0:T(8,128)(2,1)S(1)}, u32[]{:S(2)}, u32[]{:S(2)}) collective-permute-start(bf16[32,4096]{1,0:T(8,128)(2,1)S(1)} %collective-permute-done.8.refs_2_), channel_id=1, source_target_pairs={{0,4},{1,5},{4,8},{5,9},{8,12},{9,13},{12,14},{13,15},{14,10},{15,... | collective-permute-start | bytes 786440 | tf_op jit(solution)/shard_map/ppermute | solution.py:286
  47.8 6.6 %collective-permute-done.13.refs_3_ = bf16[32,4096]{1,0:T(8,128)(2,1)S(1)} collective-permute-done((bf16[32,4096]{1,0:T(8,128)(2,1)S(1)}, bf16[32,4096]{1,0:T(8,128)(2,1)S(1)}, u32[]{:S(2)}, u32[]{:S(2)}) %collective-permute-start.13) | collective-permute-done | bytes 262176 | tf_op jit(solution)/shard_map/ppermute | solution.py:286
  57.8 2.9 %collective-permute-done.16.refs_5_ = bf16[16,4096]{1,0:T(8,128)(2,1)S(1)} collective-permute-done((bf16[16,4096]{1,0:T(8,128)(2,1)S(1)}, bf16[16,4096]{1,0:T(8,128)(2,1)S(1)}, u32[]{:S(2)}, u32[]{:S(2)}) %collective-permute-start.16) | collective-permute-done | bytes 131104 | tf_op jit(solution)/shard_map/ppermute | solution.py:289
  62.4 19.6 %gate_up.1 = (f32[512,1792]{1,0:T(8,128)S(1)}, f32[512,1792]{1,0:T(8,128)S(1)}, bf16[512,4096]{1,0:T(8,128)(2,1)S(1)}) custom-call(s32[8]{0:T(128)S(1)} %and_select_fusion.refs_9_.spot_ref, bf16[256,4096]{1,0:T(8,128)(2,1)S(1)} %pack.2.near_ref, bf16[256,4096]{1,0:T(8,128)(2,1)S(1)} %collective-permute-done.12.far_ref, bf16[4096,1792]{1,0:T(8,128)(2,1)} %wg_ref.3, ...), custom_call_target="tpu_custom_call" | custom-call | flops 15032385536 | bytes 29360128 | tf_op jit(solution)/shard_map/gate_up/pallas_call | solution.py:101
  82.0 35.4 %hidden_back.1 = (bf16[512,1792]{1,0:T(8,128)(2,1)S(1)}, bf16[512,1792]{1,0:T(8,128)(2,1)S(1)}, f32[256,4096]{1,0:T(8,128)}, bf16[256,4096]{1,0:T(8,128)(2,1)S(1)}) custom-call(s32[8]{0:T(128)S(1)} %and_select_fusion.refs_9_.spot_ref, bf16[256,4096]{1,0:T(8,128)(2,1)S(1)} %pack.3.rest_0_.near_ref, bf16[256,4096]{1,0:T(8,128)(2,1)S(1)} %collective-permute-done.17.far_ref, ...), custom_call_target="tpu_custom_call" | custom-call | flops 22548578304 | bytes 44040192 | tf_op jit(solution)/shard_map/hidden_back/pallas_call | solution.py:165
  117.8 5.7 %fisher.5 = (bf16[4096,1792]{1,0:T(8,128)(2,1)}, bf16[4096,1792]{1,0:T(8,128)(2,1)}, f32[8,128]{1,0:T(8,128)S(1)}) custom-call(bf16[512,4096]{1,0:T(8,128)(2,1)S(1)} %get-tuple-element.64.x_ref, bf16[512,1792]{1,0:T(8,128)(2,1)S(1)} %get-tuple-element.67.gg_ref, bf16[512,1792]{1,0:T(8,128)(2,1)S(1)} %get-tuple-element.68.gu_ref), custom_call_target="tpu_custom_call" | custom-call | flops 3758096384 | bytes 7340032 | tf_op jit(solution)/shard_map/fisher/pallas_call | solution.py:262
  123.6 1.6 %collective-permute-start.19 = (bf16[16,4096]{1,0:T(8,128)(2,1)S(1)}, bf16[16,4096]{1,0:T(8,128)(2,1)S(1)}, u32[]{:S(2)}, u32[]{:S(2)}) collective-permute-start(bf16[16,4096]{1,0:T(8,128)(2,1)S(1)} %get-tuple-element.74.rest_2_), channel_id=1, source_target_pairs={{0,4},{1,5},{4,8},{5,9},{8,12},{9,13},{12,14},{13,15},{14,10},{15,... | collective-permute-start | bytes 393224 | tf_op jit(solution)/shard_map/ppermute | solution.py:286
  125.7 3.3 %fisher.6 = (bf16[4096,1792]{1,0:T(8,128)(2,1)}, bf16[4096,1792]{1,0:T(8,128)(2,1)}, f32[8,128]{1,0:T(8,128)S(1)}) custom-call(bf16[512,4096]{1,0:T(8,128)(2,1)S(1)} %get-tuple-element.64.x_ref, bf16[512,1792]{1,0:T(8,128)(2,1)S(1)} %get-tuple-element.67.gg_ref, ...), custom_call_target="tpu_custom_call", output_to_operand_aliasing={{0}: (3, {}), {1}: (4, {})} | custom-call | flops 1879048192 | bytes 3670016 | tf_op jit(solution)/shard_map/fisher/pallas_call | solution.py:262
  132.6 5.7 %fisher.7 = (bf16[4096,1792]{1,0:T(8,128)(2,1)}, bf16[4096,1792]{1,0:T(8,128)(2,1)}, f32[8,128]{1,0:T(8,128)S(1)}) custom-call(bf16[512,4096]{1,0:T(8,128)(2,1)S(1)} %get-tuple-element.64.x_ref, bf16[512,1792]{1,0:T(8,128)(2,1)S(1)} %get-tuple-element.67.gg_ref, ...), custom_call_target="tpu_custom_call", output_to_operand_aliasing={{0}: (3, {}), {1}: (4, {})} | custom-call | flops 3758096384 | bytes 7340032 | tf_op jit(solution)/shard_map/fisher/pallas_call | solution.py:262
  141.1 5.7 %fisher.8 = (bf16[4096,1792]{1,0:T(8,128)(2,1)}, bf16[4096,1792]{1,0:T(8,128)(2,1)}, f32[8,128]{1,0:T(8,128)S(1)}) custom-call(bf16[512,4096]{1,0:T(8,128)(2,1)S(1)} %get-tuple-element.64.x_ref, bf16[512,1792]{1,0:T(8,128)(2,1)S(1)} %get-tuple-element.67.gg_ref, ...), custom_call_target="tpu_custom_call", output_to_operand_aliasing={{0}: (3, {}), {1}: (4, {})} | custom-call | flops 3758096384 | bytes 7340032 | tf_op jit(solution)/shard_map/fisher/pallas_call | solution.py:262
  149.1 3.3 %fisher.9 = (bf16[4096,1792]{1,0:T(8,128)(2,1)}, bf16[4096,1792]{1,0:T(8,128)(2,1)}, f32[8,128]{1,0:T(8,128)}) custom-call(bf16[512,4096]{1,0:T(8,128)(2,1)S(1)} %get-tuple-element.64.x_ref, bf16[512,1792]{1,0:T(8,128)(2,1)S(1)} %get-tuple-element.67.gg_ref, ...), custom_call_target="tpu_custom_call", output_to_operand_aliasing={{0}: (3, {}), {1}: (4, {})} | custom-call | flops 1879048192 | bytes 3670016 | tf_op jit(solution)/shard_map/fisher/pallas_call | solution.py:262
  (56 shorter events, 30.0 us)
Async XLA Ops:
  0.6 9.5 %collective-permute-start = (bf16[32,4096]{1,0:T(8,128)(2,1)}, bf16[32,4096]{1,0:T(8,128)(2,1)S(1)}, u32[]{:S(2)}, u32[]{:S(2)}) collective-permute-start(bf16[32,4096]{1,0:T(8,128)(2,1)} %refs_0_.2), channel_id=1, source_target_pairs={{0,4},{1,5},{4,8},{5,9},{8,12},{9,13},{12,14},{13,15},{14,10},{15,... | collective-permute-start | bytes 786440 | tf_op jit(solution)/shard_map/ppermute | solution.py:286
  3.7 8.0 %collective-permute-start.1 = (bf16[32,4096]{1,0:T(8,128)(2,1)}, bf16[32,4096]{1,0:T(8,128)(2,1)S(1)}, u32[]{:S(2)}, u32[]{:S(2)}) collective-permute-start(bf16[32,4096]{1,0:T(8,128)(2,1)} %refs_0_.2), channel_id=1, source_target_pairs={{4,0},{5,1},{8,4},{9,5},{12,8},{13,9},{14,12},{15,13},{10,14},{11,... | collective-permute-start | bytes 786440 | tf_op jit(solution)/shard_map/ppermute | solution.py:289
  11.7 9.2 %collective-permute-start.2 = (bf16[32,4096]{1,0:T(8,128)(2,1)S(1)}, bf16[32,4096]{1,0:T(8,128)(2,1)S(1)}, u32[]{:S(2)}, u32[]{:S(2)}) collective-permute-start(bf16[32,4096]{1,0:T(8,128)(2,1)S(1)} %collective-permute-done.refs_1_), channel_id=1, source_target_pairs={{0,4},{1,5},{4,8},{5,9},{8,12},{9,13},{12,14},{13,15},{14,10},{15,... | collective-permute-start | bytes 786440 | tf_op jit(solution)/shard_map/ppermute | solution.py:286
  13.3 9.2 %collective-permute-start.3 = (bf16[32,4096]{1,0:T(8,128)(2,1)S(1)}, bf16[32,4096]{1,0:T(8,128)(2,1)S(1)}, u32[]{:S(2)}, u32[]{:S(2)}) collective-permute-start(bf16[32,4096]{1,0:T(8,128)(2,1)S(1)} %collective-permute-done.1.refs_8_), channel_id=1, source_target_pairs={{4,0},{5,1},{8,4},{9,5},{12,8},{13,9},{14,12},{15,13},{10,14},{11,... | collective-permute-start | bytes 786440 | tf_op jit(solution)/shard_map/ppermute | solution.py:289
  13.7 10.4 %collective-permute-start.4 = (bf16[32,4096]{1,0:T(8,128)(2,1)}, bf16[32,4096]{1,0:T(8,128)(2,1)S(1)}, u32[]{:S(2)}, u32[]{:S(2)}) collective-permute-start(bf16[32,4096]{1,0:T(8,128)(2,1)} %refs_0_.3), channel_id=1, source_target_pairs={{0,4},{1,5},{4,8},{5,9},{8,12},{9,13},{12,14},{13,15},{14,10},{15,... | collective-permute-start | bytes 786440 | tf_op jit(solution)/shard_map/ppermute | solution.py:286
  15.3 10.2 %collective-permute-start.5 = (bf16[32,4096]{1,0:T(8,128)(2,1)}, bf16[32,4096]{1,0:T(8,128)(2,1)S(1)}, u32[]{:S(2)}, u32[]{:S(2)}) collective-permute-start(bf16[32,4096]{1,0:T(8,128)(2,1)} %refs_0_.3), channel_id=1, source_target_pairs={{4,0},{5,1},{8,4},{9,5},{12,8},{13,9},{14,12},{15,13},{10,14},{11,... | collective-permute-start | bytes 786440 | tf_op jit(solution)/shard_map/ppermute | solution.py:289
  25.5 8.5 %collective-permute-start.6 = (bf16[32,4096]{1,0:T(8,128)(2,1)S(1)}, bf16[32,4096]{1,0:T(8,128)(2,1)S(1)}, u32[]{:S(2)}, u32[]{:S(2)}) collective-permute-start(bf16[32,4096]{1,0:T(8,128)(2,1)S(1)} %collective-permute-done.2.refs_2_), channel_id=1, source_target_pairs={{0,4},{1,5},{4,8},{5,9},{8,12},{9,13},{12,14},{13,15},{14,10},{15,... | collective-permute-start | bytes 786440 | tf_op jit(solution)/shard_map/ppermute | solution.py:286
  27.0 8.2 %collective-permute-start.7 = (bf16[32,4096]{1,0:T(8,128)(2,1)S(1)}, bf16[32,4096]{1,0:T(8,128)(2,1)S(1)}, u32[]{:S(2)}, u32[]{:S(2)}) collective-permute-start(bf16[32,4096]{1,0:T(8,128)(2,1)S(1)} %collective-permute-done.3.refs_7_), channel_id=1, source_target_pairs={{4,0},{5,1},{8,4},{9,5},{12,8},{13,9},{14,12},{15,13},{10,14},{11,... | collective-permute-start | bytes 786440 | tf_op jit(solution)/shard_map/ppermute | solution.py:289
  27.5 9.2 %collective-permute-start.8 = (bf16[32,4096]{1,0:T(8,128)(2,1)S(1)}, bf16[32,4096]{1,0:T(8,128)(2,1)S(1)}, u32[]{:S(2)}, u32[]{:S(2)}) collective-permute-start(bf16[32,4096]{1,0:T(8,128)(2,1)S(1)} %collective-permute-done.4.refs_1_), channel_id=1, source_target_pairs={{0,4},{1,5},{4,8},{5,9},{8,12},{9,13},{12,14},{13,15},{14,10},{15,... | collective-permute-start | bytes 786440 | tf_op jit(solution)/shard_map/ppermute | solution.py:286
  29.1 10.0 %collective-permute-start.9 = (bf16[32,4096]{1,0:T(8,128)(2,1)S(1)}, bf16[32,4096]{1,0:T(8,128)(2,1)S(1)}, u32[]{:S(2)}, u32[]{:S(2)}) collective-permute-start(bf16[32,4096]{1,0:T(8,128)(2,1)S(1)} %collective-permute-done.5.refs_8_), channel_id=1, source_target_pairs={{4,0},{5,1},{8,4},{9,5},{12,8},{13,9},{14,12},{15,13},{10,14},{11,... | collective-permute-start | bytes 786440 | tf_op jit(solution)/shard_map/ppermute | solution.py:289
  39.1 5.0 %collective-permute-start.11 = (bf16[16,4096]{1,0:T(8,128)(2,1)S(1)}, bf16[16,4096]{1,0:T(8,128)(2,1)S(1)}, u32[]{:S(2)}, u32[]{:S(2)}) collective-permute-start(bf16[16,4096]{1,0:T(8,128)(2,1)S(1)} %slice.13), channel_id=1, source_target_pairs={{4,0},{5,1},{8,4},{9,5},{12,8},{13,9},{14,12},{15,13},{10,14},{11,... | collective-permute-start | bytes 393224 | tf_op jit(solution)/shard_map/ppermute | solution.py:289
  45.6 16.8 %collective-permute-start.12 = (bf16[256,4096]{1,0:T(8,128)(2,1)S(1)}, bf16[256,4096]{1,0:T(8,128)(2,1)S(1)}, u32[]{:S(2)}, u32[]{:S(2)}) collective-permute-start(bf16[256,4096]{1,0:T(8,128)(2,1)S(1)} %pack.2.near_ref), channel_id=1, source_target_pairs={{0,1},{1,0},{2,3},{3,2},{4,5},{5,4},{6,7},{7,6},{8,9},{9,8},{10,11... | collective-permute-start | bytes 6291464 | tf_op jit(solution)/shard_map/ppermute | solution.py:292
  45.7 8.7 %collective-permute-start.13 = (bf16[32,4096]{1,0:T(8,128)(2,1)S(1)}, bf16[32,4096]{1,0:T(8,128)(2,1)S(1)}, u32[]{:S(2)}, u32[]{:S(2)}) collective-permute-start(bf16[32,4096]{1,0:T(8,128)(2,1)S(1)} %collective-permute-done.8.refs_2_), channel_id=1, source_target_pairs={{0,4},{1,5},{4,8},{5,9},{8,12},{9,13},{12,14},{13,15},{14,10},{15,... | collective-permute-start | bytes 786440 | tf_op jit(solution)/shard_map/ppermute | solution.py:286
  47.3 8.4 %collective-permute-start.14 = (bf16[32,4096]{1,0:T(8,128)(2,1)S(1)}, bf16[32,4096]{1,0:T(8,128)(2,1)S(1)}, u32[]{:S(2)}, u32[]{:S(2)}) collective-permute-start(bf16[32,4096]{1,0:T(8,128)(2,1)S(1)} %collective-permute-done.9.refs_7_), channel_id=1, source_target_pairs={{4,0},{5,1},{8,4},{9,5},{12,8},{13,9},{14,12},{15,13},{10,14},{11,... | collective-permute-start | bytes 786440 | tf_op jit(solution)/shard_map/ppermute | solution.py:289
  62.3 19.7 %collective-permute-start.17 = (bf16[256,4096]{1,0:T(8,128)(2,1)S(1)}, bf16[256,4096]{1,0:T(8,128)(2,1)S(1)}, u32[]{:S(2)}, u32[]{:S(2)}) collective-permute-start(bf16[256,4096]{1,0:T(8,128)(2,1)S(1)} %pack.3.rest_0_.near_ref), channel_id=1, source_target_pairs={{0,1},{1,0},{2,3},{3,2},{4,5},{5,4},{6,7},{7,6},{8,9},{9,8},{10,11... | collective-permute-start | bytes 6291464 | tf_op jit(solution)/shard_map/ppermute | solution.py:292
  117.4 6.2 %collective-permute-start.18 = (bf16[256,4096]{1,0:T(8,128)(2,1)S(1)}, bf16[256,4096]{1,0:T(8,128)(2,1)S(1)}, u32[]{:S(2)}, u32[]{:S(2)}) collective-permute-start(bf16[256,4096]{1,0:T(8,128)(2,1)S(1)} %get-tuple-element.72), channel_id=1, source_target_pairs={{0,1},{1,0},{2,3},{3,2},{4,5},{5,4},{6,7},{7,6},{8,9},{9,8},{10,11... | collective-permute-start | bytes 6291464 | tf_op jit(solution)/shard_map/ppermute | solution.py:292
  123.6 5.5 %collective-permute-start.19 = (bf16[16,4096]{1,0:T(8,128)(2,1)S(1)}, bf16[16,4096]{1,0:T(8,128)(2,1)S(1)}, u32[]{:S(2)}, u32[]{:S(2)}) collective-permute-start(bf16[16,4096]{1,0:T(8,128)(2,1)S(1)} %get-tuple-element.74.rest_2_), channel_id=1, source_target_pairs={{0,4},{1,5},{4,8},{5,9},{8,12},{9,13},{12,14},{13,15},{14,10},{15,... | collective-permute-start | bytes 393224 | tf_op jit(solution)/shard_map/ppermute | solution.py:286
  125.3 5.2 %collective-permute-start.20 = (bf16[16,4096]{1,0:T(8,128)(2,1)S(1)}, bf16[16,4096]{1,0:T(8,128)(2,1)S(1)}, u32[]{:S(2)}, u32[]{:S(2)}) collective-permute-start(bf16[16,4096]{1,0:T(8,128)(2,1)S(1)} %get-tuple-element.75.rest_3_), channel_id=1, source_target_pairs={{4,0},{5,1},{8,4},{9,5},{12,8},{13,9},{14,12},{15,13},{10,14},{11,... | collective-permute-start | bytes 393224 | tf_op jit(solution)/shard_map/ppermute | solution.py:289
  130.5 7.8 %collective-permute-start.21 = (bf16[32,4096]{1,0:T(8,128)(2,1)S(1)}, bf16[32,4096]{1,0:T(8,128)(2,1)S(1)}, u32[]{:S(2)}, u32[]{:S(2)}) collective-permute-start(bf16[32,4096]{1,0:T(8,128)(2,1)S(1)} %get-tuple-element.79.rest_2_), channel_id=1, source_target_pairs={{0,4},{1,5},{4,8},{5,9},{8,12},{9,13},{12,14},{13,15},{14,10},{15,... | collective-permute-start | bytes 786440 | tf_op jit(solution)/shard_map/ppermute | solution.py:286
  132.1 6.8 %collective-permute-start.22 = (bf16[32,4096]{1,0:T(8,128)(2,1)S(1)}, bf16[32,4096]{1,0:T(8,128)(2,1)S(1)}, u32[]{:S(2)}, u32[]{:S(2)}) collective-permute-start(bf16[32,4096]{1,0:T(8,128)(2,1)S(1)} %get-tuple-element.80.rest_3_), channel_id=1, source_target_pairs={{4,0},{5,1},{8,4},{9,5},{12,8},{13,9},{14,12},{15,13},{10,14},{11,... | collective-permute-start | bytes 786440 | tf_op jit(solution)/shard_map/ppermute | solution.py:289
  139.1 7.8 %collective-permute-start.23 = (bf16[32,4096]{1,0:T(8,128)(2,1)S(1)}, bf16[32,4096]{1,0:T(8,128)(2,1)S(1)}, u32[]{:S(2)}, u32[]{:S(2)}) collective-permute-start(bf16[32,4096]{1,0:T(8,128)(2,1)S(1)} %get-tuple-element.84.rest_2_), channel_id=1, source_target_pairs={{0,4},{1,5},{4,8},{5,9},{8,12},{9,13},{12,14},{13,15},{14,10},{15,... | collective-permute-start | bytes 786440 | tf_op jit(solution)/shard_map/ppermute | solution.py:286
  140.1 6.8 %collective-permute-start.24 = (bf16[32,4096]{1,0:T(8,128)(2,1)S(1)}, bf16[32,4096]{1,0:T(8,128)(2,1)S(1)}, u32[]{:S(2)}, u32[]{:S(2)}) collective-permute-start(bf16[32,4096]{1,0:T(8,128)(2,1)S(1)} %get-tuple-element.85.rest_3_), channel_id=1, source_target_pairs={{4,0},{5,1},{8,4},{9,5},{12,8},{13,9},{14,12},{15,13},{10,14},{11,... | collective-permute-start | bytes 786440 | tf_op jit(solution)/shard_map/ppermute | solution.py:289
  147.1 6.4 %collective-permute-start.25 = (bf16[32,4096]{1,0:T(8,128)(2,1)S(1)}, bf16[32,4096]{1,0:T(8,128)(2,1)S(1)}, u32[]{:S(2)}, u32[]{:S(2)}) collective-permute-start(bf16[32,4096]{1,0:T(8,128)(2,1)S(1)} %get-tuple-element.89.rest_2_), channel_id=1, source_target_pairs={{0,4},{1,5},{4,8},{5,9},{8,12},{9,13},{12,14},{13,15},{14,10},{15,... | collective-permute-start | bytes 786440 | tf_op jit(solution)/shard_map/ppermute | solution.py:286
  148.1 6.4 %collective-permute-start.26 = (bf16[32,4096]{1,0:T(8,128)(2,1)S(1)}, bf16[32,4096]{1,0:T(8,128)(2,1)S(1)}, u32[]{:S(2)}, u32[]{:S(2)}) collective-permute-start(bf16[32,4096]{1,0:T(8,128)(2,1)S(1)} %get-tuple-element.90.rest_3_), channel_id=1, source_target_pairs={{4,0},{5,1},{8,4},{9,5},{12,8},{13,9},{14,12},{15,13},{10,14},{11,... | collective-permute-start | bytes 786440 | tf_op jit(solution)/shard_map/ppermute | solution.py:289
  (6 other events, 23.1 us)

commit v6 on v5

--- a/solution.py
+++ b/solution.py
@@ -29,6 +29,10 @@
 
 def any_specs(values):
     return [pl.BlockSpec(memory_space=pl.ANY)] * len(values)
+
+
+def hbm_specs(count):
+    return [pl.BlockSpec(memory_space=pltpu.HBM)] * count
 
 
 def held_specs(count):
@@ -58,129 +62,257 @@
     )(*pieces, *after)
 
 
-def places(chips, row):
-    span = chips // SEQS
-    for q in range(SEQS):
-        for side in range(2):
-            for k in range(span):
-                yield q * span + k, side, ((q * 2 + side) * span + k) * row
-
-
-def arrange(spot_ref, near_ref, far_ref, out_ref):
+def pack_turned_kernel(count, *refs):
+    pieces, out_ref = refs[:count], refs[-1]
+    step = 512
+    for c in range(0, out_ref.shape[0], step):
+        block = jnp.concatenate([piece[:, c : c + step] for piece in pieces], axis=0)
+        out_ref[c : c + step, :] = block.T
+
+
+def pack_turned(pieces, after):
+    depth = pieces[0].shape[1]
+    rows = sum(piece.shape[0] for piece in pieces)
+    return pl.pallas_call(
+        functools.partial(pack_turned_kernel, len(pieces)),
+        in_specs=held_specs(len(pieces)) + any_specs(after),
+        out_specs=pl.BlockSpec(memory_space=pltpu.VMEM),
+        out_shape=jax.ShapeDtypeStruct((depth, rows), BF16),
+        compiler_params=params(8),
+        cost_estimate=cost(0, 4 * rows * depth),
+        name="pack_turned",
+    )(*pieces, *after)
+
+
+def put_rows(spot_ref, side, value, out_ref, cols):
     chips = spot_ref.shape[0]
-    row = near_ref.shape[0] // chips
-    for chip, side, place in places(chips, row):
-        start = pl.multiple_of(spot_ref[chip] * row, row)
-        out_ref[pl.ds(place, row), :] = (near_ref, far_ref)[side][pl.ds(start, row), :]
-
-
-def gate_up_kernel(parts, spot_ref, near_ref, far_ref, wg_ref, wu_ref, *rest):
-    a_ref, b_ref, x_ref = rest[-3:]
-
-    @pl.when(pl.program_id(0) == 0)
-    def _():
-        arrange(spot_ref, near_ref, far_ref, x_ref)
-
-    rows = x_ref.shape[0] // parts
-    step = wg_ref.shape[1]
-    to = pl.ds(pl.multiple_of(pl.program_id(0) * step, step), step)
-    for p in range(parts):
-        at = pl.ds(p * rows, rows)
-        gate = jnp.dot(x_ref[at, :], wg_ref[...], preferred_element_type=F32)
-        up = jnp.dot(x_ref[at, :], wu_ref[...], preferred_element_type=F32)
-        sigma = jax.nn.sigmoid(gate)
-        a_ref[at, to] = up * sigma * (1.0 + gate * (1.0 - sigma))
-        b_ref[at, to] = gate * sigma
-
-
-def gate_up(spot, near, far, wg, wu, after):
+    row = value.shape[0] // chips
+    for p in range(chips):
+        start = pl.multiple_of(spot_ref[p] + side * chips // SEQS * row, row)
+        out_ref[pl.ds(start, row), cols] = value[p * row : (p + 1) * row, :]
+
+
+def arrange_kernel(spot_ref, near_ref, far_ref, *rest):
+    for side, ref in enumerate((near_ref, far_ref)):
+        put_rows(spot_ref, side, ref[...], rest[-1], slice(None))
+
+
+def arrange(spot, near, far, after):
     rows, depth = near.shape
-    width = wg.shape[1]
+    return pl.pallas_call(
+        arrange_kernel,
+        in_specs=[pl.BlockSpec(memory_space=pltpu.SMEM)] + held_specs(2) + any_specs(after),
+        out_specs=pl.BlockSpec(memory_space=pltpu.VMEM),
+        out_shape=jax.ShapeDtypeStruct((2 * rows, depth), BF16),
+        compiler_params=params(6),
+        cost_estimate=cost(0, 8 * rows * depth),
+        name="arrange",
+    )(spot, near, far, *after)
+
+
+CHUNKS = 4
+
+
+def gate_up_kernel(first, step, near_ref, far_ref, wg_ref, wu_ref, *rest):
+    a_ref, b_ref, w_buf, out_buf, sems, out_sems = rest[-6:]
+    rows, depth = near_ref.shape
+    part = depth // CHUNKS
+    tiles = a_ref.shape[0] // step
+
+    def fetch(t, k):
+        cols, deep, slot = pl.ds((first + t) * step, step), pl.ds(k * part, part), t % 2
+        return [
+            pltpu.make_async_copy(w_ref.at[deep, cols], w_buf.at[slot, i, deep], sems.at[slot, i, k])
+            for i, w_ref in enumerate((wg_ref, wu_ref))
+        ]
+
+    def store(t):
+        to = pl.ds(t * step, step)
+        return [
+            pltpu.make_async_copy(out_buf.at[t, i], ref.at[to, :], out_sems.at[t, i])
+            for i, ref in enumerate((a_ref, b_ref))
+        ]
+
+    def begin(t):
+        for k in range(CHUNKS):
+            for copy in fetch(t, k):
+                copy.start()
+
+    for t in range(min(2, tiles)):
+        begin(t)
+    for t in range(tiles):
+        sums = [[None, None], [None, None]]
+        for k in range(CHUNKS):
+            deep = pl.ds(k * part, part)
+            for copy in fetch(t, k):
+                copy.wait()
+            for side, x_ref in enumerate((near_ref, far_ref)):
+                for i in range(2):
+                    term = jnp.dot(
+                        x_ref[:, deep], w_buf[t % 2, i, deep, :], preferred_element_type=F32
+                    )
+                    before = sums[side][i]
+                    sums[side][i] = term if before is None else before + term
+        if t + 2 < tiles:
+            begin(t + 2)
+        for side, (gate, up) in enumerate(sums):
+            at = pl.ds(side * rows, rows)
+            sigma = jax.nn.sigmoid(gate)
+            out_buf[t, 0, :, at] = (up * sigma * (1.0 + gate * (1.0 - sigma))).T
+            out_buf[t, 1, :, at] = (gate * sigma).T
+        for copy in store(t):
+            copy.start()
+    for t in range(tiles):
+        for copy in store(t):
+            copy.wait()
+
+
+def gate_up(near, far, wg, wu, first, count, step, grant, after):
+    rows, depth = near.shape
+    return pl.pallas_call(
+        functools.partial(gate_up_kernel, first, step),
+        in_specs=held_specs(2)
+        + hbm_specs(2)
+        + any_specs(after),
+        out_specs=hbm_specs(2),
+        out_shape=[jax.ShapeDtypeStruct((count * step, 2 * rows), F32)] * 2,
+        scratch_shapes=[
+            pltpu.VMEM((2, 2, depth, step), BF16),
+            pltpu.VMEM((count, 2, step, 2 * rows), F32),
+            pltpu.SemaphoreType.DMA((2, 2, CHUNKS)),
+            pltpu.SemaphoreType.DMA((count, 2)),
+        ],
+        compiler_params=params(grant),
+        cost_estimate=cost(8 * rows * depth * count * step, 4 * depth * count * step),
+        name="gate_up",
+    )(near, far, wg, wu, *after)
+
+
+def back_kernel(step, deep, pieces, spot_ref, near_ref, far_ref, wg_ref, wu_ref, wd_ref, *refs):
+    a_refs, b_refs = refs[:pieces], refs[pieces : 2 * pieces]
+    ggs_ref, gus_ref, own_ref, sent_ref, gg_ref, gu_ref = refs[2 * pieces : 2 * pieces + 6]
+    wd_buf, w_buf, factor_buf, sems, w_sems, factor_sems = refs[2 * pieces + 6 :]
+    rows = near_ref.shape[1]
+    tiles = wd_ref.shape[0] // step
+
+    part = wd_ref.shape[1] // CHUNKS
+
+    def fetch(t, k):
+        at = pl.ds(pl.multiple_of(t * step, step), step)
+        deep = pl.ds(k * part, part)
+        slot = lax.rem(t, 2)
+        return pltpu.make_async_copy(
+            wd_ref.at[at, deep], wd_buf.at[slot, :, deep], sems.at[slot, k]
+        )
+
+    def fetch_rows(i):
+        at = pl.ds(pl.multiple_of(i * deep, deep), deep)
+        slot = lax.rem(i, 2)
+        return [
+            pltpu.make_async_copy(w_ref.at[at, :], w_buf.at[slot, k], w_sems.at[slot, k])
+            for k, w_ref in enumerate((wg_ref, wu_ref))
+        ]
+
+    starts = [0]
+    for a_ref in a_refs:
+        starts.append(starts[-1] + a_ref.shape[0])
+
+    def fetch_factors(p):
+        at = pl.ds(starts[p], starts[p + 1] - starts[p])
+        return [
+            pltpu.make_async_copy(ref, factor_buf.at[k, at, :], factor_sems.at[k, p])
+            for k, ref in enumerate((a_refs[p], b_refs[p]))
+        ]
+
+    blocks = wg_ref.shape[0] // deep
+    for t in range(min(2, tiles)):
+        for k in range(CHUNKS):
+            fetch(jnp.int32(t), k).start()
+        if t == 0:
+            for copy in fetch_factors(0):
+                copy.start()
+    for p in range(pieces):
+        if p + 1 < pieces:
+            for copy in fetch_factors(p + 1):
+                copy.start()
+        else:
+            for i in range(2):
+                for copy in fetch_rows(jnp.int32(i)):
+                    copy.start()
+        for copy in fetch_factors(p):
+            copy.wait()
+
+        @pl.loop(starts[p] // step, starts[p + 1] // step)
+        def _(t):
+            cols = pl.ds(pl.multiple_of(t * step, step), step)
+            sums = [None, None]
+            for k in range(CHUNKS):
+                deep_k = pl.ds(k * part, part)
+                fetch(t, k).wait()
+                for side, dy_ref in enumerate((near_ref, far_ref)):
+                    term = jnp.dot(
+                        wd_buf[lax.rem(t, 2), :, deep_k], dy_ref[deep_k, :],
+                        preferred_element_type=F32,
+                    )
+                    sums[side] = term if sums[side] is None else sums[side] + term
+            for side, hidden in enumerate(sums):
+                at = pl.ds(side * rows, rows)
+                for f, (g_ref, gs_ref) in enumerate(((gg_ref, ggs_ref), (gu_ref, gus_ref))):
+                    grad = (hidden * factor_buf[f, cols, at]).astype(BF16)
+                    g_ref[cols, at] = grad
+                    put_rows(spot_ref, side, grad.T, gs_ref, cols)
+
+            @pl.when(t + 2 < tiles)
+            def _():
+                for k in range(CHUNKS):
+                    fetch(t + 2, k).start()
+
+    @pl.loop(0, blocks)
+    def _(i):
+        at = pl.ds(pl.multiple_of(i * deep, deep), deep)
+        slot = lax.rem(i, 2)
+        for copy in fetch_rows(i):
+            copy.wait()
+        for side, out_ref in enumerate((own_ref, sent_ref)):
+            of = pl.ds(side * rows, rows)
+            total = jnp.dot(w_buf[slot, 0], gg_ref[:, of], preferred_element_type=F32)
+            total += jnp.dot(w_buf[slot, 1], gu_ref[:, of], preferred_element_type=F32)
+            out_ref[:, at] = total.astype(BF16).T
+
+        @pl.when(i + 2 < blocks)
+        def _():
+            for copy in fetch_rows(i + 2):
+                copy.start()
+
+
+def back(spot, near, far, wg, wu, wd, factors):
+    depth, rows = near.shape
+    width = wd.shape[0]
     step = tile(width, 256)
-    column = pl.BlockSpec((depth, step), lambda j: (0, j))
-    return pl.pallas_call(
-        functools.partial(gate_up_kernel, 2),
-        grid=(width // step,),
+    a = [pair[0] for pair in factors]
+    b = [pair[1] for pair in factors]
+    return pl.pallas_call(
+        functools.partial(back_kernel, step, 512, len(a)),
         in_specs=[pl.BlockSpec(memory_space=pltpu.SMEM)]
         + held_specs(2)
-        + [column, column]
-        + any_specs(after),
-        out_specs=held_specs(3),
-        out_shape=[jax.ShapeDtypeStruct((2 * rows, width), F32)] * 2
-        + [jax.ShapeDtypeStruct((2 * rows, depth), BF16)],
-        compiler_params=params(34),
-        cost_estimate=cost(8 * rows * depth * width, 4 * depth * width),
-        name="gate_up",
-    )(spot, near, far, wg, wu, *after)
-
-
-def back_kernel(
-    tiles, spot_ref, near_ref, far_ref, wd_ref, a_ref, b_ref, wg_ref, wu_ref,
-    gg_ref, gu_ref, own_ref, sent_ref, dy_ref,
-):
-    j = pl.program_id(0)
-    chips = spot_ref.shape[0]
-    row = near_ref.shape[0] // chips
-    step = wd_ref.shape[0]
-
-    @pl.when(j == 0)
-    def _():
-        arrange(spot_ref, near_ref, far_ref, dy_ref)
-
-    @pl.when(j < tiles)
-    def _():
-        hidden = lax.dot_general(dy_ref[...], wd_ref[...], NT, preferred_element_type=F32)
-        at = pl.ds(pl.multiple_of(j * step, step), step)
-        gg_ref[:, at] = (hidden * a_ref[:, at]).astype(BF16)
-        gu_ref[:, at] = (hidden * b_ref[:, at]).astype(BF16)
-
-    @pl.when(j >= tiles)
-    def _():
-        total = lax.dot_general(gg_ref[...], wg_ref[...], NT, preferred_element_type=F32)
-        total += lax.dot_general(gu_ref[...], wu_ref[...], NT, preferred_element_type=F32)
-        for chip, side, place in places(chips, row):
-            start = pl.multiple_of(spot_ref[chip] * row, row)
-            terms = total[place : place + row, :]
-            if side:
-                sent_ref[pl.ds(start, row), :] = terms.astype(BF16)
-            else:
-                own_ref[pl.ds(start, row), :] = terms
-
-
-def back(spot, near, far, wd, a, b, wg, wu):
-    rows, depth = near.shape
-    width = wd.shape[0]
-    step = tile(width, 256)
-    tiles = width // step
-    deep = 256
-
-    def early(j):
-        return jnp.minimum(j, tiles - 1)
-
-    def late(j):
-        return jnp.maximum(j - tiles, 0)
-
-    weight = pl.BlockSpec((deep, width), lambda j: (late(j), 0))
-    terms = pl.BlockSpec((rows, deep), lambda j: (0, late(j)))
-    return pl.pallas_call(
-        functools.partial(back_kernel, tiles),
-        grid=(tiles + depth // deep,),
-        in_specs=[pl.BlockSpec(memory_space=pltpu.SMEM)]
-        + held_specs(2)
-        + [pl.BlockSpec((step, depth), lambda j: (early(j), 0))]
-        + held_specs(2)
-        + [weight, weight],
-        out_specs=held_specs(2) + [terms, terms],
+        + hbm_specs(3)
+        + any_specs(a + b),
+        out_specs=held_specs(4),
         out_shape=[jax.ShapeDtypeStruct((2 * rows, width), BF16)] * 2
+        + [jax.ShapeDtypeStruct((rows, depth), BF16)] * 2,
+        scratch_shapes=[pltpu.VMEM((width, 2 * rows), BF16)] * 2
         + [
-            jax.ShapeDtypeStruct((rows, depth), F32),
-            jax.ShapeDtypeStruct((rows, depth), BF16),
+            pltpu.VMEM((2, step, depth), BF16),
+            pltpu.VMEM((2, 2, 512, width), BF16),
+            pltpu.VMEM((2, width, 2 * rows), F32),
+            pltpu.SemaphoreType.DMA((2, CHUNKS)),
+            pltpu.SemaphoreType.DMA((2, 2)),
+            pltpu.SemaphoreType.DMA((2, len(a))),
         ],
-        scratch_shapes=[pltpu.VMEM((2 * rows, depth), BF16)],
-        compiler_params=params(34),
+        compiler_params=params(28),
         cost_estimate=cost(12 * rows * depth * width, 6 * depth * width),
         name="hidden_back",
-    )(spot, near, far, wd, a, b, wg, wu)
+    )(spot, near, far, wg, wu, wd, *a, *b)
 
 
 def fold_kernel(cuts, *refs):
@@ -189,9 +321,9 @@
     for i, (at, got_at) in enumerate(cuts):
         own_ref, near_ref, got_ref = refs[3 * i : 3 * i + 3]
         out_ref = outs[i]
-        out_ref[...] = (own_ref[at, :] + near_ref[at, :].astype(F32)).astype(BF16)
+        out_ref[...] = (own_ref[at, :].astype(F32) + near_ref[at, :].astype(F32)).astype(BF16)
         if got_at is not None:
-            total = own_ref[got_at, :] + near_ref[got_at, :].astype(F32)
+            total = own_ref[got_at, :].astype(F32) + near_ref[got_at, :].astype(F32)
             out_ref[got_at, :] = (total + got_ref[...].astype(F32)).astype(BF16)
 
 
@@ -219,7 +351,7 @@
 
 
 def last_kernel(own_ref, near_ref, r_ref, l_ref, out_ref):
-    total = own_ref[...] + near_ref[...].astype(F32)
+    total = own_ref[...].astype(F32) + near_ref[...].astype(F32)
     out_ref[...] = (total + r_ref[...].astype(F32) + l_ref[...].astype(F32)).astype(BF16)
 
 
@@ -237,14 +369,12 @@
     )(own, near, r, l)
 
 
-def fisher_kernel(step, first, x_ref, gg_ref, gu_ref, *rest):
+def fisher_kernel(step, x_ref, gg_ref, gu_ref, *rest):
     fg_ref, fu_ref, done_ref = rest[-3:]
-    deep = fg_ref.shape[0]
-    here = pl.ds(pl.multiple_of((first + pl.program_id(0)) * deep, deep), deep)
     done_ref[...] = jnp.zeros_like(done_ref)
     span = x_ref.shape[0] // SEQS
     seqs = [pl.ds(q * span, span) for q in range(SEQS)]
-    cols = [x_ref[at, here].T for at in seqs]
+    cols = [x_ref[at, :].T for at in seqs]
     for g_ref, f_ref in ((gg_ref, fg_ref), (gu_ref, fu_ref)):
         for c in range(g_ref.shape[1] // step):
             at = pl.ds(c * step, step)
@@ -260,9 +390,11 @@
     width = gg.shape[1]
     block = pl.BlockSpec((step, width), lambda j: (first + j, 0))
     return pl.pallas_call(
-        functools.partial(fisher_kernel, tile(width, 256), first),
+        functools.partial(fisher_kernel, tile(width, 256)),
         grid=(count,),
-        in_specs=held_specs(3) + any_specs((*held, *after)),
+        in_specs=[pl.BlockSpec((rows, step), lambda j: (0, first + j))]
+        + held_specs(2)
+        + any_specs((*held, *after)),
         out_specs=[block, block, pl.BlockSpec((8, 128), lambda j: (0, 0))],
         out_shape=[jax.ShapeDtypeStruct((depth, width), BF16)] * 2
         + [jax.ShapeDtypeStruct((8, 128), F32)],
@@ -277,6 +409,7 @@
     chips = len(CYCLE)
     far = chips // 2
     row, depth = tokens.shape
+    width = wg.shape[1]
     links = [(CYCLE[i], CYCLE[(i + 1) % chips]) for i in range(chips)]
     to_right = [(2 * a + c, 2 * b + c) for a, b in links for c in range(2)]
     to_left = [(b, a) for a, b in to_right]
@@ -291,33 +424,52 @@
     def swap(value):
         return lax.ppermute(value, "hid", across)
 
-    def gather_both(x, dy):
-        r, l = [[x], [dy]], [[x], [dy]]
-        halves = slice(None, row // 2), slice(row // 2, None)
-        busy = ()
-        for step in range(far + 1):
-            live = [(i, step - i) for i in range(2) if 0 <= step - i < far]
-            ends = [side[i][-1] for i, _ in live for side in (r, l)]
-            ends, busy = lax.optimization_barrier((ends, busy))
-            for at, (i, k) in enumerate(live):
-                to_r, to_l = ends[2 * at : 2 * at + 2]
-                if k == far - 1:
-                    to_r, to_l = to_r[halves[0]], to_l[halves[1]]
-                r[i].append(right(to_r))
-                l[i].append(left(to_l))
-            busy = [side[i][-1] for i, _ in live for side in (r, l)]
-        return [r[i] + l[i][:0:-1] for i in range(2)]
-
-    cycle = jnp.array([CYCLE.index(c) for c in range(chips)], jnp.int32)
-    spot = (cycle[lax.axis_index("hid") // 2] - cycle) % chips
-
-    blocks_x, blocks_dy = gather_both(tokens, grad_out)
-    near_x = pack(blocks_x, (spot,))
+    cycle = jnp.array(CYCLE, jnp.int32)
+    where = jnp.array([CYCLE.index(c) for c in range(chips)], jnp.int32)
+    around = jnp.arange(chips, dtype=jnp.int32)
+    chip = cycle[(where[lax.axis_index("hid") // 2] - around) % chips]
+    span = chips // SEQS
+    spot = (chip // span * 2 * span + chip % span) * row
+
+    def both(r, l, after=()):
+        (r, l), _ = lax.optimization_barrier(((r, l), after))
+        return right(r), left(l)
+
+    def halves(r, l):
+        return r[: row // 2], l[row // 2 :]
+
+    def blocks(own, rounds):
+        return [own] + [r for r, _ in rounds] + [l for _, l in rounds[::-1]]
+
+    lane = tile(width, 256)
+    tiles = width // lane
+    cuts = [0, 2, 5, 7] if tiles == 7 else [0, 0, 0, tiles]
+
+    def piece(i, after):
+        if cuts[i] == cuts[i + 1]:
+            return []
+        count = cuts[i + 1] - cuts[i]
+        grant = (40, 38, 32)[i]
+        return [gate_up(near_x, far_x, wg, wu, cuts[i], count, lane, grant, after)]
+
+    in_x = [both(tokens, tokens)]
+    for _ in range(2, far):
+        in_x.append(both(*in_x[-1]))
+    in_x.append(both(*halves(*in_x[-1])))
+    near_x = pack(blocks(tokens, in_x), (spot,))
     far_x = swap(near_x)
-    near_dy = pack(blocks_dy, ())
+
+    in_dy = [both(grad_out, grad_out, in_x[-2])]
+    in_dy.append(both(*in_dy[-1]))
+    factors = piece(0, in_dy[0])
+    in_dy.append(both(*in_dy[-1], factors))
+    factors += piece(1, in_dy[1])
+    in_dy.append(both(*halves(*in_dy[-1]), factors))
+    x = arrange(spot, near_x, far_x, in_dy[2])
+    near_dy = pack_turned(blocks(grad_out, in_dy), (x,))
     far_dy = swap(near_dy)
-    a, b, x = gate_up(spot, near_x, far_x, wg, wu, (near_dy,))
-    gg, gu, own, sent = back(spot, near_dy, far_dy, wd, a, b, wg, wu)
+    factors += piece(2, (near_dy,))
+    gg, gu, own, sent = back(spot, near_dy, far_dy, wg, wu, wd, factors)
 
     near = swap(sent)
     full, head, tail = pl.ds(0, row), pl.ds(0, row // 2), pl.ds(row // 2, row // 2)

time: 156 us -> 148 us (0.949)
  waiting for transfers between devices: 43.3 us -> 33.4 us
  Pallas kernels: 80.4 us -> 82.3 us
    ppermute x12, waiting for transfers between devices: 16.7 us -> 8.32 us  [left(): return lax.ppermute(value, 'hid', to_left)]
    ppermute x12, starting transfers between devices: 6.36 us -> 13.8 us  [left(): return lax.ppermute(value, 'hid', to_left)]
    ppermute x12, starting transfers between devices: 19.4 us -> 12.2 us  [right(): return lax.ppermute(value, 'hid', to_right)]
    pallas_call x7 -> x11, Pallas kernels: 78.8 us -> 80.8 us  [the longest x1 30.7 us: back(): pl.pallas_call(functools.partial(back_kernel, step, 512, len(a)), in_spec...]
  transfers between devices with their start and end apart: 27 -> 27, of which waited for: 21 -> 16; matrix products, arithmetic and copies ran while one was open for 2% -> 2% of each run, Pallas kernels for 28% -> 34%
where the time goes in v6:
time: 148 us
  Pallas kernels  82.3 us (56%)
  waiting for transfers between devices  33.4 us (23%)
  starting transfers between devices  26.7 us (18%)
  local copies, waits for them, and re-layouts  3.55 us (2%)
    pallas_call x1, Pallas kernels, back(): pl.pallas_call(functools.partial(back_kernel, step, 512, len(a)), in_spec...  30.7 us
    ppermute x12, waiting for transfers between devices, right(): return lax.ppermute(value, 'hid', to_right)  25.1 us
    pallas_call x3, Pallas kernels, gate_up(): pl.pallas_call(functools.partial(gate_up_kernel, first, step), in_specs=h...  24.5 us
    pallas_call x5, Pallas kernels, fisher(): pl.pallas_call(functools.partial(fisher_kernel, tile(width, 256)), grid=(...  24.1 us
    ppermute x12, starting transfers between devices, left(): return lax.ppermute(value, 'hid', to_left)  13.8 us
    ppermute x12, starting transfers between devices, right(): return lax.ppermute(value, 'hid', to_right)  12.2 us
    ppermute x12, waiting for transfers between devices, left(): return lax.ppermute(value, 'hid', to_left)  8.32 us
  transfers between devices with their start and end apart: 27, of which 16 were waited for; matrix products, arithmetic and copies ran while one was open for 2% of the time, Pallas kernels for 34%

profile of v6, /device:TPU:0, one launch (start us, length us, event | category | flops | bytes accessed | tf_op | source)
XLA Modules:
  0.0 147.5 jit_solution(3448420019992533201)
XLA Ops:
  0.6 3.1 %collective-permute-start = (bf16[32,4096]{1,0:T(8,128)(2,1)}, bf16[32,4096]{1,0:T(8,128)(2,1)S(1)}, u32[]{:S(2)}, u32[]{:S(2)}) collective-permute-start(bf16[32,4096]{1,0:T(8,128)(2,1)} %refs_0_.2), channel_id=1, source_target_pairs={{0,4},{1,5},{4,8},{5,9},{8,12},{9,13},{12,14},{13,15},{14,10},{15,... | collective-permute-start | bytes 786440 | tf_op jit(solution)/shard_map/ppermute | solution.py:419
  3.7 6.4 %collective-permute-done.refs_1_ = bf16[32,4096]{1,0:T(8,128)(2,1)S(1)} collective-permute-done((bf16[32,4096]{1,0:T(8,128)(2,1)}, bf16[32,4096]{1,0:T(8,128)(2,1)S(1)}, u32[]{:S(2)}, u32[]{:S(2)}) %collective-permute-start) | collective-permute-done | bytes 262176 | tf_op jit(solution)/shard_map/ppermute | solution.py:419
  11.7 1.6 %collective-permute-start.2 = (bf16[32,4096]{1,0:T(8,128)(2,1)S(1)}, bf16[32,4096]{1,0:T(8,128)(2,1)S(1)}, u32[]{:S(2)}, u32[]{:S(2)}) collective-permute-start(bf16[32,4096]{1,0:T(8,128)(2,1)S(1)} %collective-permute-done.refs_1_), channel_id=1, source_target_pairs={{0,4},{1,5},{4,8},{5,9},{8,12},{9,13},{12,14},{13,15},{14,10},{15,... | collective-permute-start | bytes 786440 | tf_op jit(solution)/shard_map/ppermute | solution.py:419
  13.7 4.8 %collective-permute-done.2.refs_2_ = bf16[32,4096]{1,0:T(8,128)(2,1)S(1)} collective-permute-done((bf16[32,4096]{1,0:T(8,128)(2,1)S(1)}, bf16[32,4096]{1,0:T(8,128)(2,1)S(1)}, u32[]{:S(2)}, u32[]{:S(2)}) %collective-permute-start.2) | collective-permute-done | bytes 262176 | tf_op jit(solution)/shard_map/ppermute | solution.py:419
  19.8 1.6 %collective-permute-start.4 = (bf16[32,4096]{1,0:T(8,128)(2,1)S(1)}, bf16[32,4096]{1,0:T(8,128)(2,1)S(1)}, u32[]{:S(2)}, u32[]{:S(2)}) collective-permute-start(bf16[32,4096]{1,0:T(8,128)(2,1)S(1)} %collective-permute-done.2.refs_2_), channel_id=1, source_target_pairs={{0,4},{1,5},{4,8},{5,9},{8,12},{9,13},{12,14},{13,15},{14,10},{15,... | collective-permute-start | bytes 786440 | tf_op jit(solution)/shard_map/ppermute | solution.py:419
  27.8 2.3 %collective-permute-start.6 = (bf16[16,4096]{1,0:T(8,128)(2,1)S(1)}, bf16[16,4096]{1,0:T(8,128)(2,1)S(1)}, u32[]{:S(2)}, u32[]{:S(2)}) collective-permute-start(bf16[16,4096]{1,0:T(8,128)(2,1)S(1)} %slice.18), channel_id=1, source_target_pairs={{0,4},{1,5},{4,8},{5,9},{8,12},{9,13},{12,14},{13,15},{14,10},{15,... | collective-permute-start | bytes 393224 | tf_op jit(solution)/shard_map/ppermute | solution.py:419
  30.1 2.7 %collective-permute-done.6.refs_4_ = bf16[16,4096]{1,0:T(8,128)(2,1)S(1)} collective-permute-done((bf16[16,4096]{1,0:T(8,128)(2,1)S(1)}, bf16[16,4096]{1,0:T(8,128)(2,1)S(1)}, u32[]{:S(2)}, u32[]{:S(2)}) %collective-permute-start.6) | collective-permute-done | bytes 131104 | tf_op jit(solution)/shard_map/ppermute | solution.py:419
  32.8 2.3 %collective-permute-done.7.refs_5_ = bf16[16,4096]{1,0:T(8,128)(2,1)S(1)} collective-permute-done((bf16[16,4096]{1,0:T(8,128)(2,1)S(1)}, bf16[16,4096]{1,0:T(8,128)(2,1)S(1)}, u32[]{:S(2)}, u32[]{:S(2)}) %collective-permute-start.7) | collective-permute-done | bytes 131104 | tf_op jit(solution)/shard_map/ppermute | solution.py:422
  38.3 6.8 %collective-permute-done.9.rest_0_.refs_1_ = bf16[32,4096]{1,0:T(8,128)(2,1)S(1)} collective-permute-done((bf16[32,4096]{1,0:T(8,128)(2,1)}, bf16[32,4096]{1,0:T(8,128)(2,1)S(1)}, u32[]{:S(2)}, u32[]{:S(2)}) %collective-permute-start.9) | collective-permute-done | bytes 262176 | tf_op jit(solution)/shard_map/ppermute | solution.py:419
  46.0 1.6 %collective-permute-start.12 = (bf16[32,4096]{1,0:T(8,128)(2,1)S(1)}, bf16[32,4096]{1,0:T(8,128)(2,1)S(1)}, u32[]{:S(2)}, u32[]{:S(2)}) collective-permute-start(bf16[32,4096]{1,0:T(8,128)(2,1)S(1)} %collective-permute-done.10.rest_1_.refs_8_), channel_id=1, source_target_pairs={{4,0},{5,1},{8,4},{9,5},{12,8},{13,9},{14,12},{15,13},{10,14},{11,... | collective-permute-start | bytes 786440 | tf_op jit(solution)/shard_map/ppermute | solution.py:422
  47.6 7.2 %gate_up.3 = (f32[512,512]{1,0:T(8,128)S(1)}, f32[512,512]{1,0:T(8,128)S(1)}) custom-call(bf16[256,4096]{1,0:T(8,128)(2,1)S(1)} %pack.1.near_ref, bf16[256,4096]{1,0:T(8,128)(2,1)S(1)} %collective-permute-done.8.far_ref, bf16[4096,1792]{1,0:T(8,128)(2,1)} %wg_ref.7, bf16[4096,1792]{1,0:T(8,128)(2,1)} %wu_ref.7, ...), custom_call_target="tpu_custom_call" | custom-call | flops 4294967296 | bytes 8388608 | tf_op jit(solution)/shard_map/gate_up/pallas_call | solution.py:172
  55.3 1.6 %collective-permute-start.14 = (bf16[32,4096]{1,0:T(8,128)(2,1)S(1)}, bf16[32,4096]{1,0:T(8,128)(2,1)S(1)}, u32[]{:S(2)}, u32[]{:S(2)}) collective-permute-start(bf16[32,4096]{1,0:T(8,128)(2,1)S(1)} %collective-permute-done.12.rest_1_.refs_7_), channel_id=1, source_target_pairs={{4,0},{5,1},{8,4},{9,5},{12,8},{13,9},{14,12},{15,13},{10,14},{11,... | collective-permute-start | bytes 786440 | tf_op jit(solution)/shard_map/ppermute | solution.py:422
  56.9 10.0 %gate_up.4 = (f32[768,512]{1,0:T(8,128)S(1)}, f32[768,512]{1,0:T(8,128)S(1)}) custom-call(bf16[256,4096]{1,0:T(8,128)(2,1)S(1)} %pack.1.near_ref, bf16[256,4096]{1,0:T(8,128)(2,1)S(1)} %collective-permute-done.8.far_ref, bf16[4096,1792]{1,0:T(8,128)(2,1)} %wg_ref.7, bf16[4096,1792]{1,0:T(8,128)(2,1)} %wu_ref.7, ...), custom_call_target="tpu_custom_call" | custom-call | flops 6442450944 | bytes 12582912 | tf_op jit(solution)/shard_map/gate_up/pallas_call | solution.py:172
  69.9 2.1 %collective-permute-done.15.refs_4_ = bf16[16,4096]{1,0:T(8,128)(2,1)S(1)} collective-permute-done((bf16[16,4096]{1,0:T(8,128)(2,1)S(1)}, bf16[16,4096]{1,0:T(8,128)(2,1)S(1)}, u32[]{:S(2)}, u32[]{:S(2)}) %collective-permute-start.15) | collective-permute-done | bytes 131104 | tf_op jit(solution)/shard_map/ppermute | solution.py:419
  73.2 7.3 %gate_up.5 = (f32[512,512]{1,0:T(8,128)S(1)}, f32[512,512]{1,0:T(8,128)S(1)}) custom-call(bf16[256,4096]{1,0:T(8,128)(2,1)S(1)} %pack.1.near_ref, bf16[256,4096]{1,0:T(8,128)(2,1)S(1)} %collective-permute-done.8.far_ref, bf16[4096,1792]{1,0:T(8,128)(2,1)} %wg_ref.7, bf16[4096,1792]{1,0:T(8,128)(2,1)} %wu_ref.7, bf16[4096,256]{1,0:T(8,128)(2,1)S(1)} %pack_turned.1.rest_0_.near_ref), custom_call_target="tpu_custom_call" | custom-call | flops 4294967296 | bytes 8388608 | tf_op jit(solution)/shard_map/gate_up/pallas_call | solution.py:172
  80.5 30.7 %hidden_back.1 = (bf16[512,1792]{1,0:T(8,128)(2,1)S(1)}, bf16[512,1792]{1,0:T(8,128)(2,1)S(1)}, bf16[256,4096]{1,0:T(8,128)(2,1)S(1)}, bf16[256,4096]{1,0:T(8,128)(2,1)S(1)}) custom-call(s32[8]{0:T(128)S(1)} %fusion.3.refs_9_.spot_ref, bf16[4096,256]{1,0:T(8,128)(2,1)S(1)} %pack_turned.1.rest_0_.near_ref, ...), custom_call_target="tpu_custom_call" | custom-call | flops 22548578304 | bytes 44040192 | tf_op jit(solution)/shard_map/hidden_back/pallas_call | solution.py:294
  111.7 5.8 %fisher.5 = (bf16[4096,1792]{1,0:T(8,128)(2,1)}, bf16[4096,1792]{1,0:T(8,128)(2,1)}, f32[8,128]{1,0:T(8,128)S(1)}) custom-call(bf16[512,4096]{1,0:T(8,128)(2,1)S(1)} %arrange.1.refs_9_.x_ref, bf16[512,1792]{1,0:T(8,128)(2,1)S(1)} %get-tuple-element.73.gg_ref, bf16[512,1792]{1,0:T(8,128)(2,1)S(1)} %get-tuple-element.74.gu_ref), custom_call_target="tpu_custom_call" | custom-call | flops 3758096384 | bytes 7340032 | tf_op jit(solution)/shard_map/fisher/pallas_call | solution.py:392
  117.9 1.8 %collective-permute-start.20 = (bf16[16,4096]{1,0:T(8,128)(2,1)S(1)}, bf16[16,4096]{1,0:T(8,128)(2,1)S(1)}, u32[]{:S(2)}, u32[]{:S(2)}) collective-permute-start(bf16[16,4096]{1,0:T(8,128)(2,1)S(1)} %get-tuple-element.81.rest_3_), channel_id=1, source_target_pairs={{4,0},{5,1},{8,4},{9,5},{12,8},{13,9},{14,12},{15,13},{10,14},{11,... | collective-permute-start | bytes 393224 | tf_op jit(solution)/shard_map/ppermute | solution.py:422
  119.7 3.4 %fisher.6 = (bf16[4096,1792]{1,0:T(8,128)(2,1)}, bf16[4096,1792]{1,0:T(8,128)(2,1)}, f32[8,128]{1,0:T(8,128)S(1)}) custom-call(bf16[512,4096]{1,0:T(8,128)(2,1)S(1)} %arrange.1.refs_9_.x_ref, bf16[512,1792]{1,0:T(8,128)(2,1)S(1)} %get-tuple-element.73.gg_ref, ...), custom_call_target="tpu_custom_call", output_to_operand_aliasing={{0}: (3, {}), {1}: (4, {})} | custom-call | flops 1879048192 | bytes 3670016 | tf_op jit(solution)/shard_map/fisher/pallas_call | solution.py:392
  123.9 1.8 %collective-permute-start.22 = (bf16[32,4096]{1,0:T(8,128)(2,1)S(1)}, bf16[32,4096]{1,0:T(8,128)(2,1)S(1)}, u32[]{:S(2)}, u32[]{:S(2)}) collective-permute-start(bf16[32,4096]{1,0:T(8,128)(2,1)S(1)} %get-tuple-element.86.rest_3_), channel_id=1, source_target_pairs={{4,0},{5,1},{8,4},{9,5},{12,8},{13,9},{14,12},{15,13},{10,14},{11,... | collective-permute-start | bytes 786440 | tf_op jit(solution)/shard_map/ppermute | solution.py:422
  125.7 5.8 %fisher.7 = (bf16[4096,1792]{1,0:T(8,128)(2,1)}, bf16[4096,1792]{1,0:T(8,128)(2,1)}, f32[8,128]{1,0:T(8,128)S(1)}) custom-call(bf16[512,4096]{1,0:T(8,128)(2,1)S(1)} %arrange.1.refs_9_.x_ref, bf16[512,1792]{1,0:T(8,128)(2,1)S(1)} %get-tuple-element.73.gg_ref, ...), custom_call_target="tpu_custom_call", output_to_operand_aliasing={{0}: (3, {}), {1}: (4, {})} | custom-call | flops 3758096384 | bytes 7340032 | tf_op jit(solution)/shard_map/fisher/pallas_call | solution.py:392
  132.0 1.8 %collective-permute-start.24 = (bf16[32,4096]{1,0:T(8,128)(2,1)S(1)}, bf16[32,4096]{1,0:T(8,128)(2,1)S(1)}, u32[]{:S(2)}, u32[]{:S(2)}) collective-permute-start(bf16[32,4096]{1,0:T(8,128)(2,1)S(1)} %get-tuple-element.91.rest_3_), channel_id=1, source_target_pairs={{4,0},{5,1},{8,4},{9,5},{12,8},{13,9},{14,12},{15,13},{10,14},{11,... | collective-permute-start | bytes 786440 | tf_op jit(solution)/shard_map/ppermute | solution.py:422
  133.8 5.8 %fisher.8 = (bf16[4096,1792]{1,0:T(8,128)(2,1)}, bf16[4096,1792]{1,0:T(8,128)(2,1)}, f32[8,128]{1,0:T(8,128)S(1)}) custom-call(bf16[512,4096]{1,0:T(8,128)(2,1)S(1)} %arrange.1.refs_9_.x_ref, bf16[512,1792]{1,0:T(8,128)(2,1)S(1)} %get-tuple-element.73.gg_ref, ...), custom_call_target="tpu_custom_call", output_to_operand_aliasing={{0}: (3, {}), {1}: (4, {})} | custom-call | flops 3758096384 | bytes 7340032 | tf_op jit(solution)/shard_map/fisher/pallas_call | solution.py:392
  141.8 3.4 %fisher.9 = (bf16[4096,1792]{1,0:T(8,128)(2,1)}, bf16[4096,1792]{1,0:T(8,128)(2,1)}, f32[8,128]{1,0:T(8,128)}) custom-call(bf16[512,4096]{1,0:T(8,128)(2,1)S(1)} %arrange.1.refs_9_.x_ref, bf16[512,1792]{1,0:T(8,128)(2,1)S(1)} %get-tuple-element.73.gg_ref, ...), custom_call_target="tpu_custom_call", output_to_operand_aliasing={{0}: (3, {}), {1}: (4, {})} | custom-call | flops 1879048192 | bytes 3670016 | tf_op jit(solution)/shard_map/fisher/pallas_call | solution.py:392
  (64 shorter events, 25.2 us)
Async XLA Ops:
  0.6 9.5 %collective-permute-start = (bf16[32,4096]{1,0:T(8,128)(2,1)}, bf16[32,4096]{1,0:T(8,128)(2,1)S(1)}, u32[]{:S(2)}, u32[]{:S(2)}) collective-permute-start(bf16[32,4096]{1,0:T(8,128)(2,1)} %refs_0_.2), channel_id=1, source_target_pairs={{0,4},{1,5},{4,8},{5,9},{8,12},{9,13},{12,14},{13,15},{14,10},{15,... | collective-permute-start | bytes 786440 | tf_op jit(solution)/shard_map/ppermute | solution.py:419
  3.7 8.0 %collective-permute-start.1 = (bf16[32,4096]{1,0:T(8,128)(2,1)}, bf16[32,4096]{1,0:T(8,128)(2,1)S(1)}, u32[]{:S(2)}, u32[]{:S(2)}) collective-permute-start(bf16[32,4096]{1,0:T(8,128)(2,1)} %refs_0_.2), channel_id=1, source_target_pairs={{4,0},{5,1},{8,4},{9,5},{12,8},{13,9},{14,12},{15,13},{10,14},{11,... | collective-permute-start | bytes 786440 | tf_op jit(solution)/shard_map/ppermute | solution.py:422
  11.7 6.9 %collective-permute-start.2 = (bf16[32,4096]{1,0:T(8,128)(2,1)S(1)}, bf16[32,4096]{1,0:T(8,128)(2,1)S(1)}, u32[]{:S(2)}, u32[]{:S(2)}) collective-permute-start(bf16[32,4096]{1,0:T(8,128)(2,1)S(1)} %collective-permute-done.refs_1_), channel_id=1, source_target_pairs={{0,4},{1,5},{4,8},{5,9},{8,12},{9,13},{12,14},{13,15},{14,10},{15,... | collective-permute-start | bytes 786440 | tf_op jit(solution)/shard_map/ppermute | solution.py:419
  13.3 6.6 %collective-permute-start.3 = (bf16[32,4096]{1,0:T(8,128)(2,1)S(1)}, bf16[32,4096]{1,0:T(8,128)(2,1)S(1)}, u32[]{:S(2)}, u32[]{:S(2)}) collective-permute-start(bf16[32,4096]{1,0:T(8,128)(2,1)S(1)} %collective-permute-done.1.refs_8_), channel_id=1, source_target_pairs={{4,0},{5,1},{8,4},{9,5},{12,8},{13,9},{14,12},{15,13},{10,14},{11,... | collective-permute-start | bytes 786440 | tf_op jit(solution)/shard_map/ppermute | solution.py:422
  19.8 6.4 %collective-permute-start.4 = (bf16[32,4096]{1,0:T(8,128)(2,1)S(1)}, bf16[32,4096]{1,0:T(8,128)(2,1)S(1)}, u32[]{:S(2)}, u32[]{:S(2)}) collective-permute-start(bf16[32,4096]{1,0:T(8,128)(2,1)S(1)} %collective-permute-done.2.refs_2_), channel_id=1, source_target_pairs={{0,4},{1,5},{4,8},{5,9},{8,12},{9,13},{12,14},{13,15},{14,10},{15,... | collective-permute-start | bytes 786440 | tf_op jit(solution)/shard_map/ppermute | solution.py:419
  21.4 6.4 %collective-permute-start.5 = (bf16[32,4096]{1,0:T(8,128)(2,1)S(1)}, bf16[32,4096]{1,0:T(8,128)(2,1)S(1)}, u32[]{:S(2)}, u32[]{:S(2)}) collective-permute-start(bf16[32,4096]{1,0:T(8,128)(2,1)S(1)} %collective-permute-done.3.refs_7_), channel_id=1, source_target_pairs={{4,0},{5,1},{8,4},{9,5},{12,8},{13,9},{14,12},{15,13},{10,14},{11,... | collective-permute-start | bytes 786440 | tf_op jit(solution)/shard_map/ppermute | solution.py:422
  27.8 5.0 %collective-permute-start.6 = (bf16[16,4096]{1,0:T(8,128)(2,1)S(1)}, bf16[16,4096]{1,0:T(8,128)(2,1)S(1)}, u32[]{:S(2)}, u32[]{:S(2)}) collective-permute-start(bf16[16,4096]{1,0:T(8,128)(2,1)S(1)} %slice.18), channel_id=1, source_target_pairs={{0,4},{1,5},{4,8},{5,9},{8,12},{9,13},{12,14},{13,15},{14,10},{15,... | collective-permute-start | bytes 393224 | tf_op jit(solution)/shard_map/ppermute | solution.py:419
  36.2 11.4 %collective-permute-start.8 = (bf16[256,4096]{1,0:T(8,128)(2,1)S(1)}, bf16[256,4096]{1,0:T(8,128)(2,1)S(1)}, u32[]{:S(2)}, u32[]{:S(2)}) collective-permute-start(bf16[256,4096]{1,0:T(8,128)(2,1)S(1)} %pack.1.near_ref), channel_id=1, source_target_pairs={{0,1},{1,0},{2,3},{3,2},{4,5},{5,4},{6,7},{7,6},{8,9},{9,8},{10,11... | collective-permute-start | bytes 6291464 | tf_op jit(solution)/shard_map/ppermute | solution.py:425
  36.3 8.9 %collective-permute-start.9 = (bf16[32,4096]{1,0:T(8,128)(2,1)}, bf16[32,4096]{1,0:T(8,128)(2,1)S(1)}, u32[]{:S(2)}, u32[]{:S(2)}) collective-permute-start(bf16[32,4096]{1,0:T(8,128)(2,1)} %refs_0_.3), channel_id=1, source_target_pairs={{0,4},{1,5},{4,8},{5,9},{8,12},{9,13},{12,14},{13,15},{14,10},{15,... | collective-permute-start | bytes 786440 | tf_op jit(solution)/shard_map/ppermute | solution.py:419
  37.0 8.6 %collective-permute-start.10 = (bf16[32,4096]{1,0:T(8,128)(2,1)}, bf16[32,4096]{1,0:T(8,128)(2,1)S(1)}, u32[]{:S(2)}, u32[]{:S(2)}) collective-permute-start(bf16[32,4096]{1,0:T(8,128)(2,1)} %refs_0_.3), channel_id=1, source_target_pairs={{4,0},{5,1},{8,4},{9,5},{12,8},{13,9},{14,12},{15,13},{10,14},{11,... | collective-permute-start | bytes 786440 | tf_op jit(solution)/shard_map/ppermute | solution.py:422
  45.5 9.3 %collective-permute-start.11 = (bf16[32,4096]{1,0:T(8,128)(2,1)S(1)}, bf16[32,4096]{1,0:T(8,128)(2,1)S(1)}, u32[]{:S(2)}, u32[]{:S(2)}) collective-permute-start(bf16[32,4096]{1,0:T(8,128)(2,1)S(1)} %collective-permute-done.9.rest_0_.refs_1_), channel_id=1, source_target_pairs={{0,4},{1,5},{4,8},{5,9},{8,12},{9,13},{12,14},{13,15},{14,10},{15,... | collective-permute-start | bytes 786440 | tf_op jit(solution)/shard_map/ppermute | solution.py:419
  46.0 8.8 %collective-permute-start.12 = (bf16[32,4096]{1,0:T(8,128)(2,1)S(1)}, bf16[32,4096]{1,0:T(8,128)(2,1)S(1)}, u32[]{:S(2)}, u32[]{:S(2)}) collective-permute-start(bf16[32,4096]{1,0:T(8,128)(2,1)S(1)} %collective-permute-done.10.rest_1_.refs_8_), channel_id=1, source_target_pairs={{4,0},{5,1},{8,4},{9,5},{12,8},{13,9},{14,12},{15,13},{10,14},{11,... | collective-permute-start | bytes 786440 | tf_op jit(solution)/shard_map/ppermute | solution.py:422
  54.8 12.1 %collective-permute-start.13 = (bf16[32,4096]{1,0:T(8,128)(2,1)S(1)}, bf16[32,4096]{1,0:T(8,128)(2,1)S(1)}, u32[]{:S(2)}, u32[]{:S(2)}) collective-permute-start(bf16[32,4096]{1,0:T(8,128)(2,1)S(1)} %collective-permute-done.11.rest_0_.refs_2_), channel_id=1, source_target_pairs={{0,4},{1,5},{4,8},{5,9},{8,12},{9,13},{12,14},{13,15},{14,10},{15,... | collective-permute-start | bytes 786440 | tf_op jit(solution)/shard_map/ppermute | solution.py:419
  55.3 11.7 %collective-permute-start.14 = (bf16[32,4096]{1,0:T(8,128)(2,1)S(1)}, bf16[32,4096]{1,0:T(8,128)(2,1)S(1)}, u32[]{:S(2)}, u32[]{:S(2)}) collective-permute-start(bf16[32,4096]{1,0:T(8,128)(2,1)S(1)} %collective-permute-done.12.rest_1_.refs_7_), channel_id=1, source_target_pairs={{4,0},{5,1},{8,4},{9,5},{12,8},{13,9},{14,12},{15,13},{10,14},{11,... | collective-permute-start | bytes 786440 | tf_op jit(solution)/shard_map/ppermute | solution.py:422
  73.1 7.4 %collective-permute-start.17 = (bf16[4096,256]{1,0:T(8,128)(2,1)S(1)}, bf16[4096,256]{1,0:T(8,128)(2,1)S(1)}, u32[]{:S(2)}, u32[]{:S(2)}) collective-permute-start(bf16[4096,256]{1,0:T(8,128)(2,1)S(1)} %pack_turned.1.rest_0_.near_ref), channel_id=1, source_target_pairs={{0,1},{1,0},{2,3},{3,2},{4,5},{5,4},{6,7},{7,6},{8,9},{9,8},{10,11... | collective-permute-start | bytes 6291464 | tf_op jit(solution)/shard_map/ppermute | solution.py:425
  111.2 6.3 %collective-permute-start.18 = (bf16[256,4096]{1,0:T(8,128)(2,1)S(1)}, bf16[256,4096]{1,0:T(8,128)(2,1)S(1)}, u32[]{:S(2)}, u32[]{:S(2)}) collective-permute-start(bf16[256,4096]{1,0:T(8,128)(2,1)S(1)} %get-tuple-element.78), channel_id=1, source_target_pairs={{0,1},{1,0},{2,3},{3,2},{4,5},{5,4},{6,7},{7,6},{8,9},{9,8},{10,11... | collective-permute-start | bytes 6291464 | tf_op jit(solution)/shard_map/ppermute | solution.py:425
  117.6 5.5 %collective-permute-start.19 = (bf16[16,4096]{1,0:T(8,128)(2,1)S(1)}, bf16[16,4096]{1,0:T(8,128)(2,1)S(1)}, u32[]{:S(2)}, u32[]{:S(2)}) collective-permute-start(bf16[16,4096]{1,0:T(8,128)(2,1)S(1)} %get-tuple-element.80.rest_2_), channel_id=1, source_target_pairs={{0,4},{1,5},{4,8},{5,9},{8,12},{9,13},{12,14},{13,15},{14,10},{15,... | collective-permute-start | bytes 393224 | tf_op jit(solution)/shard_map/ppermute | solution.py:419
  117.9 5.5 %collective-permute-start.20 = (bf16[16,4096]{1,0:T(8,128)(2,1)S(1)}, bf16[16,4096]{1,0:T(8,128)(2,1)S(1)}, u32[]{:S(2)}, u32[]{:S(2)}) collective-permute-start(bf16[16,4096]{1,0:T(8,128)(2,1)S(1)} %get-tuple-element.81.rest_3_), channel_id=1, source_target_pairs={{4,0},{5,1},{8,4},{9,5},{12,8},{13,9},{14,12},{15,13},{10,14},{11,... | collective-permute-start | bytes 393224 | tf_op jit(solution)/shard_map/ppermute | solution.py:422
  123.6 7.9 %collective-permute-start.21 = (bf16[32,4096]{1,0:T(8,128)(2,1)S(1)}, bf16[32,4096]{1,0:T(8,128)(2,1)S(1)}, u32[]{:S(2)}, u32[]{:S(2)}) collective-permute-start(bf16[32,4096]{1,0:T(8,128)(2,1)S(1)} %get-tuple-element.85.rest_2_), channel_id=1, source_target_pairs={{0,4},{1,5},{4,8},{5,9},{8,12},{9,13},{12,14},{13,15},{14,10},{15,... | collective-permute-start | bytes 786440 | tf_op jit(solution)/shard_map/ppermute | solution.py:419
  123.9 7.6 %collective-permute-start.22 = (bf16[32,4096]{1,0:T(8,128)(2,1)S(1)}, bf16[32,4096]{1,0:T(8,128)(2,1)S(1)}, u32[]{:S(2)}, u32[]{:S(2)}) collective-permute-start(bf16[32,4096]{1,0:T(8,128)(2,1)S(1)} %get-tuple-element.86.rest_3_), channel_id=1, source_target_pairs={{4,0},{5,1},{8,4},{9,5},{12,8},{13,9},{14,12},{15,13},{10,14},{11,... | collective-permute-start | bytes 786440 | tf_op jit(solution)/shard_map/ppermute | solution.py:422
  131.7 7.9 %collective-permute-start.23 = (bf16[32,4096]{1,0:T(8,128)(2,1)S(1)}, bf16[32,4096]{1,0:T(8,128)(2,1)S(1)}, u32[]{:S(2)}, u32[]{:S(2)}) collective-permute-start(bf16[32,4096]{1,0:T(8,128)(2,1)S(1)} %get-tuple-element.90.rest_2_), channel_id=1, source_target_pairs={{0,4},{1,5},{4,8},{5,9},{8,12},{9,13},{12,14},{13,15},{14,10},{15,... | collective-permute-start | bytes 786440 | tf_op jit(solution)/shard_map/ppermute | solution.py:419
  132.0 7.6 %collective-permute-start.24 = (bf16[32,4096]{1,0:T(8,128)(2,1)S(1)}, bf16[32,4096]{1,0:T(8,128)(2,1)S(1)}, u32[]{:S(2)}, u32[]{:S(2)}) collective-permute-start(bf16[32,4096]{1,0:T(8,128)(2,1)S(1)} %get-tuple-element.91.rest_3_), channel_id=1, source_target_pairs={{4,0},{5,1},{8,4},{9,5},{12,8},{13,9},{14,12},{15,13},{10,14},{11,... | collective-permute-start | bytes 786440 | tf_op jit(solution)/shard_map/ppermute | solution.py:422
  139.8 6.4 %collective-permute-start.25 = (bf16[32,4096]{1,0:T(8,128)(2,1)S(1)}, bf16[32,4096]{1,0:T(8,128)(2,1)S(1)}, u32[]{:S(2)}, u32[]{:S(2)}) collective-permute-start(bf16[32,4096]{1,0:T(8,128)(2,1)S(1)} %get-tuple-element.95.rest_2_), channel_id=1, source_target_pairs={{0,4},{1,5},{4,8},{5,9},{8,12},{9,13},{12,14},{13,15},{14,10},{15,... | collective-permute-start | bytes 786440 | tf_op jit(solution)/shard_map/ppermute | solution.py:419
  140.3 6.4 %collective-permute-start.26 = (bf16[32,4096]{1,0:T(8,128)(2,1)S(1)}, bf16[32,4096]{1,0:T(8,128)(2,1)S(1)}, u32[]{:S(2)}, u32[]{:S(2)}) collective-permute-start(bf16[32,4096]{1,0:T(8,128)(2,1)S(1)} %get-tuple-element.96.rest_3_), channel_id=1, source_target_pairs={{4,0},{5,1},{8,4},{9,5},{12,8},{13,9},{14,12},{15,13},{10,14},{11,... | collective-permute-start | bytes 786440 | tf_op jit(solution)/shard_map/ppermute | solution.py:422
  (7 other events, 53.1 us)

commit v7 on v6

--- a/solution.py
+++ b/solution.py
@@ -37,6 +37,23 @@
 
 def held_specs(count):
     return [pl.BlockSpec(memory_space=pltpu.VMEM)] * count
+
+
+def bring_kernel(x_ref, dy_ref, x_out, dy_out):
+    x_out[...] = x_ref[...]
+    dy_out[...] = dy_ref[...]
+
+
+def bring(x, dy):
+    return pl.pallas_call(
+        bring_kernel,
+        in_specs=held_specs(2),
+        out_specs=held_specs(2),
+        out_shape=[jax.ShapeDtypeStruct(x.shape, BF16)] * 2,
+        compiler_params=params(4),
+        cost_estimate=cost(0, 8 * x.size),
+        name="bring",
+    )(x, dy)
 
 
 def pack_kernel(count, *refs):
@@ -142,10 +159,12 @@
         begin(t)
     for t in range(tiles):
         sums = [[None, None], [None, None]]
-        for k in range(CHUNKS):
-            deep = pl.ds(k * part, part)
-            for copy in fetch(t, k):
-                copy.wait()
+        pieces = CHUNKS if t == 0 else 1
+        for k in range(pieces):
+            deep = pl.ds(k * (depth // pieces), depth // pieces)
+            for c in range(k, k + 1) if t == 0 else range(CHUNKS):
+                for copy in fetch(t, c):
+                    copy.wait()
             for side, x_ref in enumerate((near_ref, far_ref)):
                 for i in range(2):
                     term = jnp.dot(
@@ -190,8 +209,9 @@
 
 def back_kernel(step, deep, pieces, spot_ref, near_ref, far_ref, wg_ref, wu_ref, wd_ref, *refs):
     a_refs, b_refs = refs[:pieces], refs[pieces : 2 * pieces]
-    ggs_ref, gus_ref, own_ref, sent_ref, gg_ref, gu_ref = refs[2 * pieces : 2 * pieces + 6]
-    wd_buf, w_buf, factor_buf, sems, w_sems, factor_sems = refs[2 * pieces + 6 :]
+    ggs_ref, gus_ref, own_ref, sent_ref, g_ref = refs[2 * pieces : 2 * pieces + 5]
+    wd_buf, w_buf, factor_buf, sems, w_sems, factor_sems = refs[2 * pieces + 5 :]
+    width = wg_ref.shape[1]
     rows = near_ref.shape[1]
     tiles = wd_ref.shape[0] // step
 
@@ -209,7 +229,9 @@
         at = pl.ds(pl.multiple_of(i * deep, deep), deep)
         slot = lax.rem(i, 2)
         return [
-            pltpu.make_async_copy(w_ref.at[at, :], w_buf.at[slot, k], w_sems.at[slot, k])
+            pltpu.make_async_copy(
+                w_ref.at[at, :], w_buf.at[slot, :, pl.ds(k * width, width)], w_sems.at[slot, k]
+            )
             for k, w_ref in enumerate((wg_ref, wu_ref))
         ]
 
@@ -223,6 +245,33 @@
             pltpu.make_async_copy(ref, factor_buf.at[k, at, :], factor_sems.at[k, p])
             for k, ref in enumerate((a_refs[p], b_refs[p]))
         ]
+
+    def hidden_tile(t, pieces):
+        cols = pl.ds(pl.multiple_of(t * step, step), step)
+        sums = [None, None]
+        size = wd_ref.shape[1] // pieces
+        for k in range(pieces):
+            part_k = pl.ds(k * size, size)
+            for c in range(k, k + 1) if pieces > 1 else range(CHUNKS):
+                fetch(t, c).wait()
+            for side, dy_ref in enumerate((near_ref, far_ref)):
+                term = jnp.dot(
+                    wd_buf[lax.rem(t, 2), :, part_k], dy_ref[part_k, :],
+                    preferred_element_type=F32,
+                )
+                sums[side] = term if sums[side] is None else sums[side] + term
+        for side, hidden in enumerate(sums):
+            at = pl.ds(side * rows, rows)
+            for f, gs_ref in enumerate((ggs_ref, gus_ref)):
+                grad = (hidden * factor_buf[f, cols, at]).astype(BF16)
+                to = pl.multiple_of(t * step + f * width, step)
+                g_ref[pl.ds(to, step), at] = grad
+                put_rows(spot_ref, side, grad.T, gs_ref, cols)
+
+        @pl.when(t + 2 < tiles)
+        def _():
+            for k in range(CHUNKS):
+                fetch(t + 2, k).start()
 
     blocks = wg_ref.shape[0] // deep
     for t in range(min(2, tiles)):
@@ -242,30 +291,12 @@
         for copy in fetch_factors(p):
             copy.wait()
 
-        @pl.loop(starts[p] // step, starts[p + 1] // step)
+        if p == 0:
+            hidden_tile(0, CHUNKS)
+
+        @pl.loop(max(starts[p] // step, 1), starts[p + 1] // step)
         def _(t):
-            cols = pl.ds(pl.multiple_of(t * step, step), step)
-            sums = [None, None]
-            for k in range(CHUNKS):
-                deep_k = pl.ds(k * part, part)
-                fetch(t, k).wait()
-                for side, dy_ref in enumerate((near_ref, far_ref)):
-                    term = jnp.dot(
-                        wd_buf[lax.rem(t, 2), :, deep_k], dy_ref[deep_k, :],
-                        preferred_element_type=F32,
-                    )
-                    sums[side] = term if sums[side] is None else sums[side] + term
-            for side, hidden in enumerate(sums):
-                at = pl.ds(side * rows, rows)
-                for f, (g_ref, gs_ref) in enumerate(((gg_ref, ggs_ref), (gu_ref, gus_ref))):
-                    grad = (hidden * factor_buf[f, cols, at]).astype(BF16)
-                    g_ref[cols, at] = grad
-                    put_rows(spot_ref, side, grad.T, gs_ref, cols)
-
-            @pl.when(t + 2 < tiles)
-            def _():
-                for k in range(CHUNKS):
-                    fetch(t + 2, k).start()
+            hidden_tile(t, 1)
 
     @pl.loop(0, blocks)
     def _(i):
@@ -275,8 +306,7 @@
             copy.wait()
         for side, out_ref in enumerate((own_ref, sent_ref)):
             of = pl.ds(side * rows, rows)
-            total = jnp.dot(w_buf[slot, 0], gg_ref[:, of], preferred_element_type=F32)
-            total += jnp.dot(w_buf[slot, 1], gu_ref[:, of], preferred_element_type=F32)
+            total = jnp.dot(w_buf[slot], g_ref[:, of], preferred_element_type=F32)
             out_ref[:, at] = total.astype(BF16).T
 
         @pl.when(i + 2 < blocks)
@@ -300,10 +330,10 @@
         out_specs=held_specs(4),
         out_shape=[jax.ShapeDtypeStruct((2 * rows, width), BF16)] * 2
         + [jax.ShapeDtypeStruct((rows, depth), BF16)] * 2,
-        scratch_shapes=[pltpu.VMEM((width, 2 * rows), BF16)] * 2
-        + [
+        scratch_shapes=[
+            pltpu.VMEM((2 * width, 2 * rows), BF16),
             pltpu.VMEM((2, step, depth), BF16),
-            pltpu.VMEM((2, 2, 512, width), BF16),
+            pltpu.VMEM((2, 512, 2 * width), BF16),
             pltpu.VMEM((2, width, 2 * rows), F32),
             pltpu.SemaphoreType.DMA((2, CHUNKS)),
             pltpu.SemaphoreType.DMA((2, 2)),
@@ -431,12 +461,11 @@
     span = chips // SEQS
     spot = (chip // span * 2 * span + chip % span) * row
 
-    def both(r, l, after=()):
+    def both(r, l, after=(), ends=False):
         (r, l), _ = lax.optimization_barrier(((r, l), after))
+        if ends:
+            r, l = r[: row // 2], l[row // 2 :]
         return right(r), left(l)
-
-    def halves(r, l):
-        return r[: row // 2], l[row // 2 :]
 
     def blocks(own, rounds):
         return [own] + [r for r, _ in rounds] + [l for _, l in rounds[::-1]]
@@ -452,21 +481,28 @@
         grant = (40, 38, 32)[i]
         return [gate_up(near_x, far_x, wg, wu, cuts[i], count, lane, grant, after)]
 
-    in_x = [both(tokens, tokens)]
-    for _ in range(2, far):
-        in_x.append(both(*in_x[-1]))
-    in_x.append(both(*halves(*in_x[-1])))
-    near_x = pack(blocks(tokens, in_x), (spot,))
+    def two(x, dy, after=()):
+        (x, dy), _ = lax.optimization_barrier(((x, dy), after))
+        return (right(x[0]), left(x[1])), (right(dy[0]), left(dy[1]))
+
+    own_x, own_dy = bring(tokens, grad_out)
+    in_x, in_dy = [both(tokens, tokens)], []
+    got = two(in_x[0], (own_dy, own_dy), own_x)
+    for k in range(2, far):
+        in_x.append(got[0])
+        in_dy.append(got[1])
+        if k < far - 1:
+            got = two(in_x[-1], in_dy[-1])
+    in_x.append(both(*in_x[-1], in_dy[-1], True))
+    near_x = pack(blocks(own_x, in_x), (spot,))
     far_x = swap(near_x)
 
-    in_dy = [both(grad_out, grad_out, in_x[-2])]
-    in_dy.append(both(*in_dy[-1]))
-    factors = piece(0, in_dy[0])
-    in_dy.append(both(*in_dy[-1], factors))
-    factors += piece(1, in_dy[1])
-    in_dy.append(both(*halves(*in_dy[-1]), factors))
-    x = arrange(spot, near_x, far_x, in_dy[2])
-    near_dy = pack_turned(blocks(grad_out, in_dy), (x,))
+    in_dy.append(both(*in_dy[-1], in_x[-2]))
+    factors = piece(0, in_dy[-2])
+    in_dy.append(both(*in_dy[-1], factors, True))
+    factors += piece(1, in_dy[-2])
+    x = arrange(spot, near_x, far_x, in_dy[-2])
+    near_dy = pack_turned(blocks(own_dy, in_dy), (x, *factors[-1]))
     far_dy = swap(near_dy)
     factors += piece(2, (near_dy,))
     gg, gu, own, sent = back(spot, near_dy, far_dy, wg, wu, wd, factors)

time: 148 us -> 145 us (0.980)
  waiting for transfers between devices: 33.4 us -> 31.4 us
  Pallas kernels: 82.3 us -> 80.5 us
    ppermute x12, waiting for transfers between devices: 25.1 us -> 15.6 us  [right(): return lax.ppermute(value, 'hid', to_right)]
    ppermute x12, starting transfers between devices: 13.8 us -> 6.33 us  [left(): return lax.ppermute(value, 'hid', to_left)]
    ppermute x12, starting transfers between devices: 12.2 us -> 19.4 us  [right(): return lax.ppermute(value, 'hid', to_right)]
    ppermute x12, waiting for transfers between devices: 8.32 us -> 13.8 us  [left(): return lax.ppermute(value, 'hid', to_left)]
    ppermute x3, waiting for transfers between devices: 0.01 us -> 2.07 us  [swap(): return lax.ppermute(value, 'hid', across)]
  transfers between devices with their start and end apart: 27 -> 27, of which waited for: 16 -> 18; matrix products, arithmetic and copies ran while one was open for 2% -> 2% of each run, Pallas kernels for 34% -> 34%
where the time goes in v7:
time: 145 us; the launch traced here: 144 us
  Pallas kernels  80.5 us (56%)
  waiting for transfers between devices  31.4 us (22%)
  starting transfers between devices  26.4 us (18%)
  local copies, waits for them, and re-layouts  4.49 us (3%)
    pallas_call x1, Pallas kernels, back(): pl.pallas_call(functools.partial(back_kernel, step, 512, len(a)), in_spec...  29.7 us
    pallas_call x5, Pallas kernels, fisher(): pl.pallas_call(functools.partial(fisher_kernel, tile(width, 256)), grid=(...  24.1 us
    pallas_call x3, Pallas kernels, gate_up(): pl.pallas_call(functools.partial(gate_up_kernel, first, step), in_specs=h...  23.6 us
    ppermute x12, starting transfers between devices, right(): return lax.ppermute(value, 'hid', to_right)  19.4 us
    ppermute x12, waiting for transfers between devices, right(): return lax.ppermute(value, 'hid', to_right)  15.6 us
    ppermute x12, waiting for transfers between devices, left(): return lax.ppermute(value, 'hid', to_left)  13.8 us
    ppermute x12, starting transfers between devices, left(): return lax.ppermute(value, 'hid', to_left)  6.33 us
  transfers between devices with their start and end apart: 27, of which 18 were waited for; matrix products, arithmetic and copies ran while one was open for 2% of the time, Pallas kernels for 34%

profile of v7, /device:TPU:0, one launch (start us, length us, event | category | flops | bytes accessed | tf_op | source)
XLA Modules:
  0.0 144.3 jit_solution(7899882584120714971)
XLA Ops:
  0.6 3.1 %collective-permute-start = (bf16[32,4096]{1,0:T(8,128)(2,1)}, bf16[32,4096]{1,0:T(8,128)(2,1)S(1)}, u32[]{:S(2)}, u32[]{:S(2)}) collective-permute-start(bf16[32,4096]{1,0:T(8,128)(2,1)} %x_ref.1), channel_id=1, source_target_pairs={{0,4},{1,5},{4,8},{5,9},{8,12},{9,13},{12,14},{13,15},{14,10},{15,... | collective-permute-start | bytes 786440 | tf_op jit(solution)/shard_map/ppermute | solution.py:449
  5.6 4.5 %collective-permute-done.refs_1_ = bf16[32,4096]{1,0:T(8,128)(2,1)S(1)} collective-permute-done((bf16[32,4096]{1,0:T(8,128)(2,1)}, bf16[32,4096]{1,0:T(8,128)(2,1)S(1)}, u32[]{:S(2)}, u32[]{:S(2)}) %collective-permute-start) | collective-permute-done | bytes 262176 | tf_op jit(solution)/shard_map/ppermute | solution.py:449
  11.7 1.6 %collective-permute-start.2 = (bf16[32,4096]{1,0:T(8,128)(2,1)S(1)}, bf16[32,4096]{1,0:T(8,128)(2,1)S(1)}, u32[]{:S(2)}, u32[]{:S(2)}) collective-permute-start(bf16[32,4096]{1,0:T(8,128)(2,1)S(1)} %collective-permute-done.refs_1_), channel_id=1, source_target_pairs={{0,4},{1,5},{4,8},{5,9},{8,12},{9,13},{12,14},{13,15},{14,10},{15,... | collective-permute-start | bytes 786440 | tf_op jit(solution)/shard_map/ppermute | solution.py:449
  13.7 1.6 %collective-permute-start.4 = (bf16[32,4096]{1,0:T(8,128)(2,1)S(1)}, bf16[32,4096]{1,0:T(8,128)(2,1)S(1)}, u32[]{:S(2)}, u32[]{:S(2)}) collective-permute-start(bf16[32,4096]{1,0:T(8,128)(2,1)S(1)} %get-tuple-element.60.refs_0_), channel_id=1, source_target_pairs={{0,4},{1,5},{4,8},{5,9},{8,12},{9,13},{12,14},{13,15},{14,10},{15,... | collective-permute-start | bytes 786440 | tf_op jit(solution)/shard_map/ppermute | solution.py:449
  15.7 5.2 %collective-permute-done.2.refs_2_ = bf16[32,4096]{1,0:T(8,128)(2,1)S(1)} collective-permute-done((bf16[32,4096]{1,0:T(8,128)(2,1)S(1)}, bf16[32,4096]{1,0:T(8,128)(2,1)S(1)}, u32[]{:S(2)}, u32[]{:S(2)}) %collective-permute-start.2) | collective-permute-done | bytes 262176 | tf_op jit(solution)/shard_map/ppermute | solution.py:449
  20.9 1.6 %collective-permute-done.3.refs_7_ = bf16[32,4096]{1,0:T(8,128)(2,1)S(1)} collective-permute-done((bf16[32,4096]{1,0:T(8,128)(2,1)S(1)}, bf16[32,4096]{1,0:T(8,128)(2,1)S(1)}, u32[]{:S(2)}, u32[]{:S(2)}) %collective-permute-start.3) | collective-permute-done | bytes 262176 | tf_op jit(solution)/shard_map/ppermute | solution.py:452
  22.5 1.7 %collective-permute-done.4.refs_1_ = bf16[32,4096]{1,0:T(8,128)(2,1)S(1)} collective-permute-done((bf16[32,4096]{1,0:T(8,128)(2,1)S(1)}, bf16[32,4096]{1,0:T(8,128)(2,1)S(1)}, u32[]{:S(2)}, u32[]{:S(2)}) %collective-permute-start.4) | collective-permute-done | bytes 262176 | tf_op jit(solution)/shard_map/ppermute | solution.py:449
  25.5 1.6 %collective-permute-start.6 = (bf16[32,4096]{1,0:T(8,128)(2,1)S(1)}, bf16[32,4096]{1,0:T(8,128)(2,1)S(1)}, u32[]{:S(2)}, u32[]{:S(2)}) collective-permute-start(bf16[32,4096]{1,0:T(8,128)(2,1)S(1)} %collective-permute-done.2.refs_2_), channel_id=1, source_target_pairs={{0,4},{1,5},{4,8},{5,9},{8,12},{9,13},{12,14},{13,15},{14,10},{15,... | collective-permute-start | bytes 786440 | tf_op jit(solution)/shard_map/ppermute | solution.py:449
  27.5 1.6 %collective-permute-start.8 = (bf16[32,4096]{1,0:T(8,128)(2,1)S(1)}, bf16[32,4096]{1,0:T(8,128)(2,1)S(1)}, u32[]{:S(2)}, u32[]{:S(2)}) collective-permute-start(bf16[32,4096]{1,0:T(8,128)(2,1)S(1)} %collective-permute-done.4.refs_1_), channel_id=1, source_target_pairs={{0,4},{1,5},{4,8},{5,9},{8,12},{9,13},{12,14},{13,15},{14,10},{15,... | collective-permute-start | bytes 786440 | tf_op jit(solution)/shard_map/ppermute | solution.py:449
  36.7 2.3 %collective-permute-done.9.rest_1_.refs_7_ = bf16[32,4096]{1,0:T(8,128)(2,1)S(1)} collective-permute-done((bf16[32,4096]{1,0:T(8,128)(2,1)S(1)}, bf16[32,4096]{1,0:T(8,128)(2,1)S(1)}, u32[]{:S(2)}, u32[]{:S(2)}) %collective-permute-start.9) | collective-permute-done | bytes 262176 | tf_op jit(solution)/shard_map/ppermute | solution.py:452
  41.2 2.9 %collective-permute-done.11.refs_5_ = bf16[16,4096]{1,0:T(8,128)(2,1)S(1)} collective-permute-done((bf16[16,4096]{1,0:T(8,128)(2,1)S(1)}, bf16[16,4096]{1,0:T(8,128)(2,1)S(1)}, u32[]{:S(2)}, u32[]{:S(2)}) %collective-permute-start.11) | collective-permute-done | bytes 131104 | tf_op jit(solution)/shard_map/ppermute | solution.py:452
  44.8 1.6 %collective-permute-start.13 = (bf16[32,4096]{1,0:T(8,128)(2,1)S(1)}, bf16[32,4096]{1,0:T(8,128)(2,1)S(1)}, u32[]{:S(2)}, u32[]{:S(2)}) collective-permute-start(bf16[32,4096]{1,0:T(8,128)(2,1)S(1)} %collective-permute-done.8.rest_0_.refs_2_), channel_id=1, source_target_pairs={{0,4},{1,5},{4,8},{5,9},{8,12},{9,13},{12,14},{13,15},{14,10},{15,... | collective-permute-start | bytes 786440 | tf_op jit(solution)/shard_map/ppermute | solution.py:449
  46.8 2.1 %collective-permute-done.12.far_ref = bf16[256,4096]{1,0:T(8,128)(2,1)S(1)} collective-permute-done((bf16[256,4096]{1,0:T(8,128)(2,1)S(1)}, bf16[256,4096]{1,0:T(8,128)(2,1)S(1)}, u32[]{:S(2)}, u32[]{:S(2)}) %collective-permute-start.12) | collective-permute-done | bytes 2097184 | tf_op jit(solution)/shard_map/ppermute | solution.py:455
  48.9 6.9 %gate_up.3 = (f32[512,512]{1,0:T(8,128)S(1)}, f32[512,512]{1,0:T(8,128)S(1)}) custom-call(bf16[256,4096]{1,0:T(8,128)(2,1)S(1)} %pack.1.near_ref, bf16[256,4096]{1,0:T(8,128)(2,1)S(1)} %collective-permute-done.12.far_ref, bf16[4096,1792]{1,0:T(8,128)(2,1)} %wg_ref.7, bf16[4096,1792]{1,0:T(8,128)(2,1)} %wu_ref.7, ...), custom_call_target="tpu_custom_call" | custom-call | flops 4294967296 | bytes 8388608 | tf_op jit(solution)/shard_map/gate_up/pallas_call | solution.py:191
  56.4 1.6 %collective-permute-start.15 = (bf16[16,4096]{1,0:T(8,128)(2,1)S(1)}, bf16[16,4096]{1,0:T(8,128)(2,1)S(1)}, u32[]{:S(2)}, u32[]{:S(2)}) collective-permute-start(bf16[16,4096]{1,0:T(8,128)(2,1)S(1)} %slice.14), channel_id=1, source_target_pairs={{0,4},{1,5},{4,8},{5,9},{8,12},{9,13},{12,14},{13,15},{14,10},{15,... | collective-permute-start | bytes 393224 | tf_op jit(solution)/shard_map/ppermute | solution.py:449
  58.0 9.7 %gate_up.4 = (f32[768,512]{1,0:T(8,128)S(1)}, f32[768,512]{1,0:T(8,128)S(1)}) custom-call(bf16[256,4096]{1,0:T(8,128)(2,1)S(1)} %pack.1.near_ref, bf16[256,4096]{1,0:T(8,128)(2,1)S(1)} %collective-permute-done.12.far_ref, bf16[4096,1792]{1,0:T(8,128)(2,1)} %wg_ref.7, bf16[4096,1792]{1,0:T(8,128)(2,1)} %wu_ref.7, ...), custom_call_target="tpu_custom_call" | custom-call | flops 6442450944 | bytes 12582912 | tf_op jit(solution)/shard_map/gate_up/pallas_call | solution.py:191
  69.3 7.0 %gate_up.5 = (f32[512,512]{1,0:T(8,128)S(1)}, f32[512,512]{1,0:T(8,128)S(1)}) custom-call(bf16[256,4096]{1,0:T(8,128)(2,1)S(1)} %pack.1.near_ref, bf16[256,4096]{1,0:T(8,128)(2,1)S(1)} %collective-permute-done.12.far_ref, bf16[4096,1792]{1,0:T(8,128)(2,1)} %wg_ref.7, bf16[4096,1792]{1,0:T(8,128)(2,1)} %wu_ref.7, ...), custom_call_target="tpu_custom_call" | custom-call | flops 4294967296 | bytes 8388608 | tf_op jit(solution)/shard_map/gate_up/pallas_call | solution.py:191
  76.3 29.7 %hidden_back.1 = (bf16[512,1792]{1,0:T(8,128)(2,1)S(1)}, bf16[512,1792]{1,0:T(8,128)(2,1)S(1)}, bf16[256,4096]{1,0:T(8,128)(2,1)S(1)}, bf16[256,4096]{1,0:T(8,128)(2,1)S(1)}) custom-call(s32[8]{0:T(128)S(1)} %fusion.3.refs_9_.spot_ref, bf16[4096,256]{1,0:T(8,128)(2,1)S(1)} %pack_turned.1.rest_0_.near_ref, ...), custom_call_target="tpu_custom_call" | custom-call | flops 22548578304 | bytes 44040192 | tf_op jit(solution)/shard_map/hidden_back/pallas_call | solution.py:324
  106.5 5.8 %fisher.5 = (bf16[4096,1792]{1,0:T(8,128)(2,1)}, bf16[4096,1792]{1,0:T(8,128)(2,1)}, f32[8,128]{1,0:T(8,128)S(1)}) custom-call(bf16[512,4096]{1,0:T(8,128)(2,1)S(1)} %arrange.1.refs_9_.x_ref, bf16[512,1792]{1,0:T(8,128)(2,1)S(1)} %get-tuple-element.77.gg_ref, bf16[512,1792]{1,0:T(8,128)(2,1)S(1)} %get-tuple-element.78.gu_ref), custom_call_target="tpu_custom_call" | custom-call | flops 3758096384 | bytes 7340032 | tf_op jit(solution)/shard_map/fisher/pallas_call | solution.py:422
  112.4 1.6 %collective-permute-start.19 = (bf16[16,4096]{1,0:T(8,128)(2,1)S(1)}, bf16[16,4096]{1,0:T(8,128)(2,1)S(1)}, u32[]{:S(2)}, u32[]{:S(2)}) collective-permute-start(bf16[16,4096]{1,0:T(8,128)(2,1)S(1)} %get-tuple-element.84.rest_2_), channel_id=1, source_target_pairs={{0,4},{1,5},{4,8},{5,9},{8,12},{9,13},{12,14},{13,15},{14,10},{15,... | collective-permute-start | bytes 393224 | tf_op jit(solution)/shard_map/ppermute | solution.py:449
  114.5 3.4 %fisher.6 = (bf16[4096,1792]{1,0:T(8,128)(2,1)}, bf16[4096,1792]{1,0:T(8,128)(2,1)}, f32[8,128]{1,0:T(8,128)S(1)}) custom-call(bf16[512,4096]{1,0:T(8,128)(2,1)S(1)} %arrange.1.refs_9_.x_ref, bf16[512,1792]{1,0:T(8,128)(2,1)S(1)} %get-tuple-element.77.gg_ref, ...), custom_call_target="tpu_custom_call", output_to_operand_aliasing={{0}: (3, {}), {1}: (4, {})} | custom-call | flops 1879048192 | bytes 3670016 | tf_op jit(solution)/shard_map/fisher/pallas_call | solution.py:422
  121.5 5.8 %fisher.7 = (bf16[4096,1792]{1,0:T(8,128)(2,1)}, bf16[4096,1792]{1,0:T(8,128)(2,1)}, f32[8,128]{1,0:T(8,128)S(1)}) custom-call(bf16[512,4096]{1,0:T(8,128)(2,1)S(1)} %arrange.1.refs_9_.x_ref, bf16[512,1792]{1,0:T(8,128)(2,1)S(1)} %get-tuple-element.77.gg_ref, ...), custom_call_target="tpu_custom_call", output_to_operand_aliasing={{0}: (3, {}), {1}: (4, {})} | custom-call | flops 3758096384 | bytes 7340032 | tf_op jit(solution)/shard_map/fisher/pallas_call | solution.py:422
  130.1 5.8 %fisher.8 = (bf16[4096,1792]{1,0:T(8,128)(2,1)}, bf16[4096,1792]{1,0:T(8,128)(2,1)}, f32[8,128]{1,0:T(8,128)S(1)}) custom-call(bf16[512,4096]{1,0:T(8,128)(2,1)S(1)} %arrange.1.refs_9_.x_ref, bf16[512,1792]{1,0:T(8,128)(2,1)S(1)} %get-tuple-element.77.gg_ref, ...), custom_call_target="tpu_custom_call", output_to_operand_aliasing={{0}: (3, {}), {1}: (4, {})} | custom-call | flops 3758096384 | bytes 7340032 | tf_op jit(solution)/shard_map/fisher/pallas_call | solution.py:422
  138.2 3.4 %fisher.9 = (bf16[4096,1792]{1,0:T(8,128)(2,1)}, bf16[4096,1792]{1,0:T(8,128)(2,1)}, f32[8,128]{1,0:T(8,128)}) custom-call(bf16[512,4096]{1,0:T(8,128)(2,1)S(1)} %arrange.1.refs_9_.x_ref, bf16[512,1792]{1,0:T(8,128)(2,1)S(1)} %get-tuple-element.77.gg_ref, ...), custom_call_target="tpu_custom_call", output_to_operand_aliasing={{0}: (3, {}), {1}: (4, {})} | custom-call | flops 1879048192 | bytes 3670016 | tf_op jit(solution)/shard_map/fisher/pallas_call | solution.py:422
  (65 shorter events, 31.5 us)
Async XLA Ops:
  0.6 9.5 %collective-permute-start = (bf16[32,4096]{1,0:T(8,128)(2,1)}, bf16[32,4096]{1,0:T(8,128)(2,1)S(1)}, u32[]{:S(2)}, u32[]{:S(2)}) collective-permute-start(bf16[32,4096]{1,0:T(8,128)(2,1)} %x_ref.1), channel_id=1, source_target_pairs={{0,4},{1,5},{4,8},{5,9},{8,12},{9,13},{12,14},{13,15},{14,10},{15,... | collective-permute-start | bytes 786440 | tf_op jit(solution)/shard_map/ppermute | solution.py:449
  3.7 8.0 %collective-permute-start.1 = (bf16[32,4096]{1,0:T(8,128)(2,1)}, bf16[32,4096]{1,0:T(8,128)(2,1)S(1)}, u32[]{:S(2)}, u32[]{:S(2)}) collective-permute-start(bf16[32,4096]{1,0:T(8,128)(2,1)} %x_ref.1), channel_id=1, source_target_pairs={{4,0},{5,1},{8,4},{9,5},{12,8},{13,9},{14,12},{15,13},{10,14},{11,... | collective-permute-start | bytes 786440 | tf_op jit(solution)/shard_map/ppermute | solution.py:452
  11.7 9.2 %collective-permute-start.2 = (bf16[32,4096]{1,0:T(8,128)(2,1)S(1)}, bf16[32,4096]{1,0:T(8,128)(2,1)S(1)}, u32[]{:S(2)}, u32[]{:S(2)}) collective-permute-start(bf16[32,4096]{1,0:T(8,128)(2,1)S(1)} %collective-permute-done.refs_1_), channel_id=1, source_target_pairs={{0,4},{1,5},{4,8},{5,9},{8,12},{9,13},{12,14},{13,15},{14,10},{15,... | collective-permute-start | bytes 786440 | tf_op jit(solution)/shard_map/ppermute | solution.py:449
  13.3 9.2 %collective-permute-start.3 = (bf16[32,4096]{1,0:T(8,128)(2,1)S(1)}, bf16[32,4096]{1,0:T(8,128)(2,1)S(1)}, u32[]{:S(2)}, u32[]{:S(2)}) collective-permute-start(bf16[32,4096]{1,0:T(8,128)(2,1)S(1)} %collective-permute-done.1.refs_8_), channel_id=1, source_target_pairs={{4,0},{5,1},{8,4},{9,5},{12,8},{13,9},{14,12},{15,13},{10,14},{11,... | collective-permute-start | bytes 786440 | tf_op jit(solution)/shard_map/ppermute | solution.py:452
  13.7 10.4 %collective-permute-start.4 = (bf16[32,4096]{1,0:T(8,128)(2,1)S(1)}, bf16[32,4096]{1,0:T(8,128)(2,1)S(1)}, u32[]{:S(2)}, u32[]{:S(2)}) collective-permute-start(bf16[32,4096]{1,0:T(8,128)(2,1)S(1)} %get-tuple-element.60.refs_0_), channel_id=1, source_target_pairs={{0,4},{1,5},{4,8},{5,9},{8,12},{9,13},{12,14},{13,15},{14,10},{15,... | collective-permute-start | bytes 786440 | tf_op jit(solution)/shard_map/ppermute | solution.py:449
  15.3 10.2 %collective-permute-start.5 = (bf16[32,4096]{1,0:T(8,128)(2,1)S(1)}, bf16[32,4096]{1,0:T(8,128)(2,1)S(1)}, u32[]{:S(2)}, u32[]{:S(2)}) collective-permute-start(bf16[32,4096]{1,0:T(8,128)(2,1)S(1)} %get-tuple-element.60.refs_0_), channel_id=1, source_target_pairs={{4,0},{5,1},{8,4},{9,5},{12,8},{13,9},{14,12},{15,13},{10,14},{11,... | collective-permute-start | bytes 786440 | tf_op jit(solution)/shard_map/ppermute | solution.py:452
  25.5 8.5 %collective-permute-start.6 = (bf16[32,4096]{1,0:T(8,128)(2,1)S(1)}, bf16[32,4096]{1,0:T(8,128)(2,1)S(1)}, u32[]{:S(2)}, u32[]{:S(2)}) collective-permute-start(bf16[32,4096]{1,0:T(8,128)(2,1)S(1)} %collective-permute-done.2.refs_2_), channel_id=1, source_target_pairs={{0,4},{1,5},{4,8},{5,9},{8,12},{9,13},{12,14},{13,15},{14,10},{15,... | collective-permute-start | bytes 786440 | tf_op jit(solution)/shard_map/ppermute | solution.py:449
  27.0 8.2 %collective-permute-start.7 = (bf16[32,4096]{1,0:T(8,128)(2,1)S(1)}, bf16[32,4096]{1,0:T(8,128)(2,1)S(1)}, u32[]{:S(2)}, u32[]{:S(2)}) collective-permute-start(bf16[32,4096]{1,0:T(8,128)(2,1)S(1)} %collective-permute-done.3.refs_7_), channel_id=1, source_target_pairs={{4,0},{5,1},{8,4},{9,5},{12,8},{13,9},{14,12},{15,13},{10,14},{11,... | collective-permute-start | bytes 786440 | tf_op jit(solution)/shard_map/ppermute | solution.py:452
  27.5 9.2 %collective-permute-start.8 = (bf16[32,4096]{1,0:T(8,128)(2,1)S(1)}, bf16[32,4096]{1,0:T(8,128)(2,1)S(1)}, u32[]{:S(2)}, u32[]{:S(2)}) collective-permute-start(bf16[32,4096]{1,0:T(8,128)(2,1)S(1)} %collective-permute-done.4.refs_1_), channel_id=1, source_target_pairs={{0,4},{1,5},{4,8},{5,9},{8,12},{9,13},{12,14},{13,15},{14,10},{15,... | collective-permute-start | bytes 786440 | tf_op jit(solution)/shard_map/ppermute | solution.py:449
  29.1 10.0 %collective-permute-start.9 = (bf16[32,4096]{1,0:T(8,128)(2,1)S(1)}, bf16[32,4096]{1,0:T(8,128)(2,1)S(1)}, u32[]{:S(2)}, u32[]{:S(2)}) collective-permute-start(bf16[32,4096]{1,0:T(8,128)(2,1)S(1)} %collective-permute-done.5.refs_8_), channel_id=1, source_target_pairs={{4,0},{5,1},{8,4},{9,5},{12,8},{13,9},{14,12},{15,13},{10,14},{11,... | collective-permute-start | bytes 786440 | tf_op jit(solution)/shard_map/ppermute | solution.py:452
  44.8 11.1 %collective-permute-start.13 = (bf16[32,4096]{1,0:T(8,128)(2,1)S(1)}, bf16[32,4096]{1,0:T(8,128)(2,1)S(1)}, u32[]{:S(2)}, u32[]{:S(2)}) collective-permute-start(bf16[32,4096]{1,0:T(8,128)(2,1)S(1)} %collective-permute-done.8.rest_0_.refs_2_), channel_id=1, source_target_pairs={{0,4},{1,5},{4,8},{5,9},{8,12},{9,13},{12,14},{13,15},{14,10},{15,... | collective-permute-start | bytes 786440 | tf_op jit(solution)/shard_map/ppermute | solution.py:449
  46.4 9.5 %collective-permute-start.14 = (bf16[32,4096]{1,0:T(8,128)(2,1)S(1)}, bf16[32,4096]{1,0:T(8,128)(2,1)S(1)}, u32[]{:S(2)}, u32[]{:S(2)}) collective-permute-start(bf16[32,4096]{1,0:T(8,128)(2,1)S(1)} %collective-permute-done.9.rest_1_.refs_7_), channel_id=1, source_target_pairs={{4,0},{5,1},{8,4},{9,5},{12,8},{13,9},{14,12},{15,13},{10,14},{11,... | collective-permute-start | bytes 786440 | tf_op jit(solution)/shard_map/ppermute | solution.py:452
  55.9 12.6 %collective-permute-start.16 = (bf16[16,4096]{1,0:T(8,128)(2,1)S(1)}, bf16[16,4096]{1,0:T(8,128)(2,1)S(1)}, u32[]{:S(2)}, u32[]{:S(2)}) collective-permute-start(bf16[16,4096]{1,0:T(8,128)(2,1)S(1)} %slice.15), channel_id=1, source_target_pairs={{4,0},{5,1},{8,4},{9,5},{12,8},{13,9},{14,12},{15,13},{10,14},{11,... | collective-permute-start | bytes 393224 | tf_op jit(solution)/shard_map/ppermute | solution.py:452
  56.4 12.1 %collective-permute-start.15 = (bf16[16,4096]{1,0:T(8,128)(2,1)S(1)}, bf16[16,4096]{1,0:T(8,128)(2,1)S(1)}, u32[]{:S(2)}, u32[]{:S(2)}) collective-permute-start(bf16[16,4096]{1,0:T(8,128)(2,1)S(1)} %slice.14), channel_id=1, source_target_pairs={{0,4},{1,5},{4,8},{5,9},{8,12},{9,13},{12,14},{13,15},{14,10},{15,... | collective-permute-start | bytes 393224 | tf_op jit(solution)/shard_map/ppermute | solution.py:449
  69.2 7.1 %collective-permute-start.17 = (bf16[4096,256]{1,0:T(8,128)(2,1)S(1)}, bf16[4096,256]{1,0:T(8,128)(2,1)S(1)}, u32[]{:S(2)}, u32[]{:S(2)}) collective-permute-start(bf16[4096,256]{1,0:T(8,128)(2,1)S(1)} %pack_turned.1.rest_0_.near_ref), channel_id=1, source_target_pairs={{0,1},{1,0},{2,3},{3,2},{4,5},{5,4},{6,7},{7,6},{8,9},{9,8},{10,11... | collective-permute-start | bytes 6291464 | tf_op jit(solution)/shard_map/ppermute | solution.py:455
  106.0 6.3 %collective-permute-start.18 = (bf16[256,4096]{1,0:T(8,128)(2,1)S(1)}, bf16[256,4096]{1,0:T(8,128)(2,1)S(1)}, u32[]{:S(2)}, u32[]{:S(2)}) collective-permute-start(bf16[256,4096]{1,0:T(8,128)(2,1)S(1)} %get-tuple-element.82), channel_id=1, source_target_pairs={{0,1},{1,0},{2,3},{3,2},{4,5},{5,4},{6,7},{7,6},{8,9},{9,8},{10,11... | collective-permute-start | bytes 6291464 | tf_op jit(solution)/shard_map/ppermute | solution.py:455
  112.4 5.5 %collective-permute-start.19 = (bf16[16,4096]{1,0:T(8,128)(2,1)S(1)}, bf16[16,4096]{1,0:T(8,128)(2,1)S(1)}, u32[]{:S(2)}, u32[]{:S(2)}) collective-permute-start(bf16[16,4096]{1,0:T(8,128)(2,1)S(1)} %get-tuple-element.84.rest_2_), channel_id=1, source_target_pairs={{0,4},{1,5},{4,8},{5,9},{8,12},{9,13},{12,14},{13,15},{14,10},{15,... | collective-permute-start | bytes 393224 | tf_op jit(solution)/shard_map/ppermute | solution.py:449
  114.0 5.2 %collective-permute-start.20 = (bf16[16,4096]{1,0:T(8,128)(2,1)S(1)}, bf16[16,4096]{1,0:T(8,128)(2,1)S(1)}, u32[]{:S(2)}, u32[]{:S(2)}) collective-permute-start(bf16[16,4096]{1,0:T(8,128)(2,1)S(1)} %get-tuple-element.85.rest_3_), channel_id=1, source_target_pairs={{4,0},{5,1},{8,4},{9,5},{12,8},{13,9},{14,12},{15,13},{10,14},{11,... | collective-permute-start | bytes 393224 | tf_op jit(solution)/shard_map/ppermute | solution.py:452
  119.4 7.9 %collective-permute-start.21 = (bf16[32,4096]{1,0:T(8,128)(2,1)S(1)}, bf16[32,4096]{1,0:T(8,128)(2,1)S(1)}, u32[]{:S(2)}, u32[]{:S(2)}) collective-permute-start(bf16[32,4096]{1,0:T(8,128)(2,1)S(1)} %get-tuple-element.89.rest_2_), channel_id=1, source_target_pairs={{0,4},{1,5},{4,8},{5,9},{8,12},{9,13},{12,14},{13,15},{14,10},{15,... | collective-permute-start | bytes 786440 | tf_op jit(solution)/shard_map/ppermute | solution.py:449
  120.9 6.9 %collective-permute-start.22 = (bf16[32,4096]{1,0:T(8,128)(2,1)S(1)}, bf16[32,4096]{1,0:T(8,128)(2,1)S(1)}, u32[]{:S(2)}, u32[]{:S(2)}) collective-permute-start(bf16[32,4096]{1,0:T(8,128)(2,1)S(1)} %get-tuple-element.90.rest_3_), channel_id=1, source_target_pairs={{4,0},{5,1},{8,4},{9,5},{12,8},{13,9},{14,12},{15,13},{10,14},{11,... | collective-permute-start | bytes 786440 | tf_op jit(solution)/shard_map/ppermute | solution.py:452
  128.0 7.9 %collective-permute-start.23 = (bf16[32,4096]{1,0:T(8,128)(2,1)S(1)}, bf16[32,4096]{1,0:T(8,128)(2,1)S(1)}, u32[]{:S(2)}, u32[]{:S(2)}) collective-permute-start(bf16[32,4096]{1,0:T(8,128)(2,1)S(1)} %get-tuple-element.94.rest_2_), channel_id=1, source_target_pairs={{0,4},{1,5},{4,8},{5,9},{8,12},{9,13},{12,14},{13,15},{14,10},{15,... | collective-permute-start | bytes 786440 | tf_op jit(solution)/shard_map/ppermute | solution.py:449
  129.0 6.9 %collective-permute-start.24 = (bf16[32,4096]{1,0:T(8,128)(2,1)S(1)}, bf16[32,4096]{1,0:T(8,128)(2,1)S(1)}, u32[]{:S(2)}, u32[]{:S(2)}) collective-permute-start(bf16[32,4096]{1,0:T(8,128)(2,1)S(1)} %get-tuple-element.95.rest_3_), channel_id=1, source_target_pairs={{4,0},{5,1},{8,4},{9,5},{12,8},{13,9},{14,12},{15,13},{10,14},{11,... | collective-permute-start | bytes 786440 | tf_op jit(solution)/shard_map/ppermute | solution.py:452
  136.1 6.4 %collective-permute-start.25 = (bf16[32,4096]{1,0:T(8,128)(2,1)S(1)}, bf16[32,4096]{1,0:T(8,128)(2,1)S(1)}, u32[]{:S(2)}, u32[]{:S(2)}) collective-permute-start(bf16[32,4096]{1,0:T(8,128)(2,1)S(1)} %get-tuple-element.99.rest_2_), channel_id=1, source_target_pairs={{0,4},{1,5},{4,8},{5,9},{8,12},{9,13},{12,14},{13,15},{14,10},{15,... | collective-permute-start | bytes 786440 | tf_op jit(solution)/shard_map/ppermute | solution.py:449
  137.1 6.4 %collective-permute-start.26 = (bf16[32,4096]{1,0:T(8,128)(2,1)S(1)}, bf16[32,4096]{1,0:T(8,128)(2,1)S(1)}, u32[]{:S(2)}, u32[]{:S(2)}) collective-permute-start(bf16[32,4096]{1,0:T(8,128)(2,1)S(1)} %get-tuple-element.100.rest_3_), channel_id=1, source_target_pairs={{4,0},{5,1},{8,4},{9,5},{12,8},{13,9},{14,12},{15,13},{10,14},{11,... | collective-permute-start | bytes 786440 | tf_op jit(solution)/shard_map/ppermute | solution.py:452
  (7 other events, 35.1 us)

commit v8 on v7

--- a/solution.py
+++ b/solution.py
@@ -39,21 +39,36 @@
     return [pl.BlockSpec(memory_space=pltpu.VMEM)] * count
 
 
-def bring_kernel(x_ref, dy_ref, x_out, dy_out):
+def head_copies(wg_ref, wu_ref, first, step, head_ref, sems):
+    cols = pl.ds(first * step, step)
+    return [
+        pltpu.make_async_copy(ref.at[:, cols], head_ref.at[i], sems.at[i])
+        for i, ref in enumerate((wg_ref, wu_ref))
+    ]
+
+
+def bring_kernel(step, x_ref, dy_ref, wg_ref, wu_ref, x_out, dy_out, head_ref, sems):
+    copies = head_copies(wg_ref, wu_ref, 0, step, head_ref, sems)
+    for copy in copies:
+        copy.start()
     x_out[...] = x_ref[...]
     dy_out[...] = dy_ref[...]
-
-
-def bring(x, dy):
-    return pl.pallas_call(
-        bring_kernel,
-        in_specs=held_specs(2),
-        out_specs=held_specs(2),
-        out_shape=[jax.ShapeDtypeStruct(x.shape, BF16)] * 2,
-        compiler_params=params(4),
-        cost_estimate=cost(0, 8 * x.size),
+    for copy in copies:
+        copy.wait()
+
+
+def bring(x, dy, wg, wu, step):
+    return pl.pallas_call(
+        functools.partial(bring_kernel, step),
+        in_specs=held_specs(2) + hbm_specs(2),
+        out_specs=held_specs(3),
+        out_shape=[jax.ShapeDtypeStruct(x.shape, BF16)] * 2
+        + [jax.ShapeDtypeStruct((2, wg.shape[0], step), BF16)],
+        scratch_shapes=[pltpu.SemaphoreType.DMA((2,))],
+        compiler_params=params(46),
+        cost_estimate=cost(0, 4 * wg.shape[0] * step),
         name="bring",
-    )(x, dy)
+    )(x, dy, wg, wu)
 
 
 def pack_kernel(count, *refs):
@@ -127,21 +142,19 @@
     )(spot, near, far, *after)
 
 
-CHUNKS = 4
-
-
-def gate_up_kernel(first, step, near_ref, far_ref, wg_ref, wu_ref, *rest):
-    a_ref, b_ref, w_buf, out_buf, sems, out_sems = rest[-6:]
-    rows, depth = near_ref.shape
-    part = depth // CHUNKS
+def gate_up_kernel(first, step, near_ref, far_ref, head_ref, wg_ref, wu_ref, wd_ref, *rest):
+    a_ref, b_ref, next_ref, w_buf, out_buf, sems, out_sems, next_sems = rest[-8:]
+    rows = near_ref.shape[0]
     tiles = a_ref.shape[0] // step
 
-    def fetch(t, k):
-        cols, deep, slot = pl.ds((first + t) * step, step), pl.ds(k * part, part), t % 2
-        return [
-            pltpu.make_async_copy(w_ref.at[deep, cols], w_buf.at[slot, i, deep], sems.at[slot, i, k])
-            for i, w_ref in enumerate((wg_ref, wu_ref))
-        ]
+    def fetch(t):
+        slot = t % 2
+        return head_copies(wg_ref, wu_ref, first + t, step, w_buf.at[slot], sems.at[slot])
+
+    def fetch_next():
+        if next_ref.shape[0] == 2:
+            return head_copies(wg_ref, wu_ref, first + tiles, step, next_ref, next_sems)
+        return [pltpu.make_async_copy(wd_ref.at[pl.ds(0, step), :], next_ref, next_sems.at[0])]
 
     def store(t):
         to = pl.ds(t * step, step)
@@ -150,64 +163,62 @@
             for i, ref in enumerate((a_ref, b_ref))
         ]
 
-    def begin(t):
-        for k in range(CHUNKS):
-            for copy in fetch(t, k):
-                copy.start()
-
-    for t in range(min(2, tiles)):
-        begin(t)
+    def begin(copies):
+        for copy in copies:
+            copy.start()
+
+    def finish(copies):
+        for copy in copies:
+            copy.wait()
+
+    for t in range(1, min(3, tiles)):
+        begin(fetch(t))
     for t in range(tiles):
-        sums = [[None, None], [None, None]]
-        pieces = CHUNKS if t == 0 else 1
-        for k in range(pieces):
-            deep = pl.ds(k * (depth // pieces), depth // pieces)
-            for c in range(k, k + 1) if t == 0 else range(CHUNKS):
-                for copy in fetch(t, c):
-                    copy.wait()
-            for side, x_ref in enumerate((near_ref, far_ref)):
-                for i in range(2):
-                    term = jnp.dot(
-                        x_ref[:, deep], w_buf[t % 2, i, deep, :], preferred_element_type=F32
-                    )
-                    before = sums[side][i]
-                    sums[side][i] = term if before is None else before + term
-        if t + 2 < tiles:
-            begin(t + 2)
-        for side, (gate, up) in enumerate(sums):
+        if t:
+            finish(fetch(t))
+        if t == tiles - 1:
+            begin(fetch_next())
+        w_ref = w_buf.at[t % 2] if t else head_ref
+        for side, x_ref in enumerate((near_ref, far_ref)):
+            gate = jnp.dot(x_ref[...], w_ref[0], preferred_element_type=F32)
+            up = jnp.dot(x_ref[...], w_ref[1], preferred_element_type=F32)
             at = pl.ds(side * rows, rows)
             sigma = jax.nn.sigmoid(gate)
             out_buf[t, 0, :, at] = (up * sigma * (1.0 + gate * (1.0 - sigma))).T
             out_buf[t, 1, :, at] = (gate * sigma).T
-        for copy in store(t):
-            copy.start()
+        if t and t + 2 < tiles:
+            begin(fetch(t + 2))
+        begin(store(t))
     for t in range(tiles):
-        for copy in store(t):
-            copy.wait()
-
-
-def gate_up(near, far, wg, wu, first, count, step, grant, after):
+        finish(store(t))
+    finish(fetch_next())
+
+
+def gate_up(near, far, head, wg, wu, wd, first, count, step, grant, after):
     rows, depth = near.shape
+    last = (first + count) * step == wg.shape[1]
     return pl.pallas_call(
         functools.partial(gate_up_kernel, first, step),
-        in_specs=held_specs(2)
-        + hbm_specs(2)
-        + any_specs(after),
-        out_specs=hbm_specs(2),
-        out_shape=[jax.ShapeDtypeStruct((count * step, 2 * rows), F32)] * 2,
+        in_specs=held_specs(3) + hbm_specs(3) + any_specs(after),
+        out_specs=hbm_specs(2) + held_specs(1),
+        out_shape=[jax.ShapeDtypeStruct((count * step, 2 * rows), F32)] * 2
+        + [jax.ShapeDtypeStruct((step, depth) if last else (2, depth, step), BF16)],
         scratch_shapes=[
             pltpu.VMEM((2, 2, depth, step), BF16),
             pltpu.VMEM((count, 2, step, 2 * rows), F32),
-            pltpu.SemaphoreType.DMA((2, 2, CHUNKS)),
+            pltpu.SemaphoreType.DMA((2, 2)),
             pltpu.SemaphoreType.DMA((count, 2)),
+            pltpu.SemaphoreType.DMA((2,)),
         ],
         compiler_params=params(grant),
         cost_estimate=cost(8 * rows * depth * count * step, 4 * depth * count * step),
         name="gate_up",
-    )(near, far, wg, wu, *after)
-
-
-def back_kernel(step, deep, pieces, spot_ref, near_ref, far_ref, wg_ref, wu_ref, wd_ref, *refs):
+    )(near, far, head, wg, wu, wd, *after)
+
+
+def back_kernel(
+    step, deep, pieces, spot_ref, near_ref, far_ref, head_ref, wg_ref, wu_ref, wd_ref, *refs
+):
     a_refs, b_refs = refs[:pieces], refs[pieces : 2 * pieces]
     ggs_ref, gus_ref, own_ref, sent_ref, g_ref = refs[2 * pieces : 2 * pieces + 5]
     wd_buf, w_buf, factor_buf, sems, w_sems, factor_sems = refs[2 * pieces + 5 :]
@@ -215,15 +226,10 @@
     rows = near_ref.shape[1]
     tiles = wd_ref.shape[0] // step
 
-    part = wd_ref.shape[1] // CHUNKS
-
-    def fetch(t, k):
+    def fetch(t):
         at = pl.ds(pl.multiple_of(t * step, step), step)
-        deep = pl.ds(k * part, part)
         slot = lax.rem(t, 2)
-        return pltpu.make_async_copy(
-            wd_ref.at[at, deep], wd_buf.at[slot, :, deep], sems.at[slot, k]
-        )
+        return pltpu.make_async_copy(wd_ref.at[at, :], wd_buf.at[slot], sems.at[slot])
 
     def fetch_rows(i):
         at = pl.ds(pl.multiple_of(i * deep, deep), deep)
@@ -246,21 +252,10 @@
             for k, ref in enumerate((a_refs[p], b_refs[p]))
         ]
 
-    def hidden_tile(t, pieces):
+    def hidden_tile(t, wd):
         cols = pl.ds(pl.multiple_of(t * step, step), step)
-        sums = [None, None]
-        size = wd_ref.shape[1] // pieces
-        for k in range(pieces):
-            part_k = pl.ds(k * size, size)
-            for c in range(k, k + 1) if pieces > 1 else range(CHUNKS):
-                fetch(t, c).wait()
-            for side, dy_ref in enumerate((near_ref, far_ref)):
-                term = jnp.dot(
-                    wd_buf[lax.rem(t, 2), :, part_k], dy_ref[part_k, :],
-                    preferred_element_type=F32,
-                )
-                sums[side] = term if sums[side] is None else sums[side] + term
-        for side, hidden in enumerate(sums):
+        for side, dy_ref in enumerate((near_ref, far_ref)):
+            hidden = jnp.dot(wd, dy_ref[...], preferred_element_type=F32)
             at = pl.ds(side * rows, rows)
             for f, gs_ref in enumerate((ggs_ref, gus_ref)):
                 grad = (hidden * factor_buf[f, cols, at]).astype(BF16)
@@ -268,18 +263,11 @@
                 g_ref[pl.ds(to, step), at] = grad
                 put_rows(spot_ref, side, grad.T, gs_ref, cols)
 
-        @pl.when(t + 2 < tiles)
-        def _():
-            for k in range(CHUNKS):
-                fetch(t + 2, k).start()
-
     blocks = wg_ref.shape[0] // deep
-    for t in range(min(2, tiles)):
-        for k in range(CHUNKS):
-            fetch(jnp.int32(t), k).start()
-        if t == 0:
-            for copy in fetch_factors(0):
-                copy.start()
+    for copy in fetch_factors(0):
+        copy.start()
+    for t in range(1, min(3, tiles)):
+        fetch(jnp.int32(t)).start()
     for p in range(pieces):
         if p + 1 < pieces:
             for copy in fetch_factors(p + 1):
@@ -292,11 +280,16 @@
             copy.wait()
 
         if p == 0:
-            hidden_tile(0, CHUNKS)
+            hidden_tile(0, head_ref[...])
 
         @pl.loop(max(starts[p] // step, 1), starts[p + 1] // step)
         def _(t):
-            hidden_tile(t, 1)
+            fetch(t).wait()
+            hidden_tile(t, wd_buf[lax.rem(t, 2)])
+
+            @pl.when(t + 2 < tiles)
+            def _():
+                fetch(t + 2).start()
 
     @pl.loop(0, blocks)
     def _(i):
@@ -315,7 +308,7 @@
                 copy.start()
 
 
-def back(spot, near, far, wg, wu, wd, factors):
+def back(spot, near, far, head, wg, wu, wd, factors):
     depth, rows = near.shape
     width = wd.shape[0]
     step = tile(width, 256)
@@ -324,7 +317,7 @@
     return pl.pallas_call(
         functools.partial(back_kernel, step, 512, len(a)),
         in_specs=[pl.BlockSpec(memory_space=pltpu.SMEM)]
-        + held_specs(2)
+        + held_specs(3)
         + hbm_specs(3)
         + any_specs(a + b),
         out_specs=held_specs(4),
@@ -335,14 +328,14 @@
             pltpu.VMEM((2, step, depth), BF16),
             pltpu.VMEM((2, 512, 2 * width), BF16),
             pltpu.VMEM((2, width, 2 * rows), F32),
-            pltpu.SemaphoreType.DMA((2, CHUNKS)),
+            pltpu.SemaphoreType.DMA((2,)),
             pltpu.SemaphoreType.DMA((2, 2)),
             pltpu.SemaphoreType.DMA((2, len(a))),
         ],
         compiler_params=params(28),
         cost_estimate=cost(12 * rows * depth * width, 6 * depth * width),
         name="hidden_back",
-    )(spot, near, far, wg, wu, wd, *a, *b)
+    )(spot, near, far, head, wg, wu, wd, *a, *b)
 
 
 def fold_kernel(cuts, *refs):
@@ -472,40 +465,39 @@
 
     lane = tile(width, 256)
     tiles = width // lane
-    cuts = [0, 2, 5, 7] if tiles == 7 else [0, 0, 0, tiles]
-
-    def piece(i, after):
-        if cuts[i] == cuts[i + 1]:
-            return []
+    cuts = [0, 2, 5, 7]
+
+    def piece(i, head, after):
+        grant = (30, 28, 28)[i]
         count = cuts[i + 1] - cuts[i]
-        grant = (40, 38, 32)[i]
-        return [gate_up(near_x, far_x, wg, wu, cuts[i], count, lane, grant, after)]
-
-    def two(x, dy, after=()):
-        (x, dy), _ = lax.optimization_barrier(((x, dy), after))
-        return (right(x[0]), left(x[1])), (right(dy[0]), left(dy[1]))
-
-    own_x, own_dy = bring(tokens, grad_out)
-    in_x, in_dy = [both(tokens, tokens)], []
-    got = two(in_x[0], (own_dy, own_dy), own_x)
-    for k in range(2, far):
-        in_x.append(got[0])
-        in_dy.append(got[1])
-        if k < far - 1:
-            got = two(in_x[-1], in_dy[-1])
+        a, b, head = gate_up(
+            near_x, far_x, head, wg, wu, wd, cuts[i], count, lane, grant, after
+        )
+        return (a, b), head
+
+    own_x, own_dy, head = bring(tokens, grad_out, wg, wu, lane)
+    in_x = [both(tokens, tokens)]
+    in_x.append(both(*in_x[-1], (own_x, head)))
+    in_dy = [both(own_dy, own_dy, in_x[0])]
+    for _ in range(3, far):
+        in_x.append(both(*in_x[-1]))
+        in_dy.append(both(*in_dy[-1]))
     in_x.append(both(*in_x[-1], in_dy[-1], True))
     near_x = pack(blocks(own_x, in_x), (spot,))
     far_x = swap(near_x)
 
     in_dy.append(both(*in_dy[-1], in_x[-2]))
-    factors = piece(0, in_dy[-2])
-    in_dy.append(both(*in_dy[-1], factors, True))
-    factors += piece(1, in_dy[-2])
+    some, head = piece(0, head, in_dy[-2])
+    factors = [some]
+    in_dy.append(both(*in_dy[-1], some, True))
+    some, head = piece(1, head, in_dy[-2])
+    factors.append(some)
     x = arrange(spot, near_x, far_x, in_dy[-2])
-    near_dy = pack_turned(blocks(own_dy, in_dy), (x, *factors[-1]))
+    near_dy = pack_turned(blocks(own_dy, in_dy), (x, *some))
     far_dy = swap(near_dy)
-    factors += piece(2, (near_dy,))
-    gg, gu, own, sent = back(spot, near_dy, far_dy, wg, wu, wd, factors)
+    some, head = piece(2, head, (near_dy,))
+    factors.append(some)
+    gg, gu, own, sent = back(spot, near_dy, far_dy, head, wg, wu, wd, factors)
 
     near = swap(sent)
     full, head, tail = pl.ds(0, row), pl.ds(0, row // 2), pl.ds(row // 2, row // 2)
@@ -683,7 +675,8 @@
 
 
 def per_device(size, tokens, grad_out, wg, wu, wd):
-    if size == 2 * len(CYCLE) and tokens.shape[0] % 32 == 0:
+    fits = tokens.shape[0] == 32 and wg.shape == (4096, 1792)
+    if size == 2 * len(CYCLE) and fits:
         return ring_part(tokens, grad_out, wg, wu, wd)
     return plain_part(size, tokens, grad_out, wg, wu, wd)
 

time: 145 us -> 138 us (0.952)
  waiting for transfers between devices: 31.4 us -> 26.6 us
  Pallas kernels: 80.5 us -> 77.7 us
    ppermute x12, waiting for transfers between devices: 15.6 us -> 10.7 us  [right(): return lax.ppermute(value, 'hid', to_right)]
    pallas_call x3, Pallas kernels: 23.6 us -> 19.5 us  [gate_up(): pl.pallas_call(functools.partial(gate_up_kernel, first, step), in_specs=h...]
    pallas_call x1, Pallas kernels: 0.03 us -> 2.27 us  [bring(): pl.pallas_call(functools.partial(bring_kernel, step), in_specs=held_specs...]
    unnamed x8 -> x20, local copies, waits for them, and re-layouts: 1.91 us -> 3.95 us
  transfers between devices with their start and end apart: 27 -> 27, of which waited for: 18 -> 17; matrix products, arithmetic and copies ran while one was open for 2% -> 1% of each run, Pallas kernels for 34% -> 34%
where the time goes in v8:
time: 138 us; the launch traced here: 137 us
  Pallas kernels  77.7 us (56%)
  waiting for transfers between devices  26.6 us (19%)
  starting transfers between devices  26.4 us (19%)
  local copies, waits for them, and re-layouts  5.21 us (4%)
    pallas_call x1, Pallas kernels, back(): pl.pallas_call(functools.partial(back_kernel, step, 512, len(a)), in_spec...  28.8 us
    pallas_call x5, Pallas kernels, fisher(): pl.pallas_call(functools.partial(fisher_kernel, tile(width, 256)), grid=(...  24.2 us
    ppermute x12, starting transfers between devices, right(): return lax.ppermute(value, 'hid', to_right)  20.1 us
    pallas_call x3, Pallas kernels, gate_up(): pl.pallas_call(functools.partial(gate_up_kernel, first, step), in_specs=h...  19.5 us
    ppermute x12, waiting for transfers between devices, left(): return lax.ppermute(value, 'hid', to_left)  13.8 us
    ppermute x12, waiting for transfers between devices, right(): return lax.ppermute(value, 'hid', to_right)  10.7 us
    ppermute x12, starting transfers between devices, left(): return lax.ppermute(value, 'hid', to_left)  5.59 us
    unnamed x20, local copies, waits for them, and re-layouts  3.95 us
  transfers between devices with their start and end apart: 27, of which 17 were waited for; matrix products, arithmetic and copies ran while one was open for 1% of the time, Pallas kernels for 34%

profile of v8, /device:TPU:0, one launch (start us, length us, event | category | flops | bytes accessed | tf_op | source)
XLA Modules:
  0.0 137.5 jit_solution(1575176675260344503)
XLA Ops:
  0.6 3.1 %collective-permute-start = (bf16[32,4096]{1,0:T(8,128)(2,1)}, bf16[32,4096]{1,0:T(8,128)(2,1)S(1)}, u32[]{:S(2)}, u32[]{:S(2)}) collective-permute-start(bf16[32,4096]{1,0:T(8,128)(2,1)} %x_ref.1), channel_id=1, source_target_pairs={{0,4},{1,5},{4,8},{5,9},{8,12},{9,13},{12,14},{13,15},{14,10},{15,... | collective-permute-start | bytes 786440 | tf_op jit(solution)/shard_map/ppermute | solution.py:442
  5.6 2.3 %bring.1 = (bf16[32,4096]{1,0:T(8,128)(2,1)S(1)}, bf16[32,4096]{1,0:T(8,128)(2,1)S(1)}, bf16[2,4096,256]{2,1,0:T(8,128)(2,1)S(1)}) custom-call(bf16[32,4096]{1,0:T(8,128)(2,1)S(1)} %copy-done.3, bf16[32,4096]{1,0:T(8,128)(2,1)S(1)} %copy-done.2, bf16[4096,1792]{1,0:T(8,128)(2,1)} %wg_ref.9, bf16[4096,1792]{1,0:T(8,128)(2,1)} %wu_ref.9), custom_call_target="tpu_custom_call" | custom-call | bytes 4194304 | tf_op jit(solution)/shard_map/bring/pallas_call | solution.py:61
  7.9 2.0 %copy-done = bf16[2,4096,256]{2,1,0:T(8,128)(2,1)} copy-done((bf16[2,4096,256]{2,1,0:T(8,128)(2,1)}, bf16[2,4096,256]{2,1,0:T(8,128)(2,1)S(1)}, u32[]{:S(2)}) %copy-start) | copy-done | bytes 4194328
  11.7 1.6 %collective-permute-start.6 = (bf16[32,4096]{1,0:T(8,128)(2,1)S(1)}, bf16[32,4096]{1,0:T(8,128)(2,1)S(1)}, u32[]{:S(2)}, u32[]{:S(2)}) collective-permute-start(bf16[32,4096]{1,0:T(8,128)(2,1)S(1)} %get-tuple-element.67.refs_0_), channel_id=1, source_target_pairs={{0,4},{1,5},{4,8},{5,9},{8,12},{9,13},{12,14},{13,15},{14,10},{15,... | collective-permute-start | bytes 786440 | tf_op jit(solution)/shard_map/ppermute | solution.py:442
  13.7 1.6 %collective-permute-start.2 = (bf16[32,4096]{1,0:T(8,128)(2,1)S(1)}, bf16[32,4096]{1,0:T(8,128)(2,1)S(1)}, u32[]{:S(2)}, u32[]{:S(2)}) collective-permute-start(bf16[32,4096]{1,0:T(8,128)(2,1)S(1)} %collective-permute-done.refs_1_), channel_id=1, source_target_pairs={{0,4},{1,5},{4,8},{5,9},{8,12},{9,13},{12,14},{13,15},{14,10},{15,... | collective-permute-start | bytes 786440 | tf_op jit(solution)/shard_map/ppermute | solution.py:442
  15.7 5.2 %collective-permute-done.6.refs_1_ = bf16[32,4096]{1,0:T(8,128)(2,1)S(1)} collective-permute-done((bf16[32,4096]{1,0:T(8,128)(2,1)S(1)}, bf16[32,4096]{1,0:T(8,128)(2,1)S(1)}, u32[]{:S(2)}, u32[]{:S(2)}) %collective-permute-start.6) | collective-permute-done | bytes 262176 | tf_op jit(solution)/shard_map/ppermute | solution.py:442
  20.9 1.6 %collective-permute-done.7.refs_8_ = bf16[32,4096]{1,0:T(8,128)(2,1)S(1)} collective-permute-done((bf16[32,4096]{1,0:T(8,128)(2,1)S(1)}, bf16[32,4096]{1,0:T(8,128)(2,1)S(1)}, u32[]{:S(2)}, u32[]{:S(2)}) %collective-permute-start.7) | collective-permute-done | bytes 262176 | tf_op jit(solution)/shard_map/ppermute | solution.py:445
  24.5 2.0 %collective-permute-done.2.refs_2_ = bf16[32,4096]{1,0:T(8,128)(2,1)S(1)} collective-permute-done((bf16[32,4096]{1,0:T(8,128)(2,1)S(1)}, bf16[32,4096]{1,0:T(8,128)(2,1)S(1)}, u32[]{:S(2)}, u32[]{:S(2)}) %collective-permute-start.2) | collective-permute-done | bytes 262176 | tf_op jit(solution)/shard_map/ppermute | solution.py:442
  26.6 1.6 %collective-permute-done.3.refs_7_ = bf16[32,4096]{1,0:T(8,128)(2,1)S(1)} collective-permute-done((bf16[32,4096]{1,0:T(8,128)(2,1)S(1)}, bf16[32,4096]{1,0:T(8,128)(2,1)S(1)}, u32[]{:S(2)}, u32[]{:S(2)}) %collective-permute-start.3) | collective-permute-done | bytes 262176 | tf_op jit(solution)/shard_map/ppermute | solution.py:445
  33.8 1.7 %collective-permute-done.4.refs_3_ = bf16[32,4096]{1,0:T(8,128)(2,1)S(1)} collective-permute-done((bf16[32,4096]{1,0:T(8,128)(2,1)S(1)}, bf16[32,4096]{1,0:T(8,128)(2,1)S(1)}, u32[]{:S(2)}, u32[]{:S(2)}) %collective-permute-start.4) | collective-permute-done | bytes 262176 | tf_op jit(solution)/shard_map/ppermute | solution.py:442
  38.8 2.9 %collective-permute-done.11.refs_5_ = bf16[16,4096]{1,0:T(8,128)(2,1)S(1)} collective-permute-done((bf16[16,4096]{1,0:T(8,128)(2,1)S(1)}, bf16[16,4096]{1,0:T(8,128)(2,1)S(1)}, u32[]{:S(2)}, u32[]{:S(2)}) %collective-permute-start.11) | collective-permute-done | bytes 131104 | tf_op jit(solution)/shard_map/ppermute | solution.py:445
  42.4 1.6 %collective-permute-start.13 = (bf16[32,4096]{1,0:T(8,128)(2,1)S(1)}, bf16[32,4096]{1,0:T(8,128)(2,1)S(1)}, u32[]{:S(2)}, u32[]{:S(2)}) collective-permute-start(bf16[32,4096]{1,0:T(8,128)(2,1)S(1)} %collective-permute-done.8.rest_0_.refs_2_), channel_id=1, source_target_pairs={{0,4},{1,5},{4,8},{5,9},{8,12},{9,13},{12,14},{13,15},{14,10},{15,... | collective-permute-start | bytes 786440 | tf_op jit(solution)/shard_map/ppermute | solution.py:442
  44.5 2.1 %collective-permute-done.12.far_ref = bf16[256,4096]{1,0:T(8,128)(2,1)S(1)} collective-permute-done((bf16[256,4096]{1,0:T(8,128)(2,1)S(1)}, bf16[256,4096]{1,0:T(8,128)(2,1)S(1)}, u32[]{:S(2)}, u32[]{:S(2)}) %collective-permute-start.12) | collective-permute-done | bytes 2097184 | tf_op jit(solution)/shard_map/ppermute | solution.py:448
  46.6 6.3 %gate_up.3 = (f32[512,512]{1,0:T(8,128)S(1)}, f32[512,512]{1,0:T(8,128)S(1)}, bf16[2,4096,256]{2,1,0:T(8,128)(2,1)S(1)}) custom-call(bf16[256,4096]{1,0:T(8,128)(2,1)S(1)} %pack.1.near_ref, bf16[256,4096]{1,0:T(8,128)(2,1)S(1)} %collective-permute-done.12.far_ref, bf16[2,4096,256]{2,1,0:T(8,128)(2,1)S(1)} %copy-done.1, bf16[4096,1792]{1,0:T(8,128)(2,1)} %wg_ref.9, ...), custom_call_target="tpu_custom_call" | custom-call | flops 4294967296 | bytes 8388608 | tf_op jit(solution)/shard_map/gate_up/pallas_call | solution.py:200
  55.1 7.9 %gate_up.4 = (f32[768,512]{1,0:T(8,128)S(1)}, f32[768,512]{1,0:T(8,128)S(1)}, bf16[2,4096,256]{2,1,0:T(8,128)(2,1)S(1)}) custom-call(bf16[256,4096]{1,0:T(8,128)(2,1)S(1)} %pack.1.near_ref, bf16[256,4096]{1,0:T(8,128)(2,1)S(1)} %collective-permute-done.12.far_ref, bf16[2,4096,256]{2,1,0:T(8,128)(2,1)S(1)} %get-tuple-element.78.head_ref, ...), custom_call_target="tpu_custom_call" | custom-call | flops 6442450944 | bytes 12582912 | tf_op jit(solution)/shard_map/gate_up/pallas_call | solution.py:200
  64.6 5.2 %gate_up.5 = (f32[512,512]{1,0:T(8,128)S(1)}, f32[512,512]{1,0:T(8,128)S(1)}, bf16[256,4096]{1,0:T(8,128)(2,1)S(1)}) custom-call(bf16[256,4096]{1,0:T(8,128)(2,1)S(1)} %pack.1.near_ref, bf16[256,4096]{1,0:T(8,128)(2,1)S(1)} %collective-permute-done.12.far_ref, bf16[2,4096,256]{2,1,0:T(8,128)(2,1)S(1)} %get-tuple-element.81.head_ref, ...), custom_call_target="tpu_custom_call" | custom-call | flops 4294967296 | bytes 8388608 | tf_op jit(solution)/shard_map/gate_up/pallas_call | solution.py:200
  69.8 28.8 %hidden_back.1 = (bf16[512,1792]{1,0:T(8,128)(2,1)S(1)}, bf16[512,1792]{1,0:T(8,128)(2,1)S(1)}, bf16[256,4096]{1,0:T(8,128)(2,1)S(1)}, bf16[256,4096]{1,0:T(8,128)(2,1)S(1)}) custom-call(s32[8]{0:T(128)S(1)} %fusion.3.refs_9_.spot_ref, bf16[4096,256]{1,0:T(8,128)(2,1)S(1)} %pack_turned.1.rest_0_.near_ref, ...), custom_call_target="tpu_custom_call" | custom-call | flops 22548578304 | bytes 44040192 | tf_op jit(solution)/shard_map/hidden_back/pallas_call | solution.py:317
  99.2 5.8 %fisher.5 = (bf16[4096,1792]{1,0:T(8,128)(2,1)}, bf16[4096,1792]{1,0:T(8,128)(2,1)}, f32[8,128]{1,0:T(8,128)S(1)}) custom-call(bf16[512,4096]{1,0:T(8,128)(2,1)S(1)} %arrange.1.refs_9_.x_ref, bf16[512,1792]{1,0:T(8,128)(2,1)S(1)} %get-tuple-element.85.gg_ref, bf16[512,1792]{1,0:T(8,128)(2,1)S(1)} %get-tuple-element.86.gu_ref), custom_call_target="tpu_custom_call" | custom-call | flops 3758096384 | bytes 7340032 | tf_op jit(solution)/shard_map/fisher/pallas_call | solution.py:415
  105.0 1.6 %collective-permute-start.19 = (bf16[16,4096]{1,0:T(8,128)(2,1)S(1)}, bf16[16,4096]{1,0:T(8,128)(2,1)S(1)}, u32[]{:S(2)}, u32[]{:S(2)}) collective-permute-start(bf16[16,4096]{1,0:T(8,128)(2,1)S(1)} %get-tuple-element.92.rest_2_), channel_id=1, source_target_pairs={{0,4},{1,5},{4,8},{5,9},{8,12},{9,13},{12,14},{13,15},{14,10},{15,... | collective-permute-start | bytes 393224 | tf_op jit(solution)/shard_map/ppermute | solution.py:442
  107.1 3.4 %fisher.6 = (bf16[4096,1792]{1,0:T(8,128)(2,1)}, bf16[4096,1792]{1,0:T(8,128)(2,1)}, f32[8,128]{1,0:T(8,128)S(1)}) custom-call(bf16[512,4096]{1,0:T(8,128)(2,1)S(1)} %arrange.1.refs_9_.x_ref, bf16[512,1792]{1,0:T(8,128)(2,1)S(1)} %get-tuple-element.85.gg_ref, ...), custom_call_target="tpu_custom_call", output_to_operand_aliasing={{0}: (3, {}), {1}: (4, {})} | custom-call | flops 1879048192 | bytes 3670016 | tf_op jit(solution)/shard_map/fisher/pallas_call | solution.py:415
  112.0 1.6 %collective-permute-start.21 = (bf16[32,4096]{1,0:T(8,128)(2,1)S(1)}, bf16[32,4096]{1,0:T(8,128)(2,1)S(1)}, u32[]{:S(2)}, u32[]{:S(2)}) collective-permute-start(bf16[32,4096]{1,0:T(8,128)(2,1)S(1)} %get-tuple-element.97.rest_2_), channel_id=1, source_target_pairs={{0,4},{1,5},{4,8},{5,9},{8,12},{9,13},{12,14},{13,15},{14,10},{15,... | collective-permute-start | bytes 786440 | tf_op jit(solution)/shard_map/ppermute | solution.py:442
  114.1 5.8 %fisher.7 = (bf16[4096,1792]{1,0:T(8,128)(2,1)}, bf16[4096,1792]{1,0:T(8,128)(2,1)}, f32[8,128]{1,0:T(8,128)S(1)}) custom-call(bf16[512,4096]{1,0:T(8,128)(2,1)S(1)} %arrange.1.refs_9_.x_ref, bf16[512,1792]{1,0:T(8,128)(2,1)S(1)} %get-tuple-element.85.gg_ref, ...), custom_call_target="tpu_custom_call", output_to_operand_aliasing={{0}: (3, {}), {1}: (4, {})} | custom-call | flops 3758096384 | bytes 7340032 | tf_op jit(solution)/shard_map/fisher/pallas_call | solution.py:415
  122.7 5.8 %fisher.8 = (bf16[4096,1792]{1,0:T(8,128)(2,1)}, bf16[4096,1792]{1,0:T(8,128)(2,1)}, f32[8,128]{1,0:T(8,128)S(1)}) custom-call(bf16[512,4096]{1,0:T(8,128)(2,1)S(1)} %arrange.1.refs_9_.x_ref, bf16[512,1792]{1,0:T(8,128)(2,1)S(1)} %get-tuple-element.85.gg_ref, ...), custom_call_target="tpu_custom_call", output_to_operand_aliasing={{0}: (3, {}), {1}: (4, {})} | custom-call | flops 3758096384 | bytes 7340032 | tf_op jit(solution)/shard_map/fisher/pallas_call | solution.py:415
  130.8 3.4 %fisher.9 = (bf16[4096,1792]{1,0:T(8,128)(2,1)}, bf16[4096,1792]{1,0:T(8,128)(2,1)}, f32[8,128]{1,0:T(8,128)}) custom-call(bf16[512,4096]{1,0:T(8,128)(2,1)S(1)} %arrange.1.refs_9_.x_ref, bf16[512,1792]{1,0:T(8,128)(2,1)S(1)} %get-tuple-element.85.gg_ref, ...), custom_call_target="tpu_custom_call", output_to_operand_aliasing={{0}: (3, {}), {1}: (4, {})} | custom-call | flops 1879048192 | bytes 3670016 | tf_op jit(solution)/shard_map/fisher/pallas_call | solution.py:415
  (77 shorter events, 31.7 us)
Async XLA Ops:
  0.6 9.5 %collective-permute-start = (bf16[32,4096]{1,0:T(8,128)(2,1)}, bf16[32,4096]{1,0:T(8,128)(2,1)S(1)}, u32[]{:S(2)}, u32[]{:S(2)}) collective-permute-start(bf16[32,4096]{1,0:T(8,128)(2,1)} %x_ref.1), channel_id=1, source_target_pairs={{0,4},{1,5},{4,8},{5,9},{8,12},{9,13},{12,14},{13,15},{14,10},{15,... | collective-permute-start | bytes 786440 | tf_op jit(solution)/shard_map/ppermute | solution.py:442
  3.7 8.0 %collective-permute-start.1 = (bf16[32,4096]{1,0:T(8,128)(2,1)}, bf16[32,4096]{1,0:T(8,128)(2,1)S(1)}, u32[]{:S(2)}, u32[]{:S(2)}) collective-permute-start(bf16[32,4096]{1,0:T(8,128)(2,1)} %x_ref.1), channel_id=1, source_target_pairs={{4,0},{5,1},{8,4},{9,5},{12,8},{13,9},{14,12},{15,13},{10,14},{11,... | collective-permute-start | bytes 786440 | tf_op jit(solution)/shard_map/ppermute | solution.py:445
  11.7 9.2 %collective-permute-start.6 = (bf16[32,4096]{1,0:T(8,128)(2,1)S(1)}, bf16[32,4096]{1,0:T(8,128)(2,1)S(1)}, u32[]{:S(2)}, u32[]{:S(2)}) collective-permute-start(bf16[32,4096]{1,0:T(8,128)(2,1)S(1)} %get-tuple-element.67.refs_0_), channel_id=1, source_target_pairs={{0,4},{1,5},{4,8},{5,9},{8,12},{9,13},{12,14},{13,15},{14,10},{15,... | collective-permute-start | bytes 786440 | tf_op jit(solution)/shard_map/ppermute | solution.py:442
  13.3 9.2 %collective-permute-start.7 = (bf16[32,4096]{1,0:T(8,128)(2,1)S(1)}, bf16[32,4096]{1,0:T(8,128)(2,1)S(1)}, u32[]{:S(2)}, u32[]{:S(2)}) collective-permute-start(bf16[32,4096]{1,0:T(8,128)(2,1)S(1)} %get-tuple-element.67.refs_0_), channel_id=1, source_target_pairs={{4,0},{5,1},{8,4},{9,5},{12,8},{13,9},{14,12},{15,13},{10,14},{11,... | collective-permute-start | bytes 786440 | tf_op jit(solution)/shard_map/ppermute | solution.py:445
  13.7 12.8 %collective-permute-start.2 = (bf16[32,4096]{1,0:T(8,128)(2,1)S(1)}, bf16[32,4096]{1,0:T(8,128)(2,1)S(1)}, u32[]{:S(2)}, u32[]{:S(2)}) collective-permute-start(bf16[32,4096]{1,0:T(8,128)(2,1)S(1)} %collective-permute-done.refs_1_), channel_id=1, source_target_pairs={{0,4},{1,5},{4,8},{5,9},{8,12},{9,13},{12,14},{13,15},{14,10},{15,... | collective-permute-start | bytes 786440 | tf_op jit(solution)/shard_map/ppermute | solution.py:442
  15.3 12.8 %collective-permute-start.3 = (bf16[32,4096]{1,0:T(8,128)(2,1)S(1)}, bf16[32,4096]{1,0:T(8,128)(2,1)S(1)}, u32[]{:S(2)}, u32[]{:S(2)}) collective-permute-start(bf16[32,4096]{1,0:T(8,128)(2,1)S(1)} %collective-permute-done.1.refs_8_), channel_id=1, source_target_pairs={{4,0},{5,1},{8,4},{9,5},{12,8},{13,9},{14,12},{15,13},{10,14},{11,... | collective-permute-start | bytes 786440 | tf_op jit(solution)/shard_map/ppermute | solution.py:445
  22.5 9.7 %collective-permute-start.8 = (bf16[32,4096]{1,0:T(8,128)(2,1)S(1)}, bf16[32,4096]{1,0:T(8,128)(2,1)S(1)}, u32[]{:S(2)}, u32[]{:S(2)}) collective-permute-start(bf16[32,4096]{1,0:T(8,128)(2,1)S(1)} %collective-permute-done.6.refs_1_), channel_id=1, source_target_pairs={{0,4},{1,5},{4,8},{5,9},{8,12},{9,13},{12,14},{13,15},{14,10},{15,... | collective-permute-start | bytes 786440 | tf_op jit(solution)/shard_map/ppermute | solution.py:442
  24.1 9.7 %collective-permute-start.9 = (bf16[32,4096]{1,0:T(8,128)(2,1)S(1)}, bf16[32,4096]{1,0:T(8,128)(2,1)S(1)}, u32[]{:S(2)}, u32[]{:S(2)}) collective-permute-start(bf16[32,4096]{1,0:T(8,128)(2,1)S(1)} %collective-permute-done.7.refs_8_), channel_id=1, source_target_pairs={{4,0},{5,1},{8,4},{9,5},{12,8},{13,9},{14,12},{15,13},{10,14},{11,... | collective-permute-start | bytes 786440 | tf_op jit(solution)/shard_map/ppermute | solution.py:445
  28.1 7.3 %collective-permute-start.4 = (bf16[32,4096]{1,0:T(8,128)(2,1)S(1)}, bf16[32,4096]{1,0:T(8,128)(2,1)S(1)}, u32[]{:S(2)}, u32[]{:S(2)}) collective-permute-start(bf16[32,4096]{1,0:T(8,128)(2,1)S(1)} %collective-permute-done.2.refs_2_), channel_id=1, source_target_pairs={{0,4},{1,5},{4,8},{5,9},{8,12},{9,13},{12,14},{13,15},{14,10},{15,... | collective-permute-start | bytes 786440 | tf_op jit(solution)/shard_map/ppermute | solution.py:442
  29.7 7.0 %collective-permute-start.5 = (bf16[32,4096]{1,0:T(8,128)(2,1)S(1)}, bf16[32,4096]{1,0:T(8,128)(2,1)S(1)}, u32[]{:S(2)}, u32[]{:S(2)}) collective-permute-start(bf16[32,4096]{1,0:T(8,128)(2,1)S(1)} %collective-permute-done.3.refs_7_), channel_id=1, source_target_pairs={{4,0},{5,1},{8,4},{9,5},{12,8},{13,9},{14,12},{15,13},{10,14},{11,... | collective-permute-start | bytes 786440 | tf_op jit(solution)/shard_map/ppermute | solution.py:445
  42.4 10.5 %collective-permute-start.13 = (bf16[32,4096]{1,0:T(8,128)(2,1)S(1)}, bf16[32,4096]{1,0:T(8,128)(2,1)S(1)}, u32[]{:S(2)}, u32[]{:S(2)}) collective-permute-start(bf16[32,4096]{1,0:T(8,128)(2,1)S(1)} %collective-permute-done.8.rest_0_.refs_2_), channel_id=1, source_target_pairs={{0,4},{1,5},{4,8},{5,9},{8,12},{9,13},{12,14},{13,15},{14,10},{15,... | collective-permute-start | bytes 786440 | tf_op jit(solution)/shard_map/ppermute | solution.py:442
  44.1 8.9 %collective-permute-start.14 = (bf16[32,4096]{1,0:T(8,128)(2,1)S(1)}, bf16[32,4096]{1,0:T(8,128)(2,1)S(1)}, u32[]{:S(2)}, u32[]{:S(2)}) collective-permute-start(bf16[32,4096]{1,0:T(8,128)(2,1)S(1)} %collective-permute-done.9.rest_1_.refs_7_), channel_id=1, source_target_pairs={{4,0},{5,1},{8,4},{9,5},{12,8},{13,9},{14,12},{15,13},{10,14},{11,... | collective-permute-start | bytes 786440 | tf_op jit(solution)/shard_map/ppermute | solution.py:445
  53.0 10.9 %collective-permute-start.16 = (bf16[16,4096]{1,0:T(8,128)(2,1)S(1)}, bf16[16,4096]{1,0:T(8,128)(2,1)S(1)}, u32[]{:S(2)}, u32[]{:S(2)}) collective-permute-start(bf16[16,4096]{1,0:T(8,128)(2,1)S(1)} %slice.15), channel_id=1, source_target_pairs={{4,0},{5,1},{8,4},{9,5},{12,8},{13,9},{14,12},{15,13},{10,14},{11,... | collective-permute-start | bytes 393224 | tf_op jit(solution)/shard_map/ppermute | solution.py:445
  53.8 10.0 %collective-permute-start.15 = (bf16[16,4096]{1,0:T(8,128)(2,1)S(1)}, bf16[16,4096]{1,0:T(8,128)(2,1)S(1)}, u32[]{:S(2)}, u32[]{:S(2)}) collective-permute-start(bf16[16,4096]{1,0:T(8,128)(2,1)S(1)} %slice.14), channel_id=1, source_target_pairs={{0,4},{1,5},{4,8},{5,9},{8,12},{9,13},{12,14},{13,15},{14,10},{15,... | collective-permute-start | bytes 393224 | tf_op jit(solution)/shard_map/ppermute | solution.py:442
  64.5 5.3 %collective-permute-start.17 = (bf16[4096,256]{1,0:T(8,128)(2,1)S(1)}, bf16[4096,256]{1,0:T(8,128)(2,1)S(1)}, u32[]{:S(2)}, u32[]{:S(2)}) collective-permute-start(bf16[4096,256]{1,0:T(8,128)(2,1)S(1)} %pack_turned.1.rest_0_.near_ref), channel_id=1, source_target_pairs={{0,1},{1,0},{2,3},{3,2},{4,5},{5,4},{6,7},{7,6},{8,9},{9,8},{10,11... | collective-permute-start | bytes 6291464 | tf_op jit(solution)/shard_map/ppermute | solution.py:448
  98.6 6.4 %collective-permute-start.18 = (bf16[256,4096]{1,0:T(8,128)(2,1)S(1)}, bf16[256,4096]{1,0:T(8,128)(2,1)S(1)}, u32[]{:S(2)}, u32[]{:S(2)}) collective-permute-start(bf16[256,4096]{1,0:T(8,128)(2,1)S(1)} %get-tuple-element.90), channel_id=1, source_target_pairs={{0,1},{1,0},{2,3},{3,2},{4,5},{5,4},{6,7},{7,6},{8,9},{9,8},{10,11... | collective-permute-start | bytes 6291464 | tf_op jit(solution)/shard_map/ppermute | solution.py:448
  105.0 5.5 %collective-permute-start.19 = (bf16[16,4096]{1,0:T(8,128)(2,1)S(1)}, bf16[16,4096]{1,0:T(8,128)(2,1)S(1)}, u32[]{:S(2)}, u32[]{:S(2)}) collective-permute-start(bf16[16,4096]{1,0:T(8,128)(2,1)S(1)} %get-tuple-element.92.rest_2_), channel_id=1, source_target_pairs={{0,4},{1,5},{4,8},{5,9},{8,12},{9,13},{12,14},{13,15},{14,10},{15,... | collective-permute-start | bytes 393224 | tf_op jit(solution)/shard_map/ppermute | solution.py:442
  106.7 5.2 %collective-permute-start.20 = (bf16[16,4096]{1,0:T(8,128)(2,1)S(1)}, bf16[16,4096]{1,0:T(8,128)(2,1)S(1)}, u32[]{:S(2)}, u32[]{:S(2)}) collective-permute-start(bf16[16,4096]{1,0:T(8,128)(2,1)S(1)} %get-tuple-element.93.rest_3_), channel_id=1, source_target_pairs={{4,0},{5,1},{8,4},{9,5},{12,8},{13,9},{14,12},{15,13},{10,14},{11,... | collective-permute-start | bytes 393224 | tf_op jit(solution)/shard_map/ppermute | solution.py:445
  112.0 7.9 %collective-permute-start.21 = (bf16[32,4096]{1,0:T(8,128)(2,1)S(1)}, bf16[32,4096]{1,0:T(8,128)(2,1)S(1)}, u32[]{:S(2)}, u32[]{:S(2)}) collective-permute-start(bf16[32,4096]{1,0:T(8,128)(2,1)S(1)} %get-tuple-element.97.rest_2_), channel_id=1, source_target_pairs={{0,4},{1,5},{4,8},{5,9},{8,12},{9,13},{12,14},{13,15},{14,10},{15,... | collective-permute-start | bytes 786440 | tf_op jit(solution)/shard_map/ppermute | solution.py:442
  113.6 6.8 %collective-permute-start.22 = (bf16[32,4096]{1,0:T(8,128)(2,1)S(1)}, bf16[32,4096]{1,0:T(8,128)(2,1)S(1)}, u32[]{:S(2)}, u32[]{:S(2)}) collective-permute-start(bf16[32,4096]{1,0:T(8,128)(2,1)S(1)} %get-tuple-element.98.rest_3_), channel_id=1, source_target_pairs={{4,0},{5,1},{8,4},{9,5},{12,8},{13,9},{14,12},{15,13},{10,14},{11,... | collective-permute-start | bytes 786440 | tf_op jit(solution)/shard_map/ppermute | solution.py:445
  120.6 7.9 %collective-permute-start.23 = (bf16[32,4096]{1,0:T(8,128)(2,1)S(1)}, bf16[32,4096]{1,0:T(8,128)(2,1)S(1)}, u32[]{:S(2)}, u32[]{:S(2)}) collective-permute-start(bf16[32,4096]{1,0:T(8,128)(2,1)S(1)} %get-tuple-element.102.rest_2_), channel_id=1, source_target_pairs={{0,4},{1,5},{4,8},{5,9},{8,12},{9,13},{12,14},{13,15},{14,10},{15,... | collective-permute-start | bytes 786440 | tf_op jit(solution)/shard_map/ppermute | solution.py:442
  122.2 6.4 %collective-permute-start.24 = (bf16[32,4096]{1,0:T(8,128)(2,1)S(1)}, bf16[32,4096]{1,0:T(8,128)(2,1)S(1)}, u32[]{:S(2)}, u32[]{:S(2)}) collective-permute-start(bf16[32,4096]{1,0:T(8,128)(2,1)S(1)} %get-tuple-element.103.rest_3_), channel_id=1, source_target_pairs={{4,0},{5,1},{8,4},{9,5},{12,8},{13,9},{14,12},{15,13},{10,14},{11,... | collective-permute-start | bytes 786440 | tf_op jit(solution)/shard_map/ppermute | solution.py:445
  128.7 6.4 %collective-permute-start.25 = (bf16[32,4096]{1,0:T(8,128)(2,1)S(1)}, bf16[32,4096]{1,0:T(8,128)(2,1)S(1)}, u32[]{:S(2)}, u32[]{:S(2)}) collective-permute-start(bf16[32,4096]{1,0:T(8,128)(2,1)S(1)} %get-tuple-element.107.rest_2_), channel_id=1, source_target_pairs={{0,4},{1,5},{4,8},{5,9},{8,12},{9,13},{12,14},{13,15},{14,10},{15,... | collective-permute-start | bytes 786440 | tf_op jit(solution)/shard_map/ppermute | solution.py:442
  130.3 6.4 %collective-permute-start.26 = (bf16[32,4096]{1,0:T(8,128)(2,1)S(1)}, bf16[32,4096]{1,0:T(8,128)(2,1)S(1)}, u32[]{:S(2)}, u32[]{:S(2)}) collective-permute-start(bf16[32,4096]{1,0:T(8,128)(2,1)S(1)} %get-tuple-element.108.rest_3_), channel_id=1, source_target_pairs={{4,0},{5,1},{8,4},{9,5},{12,8},{13,9},{14,12},{15,13},{10,14},{11,... | collective-permute-start | bytes 786440 | tf_op jit(solution)/shard_map/ppermute | solution.py:445
  (13 other events, 118.7 us)

commit v9 on v8

--- a/solution.py
+++ b/solution.py
@@ -338,58 +338,57 @@
     )(spot, near, far, head, wg, wu, wd, *a, *b)
 
 
-def fold_kernel(cuts, *refs):
-    count = len(cuts)
-    outs = refs[-count:]
-    for i, (at, got_at) in enumerate(cuts):
-        own_ref, near_ref, got_ref = refs[3 * i : 3 * i + 3]
-        out_ref = outs[i]
-        out_ref[...] = (own_ref[at, :].astype(F32) + near_ref[at, :].astype(F32)).astype(BF16)
-        if got_at is not None:
-            total = own_ref[got_at, :].astype(F32) + near_ref[got_at, :].astype(F32)
-            out_ref[got_at, :] = (total + got_ref[...].astype(F32)).astype(BF16)
+def fold_kernel(got, *refs):
+    outs = refs[-len(got) :]
+    refs = list(refs)
+    for has, out_ref in zip(got, outs):
+        total = refs.pop(0)[...].astype(F32) + refs.pop(0)[...].astype(F32)
+        if has:
+            total += refs.pop(0)[...].astype(F32)
+        out_ref[...] = total.astype(BF16)
 
 
 def fold(own, near, row, sends, after):
     depth = own.shape[1]
-    operands, specs, shapes, cuts = [], [], [], []
-    for p, at, got_at, got in sends:
+    operands, specs = [], []
+    for p, got in sends:
         block = pl.BlockSpec((row, depth), lambda i, p=p: (p, 0))
-        got = near if got is None else got
-        size = got.shape[0] if got_at is not None else row
-        operands += [own, near, got]
-        specs += [block, block, pl.BlockSpec((size, depth), lambda i: (0, 0))]
-        shapes.append(jax.ShapeDtypeStruct((at.size, depth), BF16))
-        cuts.append((at, got_at))
-    return pl.pallas_call(
-        functools.partial(fold_kernel, cuts),
+        operands += [own, near]
+        specs += [block, block]
+        if got is not None:
+            operands.append(got)
+            specs.append(pl.BlockSpec((row, depth), lambda i: (0, 0)))
+    return pl.pallas_call(
+        functools.partial(fold_kernel, [got is not None for _, got in sends]),
         grid=(1,),
         in_specs=specs + any_specs(after),
-        out_specs=[pl.BlockSpec(shape.shape, lambda i: (0, 0)) for shape in shapes],
-        out_shape=shapes,
+        out_specs=[pl.BlockSpec((row, depth), lambda i: (0, 0))] * len(sends),
+        out_shape=[jax.ShapeDtypeStruct((row, depth), BF16)] * len(sends),
         compiler_params=params(24),
         cost_estimate=cost(0, 16 * row * depth),
         name="fold",
     )(*operands, *after)
 
 
-def last_kernel(own_ref, near_ref, r_ref, l_ref, out_ref):
-    total = own_ref[...].astype(F32) + near_ref[...].astype(F32)
-    out_ref[...] = (total + r_ref[...].astype(F32) + l_ref[...].astype(F32)).astype(BF16)
-
-
-def last(own, near, r, l):
-    block = pl.BlockSpec(r.shape, lambda i: (0, 0))
+def last_kernel(*refs):
+    total = refs[0][...].astype(F32)
+    for ref in refs[1:-1]:
+        total += ref[...].astype(F32)
+    refs[-1][...] = total.astype(BF16)
+
+
+def last(own, near, got):
+    block = pl.BlockSpec(got[0].shape, lambda i: (0, 0))
     return pl.pallas_call(
         last_kernel,
         grid=(1,),
-        in_specs=[block] * 4,
+        in_specs=[block] * (2 + len(got)),
         out_specs=block,
-        out_shape=jax.ShapeDtypeStruct(r.shape, BF16),
+        out_shape=jax.ShapeDtypeStruct(got[0].shape, BF16),
         compiler_params=params(24),
-        cost_estimate=cost(0, 12 * r.size),
+        cost_estimate=cost(0, 12 * got[0].size),
         name="last",
-    )(own, near, r, l)
+    )(own, near, *got)
 
 
 def fisher_kernel(step, x_ref, gg_ref, gu_ref, *rest):
@@ -437,6 +436,11 @@
     to_right = [(2 * a + c, 2 * b + c) for a, b in links for c in range(2)]
     to_left = [(b, a) for a, b in to_right]
     across = [(2 * i + c, 2 * i + 1 - c) for i in range(chips) for c in range(2)]
+    ends = [(CYCLE[i], CYCLE[(i + far) % chips]) for i in range(chips)]
+    to_far = [(2 * a + c, 2 * b + c) for a, b in ends for c in range(2)]
+
+    def straight(value):
+        return lax.ppermute(value, "hid", to_far)
 
     def right(value):
         return lax.ppermute(value, "hid", to_right)
@@ -454,21 +458,19 @@
     span = chips // SEQS
     spot = (chip // span * 2 * span + chip % span) * row
 
-    def both(r, l, after=(), ends=False):
+    def both(r, l, after=()):
         (r, l), _ = lax.optimization_barrier(((r, l), after))
-        if ends:
-            r, l = r[: row // 2], l[row // 2 :]
         return right(r), left(l)
 
-    def blocks(own, rounds):
-        return [own] + [r for r, _ in rounds] + [l for _, l in rounds[::-1]]
+    def blocks(own, rounds, end):
+        return [own] + [r for r, _ in rounds] + [end] + [l for _, l in rounds[::-1]]
 
     lane = tile(width, 256)
     tiles = width // lane
-    cuts = [0, 2, 5, 7]
+    cuts = [0, 4, 7]
 
     def piece(i, head, after):
-        grant = (30, 28, 28)[i]
+        grant = (30, 28)[i]
         count = cuts[i + 1] - cuts[i]
         a, b, head = gate_up(
             near_x, far_x, head, wg, wu, wd, cuts[i], count, lane, grant, after
@@ -477,48 +479,43 @@
 
     own_x, own_dy, head = bring(tokens, grad_out, wg, wu, lane)
     in_x = [both(tokens, tokens)]
+    end_x = straight(tokens)
     in_x.append(both(*in_x[-1], (own_x, head)))
-    in_dy = [both(own_dy, own_dy, in_x[0])]
-    for _ in range(3, far):
-        in_x.append(both(*in_x[-1]))
-        in_dy.append(both(*in_dy[-1]))
-    in_x.append(both(*in_x[-1], in_dy[-1], True))
-    near_x = pack(blocks(own_x, in_x), (spot,))
+    in_dy = [both(own_dy, own_dy, (in_x[0], end_x))]
+    in_x.append(both(*in_x[-1], in_dy[-1]))
+    in_dy.append(both(*in_dy[-1]))
+    near_x = pack(blocks(own_x, in_x, end_x), (spot, *in_dy[-1]))
     far_x = swap(near_x)
 
-    in_dy.append(both(*in_dy[-1], in_x[-2]))
+    in_dy.append(both(*in_dy[-1], in_x[-1]))
+    end_dy = straight(lax.optimization_barrier((own_dy, in_x[-1]))[0])
     some, head = piece(0, head, in_dy[-2])
     factors = [some]
-    in_dy.append(both(*in_dy[-1], some, True))
-    some, head = piece(1, head, in_dy[-2])
-    factors.append(some)
     x = arrange(spot, near_x, far_x, in_dy[-2])
-    near_dy = pack_turned(blocks(own_dy, in_dy), (x, *some))
+    near_dy = pack_turned(blocks(own_dy, in_dy, end_dy), (x, *some))
     far_dy = swap(near_dy)
-    some, head = piece(2, head, (near_dy,))
+    some, head = piece(1, head, (near_dy,))
     factors.append(some)
     gg, gu, own, sent = back(spot, near_dy, far_dy, head, wg, wu, wd, factors)
 
     near = swap(sent)
-    full, head, tail = pl.ds(0, row), pl.ds(0, row // 2), pl.ds(row // 2, row // 2)
     step = 256
-    counts = [4, 2, 4, 4, 2]
+    counts = [3, 5, 4, 4]
     held, first = (), 0
-    r = l = None
+    r = l = end = None
     ready = ()
-    for k in range(far, 0, -1):
-        *held, done = fisher(x, gg, gu, first, counts[far - k], step, held, ready)
-        first += counts[far - k]
-        if k == far:
-            sends = [(far, head, None, None), (far, tail, None, None)]
-        elif k == far - 1:
-            sends = [(chips - k, full, head, r), (k, full, tail, l)]
-        else:
-            sends = [(chips - k, full, full, r), (k, full, full, l)]
+    for k in range(far - 1, 0, -1):
+        *held, done = fisher(x, gg, gu, first, counts[far - 1 - k], step, held, ready)
+        first += counts[far - 1 - k]
+        sends = [(chips - k, r), (k, l)]
+        if end is None:
+            sends.append((far, None))
         ready = fold(own, near, row, sends, (done,))
         r, l = right(ready[0]), left(ready[1])
-    fg, fu, _ = fisher(x, gg, gu, first, counts[far], step, held, ready)
-    mine = last(own, near, r, l)
+        if end is None:
+            end = straight(ready[2])
+    fg, fu, _ = fisher(x, gg, gu, first, counts[-1], step, held, ready)
+    mine = last(own, near, (r, l, end))
     return fg, fu, mine
 
 

time: 138 us -> 150 us (1.087)
  starting transfers between devices: 26.4 us -> 42.4 us
  waiting for transfers between devices: 26.6 us -> 21.8 us
    ppermute x12 -> x9, starting transfers between devices: 20.1 us -> 30.8 us  [right(): return lax.ppermute(value, 'hid', to_right)]
    ppermute x0 -> x3, starting transfers between devices: none -> 9.7 us  [straight(): return lax.ppermute(value, 'hid', to_far)]
    ppermute x0 -> x3, waiting for transfers between devices: none -> 4.54 us  [straight(): return lax.ppermute(value, 'hid', to_far)]
    ppermute x12 -> x9, starting transfers between devices: 5.59 us -> 1.17 us  [left(): return lax.ppermute(value, 'hid', to_left)]
    ppermute x12 -> x9, waiting for transfers between devices: 10.7 us -> 6.46 us  [right(): return lax.ppermute(value, 'hid', to_right)]
    ppermute x12 -> x9, waiting for transfers between devices: 13.8 us -> 10.8 us  [left(): return lax.ppermute(value, 'hid', to_left)]
    ppermute x3, waiting for transfers between devices: 2.07 us -> 0.01 us  [swap(): return lax.ppermute(value, 'hid', across)]
    pallas_call x1, Pallas kernels: 28.8 us -> 30.3 us  [back(): pl.pallas_call(functools.partial(back_kernel, step, 512, len(a)), in_spec...]
  transfers between devices with their start and end apart: 27 -> 24, of which waited for: 17 -> 12; matrix products, arithmetic and copies ran while one was open for 1% -> 1% of each run, Pallas kernels for 34% -> 31%
where the time goes in v9:
time: 150 us
  Pallas kernels  78.9 us (53%)
  starting transfers between devices  42.4 us (28%)
  waiting for transfers between devices  21.8 us (15%)
  local copies, waits for them, and re-layouts  5.15 us (3%)
    ppermute x9, starting transfers between devices, right(): return lax.ppermute(value, 'hid', to_right)  30.8 us
    pallas_call x1, Pallas kernels, back(): pl.pallas_call(functools.partial(back_kernel, step, 512, len(a)), in_spec...  30.3 us
    pallas_call x4, Pallas kernels, fisher(): pl.pallas_call(functools.partial(fisher_kernel, tile(width, 256)), grid=(...  23.3 us
    pallas_call x2, Pallas kernels, gate_up(): pl.pallas_call(functools.partial(gate_up_kernel, first, step), in_specs=h...  20.1 us
    ppermute x9, waiting for transfers between devices, left(): return lax.ppermute(value, 'hid', to_left)  10.8 us
    ppermute x3, starting transfers between devices, straight(): return lax.ppermute(value, 'hid', to_far)  9.7 us
    ppermute x9, waiting for transfers between devices, right(): return lax.ppermute(value, 'hid', to_right)  6.46 us
    ppermute x3, waiting for transfers between devices, straight(): return lax.ppermute(value, 'hid', to_far)  4.54 us
  transfers between devices with their start and end apart: 24, of which 12 were waited for; matrix products, arithmetic and copies ran while one was open for 1% of the time, Pallas kernels for 31%

profile of v9, /device:TPU:0, one launch (start us, length us, event | category | flops | bytes accessed | tf_op | source)
XLA Modules:
  0.0 149.7 jit_solution(6651565958456252006)
XLA Ops:
  0.6 3.1 %collective-permute-start = (bf16[32,4096]{1,0:T(8,128)(2,1)}, bf16[32,4096]{1,0:T(8,128)(2,1)S(1)}, u32[]{:S(2)}, u32[]{:S(2)}) collective-permute-start(bf16[32,4096]{1,0:T(8,128)(2,1)} %x_ref.1), channel_id=1, source_target_pairs={{0,4},{1,5},{4,8},{5,9},{8,12},{9,13},{12,14},{13,15},{14,10},{15,... | collective-permute-start | bytes 786440 | tf_op jit(solution)/shard_map/ppermute | solution.py:446
  3.7 5.0 %collective-permute-start.4 = (bf16[32,4096]{1,0:T(8,128)(2,1)}, bf16[32,4096]{1,0:T(8,128)(2,1)S(1)}, u32[]{:S(2)}, u32[]{:S(2)}) collective-permute-start(bf16[32,4096]{1,0:T(8,128)(2,1)} %x_ref.1), channel_id=1, source_target_pairs={{0,14},{1,15},{4,10},{5,11},{8,6},{9,7},{12,2},{13,3},{14,0},{15,1... | collective-permute-start | bytes 786440 | tf_op jit(solution)/shard_map/ppermute | solution.py:443
  10.6 2.3 %bring.1 = (bf16[32,4096]{1,0:T(8,128)(2,1)S(1)}, bf16[32,4096]{1,0:T(8,128)(2,1)S(1)}, bf16[2,4096,256]{2,1,0:T(8,128)(2,1)S(1)}) custom-call(bf16[32,4096]{1,0:T(8,128)(2,1)S(1)} %copy-done.3, bf16[32,4096]{1,0:T(8,128)(2,1)S(1)} %copy-done.2, bf16[4096,1792]{1,0:T(8,128)(2,1)} %wg_ref.7, bf16[4096,1792]{1,0:T(8,128)(2,1)} %wu_ref.7), custom_call_target="tpu_custom_call" | custom-call | bytes 4194304 | tf_op jit(solution)/shard_map/bring/pallas_call | solution.py:61
  12.9 2.0 %copy-done = bf16[2,4096,256]{2,1,0:T(8,128)(2,1)} copy-done((bf16[2,4096,256]{2,1,0:T(8,128)(2,1)}, bf16[2,4096,256]{2,1,0:T(8,128)(2,1)S(1)}, u32[]{:S(2)}) %copy-start) | copy-done | bytes 4194328
  14.9 4.2 %collective-permute-done.4.refs_4_ = bf16[32,4096]{1,0:T(8,128)(2,1)S(1)} collective-permute-done((bf16[32,4096]{1,0:T(8,128)(2,1)}, bf16[32,4096]{1,0:T(8,128)(2,1)S(1)}, u32[]{:S(2)}, u32[]{:S(2)}) %collective-permute-start.4) | collective-permute-done | bytes 262176 | tf_op jit(solution)/shard_map/ppermute | solution.py:443
  19.1 5.1 %collective-permute-start.5 = (bf16[32,4096]{1,0:T(8,128)(2,1)S(1)}, bf16[32,4096]{1,0:T(8,128)(2,1)S(1)}, u32[]{:S(2)}, u32[]{:S(2)}) collective-permute-start(bf16[32,4096]{1,0:T(8,128)(2,1)S(1)} %get-tuple-element.61.refs_0_), channel_id=1, source_target_pairs={{0,4},{1,5},{4,8},{5,9},{8,12},{9,13},{12,14},{13,15},{14,10},{15,... | collective-permute-start | bytes 786440 | tf_op jit(solution)/shard_map/ppermute | solution.py:446
  24.1 2.0 %collective-permute-start.2 = (bf16[32,4096]{1,0:T(8,128)(2,1)S(1)}, bf16[32,4096]{1,0:T(8,128)(2,1)S(1)}, u32[]{:S(2)}, u32[]{:S(2)}) collective-permute-start(bf16[32,4096]{1,0:T(8,128)(2,1)S(1)} %collective-permute-done.refs_1_), channel_id=1, source_target_pairs={{0,4},{1,5},{4,8},{5,9},{8,12},{9,13},{12,14},{13,15},{14,10},{15,... | collective-permute-start | bytes 786440 | tf_op jit(solution)/shard_map/ppermute | solution.py:446
  27.4 3.5 %collective-permute-done.5.refs_1_ = bf16[32,4096]{1,0:T(8,128)(2,1)S(1)} collective-permute-done((bf16[32,4096]{1,0:T(8,128)(2,1)S(1)}, bf16[32,4096]{1,0:T(8,128)(2,1)S(1)}, u32[]{:S(2)}, u32[]{:S(2)}) %collective-permute-start.5) | collective-permute-done | bytes 262176 | tf_op jit(solution)/shard_map/ppermute | solution.py:446
  30.9 2.5 %collective-permute-done.6.refs_7_ = bf16[32,4096]{1,0:T(8,128)(2,1)S(1)} collective-permute-done((bf16[32,4096]{1,0:T(8,128)(2,1)S(1)}, bf16[32,4096]{1,0:T(8,128)(2,1)S(1)}, u32[]{:S(2)}, u32[]{:S(2)}) %collective-permute-start.6) | collective-permute-done | bytes 262176 | tf_op jit(solution)/shard_map/ppermute | solution.py:449
  36.5 2.5 %collective-permute-done.3.refs_6_ = bf16[32,4096]{1,0:T(8,128)(2,1)S(1)} collective-permute-done((bf16[32,4096]{1,0:T(8,128)(2,1)S(1)}, bf16[32,4096]{1,0:T(8,128)(2,1)S(1)}, u32[]{:S(2)}, u32[]{:S(2)}) %collective-permute-start.3) | collective-permute-done | bytes 262176 | tf_op jit(solution)/shard_map/ppermute | solution.py:449
  42.5 2.1 %collective-permute-done.10.refs_10_.rest_1_.refs_6_ = bf16[32,4096]{1,0:T(8,128)(2,1)S(1)} collective-permute-done((bf16[32,4096]{1,0:T(8,128)(2,1)S(1)}, bf16[32,4096]{1,0:T(8,128)(2,1)S(1)}, u32[]{:S(2)}, u32[]{:S(2)}) %collective-permute-start.10) | collective-permute-done | bytes 262176 | tf_op jit(solution)/shard_map/ppermute | solution.py:449
  45.7 2.2 %collective-permute-done.8.refs_5_ = bf16[32,4096]{1,0:T(8,128)(2,1)S(1)} collective-permute-done((bf16[32,4096]{1,0:T(8,128)(2,1)S(1)}, bf16[32,4096]{1,0:T(8,128)(2,1)S(1)}, u32[]{:S(2)}, u32[]{:S(2)}) %collective-permute-start.8) | collective-permute-done | bytes 262176 | tf_op jit(solution)/shard_map/ppermute | solution.py:449
  50.2 2.4 %collective-permute-start.13 = (bf16[32,4096]{1,0:T(8,128)(2,1)S(1)}, bf16[32,4096]{1,0:T(8,128)(2,1)S(1)}, u32[]{:S(2)}, u32[]{:S(2)}) collective-permute-start(bf16[32,4096]{1,0:T(8,128)(2,1)S(1)} %get-tuple-element.61.refs_0_), channel_id=1, source_target_pairs={{0,14},{1,15},{4,10},{5,11},{8,6},{9,7},{12,2},{13,3},{14,0},{15,1... | collective-permute-start | bytes 786440 | tf_op jit(solution)/shard_map/ppermute | solution.py:443
  52.6 10.5 %gate_up.2 = (f32[1024,512]{1,0:T(8,128)S(1)}, f32[1024,512]{1,0:T(8,128)S(1)}, bf16[2,4096,256]{2,1,0:T(8,128)(2,1)S(1)}) custom-call(bf16[256,4096]{1,0:T(8,128)(2,1)S(1)} %pack.1.near_ref, bf16[256,4096]{1,0:T(8,128)(2,1)S(1)} %collective-permute-done.11.far_ref, bf16[2,4096,256]{2,1,0:T(8,128)(2,1)S(1)} %copy-done.1, bf16[4096,1792]{1,0:T(8,128)(2,1)} %wg_ref.7, ...), custom_call_target="tpu_custom_call" | custom-call | flops 8589934592 | bytes 16777216 | tf_op jit(solution)/shard_map/gate_up/pallas_call | solution.py:200
  65.1 9.5 %gate_up.3 = (f32[768,512]{1,0:T(8,128)S(1)}, f32[768,512]{1,0:T(8,128)S(1)}, bf16[256,4096]{1,0:T(8,128)(2,1)S(1)}) custom-call(bf16[256,4096]{1,0:T(8,128)(2,1)S(1)} %pack.1.near_ref, bf16[256,4096]{1,0:T(8,128)(2,1)S(1)} %collective-permute-done.11.far_ref, bf16[2,4096,256]{2,1,0:T(8,128)(2,1)S(1)} %get-tuple-element.65.head_ref, ...), custom_call_target="tpu_custom_call" | custom-call | flops 6442450944 | bytes 12582912 | tf_op jit(solution)/shard_map/gate_up/pallas_call | solution.py:200
  74.6 30.3 %hidden_back.1 = (bf16[512,1792]{1,0:T(8,128)(2,1)S(1)}, bf16[512,1792]{1,0:T(8,128)(2,1)S(1)}, bf16[256,4096]{1,0:T(8,128)(2,1)S(1)}, bf16[256,4096]{1,0:T(8,128)(2,1)S(1)}) custom-call(s32[8]{0:T(128)S(1)} %fusion.3.refs_8_.spot_ref, bf16[4096,256]{1,0:T(8,128)(2,1)S(1)} %pack_turned.1.rest_0_.near_ref, ...), custom_call_target="tpu_custom_call" | custom-call | flops 22548578304 | bytes 44040192 | tf_op jit(solution)/shard_map/hidden_back/pallas_call | solution.py:317
  105.5 4.6 %fisher.4 = (bf16[4096,1792]{1,0:T(8,128)(2,1)}, bf16[4096,1792]{1,0:T(8,128)(2,1)}, f32[8,128]{1,0:T(8,128)S(1)}) custom-call(bf16[512,4096]{1,0:T(8,128)(2,1)S(1)} %arrange.1.refs_8_.x_ref, bf16[512,1792]{1,0:T(8,128)(2,1)S(1)} %get-tuple-element.69.gg_ref, bf16[512,1792]{1,0:T(8,128)(2,1)S(1)} %get-tuple-element.70.gu_ref), custom_call_target="tpu_custom_call" | custom-call | flops 2818572288 | bytes 5505024 | tf_op jit(solution)/shard_map/fisher/pallas_call | solution.py:414
  110.3 5.0 %collective-permute-start.17 = (bf16[32,4096]{1,0:T(8,128)(2,1)S(1)}, bf16[32,4096]{1,0:T(8,128)(2,1)S(1)}, u32[]{:S(2)}, u32[]{:S(2)}) collective-permute-start(bf16[32,4096]{1,0:T(8,128)(2,1)S(1)} %get-tuple-element.76.rest_2_), channel_id=1, source_target_pairs={{0,4},{1,5},{4,8},{5,9},{8,12},{9,13},{12,14},{13,15},{14,10},{15,... | collective-permute-start | bytes 786440 | tf_op jit(solution)/shard_map/ppermute | solution.py:446
  115.3 2.3 %collective-permute-start.23 = (bf16[32,4096]{1,0:T(8,128)(2,1)S(1)}, bf16[32,4096]{1,0:T(8,128)(2,1)S(1)}, u32[]{:S(2)}, u32[]{:S(2)}) collective-permute-start(bf16[32,4096]{1,0:T(8,128)(2,1)S(1)} %get-tuple-element.78.rest_4_), channel_id=1, source_target_pairs={{0,14},{1,15},{4,10},{5,11},{8,6},{9,7},{12,2},{13,3},{14,0},{15,1... | collective-permute-start | bytes 786440 | tf_op jit(solution)/shard_map/ppermute | solution.py:443
  117.5 7.0 %fisher.5 = (bf16[4096,1792]{1,0:T(8,128)(2,1)}, bf16[4096,1792]{1,0:T(8,128)(2,1)}, f32[8,128]{1,0:T(8,128)S(1)}) custom-call(bf16[512,4096]{1,0:T(8,128)(2,1)S(1)} %arrange.1.refs_8_.x_ref, bf16[512,1792]{1,0:T(8,128)(2,1)S(1)} %get-tuple-element.69.gg_ref, ...), custom_call_target="tpu_custom_call", output_to_operand_aliasing={{0}: (3, {}), {1}: (4, {})} | custom-call | flops 4697620480 | bytes 9175040 | tf_op jit(solution)/shard_map/fisher/pallas_call | solution.py:414
  124.8 7.3 %collective-permute-start.19 = (bf16[32,4096]{1,0:T(8,128)(2,1)S(1)}, bf16[32,4096]{1,0:T(8,128)(2,1)S(1)}, u32[]{:S(2)}, u32[]{:S(2)}) collective-permute-start(bf16[32,4096]{1,0:T(8,128)(2,1)S(1)} %get-tuple-element.82.rest_2_), channel_id=1, source_target_pairs={{0,4},{1,5},{4,8},{5,9},{8,12},{9,13},{12,14},{13,15},{14,10},{15,... | collective-permute-start | bytes 786440 | tf_op jit(solution)/shard_map/ppermute | solution.py:446
  132.1 5.8 %fisher.6 = (bf16[4096,1792]{1,0:T(8,128)(2,1)}, bf16[4096,1792]{1,0:T(8,128)(2,1)}, f32[8,128]{1,0:T(8,128)S(1)}) custom-call(bf16[512,4096]{1,0:T(8,128)(2,1)S(1)} %arrange.1.refs_8_.x_ref, bf16[512,1792]{1,0:T(8,128)(2,1)S(1)} %get-tuple-element.69.gg_ref, ...), custom_call_target="tpu_custom_call", output_to_operand_aliasing={{0}: (3, {}), {1}: (4, {})} | custom-call | flops 3758096384 | bytes 7340032 | tf_op jit(solution)/shard_map/fisher/pallas_call | solution.py:414
  138.6 3.4 %collective-permute-start.21 = (bf16[32,4096]{1,0:T(8,128)(2,1)S(1)}, bf16[32,4096]{1,0:T(8,128)(2,1)S(1)}, u32[]{:S(2)}, u32[]{:S(2)}) collective-permute-start(bf16[32,4096]{1,0:T(8,128)(2,1)S(1)} %get-tuple-element.87.rest_2_), channel_id=1, source_target_pairs={{0,4},{1,5},{4,8},{5,9},{8,12},{9,13},{12,14},{13,15},{14,10},{15,... | collective-permute-start | bytes 786440 | tf_op jit(solution)/shard_map/ppermute | solution.py:446
  142.1 5.8 %fisher.7 = (bf16[4096,1792]{1,0:T(8,128)(2,1)}, bf16[4096,1792]{1,0:T(8,128)(2,1)}, f32[8,128]{1,0:T(8,128)}) custom-call(bf16[512,4096]{1,0:T(8,128)(2,1)S(1)} %arrange.1.refs_8_.x_ref, bf16[512,1792]{1,0:T(8,128)(2,1)S(1)} %get-tuple-element.69.gg_ref, ...), custom_call_target="tpu_custom_call", output_to_operand_aliasing={{0}: (3, {}), {1}: (4, {})} | custom-call | flops 3758096384 | bytes 7340032 | tf_op jit(solution)/shard_map/fisher/pallas_call | solution.py:414
  (56 shorter events, 18.5 us)
Async XLA Ops:
  0.6 14.3 %collective-permute-start = (bf16[32,4096]{1,0:T(8,128)(2,1)}, bf16[32,4096]{1,0:T(8,128)(2,1)S(1)}, u32[]{:S(2)}, u32[]{:S(2)}) collective-permute-start(bf16[32,4096]{1,0:T(8,128)(2,1)} %x_ref.1), channel_id=1, source_target_pairs={{0,4},{1,5},{4,8},{5,9},{8,12},{9,13},{12,14},{13,15},{14,10},{15,... | collective-permute-start | bytes 786440 | tf_op jit(solution)/shard_map/ppermute | solution.py:446
  3.7 11.2 %collective-permute-start.1 = (bf16[32,4096]{1,0:T(8,128)(2,1)}, bf16[32,4096]{1,0:T(8,128)(2,1)S(1)}, u32[]{:S(2)}, u32[]{:S(2)}) collective-permute-start(bf16[32,4096]{1,0:T(8,128)(2,1)} %x_ref.1), channel_id=1, source_target_pairs={{4,0},{5,1},{8,4},{9,5},{12,8},{13,9},{14,12},{15,13},{10,14},{11,... | collective-permute-start | bytes 786440 | tf_op jit(solution)/shard_map/ppermute | solution.py:449
  3.7 15.3 %collective-permute-start.4 = (bf16[32,4096]{1,0:T(8,128)(2,1)}, bf16[32,4096]{1,0:T(8,128)(2,1)S(1)}, u32[]{:S(2)}, u32[]{:S(2)}) collective-permute-start(bf16[32,4096]{1,0:T(8,128)(2,1)} %x_ref.1), channel_id=1, source_target_pairs={{0,14},{1,15},{4,10},{5,11},{8,6},{9,7},{12,2},{13,3},{14,0},{15,1... | collective-permute-start | bytes 786440 | tf_op jit(solution)/shard_map/ppermute | solution.py:443
  19.1 11.8 %collective-permute-start.5 = (bf16[32,4096]{1,0:T(8,128)(2,1)S(1)}, bf16[32,4096]{1,0:T(8,128)(2,1)S(1)}, u32[]{:S(2)}, u32[]{:S(2)}) collective-permute-start(bf16[32,4096]{1,0:T(8,128)(2,1)S(1)} %get-tuple-element.61.refs_0_), channel_id=1, source_target_pairs={{0,4},{1,5},{4,8},{5,9},{8,12},{9,13},{12,14},{13,15},{14,10},{15,... | collective-permute-start | bytes 786440 | tf_op jit(solution)/shard_map/ppermute | solution.py:446
  24.1 9.2 %collective-permute-start.6 = (bf16[32,4096]{1,0:T(8,128)(2,1)S(1)}, bf16[32,4096]{1,0:T(8,128)(2,1)S(1)}, u32[]{:S(2)}, u32[]{:S(2)}) collective-permute-start(bf16[32,4096]{1,0:T(8,128)(2,1)S(1)} %get-tuple-element.61.refs_0_), channel_id=1, source_target_pairs={{4,0},{5,1},{8,4},{9,5},{12,8},{13,9},{14,12},{15,13},{10,14},{11,... | collective-permute-start | bytes 786440 | tf_op jit(solution)/shard_map/ppermute | solution.py:449
  24.1 12.4 %collective-permute-start.2 = (bf16[32,4096]{1,0:T(8,128)(2,1)S(1)}, bf16[32,4096]{1,0:T(8,128)(2,1)S(1)}, u32[]{:S(2)}, u32[]{:S(2)}) collective-permute-start(bf16[32,4096]{1,0:T(8,128)(2,1)S(1)} %collective-permute-done.refs_1_), channel_id=1, source_target_pairs={{0,4},{1,5},{4,8},{5,9},{8,12},{9,13},{12,14},{13,15},{14,10},{15,... | collective-permute-start | bytes 786440 | tf_op jit(solution)/shard_map/ppermute | solution.py:446
  26.2 12.8 %collective-permute-start.3 = (bf16[32,4096]{1,0:T(8,128)(2,1)S(1)}, bf16[32,4096]{1,0:T(8,128)(2,1)S(1)}, u32[]{:S(2)}, u32[]{:S(2)}) collective-permute-start(bf16[32,4096]{1,0:T(8,128)(2,1)S(1)} %collective-permute-done.1.refs_7_), channel_id=1, source_target_pairs={{4,0},{5,1},{8,4},{9,5},{12,8},{13,9},{14,12},{15,13},{10,14},{11,... | collective-permute-start | bytes 786440 | tf_op jit(solution)/shard_map/ppermute | solution.py:449
  33.4 9.1 %collective-permute-start.9 = (bf16[32,4096]{1,0:T(8,128)(2,1)S(1)}, bf16[32,4096]{1,0:T(8,128)(2,1)S(1)}, u32[]{:S(2)}, u32[]{:S(2)}) collective-permute-start(bf16[32,4096]{1,0:T(8,128)(2,1)S(1)} %collective-permute-done.5.refs_1_), channel_id=1, source_target_pairs={{0,4},{1,5},{4,8},{5,9},{8,12},{9,13},{12,14},{13,15},{14,10},{15,... | collective-permute-start | bytes 786440 | tf_op jit(solution)/shard_map/ppermute | solution.py:446
  35.1 9.5 %collective-permute-start.10 = (bf16[32,4096]{1,0:T(8,128)(2,1)S(1)}, bf16[32,4096]{1,0:T(8,128)(2,1)S(1)}, u32[]{:S(2)}, u32[]{:S(2)}) collective-permute-start(bf16[32,4096]{1,0:T(8,128)(2,1)S(1)} %collective-permute-done.6.refs_7_), channel_id=1, source_target_pairs={{4,0},{5,1},{8,4},{9,5},{12,8},{13,9},{14,12},{15,13},{10,14},{11,... | collective-permute-start | bytes 786440 | tf_op jit(solution)/shard_map/ppermute | solution.py:449
  39.0 6.7 %collective-permute-start.7 = (bf16[32,4096]{1,0:T(8,128)(2,1)S(1)}, bf16[32,4096]{1,0:T(8,128)(2,1)S(1)}, u32[]{:S(2)}, u32[]{:S(2)}) collective-permute-start(bf16[32,4096]{1,0:T(8,128)(2,1)S(1)} %collective-permute-done.2.refs_2_), channel_id=1, source_target_pairs={{0,4},{1,5},{4,8},{5,9},{8,12},{9,13},{12,14},{13,15},{14,10},{15,... | collective-permute-start | bytes 786440 | tf_op jit(solution)/shard_map/ppermute | solution.py:446
  40.7 7.1 %collective-permute-start.8 = (bf16[32,4096]{1,0:T(8,128)(2,1)S(1)}, bf16[32,4096]{1,0:T(8,128)(2,1)S(1)}, u32[]{:S(2)}, u32[]{:S(2)}) collective-permute-start(bf16[32,4096]{1,0:T(8,128)(2,1)S(1)} %collective-permute-done.3.refs_6_), channel_id=1, source_target_pairs={{4,0},{5,1},{8,4},{9,5},{12,8},{13,9},{14,12},{15,13},{10,14},{11,... | collective-permute-start | bytes 786440 | tf_op jit(solution)/shard_map/ppermute | solution.py:449
  48.0 4.6 %collective-permute-start.11 = (bf16[256,4096]{1,0:T(8,128)(2,1)S(1)}, bf16[256,4096]{1,0:T(8,128)(2,1)S(1)}, u32[]{:S(2)}, u32[]{:S(2)}) collective-permute-start(bf16[256,4096]{1,0:T(8,128)(2,1)S(1)} %pack.1.near_ref), channel_id=1, source_target_pairs={{0,1},{1,0},{2,3},{3,2},{4,5},{5,4},{6,7},{7,6},{8,9},{9,8},{10,11... | collective-permute-start | bytes 6291464 | tf_op jit(solution)/shard_map/ppermute | solution.py:452
  48.1 15.9 %collective-permute-start.12 = (bf16[32,4096]{1,0:T(8,128)(2,1)S(1)}, bf16[32,4096]{1,0:T(8,128)(2,1)S(1)}, u32[]{:S(2)}, u32[]{:S(2)}) collective-permute-start(bf16[32,4096]{1,0:T(8,128)(2,1)S(1)} %collective-permute-done.9.refs_9_.rest_0_.refs_2_), channel_id=1, source_target_pairs={{0,4},{1,5},{4,8},{5,9},{8,12},{9,13},{12,14},{13,15},{14,10},{15,... | collective-permute-start | bytes 786440 | tf_op jit(solution)/shard_map/ppermute | solution.py:446
  49.6 14.4 %collective-permute-start.14 = (bf16[32,4096]{1,0:T(8,128)(2,1)S(1)}, bf16[32,4096]{1,0:T(8,128)(2,1)S(1)}, u32[]{:S(2)}, u32[]{:S(2)}) collective-permute-start(bf16[32,4096]{1,0:T(8,128)(2,1)S(1)} %collective-permute-done.10.refs_10_.rest_1_.refs_6_), channel_id=1, source_target_pairs={{4,0},{5,1},{8,4},{9,5},{12,8},{13,9},{14,12},{15,13},{10,14},{11,... | collective-permute-start | bytes 786440 | tf_op jit(solution)/shard_map/ppermute | solution.py:449
  50.2 14.2 %collective-permute-start.13 = (bf16[32,4096]{1,0:T(8,128)(2,1)S(1)}, bf16[32,4096]{1,0:T(8,128)(2,1)S(1)}, u32[]{:S(2)}, u32[]{:S(2)}) collective-permute-start(bf16[32,4096]{1,0:T(8,128)(2,1)S(1)} %get-tuple-element.61.refs_0_), channel_id=1, source_target_pairs={{0,14},{1,15},{4,10},{5,11},{8,6},{9,7},{12,2},{13,3},{14,0},{15,1... | collective-permute-start | bytes 786440 | tf_op jit(solution)/shard_map/ppermute | solution.py:443
  65.0 9.6 %collective-permute-start.15 = (bf16[4096,256]{1,0:T(8,128)(2,1)S(1)}, bf16[4096,256]{1,0:T(8,128)(2,1)S(1)}, u32[]{:S(2)}, u32[]{:S(2)}) collective-permute-start(bf16[4096,256]{1,0:T(8,128)(2,1)S(1)} %pack_turned.1.rest_0_.near_ref), channel_id=1, source_target_pairs={{0,1},{1,0},{2,3},{3,2},{4,5},{5,4},{6,7},{7,6},{8,9},{9,8},{10,11... | collective-permute-start | bytes 6291464 | tf_op jit(solution)/shard_map/ppermute | solution.py:452
  105.0 5.2 %collective-permute-start.16 = (bf16[256,4096]{1,0:T(8,128)(2,1)S(1)}, bf16[256,4096]{1,0:T(8,128)(2,1)S(1)}, u32[]{:S(2)}, u32[]{:S(2)}) collective-permute-start(bf16[256,4096]{1,0:T(8,128)(2,1)S(1)} %get-tuple-element.74), channel_id=1, source_target_pairs={{0,1},{1,0},{2,3},{3,2},{4,5},{5,4},{6,7},{7,6},{8,9},{9,8},{10,11... | collective-permute-start | bytes 6291464 | tf_op jit(solution)/shard_map/ppermute | solution.py:452
  110.3 14.3 %collective-permute-start.17 = (bf16[32,4096]{1,0:T(8,128)(2,1)S(1)}, bf16[32,4096]{1,0:T(8,128)(2,1)S(1)}, u32[]{:S(2)}, u32[]{:S(2)}) collective-permute-start(bf16[32,4096]{1,0:T(8,128)(2,1)S(1)} %get-tuple-element.76.rest_2_), channel_id=1, source_target_pairs={{0,4},{1,5},{4,8},{5,9},{8,12},{9,13},{12,14},{13,15},{14,10},{15,... | collective-permute-start | bytes 786440 | tf_op jit(solution)/shard_map/ppermute | solution.py:446
  115.2 9.3 %collective-permute-start.18 = (bf16[32,4096]{1,0:T(8,128)(2,1)S(1)}, bf16[32,4096]{1,0:T(8,128)(2,1)S(1)}, u32[]{:S(2)}, u32[]{:S(2)}) collective-permute-start(bf16[32,4096]{1,0:T(8,128)(2,1)S(1)} %get-tuple-element.77.rest_3_), channel_id=1, source_target_pairs={{4,0},{5,1},{8,4},{9,5},{12,8},{13,9},{14,12},{15,13},{10,14},{11,... | collective-permute-start | bytes 786440 | tf_op jit(solution)/shard_map/ppermute | solution.py:449
  115.3 32.6 %collective-permute-start.23 = (bf16[32,4096]{1,0:T(8,128)(2,1)S(1)}, bf16[32,4096]{1,0:T(8,128)(2,1)S(1)}, u32[]{:S(2)}, u32[]{:S(2)}) collective-permute-start(bf16[32,4096]{1,0:T(8,128)(2,1)S(1)} %get-tuple-element.78.rest_4_), channel_id=1, source_target_pairs={{0,14},{1,15},{4,10},{5,11},{8,6},{9,7},{12,2},{13,3},{14,0},{15,1... | collective-permute-start | bytes 786440 | tf_op jit(solution)/shard_map/ppermute | solution.py:443
  124.8 13.1 %collective-permute-start.19 = (bf16[32,4096]{1,0:T(8,128)(2,1)S(1)}, bf16[32,4096]{1,0:T(8,128)(2,1)S(1)}, u32[]{:S(2)}, u32[]{:S(2)}) collective-permute-start(bf16[32,4096]{1,0:T(8,128)(2,1)S(1)} %get-tuple-element.82.rest_2_), channel_id=1, source_target_pairs={{0,4},{1,5},{4,8},{5,9},{8,12},{9,13},{12,14},{13,15},{14,10},{15,... | collective-permute-start | bytes 786440 | tf_op jit(solution)/shard_map/ppermute | solution.py:446
  132.1 6.4 %collective-permute-start.20 = (bf16[32,4096]{1,0:T(8,128)(2,1)S(1)}, bf16[32,4096]{1,0:T(8,128)(2,1)S(1)}, u32[]{:S(2)}, u32[]{:S(2)}) collective-permute-start(bf16[32,4096]{1,0:T(8,128)(2,1)S(1)} %get-tuple-element.83.rest_3_), channel_id=1, source_target_pairs={{4,0},{5,1},{8,4},{9,5},{12,8},{13,9},{14,12},{15,13},{10,14},{11,... | collective-permute-start | bytes 786440 | tf_op jit(solution)/shard_map/ppermute | solution.py:449
  138.6 9.2 %collective-permute-start.21 = (bf16[32,4096]{1,0:T(8,128)(2,1)S(1)}, bf16[32,4096]{1,0:T(8,128)(2,1)S(1)}, u32[]{:S(2)}, u32[]{:S(2)}) collective-permute-start(bf16[32,4096]{1,0:T(8,128)(2,1)S(1)} %get-tuple-element.87.rest_2_), channel_id=1, source_target_pairs={{0,4},{1,5},{4,8},{5,9},{8,12},{9,13},{12,14},{13,15},{14,10},{15,... | collective-permute-start | bytes 786440 | tf_op jit(solution)/shard_map/ppermute | solution.py:446
  142.1 6.8 %collective-permute-start.22 = (bf16[32,4096]{1,0:T(8,128)(2,1)S(1)}, bf16[32,4096]{1,0:T(8,128)(2,1)S(1)}, u32[]{:S(2)}, u32[]{:S(2)}) collective-permute-start(bf16[32,4096]{1,0:T(8,128)(2,1)S(1)} %get-tuple-element.88.rest_3_), channel_id=1, source_target_pairs={{4,0},{5,1},{8,4},{9,5},{12,8},{13,9},{14,12},{15,13},{10,14},{11,... | collective-permute-start | bytes 786440 | tf_op jit(solution)/shard_map/ppermute | solution.py:449
  (6 other events, 70.8 us)

commit v10 on v8

--- a/solution.py
+++ b/solution.py
@@ -69,6 +69,22 @@
         cost_estimate=cost(0, 4 * wg.shape[0] * step),
         name="bring",
     )(x, dy, wg, wu)
+
+
+def relay_kernel(in_ref, *rest):
+    rest[-1][...] = in_ref[...]
+
+
+def relay(value, after):
+    return pl.pallas_call(
+        relay_kernel,
+        in_specs=held_specs(1) + any_specs(after),
+        out_specs=pl.BlockSpec(memory_space=pltpu.VMEM),
+        out_shape=jax.ShapeDtypeStruct(value.shape, value.dtype),
+        compiler_params=params(4),
+        cost_estimate=cost(0, 4 * value.size),
+        name="relay",
+    )(value, *after)
 
 
 def pack_kernel(count, *refs):
@@ -482,8 +498,8 @@
     for _ in range(3, far):
         in_x.append(both(*in_x[-1]))
         in_dy.append(both(*in_dy[-1]))
-    in_x.append(both(*in_x[-1], in_dy[-1], True))
-    near_x = pack(blocks(own_x, in_x), (spot,))
+    in_x.append(both(*in_x[-1], in_dy[0], True))
+    near_x = pack(blocks(own_x, in_x), (spot, *in_dy[-1]))
     far_x = swap(near_x)
 
     in_dy.append(both(*in_dy[-1], in_x[-2]))

time: 138 us -> 139 us (level)
  local copies, waits for them, and re-layouts: 5.21 us -> 9.06 us
  waiting for transfers between devices: 26.6 us -> 23.6 us
    unnamed x20, local copies, waits for them, and re-layouts: 3.95 us -> 7.8 us
    ppermute x12, waiting for transfers between devices: 13.8 us -> 12 us  [left(): return lax.ppermute(value, 'hid', to_left)]
  transfers between devices with their start and end apart: 27 -> 27, of which waited for: 17 -> 16; matrix products, arithmetic and copies ran while one was open for 1% -> 1% of each run, Pallas kernels for 34% -> 34%
where the time goes in v10:
time: 139 us; the launch traced here: 138 us
  Pallas kernels  77.7 us (56%)
  starting transfers between devices  26.4 us (19%)
  waiting for transfers between devices  23.6 us (17%)
  local copies, waits for them, and re-layouts  9.06 us (7%)
    pallas_call x1, Pallas kernels, back(): pl.pallas_call(functools.partial(back_kernel, step, 512, len(a)), in_spec...  28.8 us
    pallas_call x5, Pallas kernels, fisher(): pl.pallas_call(functools.partial(fisher_kernel, tile(width, 256)), grid=(...  24.2 us
    ppermute x12, starting transfers between devices, right(): return lax.ppermute(value, 'hid', to_right)  20.1 us
    pallas_call x3, Pallas kernels, gate_up(): pl.pallas_call(functools.partial(gate_up_kernel, first, step), in_specs=h...  19.5 us
    ppermute x12, waiting for transfers between devices, left(): return lax.ppermute(value, 'hid', to_left)  12 us
    ppermute x12, waiting for transfers between devices, right(): return lax.ppermute(value, 'hid', to_right)  9.49 us
    unnamed x20, local copies, waits for them, and re-layouts  7.8 us
    ppermute x12, starting transfers between devices, left(): return lax.ppermute(value, 'hid', to_left)  5.65 us
  transfers between devices with their start and end apart: 27, of which 16 were waited for; matrix products, arithmetic and copies ran while one was open for 1% of the time, Pallas kernels for 34%

profile of v10, /device:TPU:0, one launch (start us, length us, event | category | flops | bytes accessed | tf_op | source)
XLA Modules:
  0.0 138.3 jit_solution(8014817152109801681)
XLA Ops:
  0.6 3.1 %collective-permute-start = (bf16[32,4096]{1,0:T(8,128)(2,1)}, bf16[32,4096]{1,0:T(8,128)(2,1)S(1)}, u32[]{:S(2)}, u32[]{:S(2)}) collective-permute-start(bf16[32,4096]{1,0:T(8,128)(2,1)} %x_ref.1), channel_id=1, source_target_pairs={{0,4},{1,5},{4,8},{5,9},{8,12},{9,13},{12,14},{13,15},{14,10},{15,... | collective-permute-start | bytes 786440 | tf_op jit(solution)/shard_map/ppermute | solution.py:458
  5.6 2.3 %bring.1 = (bf16[32,4096]{1,0:T(8,128)(2,1)S(1)}, bf16[32,4096]{1,0:T(8,128)(2,1)S(1)}, bf16[2,4096,256]{2,1,0:T(8,128)(2,1)S(1)}) custom-call(bf16[32,4096]{1,0:T(8,128)(2,1)S(1)} %copy-done.3, bf16[32,4096]{1,0:T(8,128)(2,1)S(1)} %copy-done.2, bf16[4096,1792]{1,0:T(8,128)(2,1)} %wg_ref.9, bf16[4096,1792]{1,0:T(8,128)(2,1)} %wu_ref.9), custom_call_target="tpu_custom_call" | custom-call | bytes 4194304 | tf_op jit(solution)/shard_map/bring/pallas_call | solution.py:61
  7.9 2.0 %copy-done = bf16[2,4096,256]{2,1,0:T(8,128)(2,1)} copy-done((bf16[2,4096,256]{2,1,0:T(8,128)(2,1)}, bf16[2,4096,256]{2,1,0:T(8,128)(2,1)S(1)}, u32[]{:S(2)}) %copy-start) | copy-done | bytes 4194328
  11.7 1.6 %collective-permute-start.2 = (bf16[32,4096]{1,0:T(8,128)(2,1)S(1)}, bf16[32,4096]{1,0:T(8,128)(2,1)S(1)}, u32[]{:S(2)}, u32[]{:S(2)}) collective-permute-start(bf16[32,4096]{1,0:T(8,128)(2,1)S(1)} %collective-permute-done.refs_1_), channel_id=1, source_target_pairs={{0,4},{1,5},{4,8},{5,9},{8,12},{9,13},{12,14},{13,15},{14,10},{15,... | collective-permute-start | bytes 786440 | tf_op jit(solution)/shard_map/ppermute | solution.py:458
  13.7 1.6 %collective-permute-start.6 = (bf16[32,4096]{1,0:T(8,128)(2,1)S(1)}, bf16[32,4096]{1,0:T(8,128)(2,1)S(1)}, u32[]{:S(2)}, u32[]{:S(2)}) collective-permute-start(bf16[32,4096]{1,0:T(8,128)(2,1)S(1)} %get-tuple-element.67.refs_0_), channel_id=1, source_target_pairs={{0,4},{1,5},{4,8},{5,9},{8,12},{9,13},{12,14},{13,15},{14,10},{15,... | collective-permute-start | bytes 786440 | tf_op jit(solution)/shard_map/ppermute | solution.py:458
  15.7 5.2 %collective-permute-done.2.refs_2_ = bf16[32,4096]{1,0:T(8,128)(2,1)S(1)} collective-permute-done((bf16[32,4096]{1,0:T(8,128)(2,1)S(1)}, bf16[32,4096]{1,0:T(8,128)(2,1)S(1)}, u32[]{:S(2)}, u32[]{:S(2)}) %collective-permute-start.2) | collective-permute-done | bytes 262176 | tf_op jit(solution)/shard_map/ppermute | solution.py:458
  20.9 1.6 %collective-permute-done.3.refs_7_ = bf16[32,4096]{1,0:T(8,128)(2,1)S(1)} collective-permute-done((bf16[32,4096]{1,0:T(8,128)(2,1)S(1)}, bf16[32,4096]{1,0:T(8,128)(2,1)S(1)}, u32[]{:S(2)}, u32[]{:S(2)}) %collective-permute-start.3) | collective-permute-done | bytes 262176 | tf_op jit(solution)/shard_map/ppermute | solution.py:461
  22.5 1.6 %collective-permute-start.4 = (bf16[32,4096]{1,0:T(8,128)(2,1)S(1)}, bf16[32,4096]{1,0:T(8,128)(2,1)S(1)}, u32[]{:S(2)}, u32[]{:S(2)}) collective-permute-start(bf16[32,4096]{1,0:T(8,128)(2,1)S(1)} %collective-permute-done.2.refs_2_), channel_id=1, source_target_pairs={{0,4},{1,5},{4,8},{5,9},{8,12},{9,13},{12,14},{13,15},{14,10},{15,... | collective-permute-start | bytes 786440 | tf_op jit(solution)/shard_map/ppermute | solution.py:458
  26.6 1.6 %collective-permute-done.7.refs_8_ = bf16[32,4096]{1,0:T(8,128)(2,1)S(1)} collective-permute-done((bf16[32,4096]{1,0:T(8,128)(2,1)S(1)}, bf16[32,4096]{1,0:T(8,128)(2,1)S(1)}, u32[]{:S(2)}, u32[]{:S(2)}) %collective-permute-start.7) | collective-permute-done | bytes 262176 | tf_op jit(solution)/shard_map/ppermute | solution.py:461
  28.1 1.6 %collective-permute-start.10 = (bf16[32,4096]{1,0:T(8,128)(2,1)S(1)}, bf16[32,4096]{1,0:T(8,128)(2,1)S(1)}, u32[]{:S(2)}, u32[]{:S(2)}) collective-permute-start(bf16[32,4096]{1,0:T(8,128)(2,1)S(1)} %collective-permute-done.6.refs_1_), channel_id=1, source_target_pairs={{0,4},{1,5},{4,8},{5,9},{8,12},{9,13},{12,14},{13,15},{14,10},{15,... | collective-permute-start | bytes 786440 | tf_op jit(solution)/shard_map/ppermute | solution.py:458
  34.3 1.6 %collective-permute-start.8 = (bf16[16,4096]{1,0:T(8,128)(2,1)S(1)}, bf16[16,4096]{1,0:T(8,128)(2,1)S(1)}, u32[]{:S(2)}, u32[]{:S(2)}) collective-permute-start(bf16[16,4096]{1,0:T(8,128)(2,1)S(1)} %slice.12), channel_id=1, source_target_pairs={{0,4},{1,5},{4,8},{5,9},{8,12},{9,13},{12,14},{13,15},{14,10},{15,... | collective-permute-start | bytes 393224 | tf_op jit(solution)/shard_map/ppermute | solution.py:458
  39.7 1.6 %collective-permute-start.13 = (bf16[32,4096]{1,0:T(8,128)(2,1)S(1)}, bf16[32,4096]{1,0:T(8,128)(2,1)S(1)}, u32[]{:S(2)}, u32[]{:S(2)}) collective-permute-start(bf16[32,4096]{1,0:T(8,128)(2,1)S(1)} %collective-permute-done.10.refs_10_.rest_0_.refs_2_), channel_id=1, source_target_pairs={{0,4},{1,5},{4,8},{5,9},{8,12},{9,13},{12,14},{13,15},{14,10},{15,... | collective-permute-start | bytes 786440 | tf_op jit(solution)/shard_map/ppermute | solution.py:458
  41.8 2.1 %collective-permute-done.12.far_ref = bf16[256,4096]{1,0:T(8,128)(2,1)S(1)} collective-permute-done((bf16[256,4096]{1,0:T(8,128)(2,1)S(1)}, bf16[256,4096]{1,0:T(8,128)(2,1)S(1)}, u32[]{:S(2)}, u32[]{:S(2)}) %collective-permute-start.12) | collective-permute-done | bytes 2097184 | tf_op jit(solution)/shard_map/ppermute | solution.py:464
  43.9 6.3 %gate_up.3 = (f32[512,512]{1,0:T(8,128)S(1)}, f32[512,512]{1,0:T(8,128)S(1)}, bf16[2,4096,256]{2,1,0:T(8,128)(2,1)S(1)}) custom-call(bf16[256,4096]{1,0:T(8,128)(2,1)S(1)} %pack.1.near_ref, bf16[256,4096]{1,0:T(8,128)(2,1)S(1)} %collective-permute-done.12.far_ref, bf16[2,4096,256]{2,1,0:T(8,128)(2,1)S(1)} %copy-done.1, bf16[4096,1792]{1,0:T(8,128)(2,1)} %wg_ref.9, ...), custom_call_target="tpu_custom_call" | custom-call | flops 4294967296 | bytes 8388608 | tf_op jit(solution)/shard_map/gate_up/pallas_call | solution.py:216
  53.3 7.9 %gate_up.4 = (f32[768,512]{1,0:T(8,128)S(1)}, f32[768,512]{1,0:T(8,128)S(1)}, bf16[2,4096,256]{2,1,0:T(8,128)(2,1)S(1)}) custom-call(bf16[256,4096]{1,0:T(8,128)(2,1)S(1)} %pack.1.near_ref, bf16[256,4096]{1,0:T(8,128)(2,1)S(1)} %collective-permute-done.12.far_ref, bf16[2,4096,256]{2,1,0:T(8,128)(2,1)S(1)} %get-tuple-element.78.head_ref, ...), custom_call_target="tpu_custom_call" | custom-call | flops 6442450944 | bytes 12582912 | tf_op jit(solution)/shard_map/gate_up/pallas_call | solution.py:216
  62.8 5.2 %gate_up.5 = (f32[512,512]{1,0:T(8,128)S(1)}, f32[512,512]{1,0:T(8,128)S(1)}, bf16[256,4096]{1,0:T(8,128)(2,1)S(1)}) custom-call(bf16[256,4096]{1,0:T(8,128)(2,1)S(1)} %pack.1.near_ref, bf16[256,4096]{1,0:T(8,128)(2,1)S(1)} %collective-permute-done.12.far_ref, bf16[2,4096,256]{2,1,0:T(8,128)(2,1)S(1)} %get-tuple-element.81.head_ref, ...), custom_call_target="tpu_custom_call" | custom-call | flops 4294967296 | bytes 8388608 | tf_op jit(solution)/shard_map/gate_up/pallas_call | solution.py:216
  69.3 1.6 %copy-done.5 = bf16[256,4096]{1,0:T(8,128)(2,1)S(1)} copy-done((bf16[256,4096]{1,0:T(8,128)(2,1)S(1)}, bf16[256,4096]{1,0:T(8,128)(2,1)}, u32[]{:S(2)}) %copy-start.5) | copy-done | bytes 2097176
  70.9 28.8 %hidden_back.1 = (bf16[512,1792]{1,0:T(8,128)(2,1)S(1)}, bf16[512,1792]{1,0:T(8,128)(2,1)S(1)}, bf16[256,4096]{1,0:T(8,128)(2,1)S(1)}, bf16[256,4096]{1,0:T(8,128)(2,1)S(1)}) custom-call(s32[8]{0:T(128)S(1)} %fusion.3.refs_9_.spot_ref, bf16[4096,256]{1,0:T(8,128)(2,1)S(1)} %pack_turned.1.rest_0_.near_ref, ...), custom_call_target="tpu_custom_call" | custom-call | flops 22548578304 | bytes 44040192 | tf_op jit(solution)/shard_map/hidden_back/pallas_call | solution.py:333
  100.3 5.8 %fisher.5 = (bf16[4096,1792]{1,0:T(8,128)(2,1)}, bf16[4096,1792]{1,0:T(8,128)(2,1)}, f32[8,128]{1,0:T(8,128)S(1)}) custom-call(bf16[512,4096]{1,0:T(8,128)(2,1)S(1)} %arrange.1.refs_9_.x_ref, bf16[512,1792]{1,0:T(8,128)(2,1)S(1)} %get-tuple-element.85.gg_ref, bf16[512,1792]{1,0:T(8,128)(2,1)S(1)} %get-tuple-element.86.gu_ref), custom_call_target="tpu_custom_call" | custom-call | flops 3758096384 | bytes 7340032 | tf_op jit(solution)/shard_map/fisher/pallas_call | solution.py:431
  106.1 1.6 %collective-permute-start.19 = (bf16[16,4096]{1,0:T(8,128)(2,1)S(1)}, bf16[16,4096]{1,0:T(8,128)(2,1)S(1)}, u32[]{:S(2)}, u32[]{:S(2)}) collective-permute-start(bf16[16,4096]{1,0:T(8,128)(2,1)S(1)} %get-tuple-element.92.rest_2_), channel_id=1, source_target_pairs={{0,4},{1,5},{4,8},{5,9},{8,12},{9,13},{12,14},{13,15},{14,10},{15,... | collective-permute-start | bytes 393224 | tf_op jit(solution)/shard_map/ppermute | solution.py:458
  108.2 3.4 %fisher.6 = (bf16[4096,1792]{1,0:T(8,128)(2,1)}, bf16[4096,1792]{1,0:T(8,128)(2,1)}, f32[8,128]{1,0:T(8,128)S(1)}) custom-call(bf16[512,4096]{1,0:T(8,128)(2,1)S(1)} %arrange.1.refs_9_.x_ref, bf16[512,1792]{1,0:T(8,128)(2,1)S(1)} %get-tuple-element.85.gg_ref, ...), custom_call_target="tpu_custom_call", output_to_operand_aliasing={{0}: (3, {}), {1}: (4, {})} | custom-call | flops 1879048192 | bytes 3670016 | tf_op jit(solution)/shard_map/fisher/pallas_call | solution.py:431
  115.2 5.8 %fisher.7 = (bf16[4096,1792]{1,0:T(8,128)(2,1)}, bf16[4096,1792]{1,0:T(8,128)(2,1)}, f32[8,128]{1,0:T(8,128)S(1)}) custom-call(bf16[512,4096]{1,0:T(8,128)(2,1)S(1)} %arrange.1.refs_9_.x_ref, bf16[512,1792]{1,0:T(8,128)(2,1)S(1)} %get-tuple-element.85.gg_ref, ...), custom_call_target="tpu_custom_call", output_to_operand_aliasing={{0}: (3, {}), {1}: (4, {})} | custom-call | flops 3758096384 | bytes 7340032 | tf_op jit(solution)/shard_map/fisher/pallas_call | solution.py:431
  123.7 5.8 %fisher.8 = (bf16[4096,1792]{1,0:T(8,128)(2,1)}, bf16[4096,1792]{1,0:T(8,128)(2,1)}, f32[8,128]{1,0:T(8,128)S(1)}) custom-call(bf16[512,4096]{1,0:T(8,128)(2,1)S(1)} %arrange.1.refs_9_.x_ref, bf16[512,1792]{1,0:T(8,128)(2,1)S(1)} %get-tuple-element.85.gg_ref, ...), custom_call_target="tpu_custom_call", output_to_operand_aliasing={{0}: (3, {}), {1}: (4, {})} | custom-call | flops 3758096384 | bytes 7340032 | tf_op jit(solution)/shard_map/fisher/pallas_call | solution.py:431
  131.8 3.4 %fisher.9 = (bf16[4096,1792]{1,0:T(8,128)(2,1)}, bf16[4096,1792]{1,0:T(8,128)(2,1)}, f32[8,128]{1,0:T(8,128)}) custom-call(bf16[512,4096]{1,0:T(8,128)(2,1)S(1)} %arrange.1.refs_9_.x_ref, bf16[512,1792]{1,0:T(8,128)(2,1)S(1)} %get-tuple-element.85.gg_ref, ...), custom_call_target="tpu_custom_call", output_to_operand_aliasing={{0}: (3, {}), {1}: (4, {})} | custom-call | flops 1879048192 | bytes 3670016 | tf_op jit(solution)/shard_map/fisher/pallas_call | solution.py:431
  (77 shorter events, 34.5 us)
Async XLA Ops:
  0.6 9.5 %collective-permute-start = (bf16[32,4096]{1,0:T(8,128)(2,1)}, bf16[32,4096]{1,0:T(8,128)(2,1)S(1)}, u32[]{:S(2)}, u32[]{:S(2)}) collective-permute-start(bf16[32,4096]{1,0:T(8,128)(2,1)} %x_ref.1), channel_id=1, source_target_pairs={{0,4},{1,5},{4,8},{5,9},{8,12},{9,13},{12,14},{13,15},{14,10},{15,... | collective-permute-start | bytes 786440 | tf_op jit(solution)/shard_map/ppermute | solution.py:458
  3.7 8.0 %collective-permute-start.1 = (bf16[32,4096]{1,0:T(8,128)(2,1)}, bf16[32,4096]{1,0:T(8,128)(2,1)S(1)}, u32[]{:S(2)}, u32[]{:S(2)}) collective-permute-start(bf16[32,4096]{1,0:T(8,128)(2,1)} %x_ref.1), channel_id=1, source_target_pairs={{4,0},{5,1},{8,4},{9,5},{12,8},{13,9},{14,12},{15,13},{10,14},{11,... | collective-permute-start | bytes 786440 | tf_op jit(solution)/shard_map/ppermute | solution.py:461
  11.7 9.2 %collective-permute-start.2 = (bf16[32,4096]{1,0:T(8,128)(2,1)S(1)}, bf16[32,4096]{1,0:T(8,128)(2,1)S(1)}, u32[]{:S(2)}, u32[]{:S(2)}) collective-permute-start(bf16[32,4096]{1,0:T(8,128)(2,1)S(1)} %collective-permute-done.refs_1_), channel_id=1, source_target_pairs={{0,4},{1,5},{4,8},{5,9},{8,12},{9,13},{12,14},{13,15},{14,10},{15,... | collective-permute-start | bytes 786440 | tf_op jit(solution)/shard_map/ppermute | solution.py:458
  13.3 9.2 %collective-permute-start.3 = (bf16[32,4096]{1,0:T(8,128)(2,1)S(1)}, bf16[32,4096]{1,0:T(8,128)(2,1)S(1)}, u32[]{:S(2)}, u32[]{:S(2)}) collective-permute-start(bf16[32,4096]{1,0:T(8,128)(2,1)S(1)} %collective-permute-done.1.refs_8_), channel_id=1, source_target_pairs={{4,0},{5,1},{8,4},{9,5},{12,8},{13,9},{14,12},{15,13},{10,14},{11,... | collective-permute-start | bytes 786440 | tf_op jit(solution)/shard_map/ppermute | solution.py:461
  13.7 12.8 %collective-permute-start.6 = (bf16[32,4096]{1,0:T(8,128)(2,1)S(1)}, bf16[32,4096]{1,0:T(8,128)(2,1)S(1)}, u32[]{:S(2)}, u32[]{:S(2)}) collective-permute-start(bf16[32,4096]{1,0:T(8,128)(2,1)S(1)} %get-tuple-element.67.refs_0_), channel_id=1, source_target_pairs={{0,4},{1,5},{4,8},{5,9},{8,12},{9,13},{12,14},{13,15},{14,10},{15,... | collective-permute-start | bytes 786440 | tf_op jit(solution)/shard_map/ppermute | solution.py:458
  15.3 12.8 %collective-permute-start.7 = (bf16[32,4096]{1,0:T(8,128)(2,1)S(1)}, bf16[32,4096]{1,0:T(8,128)(2,1)S(1)}, u32[]{:S(2)}, u32[]{:S(2)}) collective-permute-start(bf16[32,4096]{1,0:T(8,128)(2,1)S(1)} %get-tuple-element.67.refs_0_), channel_id=1, source_target_pairs={{4,0},{5,1},{8,4},{9,5},{12,8},{13,9},{14,12},{15,13},{10,14},{11,... | collective-permute-start | bytes 786440 | tf_op jit(solution)/shard_map/ppermute | solution.py:461
  22.5 9.7 %collective-permute-start.4 = (bf16[32,4096]{1,0:T(8,128)(2,1)S(1)}, bf16[32,4096]{1,0:T(8,128)(2,1)S(1)}, u32[]{:S(2)}, u32[]{:S(2)}) collective-permute-start(bf16[32,4096]{1,0:T(8,128)(2,1)S(1)} %collective-permute-done.2.refs_2_), channel_id=1, source_target_pairs={{0,4},{1,5},{4,8},{5,9},{8,12},{9,13},{12,14},{13,15},{14,10},{15,... | collective-permute-start | bytes 786440 | tf_op jit(solution)/shard_map/ppermute | solution.py:458
  24.1 9.7 %collective-permute-start.5 = (bf16[32,4096]{1,0:T(8,128)(2,1)S(1)}, bf16[32,4096]{1,0:T(8,128)(2,1)S(1)}, u32[]{:S(2)}, u32[]{:S(2)}) collective-permute-start(bf16[32,4096]{1,0:T(8,128)(2,1)S(1)} %collective-permute-done.3.refs_7_), channel_id=1, source_target_pairs={{4,0},{5,1},{8,4},{9,5},{12,8},{13,9},{14,12},{15,13},{10,14},{11,... | collective-permute-start | bytes 786440 | tf_op jit(solution)/shard_map/ppermute | solution.py:461
  28.1 8.7 %collective-permute-start.10 = (bf16[32,4096]{1,0:T(8,128)(2,1)S(1)}, bf16[32,4096]{1,0:T(8,128)(2,1)S(1)}, u32[]{:S(2)}, u32[]{:S(2)}) collective-permute-start(bf16[32,4096]{1,0:T(8,128)(2,1)S(1)} %collective-permute-done.6.refs_1_), channel_id=1, source_target_pairs={{0,4},{1,5},{4,8},{5,9},{8,12},{9,13},{12,14},{13,15},{14,10},{15,... | collective-permute-start | bytes 786440 | tf_op jit(solution)/shard_map/ppermute | solution.py:458
  29.7 8.4 %collective-permute-start.11 = (bf16[32,4096]{1,0:T(8,128)(2,1)S(1)}, bf16[32,4096]{1,0:T(8,128)(2,1)S(1)}, u32[]{:S(2)}, u32[]{:S(2)}) collective-permute-start(bf16[32,4096]{1,0:T(8,128)(2,1)S(1)} %collective-permute-done.7.refs_8_), channel_id=1, source_target_pairs={{4,0},{5,1},{8,4},{9,5},{12,8},{13,9},{14,12},{15,13},{10,14},{11,... | collective-permute-start | bytes 786440 | tf_op jit(solution)/shard_map/ppermute | solution.py:461
  33.8 5.7 %collective-permute-start.9 = (bf16[16,4096]{1,0:T(8,128)(2,1)S(1)}, bf16[16,4096]{1,0:T(8,128)(2,1)S(1)}, u32[]{:S(2)}, u32[]{:S(2)}) collective-permute-start(bf16[16,4096]{1,0:T(8,128)(2,1)S(1)} %slice.13), channel_id=1, source_target_pairs={{4,0},{5,1},{8,4},{9,5},{12,8},{13,9},{14,12},{15,13},{10,14},{11,... | collective-permute-start | bytes 393224 | tf_op jit(solution)/shard_map/ppermute | solution.py:461
  39.7 11.5 %collective-permute-start.13 = (bf16[32,4096]{1,0:T(8,128)(2,1)S(1)}, bf16[32,4096]{1,0:T(8,128)(2,1)S(1)}, u32[]{:S(2)}, u32[]{:S(2)}) collective-permute-start(bf16[32,4096]{1,0:T(8,128)(2,1)S(1)} %collective-permute-done.10.refs_10_.rest_0_.refs_2_), channel_id=1, source_target_pairs={{0,4},{1,5},{4,8},{5,9},{8,12},{9,13},{12,14},{13,15},{14,10},{15,... | collective-permute-start | bytes 786440 | tf_op jit(solution)/shard_map/ppermute | solution.py:458
  41.4 9.8 %collective-permute-start.14 = (bf16[32,4096]{1,0:T(8,128)(2,1)S(1)}, bf16[32,4096]{1,0:T(8,128)(2,1)S(1)}, u32[]{:S(2)}, u32[]{:S(2)}) collective-permute-start(bf16[32,4096]{1,0:T(8,128)(2,1)S(1)} %collective-permute-done.11.refs_11_.rest_1_.refs_7_), channel_id=1, source_target_pairs={{4,0},{5,1},{8,4},{9,5},{12,8},{13,9},{14,12},{15,13},{10,14},{11,... | collective-permute-start | bytes 786440 | tf_op jit(solution)/shard_map/ppermute | solution.py:461
  51.2 10.9 %collective-permute-start.16 = (bf16[16,4096]{1,0:T(8,128)(2,1)S(1)}, bf16[16,4096]{1,0:T(8,128)(2,1)S(1)}, u32[]{:S(2)}, u32[]{:S(2)}) collective-permute-start(bf16[16,4096]{1,0:T(8,128)(2,1)S(1)} %slice.15), channel_id=1, source_target_pairs={{4,0},{5,1},{8,4},{9,5},{12,8},{13,9},{14,12},{15,13},{10,14},{11,... | collective-permute-start | bytes 393224 | tf_op jit(solution)/shard_map/ppermute | solution.py:461
  51.7 10.4 %collective-permute-start.15 = (bf16[16,4096]{1,0:T(8,128)(2,1)S(1)}, bf16[16,4096]{1,0:T(8,128)(2,1)S(1)}, u32[]{:S(2)}, u32[]{:S(2)}) collective-permute-start(bf16[16,4096]{1,0:T(8,128)(2,1)S(1)} %slice.14), channel_id=1, source_target_pairs={{0,4},{1,5},{4,8},{5,9},{8,12},{9,13},{12,14},{13,15},{14,10},{15,... | collective-permute-start | bytes 393224 | tf_op jit(solution)/shard_map/ppermute | solution.py:458
  62.7 6.6 %collective-permute-start.17 = (bf16[4096,256]{1,0:T(8,128)(2,1)S(1)}, bf16[4096,256]{1,0:T(8,128)(2,1)S(1)}, u32[]{:S(2)}, u32[]{:S(2)}) collective-permute-start(bf16[4096,256]{1,0:T(8,128)(2,1)S(1)} %pack_turned.1.rest_0_.near_ref), channel_id=1, source_target_pairs={{0,1},{1,0},{2,3},{3,2},{4,5},{5,4},{6,7},{7,6},{8,9},{9,8},{10,11... | collective-permute-start | bytes 6291464 | tf_op jit(solution)/shard_map/ppermute | solution.py:464
  99.7 6.4 %collective-permute-start.18 = (bf16[256,4096]{1,0:T(8,128)(2,1)S(1)}, bf16[256,4096]{1,0:T(8,128)(2,1)S(1)}, u32[]{:S(2)}, u32[]{:S(2)}) collective-permute-start(bf16[256,4096]{1,0:T(8,128)(2,1)S(1)} %get-tuple-element.90), channel_id=1, source_target_pairs={{0,1},{1,0},{2,3},{3,2},{4,5},{5,4},{6,7},{7,6},{8,9},{9,8},{10,11... | collective-permute-start | bytes 6291464 | tf_op jit(solution)/shard_map/ppermute | solution.py:464
  106.1 5.5 %collective-permute-start.19 = (bf16[16,4096]{1,0:T(8,128)(2,1)S(1)}, bf16[16,4096]{1,0:T(8,128)(2,1)S(1)}, u32[]{:S(2)}, u32[]{:S(2)}) collective-permute-start(bf16[16,4096]{1,0:T(8,128)(2,1)S(1)} %get-tuple-element.92.rest_2_), channel_id=1, source_target_pairs={{0,4},{1,5},{4,8},{5,9},{8,12},{9,13},{12,14},{13,15},{14,10},{15,... | collective-permute-start | bytes 393224 | tf_op jit(solution)/shard_map/ppermute | solution.py:458
  113.1 7.9 %collective-permute-start.21 = (bf16[32,4096]{1,0:T(8,128)(2,1)S(1)}, bf16[32,4096]{1,0:T(8,128)(2,1)S(1)}, u32[]{:S(2)}, u32[]{:S(2)}) collective-permute-start(bf16[32,4096]{1,0:T(8,128)(2,1)S(1)} %get-tuple-element.97.rest_2_), channel_id=1, source_target_pairs={{0,4},{1,5},{4,8},{5,9},{8,12},{9,13},{12,14},{13,15},{14,10},{15,... | collective-permute-start | bytes 786440 | tf_op jit(solution)/shard_map/ppermute | solution.py:458
  114.6 6.8 %collective-permute-start.22 = (bf16[32,4096]{1,0:T(8,128)(2,1)S(1)}, bf16[32,4096]{1,0:T(8,128)(2,1)S(1)}, u32[]{:S(2)}, u32[]{:S(2)}) collective-permute-start(bf16[32,4096]{1,0:T(8,128)(2,1)S(1)} %get-tuple-element.98.rest_3_), channel_id=1, source_target_pairs={{4,0},{5,1},{8,4},{9,5},{12,8},{13,9},{14,12},{15,13},{10,14},{11,... | collective-permute-start | bytes 786440 | tf_op jit(solution)/shard_map/ppermute | solution.py:461
  121.6 7.9 %collective-permute-start.23 = (bf16[32,4096]{1,0:T(8,128)(2,1)S(1)}, bf16[32,4096]{1,0:T(8,128)(2,1)S(1)}, u32[]{:S(2)}, u32[]{:S(2)}) collective-permute-start(bf16[32,4096]{1,0:T(8,128)(2,1)S(1)} %get-tuple-element.102.rest_2_), channel_id=1, source_target_pairs={{0,4},{1,5},{4,8},{5,9},{8,12},{9,13},{12,14},{13,15},{14,10},{15,... | collective-permute-start | bytes 786440 | tf_op jit(solution)/shard_map/ppermute | solution.py:458
  123.0 6.5 %collective-permute-start.24 = (bf16[32,4096]{1,0:T(8,128)(2,1)S(1)}, bf16[32,4096]{1,0:T(8,128)(2,1)S(1)}, u32[]{:S(2)}, u32[]{:S(2)}) collective-permute-start(bf16[32,4096]{1,0:T(8,128)(2,1)S(1)} %get-tuple-element.103.rest_3_), channel_id=1, source_target_pairs={{4,0},{5,1},{8,4},{9,5},{12,8},{13,9},{14,12},{15,13},{10,14},{11,... | collective-permute-start | bytes 786440 | tf_op jit(solution)/shard_map/ppermute | solution.py:461
  129.7 6.4 %collective-permute-start.25 = (bf16[32,4096]{1,0:T(8,128)(2,1)S(1)}, bf16[32,4096]{1,0:T(8,128)(2,1)S(1)}, u32[]{:S(2)}, u32[]{:S(2)}) collective-permute-start(bf16[32,4096]{1,0:T(8,128)(2,1)S(1)} %get-tuple-element.107.rest_2_), channel_id=1, source_target_pairs={{0,4},{1,5},{4,8},{5,9},{8,12},{9,13},{12,14},{13,15},{14,10},{15,... | collective-permute-start | bytes 786440 | tf_op jit(solution)/shard_map/ppermute | solution.py:458
  131.1 6.4 %collective-permute-start.26 = (bf16[32,4096]{1,0:T(8,128)(2,1)S(1)}, bf16[32,4096]{1,0:T(8,128)(2,1)S(1)}, u32[]{:S(2)}, u32[]{:S(2)}) collective-permute-start(bf16[32,4096]{1,0:T(8,128)(2,1)S(1)} %get-tuple-element.108.rest_3_), channel_id=1, source_target_pairs={{4,0},{5,1},{8,4},{9,5},{12,8},{13,9},{14,12},{15,13},{10,14},{11,... | collective-permute-start | bytes 786440 | tf_op jit(solution)/shard_map/ppermute | solution.py:461
  (13 other events, 90.5 us)

commit v11 on v10

--- a/solution.py
+++ b/solution.py
@@ -175,7 +175,7 @@
     def store(t):
         to = pl.ds(t * step, step)
         return [
-            pltpu.make_async_copy(out_buf.at[t, i], ref.at[to, :], out_sems.at[t, i])
+            pltpu.make_async_copy(out_buf.at[t % 2, i], ref.at[to, :], out_sems.at[t % 2, i])
             for i, ref in enumerate((a_ref, b_ref))
         ]
 
@@ -195,17 +195,19 @@
         if t == tiles - 1:
             begin(fetch_next())
         w_ref = w_buf.at[t % 2] if t else head_ref
+        if t > 1:
+            finish(store(t - 2))
         for side, x_ref in enumerate((near_ref, far_ref)):
             gate = jnp.dot(x_ref[...], w_ref[0], preferred_element_type=F32)
             up = jnp.dot(x_ref[...], w_ref[1], preferred_element_type=F32)
             at = pl.ds(side * rows, rows)
             sigma = jax.nn.sigmoid(gate)
-            out_buf[t, 0, :, at] = (up * sigma * (1.0 + gate * (1.0 - sigma))).T
-            out_buf[t, 1, :, at] = (gate * sigma).T
+            out_buf[t % 2, 0, :, at] = (up * sigma * (1.0 + gate * (1.0 - sigma))).T
+            out_buf[t % 2, 1, :, at] = (gate * sigma).T
         if t and t + 2 < tiles:
             begin(fetch(t + 2))
         begin(store(t))
-    for t in range(tiles):
+    for t in range(max(tiles - 2, 0), tiles):
         finish(store(t))
     finish(fetch_next())
 
@@ -221,9 +223,9 @@
         + [jax.ShapeDtypeStruct((step, depth) if last else (2, depth, step), BF16)],
         scratch_shapes=[
             pltpu.VMEM((2, 2, depth, step), BF16),
-            pltpu.VMEM((count, 2, step, 2 * rows), F32),
+            pltpu.VMEM((2, 2, step, 2 * rows), F32),
             pltpu.SemaphoreType.DMA((2, 2)),
-            pltpu.SemaphoreType.DMA((count, 2)),
+            pltpu.SemaphoreType.DMA((2, 2)),
             pltpu.SemaphoreType.DMA((2,)),
         ],
         compiler_params=params(grant),
@@ -348,7 +350,7 @@
             pltpu.SemaphoreType.DMA((2, 2)),
             pltpu.SemaphoreType.DMA((2, len(a))),
         ],
-        compiler_params=params(28),
+        compiler_params=params(26),
         cost_estimate=cost(12 * rows * depth * width, 6 * depth * width),
         name="hidden_back",
     )(spot, near, far, head, wg, wu, wd, *a, *b)
@@ -480,45 +482,29 @@
         return [own] + [r for r, _ in rounds] + [l for _, l in rounds[::-1]]
 
     lane = tile(width, 256)
-    tiles = width // lane
-    cuts = [0, 2, 5, 7]
-
-    def piece(i, head, after):
-        grant = (30, 28, 28)[i]
-        count = cuts[i + 1] - cuts[i]
-        a, b, head = gate_up(
-            near_x, far_x, head, wg, wu, wd, cuts[i], count, lane, grant, after
-        )
-        return (a, b), head
-
     own_x, own_dy, head = bring(tokens, grad_out, wg, wu, lane)
     in_x = [both(tokens, tokens)]
+    in_dy = [both(grad_out, grad_out)]
     in_x.append(both(*in_x[-1], (own_x, head)))
-    in_dy = [both(own_dy, own_dy, in_x[0])]
-    for _ in range(3, far):
-        in_x.append(both(*in_x[-1]))
-        in_dy.append(both(*in_dy[-1]))
-    in_x.append(both(*in_x[-1], in_dy[0], True))
-    near_x = pack(blocks(own_x, in_x), (spot, *in_dy[-1]))
+    in_dy.append(both(*in_dy[-1], in_x[0]))
+    in_x.append(both(*in_x[-1], in_dy[0]))
+    in_dy.append(both(*in_dy[-1], in_x[1]))
+    in_x.append(both(*in_x[-1], in_dy[1], True))
+    near_x = pack(blocks(own_x, in_x), (spot, *in_dy[2]))
     far_x = swap(near_x)
-
-    in_dy.append(both(*in_dy[-1], in_x[-2]))
-    some, head = piece(0, head, in_dy[-2])
-    factors = [some]
-    in_dy.append(both(*in_dy[-1], some, True))
-    some, head = piece(1, head, in_dy[-2])
-    factors.append(some)
-    x = arrange(spot, near_x, far_x, in_dy[-2])
-    near_dy = pack_turned(blocks(own_dy, in_dy), (x, *some))
+    in_dy.append(both(*in_dy[-1], in_x[2], True))
+    near_dy = pack_turned(blocks(own_dy, in_dy), ())
     far_dy = swap(near_dy)
-    some, head = piece(2, head, (near_dy,))
-    factors.append(some)
-    gg, gu, own, sent = back(spot, near_dy, far_dy, head, wg, wu, wd, factors)
+    a, b, head = gate_up(
+        near_x, far_x, head, wg, wu, wd, 0, width // lane, lane, 26, (near_dy,)
+    )
+    gg, gu, own, sent = back(spot, near_dy, far_dy, head, wg, wu, wd, [(a, b)])
+    x = arrange(spot, near_x, far_x, (own,))
 
     near = swap(sent)
     full, head, tail = pl.ds(0, row), pl.ds(0, row // 2), pl.ds(row // 2, row // 2)
     step = 256
-    counts = [4, 2, 4, 4, 2]
+    counts = [3, 3, 4, 4, 2]
     held, first = (), 0
     r = l = None
     ready = ()

time: 139 us -> 140 us (level)
  local copies, waits for them, and re-layouts: 9.06 us -> 5.19 us
  Pallas kernels: 77.7 us -> 80.7 us
  waiting for transfers between devices: 23.6 us -> 26.4 us
    ppermute x12, waiting for transfers between devices: 12 us -> 18.9 us  [left(): return lax.ppermute(value, 'hid', to_left)]
    unnamed x20 -> x12, local copies, waits for them, and re-layouts: 7.8 us -> 3.92 us
    ppermute x3, waiting for transfers between devices: 2.07 us -> 0.01 us  [swap(): return lax.ppermute(value, 'hid', across)]
    ppermute x12, waiting for transfers between devices: 9.49 us -> 7.49 us  [right(): return lax.ppermute(value, 'hid', to_right)]
    pallas_call x3 -> x1, Pallas kernels: 19.5 us -> 20.2 us  [gate_up(): pl.pallas_call(functools.partial(gate_up_kernel, first, step), in_specs=h...]
  transfers between devices with their start and end apart: 27 -> 27, of which waited for: 16 -> 19; matrix products, arithmetic and copies ran while one was open for 1% -> 1% of each run, Pallas kernels for 34% -> 34%
where the time goes in v11:
time: 140 us
  Pallas kernels  80.7 us (58%)
  starting transfers between devices  26.4 us (19%)
  waiting for transfers between devices  26.4 us (19%)
  local copies, waits for them, and re-layouts  5.19 us (4%)
    pallas_call x1, Pallas kernels, back(): pl.pallas_call(functools.partial(back_kernel, step, 512, len(a)), in_spec...  30.1 us
    pallas_call x5, Pallas kernels, fisher(): pl.pallas_call(functools.partial(fisher_kernel, tile(width, 256)), grid=(...  24.1 us
    ppermute x12, starting transfers between devices, right(): return lax.ppermute(value, 'hid', to_right)  21.4 us
    pallas_call x1, Pallas kernels, gate_up(): pl.pallas_call(functools.partial(gate_up_kernel, first, step), in_specs=h...  20.2 us
    ppermute x12, waiting for transfers between devices, left(): return lax.ppermute(value, 'hid', to_left)  18.9 us
    ppermute x12, waiting for transfers between devices, right(): return lax.ppermute(value, 'hid', to_right)  7.49 us
    ppermute x12, starting transfers between devices, left(): return lax.ppermute(value, 'hid', to_left)  4.26 us
    unnamed x12, local copies, waits for them, and re-layouts  3.92 us
  transfers between devices with their start and end apart: 27, of which 19 were waited for; matrix products, arithmetic and copies ran while one was open for 1% of the time, Pallas kernels for 34%

profile of v11, /device:TPU:0, one launch (start us, length us, event | category | flops | bytes accessed | tf_op | source)
XLA Modules:
  0.0 140.2 jit_solution(5994750918837734748)
XLA Ops:
  0.6 3.1 %collective-permute-start = (bf16[32,4096]{1,0:T(8,128)(2,1)}, bf16[32,4096]{1,0:T(8,128)(2,1)S(1)}, u32[]{:S(2)}, u32[]{:S(2)}) collective-permute-start(bf16[32,4096]{1,0:T(8,128)(2,1)} %x_ref.1), channel_id=1, source_target_pairs={{0,4},{1,5},{4,8},{5,9},{8,12},{9,13},{12,14},{13,15},{14,10},{15,... | collective-permute-start | bytes 786440 | tf_op jit(solution)/shard_map/ppermute | solution.py:460
  3.7 2.0 %collective-permute-start.4 = (bf16[32,4096]{1,0:T(8,128)(2,1)}, bf16[32,4096]{1,0:T(8,128)(2,1)S(1)}, u32[]{:S(2)}, u32[]{:S(2)}) collective-permute-start(bf16[32,4096]{1,0:T(8,128)(2,1)} %dy_ref.1), channel_id=1, source_target_pairs={{0,4},{1,5},{4,8},{5,9},{8,12},{9,13},{12,14},{13,15},{14,10},{15,... | collective-permute-start | bytes 786440 | tf_op jit(solution)/shard_map/ppermute | solution.py:460
  7.7 2.3 %bring.1 = (bf16[32,4096]{1,0:T(8,128)(2,1)S(1)}, bf16[32,4096]{1,0:T(8,128)(2,1)S(1)}, bf16[2,4096,256]{2,1,0:T(8,128)(2,1)S(1)}) custom-call(bf16[32,4096]{1,0:T(8,128)(2,1)S(1)} %copy-done, bf16[32,4096]{1,0:T(8,128)(2,1)S(1)} %copy-done.1, bf16[4096,1792]{1,0:T(8,128)(2,1)} %wg_ref.5, bf16[4096,1792]{1,0:T(8,128)(2,1)} %wu_ref.5), custom_call_target="tpu_custom_call" | custom-call | bytes 4194304 | tf_op jit(solution)/shard_map/bring/pallas_call | solution.py:61
  9.9 2.0 %copy-done.2 = bf16[2,4096,256]{2,1,0:T(8,128)(2,1)} copy-done((bf16[2,4096,256]{2,1,0:T(8,128)(2,1)}, bf16[2,4096,256]{2,1,0:T(8,128)(2,1)S(1)}, u32[]{:S(2)}) %copy-start.2) | copy-done | bytes 4194328
  16.6 2.2 %collective-permute-done.5.refs_8_ = bf16[32,4096]{1,0:T(8,128)(2,1)S(1)} collective-permute-done((bf16[32,4096]{1,0:T(8,128)(2,1)}, bf16[32,4096]{1,0:T(8,128)(2,1)S(1)}, u32[]{:S(2)}, u32[]{:S(2)}) %collective-permute-start.5) | collective-permute-done | bytes 262176 | tf_op jit(solution)/shard_map/ppermute | solution.py:463
  20.8 1.7 %collective-permute-done.2.refs_2_ = bf16[32,4096]{1,0:T(8,128)(2,1)} collective-permute-done((bf16[32,4096]{1,0:T(8,128)(2,1)S(1)}, bf16[32,4096]{1,0:T(8,128)(2,1)}, u32[]{:S(2)}, u32[]{:S(2)}) %collective-permute-start.2) | collective-permute-done | bytes 262176 | tf_op jit(solution)/shard_map/ppermute | solution.py:460
  22.5 2.0 %collective-permute-done.3.refs_7_ = bf16[32,4096]{1,0:T(8,128)(2,1)} collective-permute-done((bf16[32,4096]{1,0:T(8,128)(2,1)S(1)}, bf16[32,4096]{1,0:T(8,128)(2,1)}, u32[]{:S(2)}, u32[]{:S(2)}) %collective-permute-start.3) | collective-permute-done | bytes 262176 | tf_op jit(solution)/shard_map/ppermute | solution.py:463
  28.0 2.0 %collective-permute-done.9.refs_7_ = bf16[32,4096]{1,0:T(8,128)(2,1)S(1)} collective-permute-done((bf16[32,4096]{1,0:T(8,128)(2,1)S(1)}, bf16[32,4096]{1,0:T(8,128)(2,1)S(1)}, u32[]{:S(2)}, u32[]{:S(2)}) %collective-permute-start.9) | collective-permute-done | bytes 262176 | tf_op jit(solution)/shard_map/ppermute | solution.py:463
  34.0 1.7 %collective-permute-done.7.refs_6_ = bf16[32,4096]{1,0:T(8,128)(2,1)S(1)} collective-permute-done((bf16[32,4096]{1,0:T(8,128)(2,1)}, bf16[32,4096]{1,0:T(8,128)(2,1)S(1)}, u32[]{:S(2)}, u32[]{:S(2)}) %collective-permute-start.7) | collective-permute-done | bytes 262176 | tf_op jit(solution)/shard_map/ppermute | solution.py:463
  36.1 1.7 %collective-permute-start.10 = (bf16[16,4096]{1,0:T(8,128)(2,1)S(1)}, bf16[16,4096]{1,0:T(8,128)(2,1)S(1)}, u32[]{:S(2)}, u32[]{:S(2)}) collective-permute-start(bf16[16,4096]{1,0:T(8,128)(2,1)S(1)} %slice.12), channel_id=1, source_target_pairs={{0,4},{1,5},{4,8},{5,9},{8,12},{9,13},{12,14},{13,15},{14,10},{15,... | collective-permute-start | bytes 393224 | tf_op jit(solution)/shard_map/ppermute | solution.py:460
  37.8 1.8 %collective-permute-done.12.refs_10_.refs_3_ = bf16[32,4096]{1,0:T(8,128)(2,1)S(1)} collective-permute-done((bf16[32,4096]{1,0:T(8,128)(2,1)S(1)}, bf16[32,4096]{1,0:T(8,128)(2,1)S(1)}, u32[]{:S(2)}, u32[]{:S(2)}) %collective-permute-start.12) | collective-permute-done | bytes 262176 | tf_op jit(solution)/shard_map/ppermute | solution.py:460
  44.2 1.7 %collective-permute-start.15 = (bf16[16,4096]{1,0:T(8,128)(2,1)S(1)}, bf16[16,4096]{1,0:T(8,128)(2,1)S(1)}, u32[]{:S(2)}, u32[]{:S(2)}) collective-permute-start(bf16[16,4096]{1,0:T(8,128)(2,1)S(1)} %slice.14), channel_id=1, source_target_pairs={{0,4},{1,5},{4,8},{5,9},{8,12},{9,13},{12,14},{13,15},{14,10},{15,... | collective-permute-start | bytes 393224 | tf_op jit(solution)/shard_map/ppermute | solution.py:460
  46.0 3.9 %collective-permute-done.16.refs_5_ = bf16[16,4096]{1,0:T(8,128)(2,1)S(1)} collective-permute-done((bf16[16,4096]{1,0:T(8,128)(2,1)S(1)}, bf16[16,4096]{1,0:T(8,128)(2,1)S(1)}, u32[]{:S(2)}, u32[]{:S(2)}) %collective-permute-start.16) | collective-permute-done | bytes 131104 | tf_op jit(solution)/shard_map/ppermute | solution.py:463
  50.6 20.2 %gate_up.1 = (f32[1792,512]{1,0:T(8,128)S(1)}, f32[1792,512]{1,0:T(8,128)S(1)}, bf16[256,4096]{1,0:T(8,128)(2,1)S(1)}) custom-call(bf16[256,4096]{1,0:T(8,128)(2,1)S(1)} %pack.1.near_ref, bf16[256,4096]{1,0:T(8,128)(2,1)S(1)} %collective-permute-done.14.far_ref, bf16[2,4096,256]{2,1,0:T(8,128)(2,1)S(1)} %copy-done.3, bf16[4096,1792]{1,0:T(8,128)(2,1)} %wg_ref.5, ...), custom_call_target="tpu_custom_call" | custom-call | flops 15032385536 | bytes 29360128 | tf_op jit(solution)/shard_map/gate_up/pallas_call | solution.py:218
  70.8 30.1 %hidden_back.1 = (bf16[512,1792]{1,0:T(8,128)(2,1)S(1)}, bf16[512,1792]{1,0:T(8,128)(2,1)S(1)}, bf16[256,4096]{1,0:T(8,128)(2,1)S(1)}, bf16[256,4096]{1,0:T(8,128)(2,1)S(1)}) custom-call(s32[8]{0:T(128)S(1)} %fusion.3.refs_9_.spot_ref, bf16[4096,256]{1,0:T(8,128)(2,1)S(1)} %pack_turned.1.rest_0_.near_ref, ...), custom_call_target="tpu_custom_call" | custom-call | flops 22548578304 | bytes 44040192 | tf_op jit(solution)/shard_map/hidden_back/pallas_call | solution.py:335
  102.3 4.6 %fisher.5 = (bf16[4096,1792]{1,0:T(8,128)(2,1)}, bf16[4096,1792]{1,0:T(8,128)(2,1)}, f32[8,128]{1,0:T(8,128)S(1)}) custom-call(bf16[512,4096]{1,0:T(8,128)(2,1)S(1)} %arrange.1.x_ref, bf16[512,1792]{1,0:T(8,128)(2,1)S(1)} %get-tuple-element.74.gg_ref, bf16[512,1792]{1,0:T(8,128)(2,1)S(1)} %get-tuple-element.75.gu_ref), custom_call_target="tpu_custom_call" | custom-call | flops 2818572288 | bytes 5505024 | tf_op jit(solution)/shard_map/fisher/pallas_call | solution.py:433
  107.0 1.7 %collective-permute-start.19 = (bf16[16,4096]{1,0:T(8,128)(2,1)S(1)}, bf16[16,4096]{1,0:T(8,128)(2,1)S(1)}, u32[]{:S(2)}, u32[]{:S(2)}) collective-permute-start(bf16[16,4096]{1,0:T(8,128)(2,1)S(1)} %get-tuple-element.80.rest_2_), channel_id=1, source_target_pairs={{0,4},{1,5},{4,8},{5,9},{8,12},{9,13},{12,14},{13,15},{14,10},{15,... | collective-permute-start | bytes 393224 | tf_op jit(solution)/shard_map/ppermute | solution.py:460
  109.1 4.6 %fisher.6 = (bf16[4096,1792]{1,0:T(8,128)(2,1)}, bf16[4096,1792]{1,0:T(8,128)(2,1)}, f32[8,128]{1,0:T(8,128)S(1)}) custom-call(bf16[512,4096]{1,0:T(8,128)(2,1)S(1)} %arrange.1.x_ref, bf16[512,1792]{1,0:T(8,128)(2,1)S(1)} %get-tuple-element.74.gg_ref, bf16[512,1792]{1,0:T(8,128)(2,1)S(1)} %get-tuple-element.75.gu_ref, ...), custom_call_target="tpu_custom_call", output_to_operand_aliasing={{0}: (3, {}), {1}: (4, {})} | custom-call | flops 2818572288 | bytes 5505024 | tf_op jit(solution)/shard_map/fisher/pallas_call | solution.py:433
  114.0 1.6 %collective-permute-start.21 = (bf16[32,4096]{1,0:T(8,128)(2,1)S(1)}, bf16[32,4096]{1,0:T(8,128)(2,1)S(1)}, u32[]{:S(2)}, u32[]{:S(2)}) collective-permute-start(bf16[32,4096]{1,0:T(8,128)(2,1)S(1)} %get-tuple-element.85.rest_2_), channel_id=1, source_target_pairs={{0,4},{1,5},{4,8},{5,9},{8,12},{9,13},{12,14},{13,15},{14,10},{15,... | collective-permute-start | bytes 786440 | tf_op jit(solution)/shard_map/ppermute | solution.py:460
  116.1 5.8 %fisher.7 = (bf16[4096,1792]{1,0:T(8,128)(2,1)}, bf16[4096,1792]{1,0:T(8,128)(2,1)}, f32[8,128]{1,0:T(8,128)S(1)}) custom-call(bf16[512,4096]{1,0:T(8,128)(2,1)S(1)} %arrange.1.x_ref, bf16[512,1792]{1,0:T(8,128)(2,1)S(1)} %get-tuple-element.74.gg_ref, bf16[512,1792]{1,0:T(8,128)(2,1)S(1)} %get-tuple-element.75.gu_ref, ...), custom_call_target="tpu_custom_call", output_to_operand_aliasing={{0}: (3, {}), {1}: (4, {})} | custom-call | flops 3758096384 | bytes 7340032 | tf_op jit(solution)/shard_map/fisher/pallas_call | solution.py:433
  123.1 1.6 %collective-permute-start.23 = (bf16[32,4096]{1,0:T(8,128)(2,1)S(1)}, bf16[32,4096]{1,0:T(8,128)(2,1)S(1)}, u32[]{:S(2)}, u32[]{:S(2)}) collective-permute-start(bf16[32,4096]{1,0:T(8,128)(2,1)S(1)} %get-tuple-element.90.rest_2_), channel_id=1, source_target_pairs={{0,4},{1,5},{4,8},{5,9},{8,12},{9,13},{12,14},{13,15},{14,10},{15,... | collective-permute-start | bytes 786440 | tf_op jit(solution)/shard_map/ppermute | solution.py:460
  125.2 5.8 %fisher.8 = (bf16[4096,1792]{1,0:T(8,128)(2,1)}, bf16[4096,1792]{1,0:T(8,128)(2,1)}, f32[8,128]{1,0:T(8,128)S(1)}) custom-call(bf16[512,4096]{1,0:T(8,128)(2,1)S(1)} %arrange.1.x_ref, bf16[512,1792]{1,0:T(8,128)(2,1)S(1)} %get-tuple-element.74.gg_ref, bf16[512,1792]{1,0:T(8,128)(2,1)S(1)} %get-tuple-element.75.gu_ref, ...), custom_call_target="tpu_custom_call", output_to_operand_aliasing={{0}: (3, {}), {1}: (4, {})} | custom-call | flops 3758096384 | bytes 7340032 | tf_op jit(solution)/shard_map/fisher/pallas_call | solution.py:433
  131.3 1.6 %collective-permute-start.25 = (bf16[32,4096]{1,0:T(8,128)(2,1)S(1)}, bf16[32,4096]{1,0:T(8,128)(2,1)S(1)}, u32[]{:S(2)}, u32[]{:S(2)}) collective-permute-start(bf16[32,4096]{1,0:T(8,128)(2,1)S(1)} %get-tuple-element.95.rest_2_), channel_id=1, source_target_pairs={{0,4},{1,5},{4,8},{5,9},{8,12},{9,13},{12,14},{13,15},{14,10},{15,... | collective-permute-start | bytes 786440 | tf_op jit(solution)/shard_map/ppermute | solution.py:460
  133.4 3.4 %fisher.9 = (bf16[4096,1792]{1,0:T(8,128)(2,1)}, bf16[4096,1792]{1,0:T(8,128)(2,1)}, f32[8,128]{1,0:T(8,128)}) custom-call(bf16[512,4096]{1,0:T(8,128)(2,1)S(1)} %arrange.1.x_ref, bf16[512,1792]{1,0:T(8,128)(2,1)S(1)} %get-tuple-element.74.gg_ref, bf16[512,1792]{1,0:T(8,128)(2,1)S(1)} %get-tuple-element.75.gu_ref, ...), custom_call_target="tpu_custom_call", output_to_operand_aliasing={{0}: (3, {}), {1}: (4, {})} | custom-call | flops 1879048192 | bytes 3670016 | tf_op jit(solution)/shard_map/fisher/pallas_call | solution.py:433
  (67 shorter events, 30.3 us)
Async XLA Ops:
  0.6 11.3 %collective-permute-start = (bf16[32,4096]{1,0:T(8,128)(2,1)}, bf16[32,4096]{1,0:T(8,128)(2,1)S(1)}, u32[]{:S(2)}, u32[]{:S(2)}) collective-permute-start(bf16[32,4096]{1,0:T(8,128)(2,1)} %x_ref.1), channel_id=1, source_target_pairs={{0,4},{1,5},{4,8},{5,9},{8,12},{9,13},{12,14},{13,15},{14,10},{15,... | collective-permute-start | bytes 786440 | tf_op jit(solution)/shard_map/ppermute | solution.py:460
  3.7 9.4 %collective-permute-start.1 = (bf16[32,4096]{1,0:T(8,128)(2,1)}, bf16[32,4096]{1,0:T(8,128)(2,1)S(1)}, u32[]{:S(2)}, u32[]{:S(2)}) collective-permute-start(bf16[32,4096]{1,0:T(8,128)(2,1)} %x_ref.1), channel_id=1, source_target_pairs={{4,0},{5,1},{8,4},{9,5},{12,8},{13,9},{14,12},{15,13},{10,14},{11,... | collective-permute-start | bytes 786440 | tf_op jit(solution)/shard_map/ppermute | solution.py:463
  3.7 12.9 %collective-permute-start.4 = (bf16[32,4096]{1,0:T(8,128)(2,1)}, bf16[32,4096]{1,0:T(8,128)(2,1)S(1)}, u32[]{:S(2)}, u32[]{:S(2)}) collective-permute-start(bf16[32,4096]{1,0:T(8,128)(2,1)} %dy_ref.1), channel_id=1, source_target_pairs={{0,4},{1,5},{4,8},{5,9},{8,12},{9,13},{12,14},{13,15},{14,10},{15,... | collective-permute-start | bytes 786440 | tf_op jit(solution)/shard_map/ppermute | solution.py:460
  5.7 13.0 %collective-permute-start.5 = (bf16[32,4096]{1,0:T(8,128)(2,1)}, bf16[32,4096]{1,0:T(8,128)(2,1)S(1)}, u32[]{:S(2)}, u32[]{:S(2)}) collective-permute-start(bf16[32,4096]{1,0:T(8,128)(2,1)} %dy_ref.1), channel_id=1, source_target_pairs={{4,0},{5,1},{8,4},{9,5},{12,8},{13,9},{14,12},{15,13},{10,14},{11,... | collective-permute-start | bytes 786440 | tf_op jit(solution)/shard_map/ppermute | solution.py:463
  13.2 9.3 %collective-permute-start.2 = (bf16[32,4096]{1,0:T(8,128)(2,1)S(1)}, bf16[32,4096]{1,0:T(8,128)(2,1)}, u32[]{:S(2)}, u32[]{:S(2)}) collective-permute-start(bf16[32,4096]{1,0:T(8,128)(2,1)S(1)} %collective-permute-done.refs_1_), channel_id=1, source_target_pairs={{0,4},{1,5},{4,8},{5,9},{8,12},{9,13},{12,14},{13,15},{14,10},{15,... | collective-permute-start | bytes 786440 | tf_op jit(solution)/shard_map/ppermute | solution.py:460
  14.7 9.8 %collective-permute-start.3 = (bf16[32,4096]{1,0:T(8,128)(2,1)S(1)}, bf16[32,4096]{1,0:T(8,128)(2,1)}, u32[]{:S(2)}, u32[]{:S(2)}) collective-permute-start(bf16[32,4096]{1,0:T(8,128)(2,1)S(1)} %collective-permute-done.1.refs_8_), channel_id=1, source_target_pairs={{4,0},{5,1},{8,4},{9,5},{12,8},{13,9},{14,12},{15,13},{10,14},{11,... | collective-permute-start | bytes 786440 | tf_op jit(solution)/shard_map/ppermute | solution.py:463
  18.8 9.2 %collective-permute-start.8 = (bf16[32,4096]{1,0:T(8,128)(2,1)S(1)}, bf16[32,4096]{1,0:T(8,128)(2,1)S(1)}, u32[]{:S(2)}, u32[]{:S(2)}) collective-permute-start(bf16[32,4096]{1,0:T(8,128)(2,1)S(1)} %collective-permute-done.4.refs_1_), channel_id=1, source_target_pairs={{0,4},{1,5},{4,8},{5,9},{8,12},{9,13},{12,14},{13,15},{14,10},{15,... | collective-permute-start | bytes 786440 | tf_op jit(solution)/shard_map/ppermute | solution.py:460
  20.4 9.7 %collective-permute-start.9 = (bf16[32,4096]{1,0:T(8,128)(2,1)S(1)}, bf16[32,4096]{1,0:T(8,128)(2,1)S(1)}, u32[]{:S(2)}, u32[]{:S(2)}) collective-permute-start(bf16[32,4096]{1,0:T(8,128)(2,1)S(1)} %collective-permute-done.5.refs_8_), channel_id=1, source_target_pairs={{4,0},{5,1},{8,4},{9,5},{12,8},{13,9},{14,12},{15,13},{10,14},{11,... | collective-permute-start | bytes 786440 | tf_op jit(solution)/shard_map/ppermute | solution.py:463
  24.5 9.5 %collective-permute-start.6 = (bf16[32,4096]{1,0:T(8,128)(2,1)}, bf16[32,4096]{1,0:T(8,128)(2,1)S(1)}, u32[]{:S(2)}, u32[]{:S(2)}) collective-permute-start(bf16[32,4096]{1,0:T(8,128)(2,1)} %collective-permute-done.2.refs_2_), channel_id=1, source_target_pairs={{0,4},{1,5},{4,8},{5,9},{8,12},{9,13},{12,14},{13,15},{14,10},{15,... | collective-permute-start | bytes 786440 | tf_op jit(solution)/shard_map/ppermute | solution.py:460
  26.1 9.6 %collective-permute-start.7 = (bf16[32,4096]{1,0:T(8,128)(2,1)}, bf16[32,4096]{1,0:T(8,128)(2,1)S(1)}, u32[]{:S(2)}, u32[]{:S(2)}) collective-permute-start(bf16[32,4096]{1,0:T(8,128)(2,1)} %collective-permute-done.3.refs_7_), channel_id=1, source_target_pairs={{4,0},{5,1},{8,4},{9,5},{12,8},{13,9},{14,12},{15,13},{10,14},{11,... | collective-permute-start | bytes 786440 | tf_op jit(solution)/shard_map/ppermute | solution.py:463
  30.0 9.6 %collective-permute-start.12 = (bf16[32,4096]{1,0:T(8,128)(2,1)S(1)}, bf16[32,4096]{1,0:T(8,128)(2,1)S(1)}, u32[]{:S(2)}, u32[]{:S(2)}) collective-permute-start(bf16[32,4096]{1,0:T(8,128)(2,1)S(1)} %collective-permute-done.8.refs_2_), channel_id=1, source_target_pairs={{0,4},{1,5},{4,8},{5,9},{8,12},{9,13},{12,14},{13,15},{14,10},{15,... | collective-permute-start | bytes 786440 | tf_op jit(solution)/shard_map/ppermute | solution.py:460
  31.6 9.6 %collective-permute-start.13 = (bf16[32,4096]{1,0:T(8,128)(2,1)S(1)}, bf16[32,4096]{1,0:T(8,128)(2,1)S(1)}, u32[]{:S(2)}, u32[]{:S(2)}) collective-permute-start(bf16[32,4096]{1,0:T(8,128)(2,1)S(1)} %collective-permute-done.9.refs_7_), channel_id=1, source_target_pairs={{4,0},{5,1},{8,4},{9,5},{12,8},{13,9},{14,12},{15,13},{10,14},{11,... | collective-permute-start | bytes 786440 | tf_op jit(solution)/shard_map/ppermute | solution.py:463
  35.7 6.9 %collective-permute-start.11 = (bf16[16,4096]{1,0:T(8,128)(2,1)S(1)}, bf16[16,4096]{1,0:T(8,128)(2,1)S(1)}, u32[]{:S(2)}, u32[]{:S(2)}) collective-permute-start(bf16[16,4096]{1,0:T(8,128)(2,1)S(1)} %slice.13), channel_id=1, source_target_pairs={{4,0},{5,1},{8,4},{9,5},{12,8},{13,9},{14,12},{15,13},{10,14},{11,... | collective-permute-start | bytes 393224 | tf_op jit(solution)/shard_map/ppermute | solution.py:463
  36.1 6.5 %collective-permute-start.10 = (bf16[16,4096]{1,0:T(8,128)(2,1)S(1)}, bf16[16,4096]{1,0:T(8,128)(2,1)S(1)}, u32[]{:S(2)}, u32[]{:S(2)}) collective-permute-start(bf16[16,4096]{1,0:T(8,128)(2,1)S(1)} %slice.12), channel_id=1, source_target_pairs={{0,4},{1,5},{4,8},{5,9},{8,12},{9,13},{12,14},{13,15},{14,10},{15,... | collective-permute-start | bytes 393224 | tf_op jit(solution)/shard_map/ppermute | solution.py:460
  43.8 6.8 %collective-permute-start.14 = (bf16[256,4096]{1,0:T(8,128)(2,1)S(1)}, bf16[256,4096]{1,0:T(8,128)(2,1)S(1)}, u32[]{:S(2)}, u32[]{:S(2)}) collective-permute-start(bf16[256,4096]{1,0:T(8,128)(2,1)S(1)} %pack.1.near_ref), channel_id=1, source_target_pairs={{0,1},{1,0},{2,3},{3,2},{4,5},{5,4},{6,7},{7,6},{8,9},{9,8},{10,11... | collective-permute-start | bytes 6291464 | tf_op jit(solution)/shard_map/ppermute | solution.py:466
  50.5 20.3 %collective-permute-start.17 = (bf16[4096,256]{1,0:T(8,128)(2,1)S(1)}, bf16[4096,256]{1,0:T(8,128)(2,1)S(1)}, u32[]{:S(2)}, u32[]{:S(2)}) collective-permute-start(bf16[4096,256]{1,0:T(8,128)(2,1)S(1)} %pack_turned.1.rest_0_.near_ref), channel_id=1, source_target_pairs={{0,1},{1,0},{2,3},{3,2},{4,5},{5,4},{6,7},{7,6},{8,9},{9,8},{10,11... | collective-permute-start | bytes 6291464 | tf_op jit(solution)/shard_map/ppermute | solution.py:466
  100.9 6.0 %collective-permute-start.18 = (bf16[256,4096]{1,0:T(8,128)(2,1)S(1)}, bf16[256,4096]{1,0:T(8,128)(2,1)S(1)}, u32[]{:S(2)}, u32[]{:S(2)}) collective-permute-start(bf16[256,4096]{1,0:T(8,128)(2,1)S(1)} %get-tuple-element.78), channel_id=1, source_target_pairs={{0,1},{1,0},{2,3},{3,2},{4,5},{5,4},{6,7},{7,6},{8,9},{9,8},{10,11... | collective-permute-start | bytes 6291464 | tf_op jit(solution)/shard_map/ppermute | solution.py:466
  107.0 6.7 %collective-permute-start.19 = (bf16[16,4096]{1,0:T(8,128)(2,1)S(1)}, bf16[16,4096]{1,0:T(8,128)(2,1)S(1)}, u32[]{:S(2)}, u32[]{:S(2)}) collective-permute-start(bf16[16,4096]{1,0:T(8,128)(2,1)S(1)} %get-tuple-element.80.rest_2_), channel_id=1, source_target_pairs={{0,4},{1,5},{4,8},{5,9},{8,12},{9,13},{12,14},{13,15},{14,10},{15,... | collective-permute-start | bytes 393224 | tf_op jit(solution)/shard_map/ppermute | solution.py:460
  114.0 7.9 %collective-permute-start.21 = (bf16[32,4096]{1,0:T(8,128)(2,1)S(1)}, bf16[32,4096]{1,0:T(8,128)(2,1)S(1)}, u32[]{:S(2)}, u32[]{:S(2)}) collective-permute-start(bf16[32,4096]{1,0:T(8,128)(2,1)S(1)} %get-tuple-element.85.rest_2_), channel_id=1, source_target_pairs={{0,4},{1,5},{4,8},{5,9},{8,12},{9,13},{12,14},{13,15},{14,10},{15,... | collective-permute-start | bytes 786440 | tf_op jit(solution)/shard_map/ppermute | solution.py:460
  115.6 7.3 %collective-permute-start.22 = (bf16[32,4096]{1,0:T(8,128)(2,1)S(1)}, bf16[32,4096]{1,0:T(8,128)(2,1)S(1)}, u32[]{:S(2)}, u32[]{:S(2)}) collective-permute-start(bf16[32,4096]{1,0:T(8,128)(2,1)S(1)} %get-tuple-element.86.rest_3_), channel_id=1, source_target_pairs={{4,0},{5,1},{8,4},{9,5},{12,8},{13,9},{14,12},{15,13},{10,14},{11,... | collective-permute-start | bytes 786440 | tf_op jit(solution)/shard_map/ppermute | solution.py:463
  123.1 7.9 %collective-permute-start.23 = (bf16[32,4096]{1,0:T(8,128)(2,1)S(1)}, bf16[32,4096]{1,0:T(8,128)(2,1)S(1)}, u32[]{:S(2)}, u32[]{:S(2)}) collective-permute-start(bf16[32,4096]{1,0:T(8,128)(2,1)S(1)} %get-tuple-element.90.rest_2_), channel_id=1, source_target_pairs={{0,4},{1,5},{4,8},{5,9},{8,12},{9,13},{12,14},{13,15},{14,10},{15,... | collective-permute-start | bytes 786440 | tf_op jit(solution)/shard_map/ppermute | solution.py:460
  124.8 6.4 %collective-permute-start.24 = (bf16[32,4096]{1,0:T(8,128)(2,1)S(1)}, bf16[32,4096]{1,0:T(8,128)(2,1)S(1)}, u32[]{:S(2)}, u32[]{:S(2)}) collective-permute-start(bf16[32,4096]{1,0:T(8,128)(2,1)S(1)} %get-tuple-element.91.rest_3_), channel_id=1, source_target_pairs={{4,0},{5,1},{8,4},{9,5},{12,8},{13,9},{14,12},{15,13},{10,14},{11,... | collective-permute-start | bytes 786440 | tf_op jit(solution)/shard_map/ppermute | solution.py:463
  131.3 6.4 %collective-permute-start.25 = (bf16[32,4096]{1,0:T(8,128)(2,1)S(1)}, bf16[32,4096]{1,0:T(8,128)(2,1)S(1)}, u32[]{:S(2)}, u32[]{:S(2)}) collective-permute-start(bf16[32,4096]{1,0:T(8,128)(2,1)S(1)} %get-tuple-element.95.rest_2_), channel_id=1, source_target_pairs={{0,4},{1,5},{4,8},{5,9},{8,12},{9,13},{12,14},{13,15},{14,10},{15,... | collective-permute-start | bytes 786440 | tf_op jit(solution)/shard_map/ppermute | solution.py:460
  133.0 6.4 %collective-permute-start.26 = (bf16[32,4096]{1,0:T(8,128)(2,1)S(1)}, bf16[32,4096]{1,0:T(8,128)(2,1)S(1)}, u32[]{:S(2)}, u32[]{:S(2)}) collective-permute-start(bf16[32,4096]{1,0:T(8,128)(2,1)S(1)} %get-tuple-element.96.rest_3_), channel_id=1, source_target_pairs={{4,0},{5,1},{8,4},{9,5},{12,8},{13,9},{14,12},{15,13},{10,14},{11,... | collective-permute-start | bytes 786440 | tf_op jit(solution)/shard_map/ppermute | solution.py:463
  (9 other events, 83.8 us)

commit v12 on v10

--- a/solution.py
+++ b/solution.py
@@ -348,7 +348,7 @@
             pltpu.SemaphoreType.DMA((2, 2)),
             pltpu.SemaphoreType.DMA((2, len(a))),
         ],
-        compiler_params=params(28),
+        compiler_params=params(26),
         cost_estimate=cost(12 * rows * depth * width, 6 * depth * width),
         name="hidden_back",
     )(spot, near, far, head, wg, wu, wd, *a, *b)
@@ -484,7 +484,7 @@
     cuts = [0, 2, 5, 7]
 
     def piece(i, head, after):
-        grant = (30, 28, 28)[i]
+        grant = (30, 28, 26)[i]
         count = cuts[i + 1] - cuts[i]
         a, b, head = gate_up(
             near_x, far_x, head, wg, wu, wd, cuts[i], count, lane, grant, after
@@ -508,17 +508,17 @@
     in_dy.append(both(*in_dy[-1], some, True))
     some, head = piece(1, head, in_dy[-2])
     factors.append(some)
-    x = arrange(spot, near_x, far_x, in_dy[-2])
-    near_dy = pack_turned(blocks(own_dy, in_dy), (x, *some))
+    near_dy = pack_turned(blocks(own_dy, in_dy), some)
     far_dy = swap(near_dy)
     some, head = piece(2, head, (near_dy,))
     factors.append(some)
     gg, gu, own, sent = back(spot, near_dy, far_dy, head, wg, wu, wd, factors)
+    x = arrange(spot, near_x, far_x, (own,))
 
     near = swap(sent)
     full, head, tail = pl.ds(0, row), pl.ds(0, row // 2), pl.ds(row // 2, row // 2)
     step = 256
-    counts = [4, 2, 4, 4, 2]
+    counts = [2, 3, 4, 4, 3]
     held, first = (), 0
     r = l = None
     ready = ()

time: 139 us -> 134 us (0.964)
  local copies, waits for them, and re-layouts: 9.06 us -> 6.16 us
  waiting for transfers between devices: 23.6 us -> 22 us
    unnamed x20 -> x16, local copies, waits for them, and re-layouts: 7.8 us -> 4.89 us
  transfers between devices with their start and end apart: 27 -> 27, of which waited for: 16 -> 15; matrix products, arithmetic and copies ran while one was open for 1% -> 1% of each run, Pallas kernels for 34% -> 35%
where the time goes in v12:
time: 134 us
  Pallas kernels  78.1 us (58%)
  starting transfers between devices  26.4 us (20%)
  waiting for transfers between devices  22 us (16%)
  local copies, waits for them, and re-layouts  6.16 us (5%)
    pallas_call x1, Pallas kernels, back(): pl.pallas_call(functools.partial(back_kernel, step, 512, len(a)), in_spec...  28.8 us
    pallas_call x5, Pallas kernels, fisher(): pl.pallas_call(functools.partial(fisher_kernel, tile(width, 256)), grid=(...  24.1 us
    ppermute x12, starting transfers between devices, right(): return lax.ppermute(value, 'hid', to_right)  20.4 us
    pallas_call x3, Pallas kernels, gate_up(): pl.pallas_call(functools.partial(gate_up_kernel, first, step), in_specs=h...  19.9 us
    ppermute x12, waiting for transfers between devices, left(): return lax.ppermute(value, 'hid', to_left)  11.4 us
    ppermute x12, waiting for transfers between devices, right(): return lax.ppermute(value, 'hid', to_right)  8.49 us
    ppermute x12, starting transfers between devices, left(): return lax.ppermute(value, 'hid', to_left)  5.32 us
    unnamed x16, local copies, waits for them, and re-layouts  4.89 us
  transfers between devices with their start and end apart: 27, of which 15 were waited for; matrix products, arithmetic and copies ran while one was open for 1% of the time, Pallas kernels for 35%

profile of v12, /device:TPU:0, one launch (start us, length us, event | category | flops | bytes accessed | tf_op | source)
XLA Modules:
  0.0 134.2 jit_solution(9297761698014069274)
XLA Ops:
  0.6 3.1 %collective-permute-start = (bf16[32,4096]{1,0:T(8,128)(2,1)}, bf16[32,4096]{1,0:T(8,128)(2,1)S(1)}, u32[]{:S(2)}, u32[]{:S(2)}) collective-permute-start(bf16[32,4096]{1,0:T(8,128)(2,1)} %x_ref.1), channel_id=1, source_target_pairs={{0,4},{1,5},{4,8},{5,9},{8,12},{9,13},{12,14},{13,15},{14,10},{15,... | collective-permute-start | bytes 786440 | tf_op jit(solution)/shard_map/ppermute | solution.py:458
  5.6 2.3 %bring.1 = (bf16[32,4096]{1,0:T(8,128)(2,1)S(1)}, bf16[32,4096]{1,0:T(8,128)(2,1)S(1)}, bf16[2,4096,256]{2,1,0:T(8,128)(2,1)S(1)}) custom-call(bf16[32,4096]{1,0:T(8,128)(2,1)S(1)} %copy-done.3, bf16[32,4096]{1,0:T(8,128)(2,1)S(1)} %copy-done.2, bf16[4096,1792]{1,0:T(8,128)(2,1)} %wg_ref.9, bf16[4096,1792]{1,0:T(8,128)(2,1)} %wu_ref.9), custom_call_target="tpu_custom_call" | custom-call | bytes 4194304 | tf_op jit(solution)/shard_map/bring/pallas_call | solution.py:61
  7.9 2.0 %copy-done = bf16[2,4096,256]{2,1,0:T(8,128)(2,1)} copy-done((bf16[2,4096,256]{2,1,0:T(8,128)(2,1)}, bf16[2,4096,256]{2,1,0:T(8,128)(2,1)S(1)}, u32[]{:S(2)}) %copy-start) | copy-done | bytes 4194328
  11.7 1.6 %collective-permute-start.2 = (bf16[32,4096]{1,0:T(8,128)(2,1)S(1)}, bf16[32,4096]{1,0:T(8,128)(2,1)S(1)}, u32[]{:S(2)}, u32[]{:S(2)}) collective-permute-start(bf16[32,4096]{1,0:T(8,128)(2,1)S(1)} %collective-permute-done.refs_1_), channel_id=1, source_target_pairs={{0,4},{1,5},{4,8},{5,9},{8,12},{9,13},{12,14},{13,15},{14,10},{15,... | collective-permute-start | bytes 786440 | tf_op jit(solution)/shard_map/ppermute | solution.py:458
  13.7 1.6 %collective-permute-start.6 = (bf16[32,4096]{1,0:T(8,128)(2,1)S(1)}, bf16[32,4096]{1,0:T(8,128)(2,1)S(1)}, u32[]{:S(2)}, u32[]{:S(2)}) collective-permute-start(bf16[32,4096]{1,0:T(8,128)(2,1)S(1)} %get-tuple-element.67.refs_0_), channel_id=1, source_target_pairs={{0,4},{1,5},{4,8},{5,9},{8,12},{9,13},{12,14},{13,15},{14,10},{15,... | collective-permute-start | bytes 786440 | tf_op jit(solution)/shard_map/ppermute | solution.py:458
  15.7 5.2 %collective-permute-done.2.refs_2_ = bf16[32,4096]{1,0:T(8,128)(2,1)S(1)} collective-permute-done((bf16[32,4096]{1,0:T(8,128)(2,1)S(1)}, bf16[32,4096]{1,0:T(8,128)(2,1)S(1)}, u32[]{:S(2)}, u32[]{:S(2)}) %collective-permute-start.2) | collective-permute-done | bytes 262176 | tf_op jit(solution)/shard_map/ppermute | solution.py:458
  20.9 1.6 %collective-permute-done.3.refs_7_ = bf16[32,4096]{1,0:T(8,128)(2,1)S(1)} collective-permute-done((bf16[32,4096]{1,0:T(8,128)(2,1)S(1)}, bf16[32,4096]{1,0:T(8,128)(2,1)S(1)}, u32[]{:S(2)}, u32[]{:S(2)}) %collective-permute-start.3) | collective-permute-done | bytes 262176 | tf_op jit(solution)/shard_map/ppermute | solution.py:461
  22.5 1.6 %collective-permute-start.4 = (bf16[32,4096]{1,0:T(8,128)(2,1)S(1)}, bf16[32,4096]{1,0:T(8,128)(2,1)S(1)}, u32[]{:S(2)}, u32[]{:S(2)}) collective-permute-start(bf16[32,4096]{1,0:T(8,128)(2,1)S(1)} %collective-permute-done.2.refs_2_), channel_id=1, source_target_pairs={{0,4},{1,5},{4,8},{5,9},{8,12},{9,13},{12,14},{13,15},{14,10},{15,... | collective-permute-start | bytes 786440 | tf_op jit(solution)/shard_map/ppermute | solution.py:458
  26.6 1.6 %collective-permute-done.7.refs_8_ = bf16[32,4096]{1,0:T(8,128)(2,1)S(1)} collective-permute-done((bf16[32,4096]{1,0:T(8,128)(2,1)S(1)}, bf16[32,4096]{1,0:T(8,128)(2,1)S(1)}, u32[]{:S(2)}, u32[]{:S(2)}) %collective-permute-start.7) | collective-permute-done | bytes 262176 | tf_op jit(solution)/shard_map/ppermute | solution.py:461
  28.1 1.6 %collective-permute-start.10 = (bf16[32,4096]{1,0:T(8,128)(2,1)S(1)}, bf16[32,4096]{1,0:T(8,128)(2,1)S(1)}, u32[]{:S(2)}, u32[]{:S(2)}) collective-permute-start(bf16[32,4096]{1,0:T(8,128)(2,1)S(1)} %collective-permute-done.6.refs_1_), channel_id=1, source_target_pairs={{0,4},{1,5},{4,8},{5,9},{8,12},{9,13},{12,14},{13,15},{14,10},{15,... | collective-permute-start | bytes 786440 | tf_op jit(solution)/shard_map/ppermute | solution.py:458
  32.2 1.6 %collective-permute-done.5.refs_6_ = bf16[32,4096]{1,0:T(8,128)(2,1)S(1)} collective-permute-done((bf16[32,4096]{1,0:T(8,128)(2,1)S(1)}, bf16[32,4096]{1,0:T(8,128)(2,1)S(1)}, u32[]{:S(2)}, u32[]{:S(2)}) %collective-permute-start.5) | collective-permute-done | bytes 262176 | tf_op jit(solution)/shard_map/ppermute | solution.py:461
  34.3 1.6 %collective-permute-start.8 = (bf16[16,4096]{1,0:T(8,128)(2,1)S(1)}, bf16[16,4096]{1,0:T(8,128)(2,1)S(1)}, u32[]{:S(2)}, u32[]{:S(2)}) collective-permute-start(bf16[16,4096]{1,0:T(8,128)(2,1)S(1)} %slice.12), channel_id=1, source_target_pairs={{0,4},{1,5},{4,8},{5,9},{8,12},{9,13},{12,14},{13,15},{14,10},{15,... | collective-permute-start | bytes 393224 | tf_op jit(solution)/shard_map/ppermute | solution.py:458
  39.7 1.6 %collective-permute-start.13 = (bf16[32,4096]{1,0:T(8,128)(2,1)S(1)}, bf16[32,4096]{1,0:T(8,128)(2,1)S(1)}, u32[]{:S(2)}, u32[]{:S(2)}) collective-permute-start(bf16[32,4096]{1,0:T(8,128)(2,1)S(1)} %collective-permute-done.10.refs_10_.rest_0_.refs_2_), channel_id=1, source_target_pairs={{0,4},{1,5},{4,8},{5,9},{8,12},{9,13},{12,14},{13,15},{14,10},{15,... | collective-permute-start | bytes 786440 | tf_op jit(solution)/shard_map/ppermute | solution.py:458
  41.8 2.1 %collective-permute-done.12.far_ref = bf16[256,4096]{1,0:T(8,128)(2,1)S(1)} collective-permute-done((bf16[256,4096]{1,0:T(8,128)(2,1)S(1)}, bf16[256,4096]{1,0:T(8,128)(2,1)S(1)}, u32[]{:S(2)}, u32[]{:S(2)}) %collective-permute-start.12) | collective-permute-done | bytes 2097184 | tf_op jit(solution)/shard_map/ppermute | solution.py:464
  43.9 6.5 %gate_up.3 = (f32[512,512]{1,0:T(8,128)S(1)}, f32[512,512]{1,0:T(8,128)S(1)}, bf16[2,4096,256]{2,1,0:T(8,128)(2,1)S(1)}) custom-call(bf16[256,4096]{1,0:T(8,128)(2,1)S(1)} %pack.1.near_ref, bf16[256,4096]{1,0:T(8,128)(2,1)S(1)} %collective-permute-done.12.far_ref, bf16[2,4096,256]{2,1,0:T(8,128)(2,1)S(1)} %copy-done.1, bf16[4096,1792]{1,0:T(8,128)(2,1)} %wg_ref.9, ...), custom_call_target="tpu_custom_call" | custom-call | flops 4294967296 | bytes 8388608 | tf_op jit(solution)/shard_map/gate_up/pallas_call | solution.py:216
  53.4 8.1 %gate_up.4 = (f32[768,512]{1,0:T(8,128)S(1)}, f32[768,512]{1,0:T(8,128)S(1)}, bf16[2,4096,256]{2,1,0:T(8,128)(2,1)S(1)}) custom-call(bf16[256,4096]{1,0:T(8,128)(2,1)S(1)} %pack.1.near_ref, bf16[256,4096]{1,0:T(8,128)(2,1)S(1)} %collective-permute-done.12.far_ref, bf16[2,4096,256]{2,1,0:T(8,128)(2,1)S(1)} %get-tuple-element.78.head_ref, ...), custom_call_target="tpu_custom_call" | custom-call | flops 6442450944 | bytes 12582912 | tf_op jit(solution)/shard_map/gate_up/pallas_call | solution.py:216
  62.3 5.3 %gate_up.5 = (f32[512,512]{1,0:T(8,128)S(1)}, f32[512,512]{1,0:T(8,128)S(1)}, bf16[256,4096]{1,0:T(8,128)(2,1)S(1)}) custom-call(bf16[256,4096]{1,0:T(8,128)(2,1)S(1)} %pack.1.near_ref, bf16[256,4096]{1,0:T(8,128)(2,1)S(1)} %collective-permute-done.12.far_ref, bf16[2,4096,256]{2,1,0:T(8,128)(2,1)S(1)} %get-tuple-element.81.head_ref, ...), custom_call_target="tpu_custom_call" | custom-call | flops 4294967296 | bytes 8388608 | tf_op jit(solution)/shard_map/gate_up/pallas_call | solution.py:216
  67.6 28.8 %hidden_back.1 = (bf16[512,1792]{1,0:T(8,128)(2,1)S(1)}, bf16[512,1792]{1,0:T(8,128)(2,1)S(1)}, bf16[256,4096]{1,0:T(8,128)(2,1)S(1)}, bf16[256,4096]{1,0:T(8,128)(2,1)S(1)}) custom-call(s32[8]{0:T(128)S(1)} %fusion.3.refs_9_.spot_ref, bf16[4096,256]{1,0:T(8,128)(2,1)S(1)} %pack_turned.1.rest_0_.near_ref, ...), custom_call_target="tpu_custom_call" | custom-call | flops 22548578304 | bytes 44040192 | tf_op jit(solution)/shard_map/hidden_back/pallas_call | solution.py:333
  97.9 3.4 %fisher.5 = (bf16[4096,1792]{1,0:T(8,128)(2,1)}, bf16[4096,1792]{1,0:T(8,128)(2,1)}, f32[8,128]{1,0:T(8,128)S(1)}) custom-call(bf16[512,4096]{1,0:T(8,128)(2,1)S(1)} %arrange.1.x_ref, bf16[512,1792]{1,0:T(8,128)(2,1)S(1)} %get-tuple-element.86.gg_ref, bf16[512,1792]{1,0:T(8,128)(2,1)S(1)} %get-tuple-element.87.gu_ref), custom_call_target="tpu_custom_call" | custom-call | flops 1879048192 | bytes 3670016 | tf_op jit(solution)/shard_map/fisher/pallas_call | solution.py:431
  101.3 1.6 %collective-permute-start.19 = (bf16[16,4096]{1,0:T(8,128)(2,1)S(1)}, bf16[16,4096]{1,0:T(8,128)(2,1)S(1)}, u32[]{:S(2)}, u32[]{:S(2)}) collective-permute-start(bf16[16,4096]{1,0:T(8,128)(2,1)S(1)} %get-tuple-element.92.rest_2_), channel_id=1, source_target_pairs={{0,4},{1,5},{4,8},{5,9},{8,12},{9,13},{12,14},{13,15},{14,10},{15,... | collective-permute-start | bytes 393224 | tf_op jit(solution)/shard_map/ppermute | solution.py:458
  103.4 4.6 %fisher.6 = (bf16[4096,1792]{1,0:T(8,128)(2,1)}, bf16[4096,1792]{1,0:T(8,128)(2,1)}, f32[8,128]{1,0:T(8,128)S(1)}) custom-call(bf16[512,4096]{1,0:T(8,128)(2,1)S(1)} %arrange.1.x_ref, bf16[512,1792]{1,0:T(8,128)(2,1)S(1)} %get-tuple-element.86.gg_ref, bf16[512,1792]{1,0:T(8,128)(2,1)S(1)} %get-tuple-element.87.gu_ref, ...), custom_call_target="tpu_custom_call", output_to_operand_aliasing={{0}: (3, {}), {1}: (4, {})} | custom-call | flops 2818572288 | bytes 5505024 | tf_op jit(solution)/shard_map/fisher/pallas_call | solution.py:431
  110.3 5.8 %fisher.7 = (bf16[4096,1792]{1,0:T(8,128)(2,1)}, bf16[4096,1792]{1,0:T(8,128)(2,1)}, f32[8,128]{1,0:T(8,128)S(1)}) custom-call(bf16[512,4096]{1,0:T(8,128)(2,1)S(1)} %arrange.1.x_ref, bf16[512,1792]{1,0:T(8,128)(2,1)S(1)} %get-tuple-element.86.gg_ref, bf16[512,1792]{1,0:T(8,128)(2,1)S(1)} %get-tuple-element.87.gu_ref, ...), custom_call_target="tpu_custom_call", output_to_operand_aliasing={{0}: (3, {}), {1}: (4, {})} | custom-call | flops 3758096384 | bytes 7340032 | tf_op jit(solution)/shard_map/fisher/pallas_call | solution.py:431
  119.4 5.8 %fisher.8 = (bf16[4096,1792]{1,0:T(8,128)(2,1)}, bf16[4096,1792]{1,0:T(8,128)(2,1)}, f32[8,128]{1,0:T(8,128)S(1)}) custom-call(bf16[512,4096]{1,0:T(8,128)(2,1)S(1)} %arrange.1.x_ref, bf16[512,1792]{1,0:T(8,128)(2,1)S(1)} %get-tuple-element.86.gg_ref, bf16[512,1792]{1,0:T(8,128)(2,1)S(1)} %get-tuple-element.87.gu_ref, ...), custom_call_target="tpu_custom_call", output_to_operand_aliasing={{0}: (3, {}), {1}: (4, {})} | custom-call | flops 3758096384 | bytes 7340032 | tf_op jit(solution)/shard_map/fisher/pallas_call | solution.py:431
  127.6 4.6 %fisher.9 = (bf16[4096,1792]{1,0:T(8,128)(2,1)}, bf16[4096,1792]{1,0:T(8,128)(2,1)}, f32[8,128]{1,0:T(8,128)}) custom-call(bf16[512,4096]{1,0:T(8,128)(2,1)S(1)} %arrange.1.x_ref, bf16[512,1792]{1,0:T(8,128)(2,1)S(1)} %get-tuple-element.86.gg_ref, bf16[512,1792]{1,0:T(8,128)(2,1)S(1)} %get-tuple-element.87.gu_ref, ...), custom_call_target="tpu_custom_call", output_to_operand_aliasing={{0}: (3, {}), {1}: (4, {})} | custom-call | flops 2818572288 | bytes 5505024 | tf_op jit(solution)/shard_map/fisher/pallas_call | solution.py:431
  (73 shorter events, 30.0 us)
Async XLA Ops:
  0.6 9.5 %collective-permute-start = (bf16[32,4096]{1,0:T(8,128)(2,1)}, bf16[32,4096]{1,0:T(8,128)(2,1)S(1)}, u32[]{:S(2)}, u32[]{:S(2)}) collective-permute-start(bf16[32,4096]{1,0:T(8,128)(2,1)} %x_ref.1), channel_id=1, source_target_pairs={{0,4},{1,5},{4,8},{5,9},{8,12},{9,13},{12,14},{13,15},{14,10},{15,... | collective-permute-start | bytes 786440 | tf_op jit(solution)/shard_map/ppermute | solution.py:458
  3.7 8.0 %collective-permute-start.1 = (bf16[32,4096]{1,0:T(8,128)(2,1)}, bf16[32,4096]{1,0:T(8,128)(2,1)S(1)}, u32[]{:S(2)}, u32[]{:S(2)}) collective-permute-start(bf16[32,4096]{1,0:T(8,128)(2,1)} %x_ref.1), channel_id=1, source_target_pairs={{4,0},{5,1},{8,4},{9,5},{12,8},{13,9},{14,12},{15,13},{10,14},{11,... | collective-permute-start | bytes 786440 | tf_op jit(solution)/shard_map/ppermute | solution.py:461
  11.7 9.2 %collective-permute-start.2 = (bf16[32,4096]{1,0:T(8,128)(2,1)S(1)}, bf16[32,4096]{1,0:T(8,128)(2,1)S(1)}, u32[]{:S(2)}, u32[]{:S(2)}) collective-permute-start(bf16[32,4096]{1,0:T(8,128)(2,1)S(1)} %collective-permute-done.refs_1_), channel_id=1, source_target_pairs={{0,4},{1,5},{4,8},{5,9},{8,12},{9,13},{12,14},{13,15},{14,10},{15,... | collective-permute-start | bytes 786440 | tf_op jit(solution)/shard_map/ppermute | solution.py:458
  13.3 9.2 %collective-permute-start.3 = (bf16[32,4096]{1,0:T(8,128)(2,1)S(1)}, bf16[32,4096]{1,0:T(8,128)(2,1)S(1)}, u32[]{:S(2)}, u32[]{:S(2)}) collective-permute-start(bf16[32,4096]{1,0:T(8,128)(2,1)S(1)} %collective-permute-done.1.refs_8_), channel_id=1, source_target_pairs={{4,0},{5,1},{8,4},{9,5},{12,8},{13,9},{14,12},{15,13},{10,14},{11,... | collective-permute-start | bytes 786440 | tf_op jit(solution)/shard_map/ppermute | solution.py:461
  13.7 12.8 %collective-permute-start.6 = (bf16[32,4096]{1,0:T(8,128)(2,1)S(1)}, bf16[32,4096]{1,0:T(8,128)(2,1)S(1)}, u32[]{:S(2)}, u32[]{:S(2)}) collective-permute-start(bf16[32,4096]{1,0:T(8,128)(2,1)S(1)} %get-tuple-element.67.refs_0_), channel_id=1, source_target_pairs={{0,4},{1,5},{4,8},{5,9},{8,12},{9,13},{12,14},{13,15},{14,10},{15,... | collective-permute-start | bytes 786440 | tf_op jit(solution)/shard_map/ppermute | solution.py:458
  15.3 12.8 %collective-permute-start.7 = (bf16[32,4096]{1,0:T(8,128)(2,1)S(1)}, bf16[32,4096]{1,0:T(8,128)(2,1)S(1)}, u32[]{:S(2)}, u32[]{:S(2)}) collective-permute-start(bf16[32,4096]{1,0:T(8,128)(2,1)S(1)} %get-tuple-element.67.refs_0_), channel_id=1, source_target_pairs={{4,0},{5,1},{8,4},{9,5},{12,8},{13,9},{14,12},{15,13},{10,14},{11,... | collective-permute-start | bytes 786440 | tf_op jit(solution)/shard_map/ppermute | solution.py:461
  22.5 9.7 %collective-permute-start.4 = (bf16[32,4096]{1,0:T(8,128)(2,1)S(1)}, bf16[32,4096]{1,0:T(8,128)(2,1)S(1)}, u32[]{:S(2)}, u32[]{:S(2)}) collective-permute-start(bf16[32,4096]{1,0:T(8,128)(2,1)S(1)} %collective-permute-done.2.refs_2_), channel_id=1, source_target_pairs={{0,4},{1,5},{4,8},{5,9},{8,12},{9,13},{12,14},{13,15},{14,10},{15,... | collective-permute-start | bytes 786440 | tf_op jit(solution)/shard_map/ppermute | solution.py:458
  24.1 9.7 %collective-permute-start.5 = (bf16[32,4096]{1,0:T(8,128)(2,1)S(1)}, bf16[32,4096]{1,0:T(8,128)(2,1)S(1)}, u32[]{:S(2)}, u32[]{:S(2)}) collective-permute-start(bf16[32,4096]{1,0:T(8,128)(2,1)S(1)} %collective-permute-done.3.refs_7_), channel_id=1, source_target_pairs={{4,0},{5,1},{8,4},{9,5},{12,8},{13,9},{14,12},{15,13},{10,14},{11,... | collective-permute-start | bytes 786440 | tf_op jit(solution)/shard_map/ppermute | solution.py:461
  28.1 8.7 %collective-permute-start.10 = (bf16[32,4096]{1,0:T(8,128)(2,1)S(1)}, bf16[32,4096]{1,0:T(8,128)(2,1)S(1)}, u32[]{:S(2)}, u32[]{:S(2)}) collective-permute-start(bf16[32,4096]{1,0:T(8,128)(2,1)S(1)} %collective-permute-done.6.refs_1_), channel_id=1, source_target_pairs={{0,4},{1,5},{4,8},{5,9},{8,12},{9,13},{12,14},{13,15},{14,10},{15,... | collective-permute-start | bytes 786440 | tf_op jit(solution)/shard_map/ppermute | solution.py:458
  29.7 8.4 %collective-permute-start.11 = (bf16[32,4096]{1,0:T(8,128)(2,1)S(1)}, bf16[32,4096]{1,0:T(8,128)(2,1)S(1)}, u32[]{:S(2)}, u32[]{:S(2)}) collective-permute-start(bf16[32,4096]{1,0:T(8,128)(2,1)S(1)} %collective-permute-done.7.refs_8_), channel_id=1, source_target_pairs={{4,0},{5,1},{8,4},{9,5},{12,8},{13,9},{14,12},{15,13},{10,14},{11,... | collective-permute-start | bytes 786440 | tf_op jit(solution)/shard_map/ppermute | solution.py:461
  33.8 5.7 %collective-permute-start.9 = (bf16[16,4096]{1,0:T(8,128)(2,1)S(1)}, bf16[16,4096]{1,0:T(8,128)(2,1)S(1)}, u32[]{:S(2)}, u32[]{:S(2)}) collective-permute-start(bf16[16,4096]{1,0:T(8,128)(2,1)S(1)} %slice.13), channel_id=1, source_target_pairs={{4,0},{5,1},{8,4},{9,5},{12,8},{13,9},{14,12},{15,13},{10,14},{11,... | collective-permute-start | bytes 393224 | tf_op jit(solution)/shard_map/ppermute | solution.py:461
  34.3 5.2 %collective-permute-start.8 = (bf16[16,4096]{1,0:T(8,128)(2,1)S(1)}, bf16[16,4096]{1,0:T(8,128)(2,1)S(1)}, u32[]{:S(2)}, u32[]{:S(2)}) collective-permute-start(bf16[16,4096]{1,0:T(8,128)(2,1)S(1)} %slice.12), channel_id=1, source_target_pairs={{0,4},{1,5},{4,8},{5,9},{8,12},{9,13},{12,14},{13,15},{14,10},{15,... | collective-permute-start | bytes 393224 | tf_op jit(solution)/shard_map/ppermute | solution.py:458
  39.7 11.6 %collective-permute-start.13 = (bf16[32,4096]{1,0:T(8,128)(2,1)S(1)}, bf16[32,4096]{1,0:T(8,128)(2,1)S(1)}, u32[]{:S(2)}, u32[]{:S(2)}) collective-permute-start(bf16[32,4096]{1,0:T(8,128)(2,1)S(1)} %collective-permute-done.10.refs_10_.rest_0_.refs_2_), channel_id=1, source_target_pairs={{0,4},{1,5},{4,8},{5,9},{8,12},{9,13},{12,14},{13,15},{14,10},{15,... | collective-permute-start | bytes 786440 | tf_op jit(solution)/shard_map/ppermute | solution.py:458
  41.4 10.0 %collective-permute-start.14 = (bf16[32,4096]{1,0:T(8,128)(2,1)S(1)}, bf16[32,4096]{1,0:T(8,128)(2,1)S(1)}, u32[]{:S(2)}, u32[]{:S(2)}) collective-permute-start(bf16[32,4096]{1,0:T(8,128)(2,1)S(1)} %collective-permute-done.11.refs_11_.rest_1_.refs_7_), channel_id=1, source_target_pairs={{4,0},{5,1},{8,4},{9,5},{12,8},{13,9},{14,12},{15,13},{10,14},{11,... | collective-permute-start | bytes 786440 | tf_op jit(solution)/shard_map/ppermute | solution.py:461
  51.4 10.2 %collective-permute-start.16 = (bf16[16,4096]{1,0:T(8,128)(2,1)S(1)}, bf16[16,4096]{1,0:T(8,128)(2,1)S(1)}, u32[]{:S(2)}, u32[]{:S(2)}) collective-permute-start(bf16[16,4096]{1,0:T(8,128)(2,1)S(1)} %slice.15), channel_id=1, source_target_pairs={{4,0},{5,1},{8,4},{9,5},{12,8},{13,9},{14,12},{15,13},{10,14},{11,... | collective-permute-start | bytes 393224 | tf_op jit(solution)/shard_map/ppermute | solution.py:461
  51.9 9.7 %collective-permute-start.15 = (bf16[16,4096]{1,0:T(8,128)(2,1)S(1)}, bf16[16,4096]{1,0:T(8,128)(2,1)S(1)}, u32[]{:S(2)}, u32[]{:S(2)}) collective-permute-start(bf16[16,4096]{1,0:T(8,128)(2,1)S(1)} %slice.14), channel_id=1, source_target_pairs={{0,4},{1,5},{4,8},{5,9},{8,12},{9,13},{12,14},{13,15},{14,10},{15,... | collective-permute-start | bytes 393224 | tf_op jit(solution)/shard_map/ppermute | solution.py:458
  62.2 5.4 %collective-permute-start.17 = (bf16[4096,256]{1,0:T(8,128)(2,1)S(1)}, bf16[4096,256]{1,0:T(8,128)(2,1)S(1)}, u32[]{:S(2)}, u32[]{:S(2)}) collective-permute-start(bf16[4096,256]{1,0:T(8,128)(2,1)S(1)} %pack_turned.1.rest_0_.near_ref), channel_id=1, source_target_pairs={{0,1},{1,0},{2,3},{3,2},{4,5},{5,4},{6,7},{7,6},{8,9},{9,8},{10,11... | collective-permute-start | bytes 6291464 | tf_op jit(solution)/shard_map/ppermute | solution.py:464
  101.3 6.7 %collective-permute-start.19 = (bf16[16,4096]{1,0:T(8,128)(2,1)S(1)}, bf16[16,4096]{1,0:T(8,128)(2,1)S(1)}, u32[]{:S(2)}, u32[]{:S(2)}) collective-permute-start(bf16[16,4096]{1,0:T(8,128)(2,1)S(1)} %get-tuple-element.92.rest_2_), channel_id=1, source_target_pairs={{0,4},{1,5},{4,8},{5,9},{8,12},{9,13},{12,14},{13,15},{14,10},{15,... | collective-permute-start | bytes 393224 | tf_op jit(solution)/shard_map/ppermute | solution.py:458
  108.3 7.9 %collective-permute-start.21 = (bf16[32,4096]{1,0:T(8,128)(2,1)S(1)}, bf16[32,4096]{1,0:T(8,128)(2,1)S(1)}, u32[]{:S(2)}, u32[]{:S(2)}) collective-permute-start(bf16[32,4096]{1,0:T(8,128)(2,1)S(1)} %get-tuple-element.97.rest_2_), channel_id=1, source_target_pairs={{0,4},{1,5},{4,8},{5,9},{8,12},{9,13},{12,14},{13,15},{14,10},{15,... | collective-permute-start | bytes 786440 | tf_op jit(solution)/shard_map/ppermute | solution.py:458
  109.8 7.4 %collective-permute-start.22 = (bf16[32,4096]{1,0:T(8,128)(2,1)S(1)}, bf16[32,4096]{1,0:T(8,128)(2,1)S(1)}, u32[]{:S(2)}, u32[]{:S(2)}) collective-permute-start(bf16[32,4096]{1,0:T(8,128)(2,1)S(1)} %get-tuple-element.98.rest_3_), channel_id=1, source_target_pairs={{4,0},{5,1},{8,4},{9,5},{12,8},{13,9},{14,12},{15,13},{10,14},{11,... | collective-permute-start | bytes 786440 | tf_op jit(solution)/shard_map/ppermute | solution.py:461
  117.4 7.9 %collective-permute-start.23 = (bf16[32,4096]{1,0:T(8,128)(2,1)S(1)}, bf16[32,4096]{1,0:T(8,128)(2,1)S(1)}, u32[]{:S(2)}, u32[]{:S(2)}) collective-permute-start(bf16[32,4096]{1,0:T(8,128)(2,1)S(1)} %get-tuple-element.102.rest_2_), channel_id=1, source_target_pairs={{0,4},{1,5},{4,8},{5,9},{8,12},{9,13},{12,14},{13,15},{14,10},{15,... | collective-permute-start | bytes 786440 | tf_op jit(solution)/shard_map/ppermute | solution.py:458
  118.9 6.4 %collective-permute-start.24 = (bf16[32,4096]{1,0:T(8,128)(2,1)S(1)}, bf16[32,4096]{1,0:T(8,128)(2,1)S(1)}, u32[]{:S(2)}, u32[]{:S(2)}) collective-permute-start(bf16[32,4096]{1,0:T(8,128)(2,1)S(1)} %get-tuple-element.103.rest_3_), channel_id=1, source_target_pairs={{4,0},{5,1},{8,4},{9,5},{12,8},{13,9},{14,12},{15,13},{10,14},{11,... | collective-permute-start | bytes 786440 | tf_op jit(solution)/shard_map/ppermute | solution.py:461
  125.5 6.7 %collective-permute-start.25 = (bf16[32,4096]{1,0:T(8,128)(2,1)S(1)}, bf16[32,4096]{1,0:T(8,128)(2,1)S(1)}, u32[]{:S(2)}, u32[]{:S(2)}) collective-permute-start(bf16[32,4096]{1,0:T(8,128)(2,1)S(1)} %get-tuple-element.107.rest_2_), channel_id=1, source_target_pairs={{0,4},{1,5},{4,8},{5,9},{8,12},{9,13},{12,14},{13,15},{14,10},{15,... | collective-permute-start | bytes 786440 | tf_op jit(solution)/shard_map/ppermute | solution.py:458
  127.0 6.4 %collective-permute-start.26 = (bf16[32,4096]{1,0:T(8,128)(2,1)S(1)}, bf16[32,4096]{1,0:T(8,128)(2,1)S(1)}, u32[]{:S(2)}, u32[]{:S(2)}) collective-permute-start(bf16[32,4096]{1,0:T(8,128)(2,1)S(1)} %get-tuple-element.108.rest_3_), channel_id=1, source_target_pairs={{4,0},{5,1},{8,4},{9,5},{12,8},{13,9},{14,12},{15,13},{10,14},{11,... | collective-permute-start | bytes 786440 | tf_op jit(solution)/shard_map/ppermute | solution.py:461
  (11 other events, 85.9 us)

commit v13 on v12

--- a/solution.py
+++ b/solution.py
@@ -42,7 +42,9 @@
 def head_copies(wg_ref, wu_ref, first, step, head_ref, sems):
     cols = pl.ds(first * step, step)
     return [
-        pltpu.make_async_copy(ref.at[:, cols], head_ref.at[i], sems.at[i])
+        pltpu.make_async_copy(
+            ref.at[:, cols], head_ref.at[:, pl.ds(i * step, step)], sems.at[i]
+        )
         for i, ref in enumerate((wg_ref, wu_ref))
     ]
 
@@ -63,7 +65,7 @@
         in_specs=held_specs(2) + hbm_specs(2),
         out_specs=held_specs(3),
         out_shape=[jax.ShapeDtypeStruct(x.shape, BF16)] * 2
-        + [jax.ShapeDtypeStruct((2, wg.shape[0], step), BF16)],
+        + [jax.ShapeDtypeStruct((wg.shape[0], 2 * step), BF16)],
         scratch_shapes=[pltpu.SemaphoreType.DMA((2,))],
         compiler_params=params(46),
         cost_estimate=cost(0, 4 * wg.shape[0] * step),
@@ -168,7 +170,7 @@
         return head_copies(wg_ref, wu_ref, first + t, step, w_buf.at[slot], sems.at[slot])
 
     def fetch_next():
-        if next_ref.shape[0] == 2:
+        if next_ref.shape[0] == near_ref.shape[1]:
             return head_copies(wg_ref, wu_ref, first + tiles, step, next_ref, next_sems)
         return [pltpu.make_async_copy(wd_ref.at[pl.ds(0, step), :], next_ref, next_sems.at[0])]
 
@@ -192,12 +194,12 @@
     for t in range(tiles):
         if t:
             finish(fetch(t))
-        if t == tiles - 1:
+        if t == max(tiles - 2, 0):
             begin(fetch_next())
         w_ref = w_buf.at[t % 2] if t else head_ref
         for side, x_ref in enumerate((near_ref, far_ref)):
-            gate = jnp.dot(x_ref[...], w_ref[0], preferred_element_type=F32)
-            up = jnp.dot(x_ref[...], w_ref[1], preferred_element_type=F32)
+            both = jnp.dot(x_ref[...], w_ref[...], preferred_element_type=F32)
+            gate, up = both[:, :step], both[:, step:]
             at = pl.ds(side * rows, rows)
             sigma = jax.nn.sigmoid(gate)
             out_buf[t, 0, :, at] = (up * sigma * (1.0 + gate * (1.0 - sigma))).T
@@ -218,9 +220,9 @@
         in_specs=held_specs(3) + hbm_specs(3) + any_specs(after),
         out_specs=hbm_specs(2) + held_specs(1),
         out_shape=[jax.ShapeDtypeStruct((count * step, 2 * rows), F32)] * 2
-        + [jax.ShapeDtypeStruct((step, depth) if last else (2, depth, step), BF16)],
+        + [jax.ShapeDtypeStruct((step, depth) if last else (depth, 2 * step), BF16)],
         scratch_shapes=[
-            pltpu.VMEM((2, 2, depth, step), BF16),
+            pltpu.VMEM((2, depth, 2 * step), BF16),
             pltpu.VMEM((count, 2, step, 2 * rows), F32),
             pltpu.SemaphoreType.DMA((2, 2)),
             pltpu.SemaphoreType.DMA((count, 2)),
@@ -313,10 +315,9 @@
         slot = lax.rem(i, 2)
         for copy in fetch_rows(i):
             copy.wait()
-        for side, out_ref in enumerate((own_ref, sent_ref)):
-            of = pl.ds(side * rows, rows)
-            total = jnp.dot(w_buf[slot], g_ref[:, of], preferred_element_type=F32)
-            out_ref[:, at] = total.astype(BF16).T
+        total = jnp.dot(w_buf[slot], g_ref[...], preferred_element_type=F32)
+        own_ref[:, at] = total[:, :rows].astype(BF16).T
+        sent_ref[:, at] = total[:, rows:].astype(BF16).T
 
         @pl.when(i + 2 < blocks)
         def _():

time: 134 us -> 134 us (level)
  no operation moved by 1% of the time
where the time goes in v13:
time: 134 us
  Pallas kernels  77.9 us (58%)
  starting transfers between devices  26.4 us (20%)
  waiting for transfers between devices  21.9 us (16%)
  local copies, waits for them, and re-layouts  6.16 us (5%)
    pallas_call x1, Pallas kernels, back(): pl.pallas_call(functools.partial(back_kernel, step, 512, len(a)), in_spec...  28.8 us
    pallas_call x5, Pallas kernels, fisher(): pl.pallas_call(functools.partial(fisher_kernel, tile(width, 256)), grid=(...  24.1 us
    ppermute x12, starting transfers between devices, right(): return lax.ppermute(value, 'hid', to_right)  20.4 us
    pallas_call x3, Pallas kernels, gate_up(): pl.pallas_call(functools.partial(gate_up_kernel, first, step), in_specs=h...  19.7 us
    ppermute x12, waiting for transfers between devices, left(): return lax.ppermute(value, 'hid', to_left)  11.4 us
    ppermute x12, waiting for transfers between devices, right(): return lax.ppermute(value, 'hid', to_right)  8.49 us
    ppermute x12, starting transfers between devices, left(): return lax.ppermute(value, 'hid', to_left)  5.34 us
    unnamed x16, local copies, waits for them, and re-layouts  4.89 us
  transfers between devices with their start and end apart: 27, of which 15 were waited for; matrix products, arithmetic and copies ran while one was open for 1% of the time, Pallas kernels for 35%

profile of v13, /device:TPU:0, one launch (start us, length us, event | category | flops | bytes accessed | tf_op | source)
XLA Modules:
  0.0 134.0 jit_solution(1576632366772883348)
XLA Ops:
  0.6 3.1 %collective-permute-start = (bf16[32,4096]{1,0:T(8,128)(2,1)}, bf16[32,4096]{1,0:T(8,128)(2,1)S(1)}, u32[]{:S(2)}, u32[]{:S(2)}) collective-permute-start(bf16[32,4096]{1,0:T(8,128)(2,1)} %x_ref.1), channel_id=1, source_target_pairs={{0,4},{1,5},{4,8},{5,9},{8,12},{9,13},{12,14},{13,15},{14,10},{15,... | collective-permute-start | bytes 786440 | tf_op jit(solution)/shard_map/ppermute | solution.py:459
  5.6 2.3 %bring.1 = (bf16[32,4096]{1,0:T(8,128)(2,1)S(1)}, bf16[32,4096]{1,0:T(8,128)(2,1)S(1)}, bf16[4096,512]{1,0:T(8,128)(2,1)S(1)}) custom-call(bf16[32,4096]{1,0:T(8,128)(2,1)S(1)} %copy-done.3, bf16[32,4096]{1,0:T(8,128)(2,1)S(1)} %copy-done.2, bf16[4096,1792]{1,0:T(8,128)(2,1)} %wg_ref.9, bf16[4096,1792]{1,0:T(8,128)(2,1)} %wu_ref.9), custom_call_target="tpu_custom_call" | custom-call | bytes 4194304 | tf_op jit(solution)/shard_map/bring/pallas_call | solution.py:63
  7.9 2.0 %copy-done = bf16[4096,512]{1,0:T(8,128)(2,1)} copy-done((bf16[4096,512]{1,0:T(8,128)(2,1)}, bf16[4096,512]{1,0:T(8,128)(2,1)S(1)}, u32[]{:S(2)}) %copy-start) | copy-done | bytes 4194328
  11.7 1.6 %collective-permute-start.2 = (bf16[32,4096]{1,0:T(8,128)(2,1)S(1)}, bf16[32,4096]{1,0:T(8,128)(2,1)S(1)}, u32[]{:S(2)}, u32[]{:S(2)}) collective-permute-start(bf16[32,4096]{1,0:T(8,128)(2,1)S(1)} %collective-permute-done.refs_1_), channel_id=1, source_target_pairs={{0,4},{1,5},{4,8},{5,9},{8,12},{9,13},{12,14},{13,15},{14,10},{15,... | collective-permute-start | bytes 786440 | tf_op jit(solution)/shard_map/ppermute | solution.py:459
  13.7 1.6 %collective-permute-start.6 = (bf16[32,4096]{1,0:T(8,128)(2,1)S(1)}, bf16[32,4096]{1,0:T(8,128)(2,1)S(1)}, u32[]{:S(2)}, u32[]{:S(2)}) collective-permute-start(bf16[32,4096]{1,0:T(8,128)(2,1)S(1)} %get-tuple-element.67.refs_0_), channel_id=1, source_target_pairs={{0,4},{1,5},{4,8},{5,9},{8,12},{9,13},{12,14},{13,15},{14,10},{15,... | collective-permute-start | bytes 786440 | tf_op jit(solution)/shard_map/ppermute | solution.py:459
  15.7 5.2 %collective-permute-done.2.refs_2_ = bf16[32,4096]{1,0:T(8,128)(2,1)S(1)} collective-permute-done((bf16[32,4096]{1,0:T(8,128)(2,1)S(1)}, bf16[32,4096]{1,0:T(8,128)(2,1)S(1)}, u32[]{:S(2)}, u32[]{:S(2)}) %collective-permute-start.2) | collective-permute-done | bytes 262176 | tf_op jit(solution)/shard_map/ppermute | solution.py:459
  20.9 1.6 %collective-permute-done.3.refs_7_ = bf16[32,4096]{1,0:T(8,128)(2,1)S(1)} collective-permute-done((bf16[32,4096]{1,0:T(8,128)(2,1)S(1)}, bf16[32,4096]{1,0:T(8,128)(2,1)S(1)}, u32[]{:S(2)}, u32[]{:S(2)}) %collective-permute-start.3) | collective-permute-done | bytes 262176 | tf_op jit(solution)/shard_map/ppermute | solution.py:462
  22.5 1.6 %collective-permute-start.4 = (bf16[32,4096]{1,0:T(8,128)(2,1)S(1)}, bf16[32,4096]{1,0:T(8,128)(2,1)S(1)}, u32[]{:S(2)}, u32[]{:S(2)}) collective-permute-start(bf16[32,4096]{1,0:T(8,128)(2,1)S(1)} %collective-permute-done.2.refs_2_), channel_id=1, source_target_pairs={{0,4},{1,5},{4,8},{5,9},{8,12},{9,13},{12,14},{13,15},{14,10},{15,... | collective-permute-start | bytes 786440 | tf_op jit(solution)/shard_map/ppermute | solution.py:459
  26.6 1.6 %collective-permute-done.7.refs_8_ = bf16[32,4096]{1,0:T(8,128)(2,1)S(1)} collective-permute-done((bf16[32,4096]{1,0:T(8,128)(2,1)S(1)}, bf16[32,4096]{1,0:T(8,128)(2,1)S(1)}, u32[]{:S(2)}, u32[]{:S(2)}) %collective-permute-start.7) | collective-permute-done | bytes 262176 | tf_op jit(solution)/shard_map/ppermute | solution.py:462
  28.1 1.6 %collective-permute-start.10 = (bf16[32,4096]{1,0:T(8,128)(2,1)S(1)}, bf16[32,4096]{1,0:T(8,128)(2,1)S(1)}, u32[]{:S(2)}, u32[]{:S(2)}) collective-permute-start(bf16[32,4096]{1,0:T(8,128)(2,1)S(1)} %collective-permute-done.6.refs_1_), channel_id=1, source_target_pairs={{0,4},{1,5},{4,8},{5,9},{8,12},{9,13},{12,14},{13,15},{14,10},{15,... | collective-permute-start | bytes 786440 | tf_op jit(solution)/shard_map/ppermute | solution.py:459
  32.2 1.6 %collective-permute-done.5.refs_6_ = bf16[32,4096]{1,0:T(8,128)(2,1)S(1)} collective-permute-done((bf16[32,4096]{1,0:T(8,128)(2,1)S(1)}, bf16[32,4096]{1,0:T(8,128)(2,1)S(1)}, u32[]{:S(2)}, u32[]{:S(2)}) %collective-permute-start.5) | collective-permute-done | bytes 262176 | tf_op jit(solution)/shard_map/ppermute | solution.py:462
  34.3 1.6 %collective-permute-start.8 = (bf16[16,4096]{1,0:T(8,128)(2,1)S(1)}, bf16[16,4096]{1,0:T(8,128)(2,1)S(1)}, u32[]{:S(2)}, u32[]{:S(2)}) collective-permute-start(bf16[16,4096]{1,0:T(8,128)(2,1)S(1)} %slice.12), channel_id=1, source_target_pairs={{0,4},{1,5},{4,8},{5,9},{8,12},{9,13},{12,14},{13,15},{14,10},{15,... | collective-permute-start | bytes 393224 | tf_op jit(solution)/shard_map/ppermute | solution.py:459
  39.7 1.6 %collective-permute-start.13 = (bf16[32,4096]{1,0:T(8,128)(2,1)S(1)}, bf16[32,4096]{1,0:T(8,128)(2,1)S(1)}, u32[]{:S(2)}, u32[]{:S(2)}) collective-permute-start(bf16[32,4096]{1,0:T(8,128)(2,1)S(1)} %collective-permute-done.10.refs_10_.rest_0_.refs_2_), channel_id=1, source_target_pairs={{0,4},{1,5},{4,8},{5,9},{8,12},{9,13},{12,14},{13,15},{14,10},{15,... | collective-permute-start | bytes 786440 | tf_op jit(solution)/shard_map/ppermute | solution.py:459
  41.8 2.1 %collective-permute-done.12.far_ref = bf16[256,4096]{1,0:T(8,128)(2,1)S(1)} collective-permute-done((bf16[256,4096]{1,0:T(8,128)(2,1)S(1)}, bf16[256,4096]{1,0:T(8,128)(2,1)S(1)}, u32[]{:S(2)}, u32[]{:S(2)}) %collective-permute-start.12) | collective-permute-done | bytes 2097184 | tf_op jit(solution)/shard_map/ppermute | solution.py:465
  43.9 5.7 %gate_up.3 = (f32[512,512]{1,0:T(8,128)S(1)}, f32[512,512]{1,0:T(8,128)S(1)}, bf16[4096,512]{1,0:T(8,128)(2,1)S(1)}) custom-call(bf16[256,4096]{1,0:T(8,128)(2,1)S(1)} %pack.1.near_ref, bf16[256,4096]{1,0:T(8,128)(2,1)S(1)} %collective-permute-done.12.far_ref, bf16[4096,512]{1,0:T(8,128)(2,1)S(1)} %copy-done.1, bf16[4096,1792]{1,0:T(8,128)(2,1)} %wg_ref.9, ...), custom_call_target="tpu_custom_call" | custom-call | flops 4294967296 | bytes 8388608 | tf_op jit(solution)/shard_map/gate_up/pallas_call | solution.py:218
  52.7 8.3 %gate_up.4 = (f32[768,512]{1,0:T(8,128)S(1)}, f32[768,512]{1,0:T(8,128)S(1)}, bf16[4096,512]{1,0:T(8,128)(2,1)S(1)}) custom-call(bf16[256,4096]{1,0:T(8,128)(2,1)S(1)} %pack.1.near_ref, bf16[256,4096]{1,0:T(8,128)(2,1)S(1)} %collective-permute-done.12.far_ref, bf16[4096,512]{1,0:T(8,128)(2,1)S(1)} %get-tuple-element.78.head_ref, bf16[4096,1792]{1,0:T(8,128)(2,1)} %wg_ref.9, ...), custom_call_target="tpu_custom_call" | custom-call | flops 6442450944 | bytes 12582912 | tf_op jit(solution)/shard_map/gate_up/pallas_call | solution.py:218
  61.7 5.7 %gate_up.5 = (f32[512,512]{1,0:T(8,128)S(1)}, f32[512,512]{1,0:T(8,128)S(1)}, bf16[256,4096]{1,0:T(8,128)(2,1)S(1)}) custom-call(bf16[256,4096]{1,0:T(8,128)(2,1)S(1)} %pack.1.near_ref, bf16[256,4096]{1,0:T(8,128)(2,1)S(1)} %collective-permute-done.12.far_ref, bf16[4096,512]{1,0:T(8,128)(2,1)S(1)} %get-tuple-element.81.head_ref, bf16[4096,1792]{1,0:T(8,128)(2,1)} %wg_ref.9, ...), custom_call_target="tpu_custom_call" | custom-call | flops 4294967296 | bytes 8388608 | tf_op jit(solution)/shard_map/gate_up/pallas_call | solution.py:218
  67.4 28.8 %hidden_back.1 = (bf16[512,1792]{1,0:T(8,128)(2,1)S(1)}, bf16[512,1792]{1,0:T(8,128)(2,1)S(1)}, bf16[256,4096]{1,0:T(8,128)(2,1)S(1)}, bf16[256,4096]{1,0:T(8,128)(2,1)S(1)}) custom-call(s32[8]{0:T(128)S(1)} %fusion.3.refs_9_.spot_ref, bf16[4096,256]{1,0:T(8,128)(2,1)S(1)} %pack_turned.1.rest_0_.near_ref, ...), custom_call_target="tpu_custom_call" | custom-call | flops 22548578304 | bytes 44040192 | tf_op jit(solution)/shard_map/hidden_back/pallas_call | solution.py:334
  97.6 3.4 %fisher.5 = (bf16[4096,1792]{1,0:T(8,128)(2,1)}, bf16[4096,1792]{1,0:T(8,128)(2,1)}, f32[8,128]{1,0:T(8,128)S(1)}) custom-call(bf16[512,4096]{1,0:T(8,128)(2,1)S(1)} %arrange.1.x_ref, bf16[512,1792]{1,0:T(8,128)(2,1)S(1)} %get-tuple-element.86.gg_ref, bf16[512,1792]{1,0:T(8,128)(2,1)S(1)} %get-tuple-element.87.gu_ref), custom_call_target="tpu_custom_call" | custom-call | flops 1879048192 | bytes 3670016 | tf_op jit(solution)/shard_map/fisher/pallas_call | solution.py:432
  101.1 1.6 %collective-permute-start.19 = (bf16[16,4096]{1,0:T(8,128)(2,1)S(1)}, bf16[16,4096]{1,0:T(8,128)(2,1)S(1)}, u32[]{:S(2)}, u32[]{:S(2)}) collective-permute-start(bf16[16,4096]{1,0:T(8,128)(2,1)S(1)} %get-tuple-element.92.rest_2_), channel_id=1, source_target_pairs={{0,4},{1,5},{4,8},{5,9},{8,12},{9,13},{12,14},{13,15},{14,10},{15,... | collective-permute-start | bytes 393224 | tf_op jit(solution)/shard_map/ppermute | solution.py:459
  103.2 4.6 %fisher.6 = (bf16[4096,1792]{1,0:T(8,128)(2,1)}, bf16[4096,1792]{1,0:T(8,128)(2,1)}, f32[8,128]{1,0:T(8,128)S(1)}) custom-call(bf16[512,4096]{1,0:T(8,128)(2,1)S(1)} %arrange.1.x_ref, bf16[512,1792]{1,0:T(8,128)(2,1)S(1)} %get-tuple-element.86.gg_ref, bf16[512,1792]{1,0:T(8,128)(2,1)S(1)} %get-tuple-element.87.gu_ref, ...), custom_call_target="tpu_custom_call", output_to_operand_aliasing={{0}: (3, {}), {1}: (4, {})} | custom-call | flops 2818572288 | bytes 5505024 | tf_op jit(solution)/shard_map/fisher/pallas_call | solution.py:432
  110.1 5.8 %fisher.7 = (bf16[4096,1792]{1,0:T(8,128)(2,1)}, bf16[4096,1792]{1,0:T(8,128)(2,1)}, f32[8,128]{1,0:T(8,128)S(1)}) custom-call(bf16[512,4096]{1,0:T(8,128)(2,1)S(1)} %arrange.1.x_ref, bf16[512,1792]{1,0:T(8,128)(2,1)S(1)} %get-tuple-element.86.gg_ref, bf16[512,1792]{1,0:T(8,128)(2,1)S(1)} %get-tuple-element.87.gu_ref, ...), custom_call_target="tpu_custom_call", output_to_operand_aliasing={{0}: (3, {}), {1}: (4, {})} | custom-call | flops 3758096384 | bytes 7340032 | tf_op jit(solution)/shard_map/fisher/pallas_call | solution.py:432
  119.2 5.8 %fisher.8 = (bf16[4096,1792]{1,0:T(8,128)(2,1)}, bf16[4096,1792]{1,0:T(8,128)(2,1)}, f32[8,128]{1,0:T(8,128)S(1)}) custom-call(bf16[512,4096]{1,0:T(8,128)(2,1)S(1)} %arrange.1.x_ref, bf16[512,1792]{1,0:T(8,128)(2,1)S(1)} %get-tuple-element.86.gg_ref, bf16[512,1792]{1,0:T(8,128)(2,1)S(1)} %get-tuple-element.87.gu_ref, ...), custom_call_target="tpu_custom_call", output_to_operand_aliasing={{0}: (3, {}), {1}: (4, {})} | custom-call | flops 3758096384 | bytes 7340032 | tf_op jit(solution)/shard_map/fisher/pallas_call | solution.py:432
  127.3 4.6 %fisher.9 = (bf16[4096,1792]{1,0:T(8,128)(2,1)}, bf16[4096,1792]{1,0:T(8,128)(2,1)}, f32[8,128]{1,0:T(8,128)}) custom-call(bf16[512,4096]{1,0:T(8,128)(2,1)S(1)} %arrange.1.x_ref, bf16[512,1792]{1,0:T(8,128)(2,1)S(1)} %get-tuple-element.86.gg_ref, bf16[512,1792]{1,0:T(8,128)(2,1)S(1)} %get-tuple-element.87.gu_ref, ...), custom_call_target="tpu_custom_call", output_to_operand_aliasing={{0}: (3, {}), {1}: (4, {})} | custom-call | flops 2818572288 | bytes 5505024 | tf_op jit(solution)/shard_map/fisher/pallas_call | solution.py:432
  (73 shorter events, 30.0 us)
Async XLA Ops:
  0.6 9.5 %collective-permute-start = (bf16[32,4096]{1,0:T(8,128)(2,1)}, bf16[32,4096]{1,0:T(8,128)(2,1)S(1)}, u32[]{:S(2)}, u32[]{:S(2)}) collective-permute-start(bf16[32,4096]{1,0:T(8,128)(2,1)} %x_ref.1), channel_id=1, source_target_pairs={{0,4},{1,5},{4,8},{5,9},{8,12},{9,13},{12,14},{13,15},{14,10},{15,... | collective-permute-start | bytes 786440 | tf_op jit(solution)/shard_map/ppermute | solution.py:459
  3.7 8.0 %collective-permute-start.1 = (bf16[32,4096]{1,0:T(8,128)(2,1)}, bf16[32,4096]{1,0:T(8,128)(2,1)S(1)}, u32[]{:S(2)}, u32[]{:S(2)}) collective-permute-start(bf16[32,4096]{1,0:T(8,128)(2,1)} %x_ref.1), channel_id=1, source_target_pairs={{4,0},{5,1},{8,4},{9,5},{12,8},{13,9},{14,12},{15,13},{10,14},{11,... | collective-permute-start | bytes 786440 | tf_op jit(solution)/shard_map/ppermute | solution.py:462
  11.7 9.2 %collective-permute-start.2 = (bf16[32,4096]{1,0:T(8,128)(2,1)S(1)}, bf16[32,4096]{1,0:T(8,128)(2,1)S(1)}, u32[]{:S(2)}, u32[]{:S(2)}) collective-permute-start(bf16[32,4096]{1,0:T(8,128)(2,1)S(1)} %collective-permute-done.refs_1_), channel_id=1, source_target_pairs={{0,4},{1,5},{4,8},{5,9},{8,12},{9,13},{12,14},{13,15},{14,10},{15,... | collective-permute-start | bytes 786440 | tf_op jit(solution)/shard_map/ppermute | solution.py:459
  13.3 9.2 %collective-permute-start.3 = (bf16[32,4096]{1,0:T(8,128)(2,1)S(1)}, bf16[32,4096]{1,0:T(8,128)(2,1)S(1)}, u32[]{:S(2)}, u32[]{:S(2)}) collective-permute-start(bf16[32,4096]{1,0:T(8,128)(2,1)S(1)} %collective-permute-done.1.refs_8_), channel_id=1, source_target_pairs={{4,0},{5,1},{8,4},{9,5},{12,8},{13,9},{14,12},{15,13},{10,14},{11,... | collective-permute-start | bytes 786440 | tf_op jit(solution)/shard_map/ppermute | solution.py:462
  13.7 12.8 %collective-permute-start.6 = (bf16[32,4096]{1,0:T(8,128)(2,1)S(1)}, bf16[32,4096]{1,0:T(8,128)(2,1)S(1)}, u32[]{:S(2)}, u32[]{:S(2)}) collective-permute-start(bf16[32,4096]{1,0:T(8,128)(2,1)S(1)} %get-tuple-element.67.refs_0_), channel_id=1, source_target_pairs={{0,4},{1,5},{4,8},{5,9},{8,12},{9,13},{12,14},{13,15},{14,10},{15,... | collective-permute-start | bytes 786440 | tf_op jit(solution)/shard_map/ppermute | solution.py:459
  15.3 12.8 %collective-permute-start.7 = (bf16[32,4096]{1,0:T(8,128)(2,1)S(1)}, bf16[32,4096]{1,0:T(8,128)(2,1)S(1)}, u32[]{:S(2)}, u32[]{:S(2)}) collective-permute-start(bf16[32,4096]{1,0:T(8,128)(2,1)S(1)} %get-tuple-element.67.refs_0_), channel_id=1, source_target_pairs={{4,0},{5,1},{8,4},{9,5},{12,8},{13,9},{14,12},{15,13},{10,14},{11,... | collective-permute-start | bytes 786440 | tf_op jit(solution)/shard_map/ppermute | solution.py:462
  22.5 9.7 %collective-permute-start.4 = (bf16[32,4096]{1,0:T(8,128)(2,1)S(1)}, bf16[32,4096]{1,0:T(8,128)(2,1)S(1)}, u32[]{:S(2)}, u32[]{:S(2)}) collective-permute-start(bf16[32,4096]{1,0:T(8,128)(2,1)S(1)} %collective-permute-done.2.refs_2_), channel_id=1, source_target_pairs={{0,4},{1,5},{4,8},{5,9},{8,12},{9,13},{12,14},{13,15},{14,10},{15,... | collective-permute-start | bytes 786440 | tf_op jit(solution)/shard_map/ppermute | solution.py:459
  24.1 9.7 %collective-permute-start.5 = (bf16[32,4096]{1,0:T(8,128)(2,1)S(1)}, bf16[32,4096]{1,0:T(8,128)(2,1)S(1)}, u32[]{:S(2)}, u32[]{:S(2)}) collective-permute-start(bf16[32,4096]{1,0:T(8,128)(2,1)S(1)} %collective-permute-done.3.refs_7_), channel_id=1, source_target_pairs={{4,0},{5,1},{8,4},{9,5},{12,8},{13,9},{14,12},{15,13},{10,14},{11,... | collective-permute-start | bytes 786440 | tf_op jit(solution)/shard_map/ppermute | solution.py:462
  28.1 8.7 %collective-permute-start.10 = (bf16[32,4096]{1,0:T(8,128)(2,1)S(1)}, bf16[32,4096]{1,0:T(8,128)(2,1)S(1)}, u32[]{:S(2)}, u32[]{:S(2)}) collective-permute-start(bf16[32,4096]{1,0:T(8,128)(2,1)S(1)} %collective-permute-done.6.refs_1_), channel_id=1, source_target_pairs={{0,4},{1,5},{4,8},{5,9},{8,12},{9,13},{12,14},{13,15},{14,10},{15,... | collective-permute-start | bytes 786440 | tf_op jit(solution)/shard_map/ppermute | solution.py:459
  29.7 8.4 %collective-permute-start.11 = (bf16[32,4096]{1,0:T(8,128)(2,1)S(1)}, bf16[32,4096]{1,0:T(8,128)(2,1)S(1)}, u32[]{:S(2)}, u32[]{:S(2)}) collective-permute-start(bf16[32,4096]{1,0:T(8,128)(2,1)S(1)} %collective-permute-done.7.refs_8_), channel_id=1, source_target_pairs={{4,0},{5,1},{8,4},{9,5},{12,8},{13,9},{14,12},{15,13},{10,14},{11,... | collective-permute-start | bytes 786440 | tf_op jit(solution)/shard_map/ppermute | solution.py:462
  33.8 5.7 %collective-permute-start.9 = (bf16[16,4096]{1,0:T(8,128)(2,1)S(1)}, bf16[16,4096]{1,0:T(8,128)(2,1)S(1)}, u32[]{:S(2)}, u32[]{:S(2)}) collective-permute-start(bf16[16,4096]{1,0:T(8,128)(2,1)S(1)} %slice.13), channel_id=1, source_target_pairs={{4,0},{5,1},{8,4},{9,5},{12,8},{13,9},{14,12},{15,13},{10,14},{11,... | collective-permute-start | bytes 393224 | tf_op jit(solution)/shard_map/ppermute | solution.py:462
  34.3 5.2 %collective-permute-start.8 = (bf16[16,4096]{1,0:T(8,128)(2,1)S(1)}, bf16[16,4096]{1,0:T(8,128)(2,1)S(1)}, u32[]{:S(2)}, u32[]{:S(2)}) collective-permute-start(bf16[16,4096]{1,0:T(8,128)(2,1)S(1)} %slice.12), channel_id=1, source_target_pairs={{0,4},{1,5},{4,8},{5,9},{8,12},{9,13},{12,14},{13,15},{14,10},{15,... | collective-permute-start | bytes 393224 | tf_op jit(solution)/shard_map/ppermute | solution.py:459
  39.7 10.8 %collective-permute-start.13 = (bf16[32,4096]{1,0:T(8,128)(2,1)S(1)}, bf16[32,4096]{1,0:T(8,128)(2,1)S(1)}, u32[]{:S(2)}, u32[]{:S(2)}) collective-permute-start(bf16[32,4096]{1,0:T(8,128)(2,1)S(1)} %collective-permute-done.10.refs_10_.rest_0_.refs_2_), channel_id=1, source_target_pairs={{0,4},{1,5},{4,8},{5,9},{8,12},{9,13},{12,14},{13,15},{14,10},{15,... | collective-permute-start | bytes 786440 | tf_op jit(solution)/shard_map/ppermute | solution.py:459
  41.4 9.2 %collective-permute-start.14 = (bf16[32,4096]{1,0:T(8,128)(2,1)S(1)}, bf16[32,4096]{1,0:T(8,128)(2,1)S(1)}, u32[]{:S(2)}, u32[]{:S(2)}) collective-permute-start(bf16[32,4096]{1,0:T(8,128)(2,1)S(1)} %collective-permute-done.11.refs_11_.rest_1_.refs_7_), channel_id=1, source_target_pairs={{4,0},{5,1},{8,4},{9,5},{12,8},{13,9},{14,12},{15,13},{10,14},{11,... | collective-permute-start | bytes 786440 | tf_op jit(solution)/shard_map/ppermute | solution.py:462
  50.6 10.4 %collective-permute-start.16 = (bf16[16,4096]{1,0:T(8,128)(2,1)S(1)}, bf16[16,4096]{1,0:T(8,128)(2,1)S(1)}, u32[]{:S(2)}, u32[]{:S(2)}) collective-permute-start(bf16[16,4096]{1,0:T(8,128)(2,1)S(1)} %slice.15), channel_id=1, source_target_pairs={{4,0},{5,1},{8,4},{9,5},{12,8},{13,9},{14,12},{15,13},{10,14},{11,... | collective-permute-start | bytes 393224 | tf_op jit(solution)/shard_map/ppermute | solution.py:462
  51.1 9.9 %collective-permute-start.15 = (bf16[16,4096]{1,0:T(8,128)(2,1)S(1)}, bf16[16,4096]{1,0:T(8,128)(2,1)S(1)}, u32[]{:S(2)}, u32[]{:S(2)}) collective-permute-start(bf16[16,4096]{1,0:T(8,128)(2,1)S(1)} %slice.14), channel_id=1, source_target_pairs={{0,4},{1,5},{4,8},{5,9},{8,12},{9,13},{12,14},{13,15},{14,10},{15,... | collective-permute-start | bytes 393224 | tf_op jit(solution)/shard_map/ppermute | solution.py:459
  61.6 5.8 %collective-permute-start.17 = (bf16[4096,256]{1,0:T(8,128)(2,1)S(1)}, bf16[4096,256]{1,0:T(8,128)(2,1)S(1)}, u32[]{:S(2)}, u32[]{:S(2)}) collective-permute-start(bf16[4096,256]{1,0:T(8,128)(2,1)S(1)} %pack_turned.1.rest_0_.near_ref), channel_id=1, source_target_pairs={{0,1},{1,0},{2,3},{3,2},{4,5},{5,4},{6,7},{7,6},{8,9},{9,8},{10,11... | collective-permute-start | bytes 6291464 | tf_op jit(solution)/shard_map/ppermute | solution.py:465
  101.1 6.7 %collective-permute-start.19 = (bf16[16,4096]{1,0:T(8,128)(2,1)S(1)}, bf16[16,4096]{1,0:T(8,128)(2,1)S(1)}, u32[]{:S(2)}, u32[]{:S(2)}) collective-permute-start(bf16[16,4096]{1,0:T(8,128)(2,1)S(1)} %get-tuple-element.92.rest_2_), channel_id=1, source_target_pairs={{0,4},{1,5},{4,8},{5,9},{8,12},{9,13},{12,14},{13,15},{14,10},{15,... | collective-permute-start | bytes 393224 | tf_op jit(solution)/shard_map/ppermute | solution.py:459
  108.0 7.9 %collective-permute-start.21 = (bf16[32,4096]{1,0:T(8,128)(2,1)S(1)}, bf16[32,4096]{1,0:T(8,128)(2,1)S(1)}, u32[]{:S(2)}, u32[]{:S(2)}) collective-permute-start(bf16[32,4096]{1,0:T(8,128)(2,1)S(1)} %get-tuple-element.97.rest_2_), channel_id=1, source_target_pairs={{0,4},{1,5},{4,8},{5,9},{8,12},{9,13},{12,14},{13,15},{14,10},{15,... | collective-permute-start | bytes 786440 | tf_op jit(solution)/shard_map/ppermute | solution.py:459
  109.6 7.4 %collective-permute-start.22 = (bf16[32,4096]{1,0:T(8,128)(2,1)S(1)}, bf16[32,4096]{1,0:T(8,128)(2,1)S(1)}, u32[]{:S(2)}, u32[]{:S(2)}) collective-permute-start(bf16[32,4096]{1,0:T(8,128)(2,1)S(1)} %get-tuple-element.98.rest_3_), channel_id=1, source_target_pairs={{4,0},{5,1},{8,4},{9,5},{12,8},{13,9},{14,12},{15,13},{10,14},{11,... | collective-permute-start | bytes 786440 | tf_op jit(solution)/shard_map/ppermute | solution.py:462
  117.1 7.9 %collective-permute-start.23 = (bf16[32,4096]{1,0:T(8,128)(2,1)S(1)}, bf16[32,4096]{1,0:T(8,128)(2,1)S(1)}, u32[]{:S(2)}, u32[]{:S(2)}) collective-permute-start(bf16[32,4096]{1,0:T(8,128)(2,1)S(1)} %get-tuple-element.102.rest_2_), channel_id=1, source_target_pairs={{0,4},{1,5},{4,8},{5,9},{8,12},{9,13},{12,14},{13,15},{14,10},{15,... | collective-permute-start | bytes 786440 | tf_op jit(solution)/shard_map/ppermute | solution.py:459
  118.7 6.4 %collective-permute-start.24 = (bf16[32,4096]{1,0:T(8,128)(2,1)S(1)}, bf16[32,4096]{1,0:T(8,128)(2,1)S(1)}, u32[]{:S(2)}, u32[]{:S(2)}) collective-permute-start(bf16[32,4096]{1,0:T(8,128)(2,1)S(1)} %get-tuple-element.103.rest_3_), channel_id=1, source_target_pairs={{4,0},{5,1},{8,4},{9,5},{12,8},{13,9},{14,12},{15,13},{10,14},{11,... | collective-permute-start | bytes 786440 | tf_op jit(solution)/shard_map/ppermute | solution.py:462
  125.3 6.7 %collective-permute-start.25 = (bf16[32,4096]{1,0:T(8,128)(2,1)S(1)}, bf16[32,4096]{1,0:T(8,128)(2,1)S(1)}, u32[]{:S(2)}, u32[]{:S(2)}) collective-permute-start(bf16[32,4096]{1,0:T(8,128)(2,1)S(1)} %get-tuple-element.107.rest_2_), channel_id=1, source_target_pairs={{0,4},{1,5},{4,8},{5,9},{8,12},{9,13},{12,14},{13,15},{14,10},{15,... | collective-permute-start | bytes 786440 | tf_op jit(solution)/shard_map/ppermute | solution.py:459
  126.8 6.4 %collective-permute-start.26 = (bf16[32,4096]{1,0:T(8,128)(2,1)S(1)}, bf16[32,4096]{1,0:T(8,128)(2,1)S(1)}, u32[]{:S(2)}, u32[]{:S(2)}) collective-permute-start(bf16[32,4096]{1,0:T(8,128)(2,1)S(1)} %get-tuple-element.108.rest_3_), channel_id=1, source_target_pairs={{4,0},{5,1},{8,4},{9,5},{12,8},{13,9},{14,12},{15,13},{10,14},{11,... | collective-permute-start | bytes 786440 | tf_op jit(solution)/shard_map/ppermute | solution.py:462
  (11 other events, 86.3 us)

commit v14 on v12

--- a/solution.py
+++ b/solution.py
@@ -192,7 +192,7 @@
     for t in range(tiles):
         if t:
             finish(fetch(t))
-        if t == tiles - 1:
+        if t == (max(tiles - 2, 0) if next_ref.shape[0] == 2 else tiles - 1):
             begin(fetch_next())
         w_ref = w_buf.at[t % 2] if t else head_ref
         for side, x_ref in enumerate((near_ref, far_ref)):
@@ -484,7 +484,7 @@
     cuts = [0, 2, 5, 7]
 
     def piece(i, head, after):
-        grant = (30, 28, 26)[i]
+        grant = (30, 26, 26)[i]
         count = cuts[i + 1] - cuts[i]
         a, b, head = gate_up(
             near_x, far_x, head, wg, wu, wd, cuts[i], count, lane, grant, after

time: 134 us -> 133 us (level)
    unnamed x16 -> x12, local copies, waits for them, and re-layouts: 4.89 us -> 3.92 us
where the time goes in v14:
time: 133 us; the launch traced here: 132 us
  Pallas kernels  77.3 us (58%)
  starting transfers between devices  26.4 us (20%)
  waiting for transfers between devices  21.9 us (16%)
  local copies, waits for them, and re-layouts  5.19 us (4%)
    pallas_call x1, Pallas kernels, back(): pl.pallas_call(functools.partial(back_kernel, step, 512, len(a)), in_spec...  28.8 us
    pallas_call x5, Pallas kernels, fisher(): pl.pallas_call(functools.partial(fisher_kernel, tile(width, 256)), grid=(...  24.1 us
    ppermute x12, starting transfers between devices, right(): return lax.ppermute(value, 'hid', to_right)  20.1 us
    pallas_call x3, Pallas kernels, gate_up(): pl.pallas_call(functools.partial(gate_up_kernel, first, step), in_specs=h...  19.1 us
    ppermute x12, waiting for transfers between devices, left(): return lax.ppermute(value, 'hid', to_left)  11.4 us
    ppermute x12, waiting for transfers between devices, right(): return lax.ppermute(value, 'hid', to_right)  8.49 us
    ppermute x12, starting transfers between devices, left(): return lax.ppermute(value, 'hid', to_left)  5.64 us
    unnamed x12, local copies, waits for them, and re-layouts  3.92 us
  transfers between devices with their start and end apart: 27, of which 15 were waited for; matrix products, arithmetic and copies ran while one was open for 1% of the time, Pallas kernels for 35%

profile of v14, /device:TPU:0, one launch (start us, length us, event | category | flops | bytes accessed | tf_op | source)
XLA Modules:
  0.0 132.4 jit_solution(132510647500998807)
XLA Ops:
  0.6 3.1 %collective-permute-start = (bf16[32,4096]{1,0:T(8,128)(2,1)}, bf16[32,4096]{1,0:T(8,128)(2,1)S(1)}, u32[]{:S(2)}, u32[]{:S(2)}) collective-permute-start(bf16[32,4096]{1,0:T(8,128)(2,1)} %x_ref.1), channel_id=1, source_target_pairs={{0,4},{1,5},{4,8},{5,9},{8,12},{9,13},{12,14},{13,15},{14,10},{15,... | collective-permute-start | bytes 786440 | tf_op jit(solution)/shard_map/ppermute | solution.py:458
  5.6 2.3 %bring.1 = (bf16[32,4096]{1,0:T(8,128)(2,1)S(1)}, bf16[32,4096]{1,0:T(8,128)(2,1)S(1)}, bf16[2,4096,256]{2,1,0:T(8,128)(2,1)S(1)}) custom-call(bf16[32,4096]{1,0:T(8,128)(2,1)S(1)} %copy-done.3, bf16[32,4096]{1,0:T(8,128)(2,1)S(1)} %copy-done.2, bf16[4096,1792]{1,0:T(8,128)(2,1)} %wg_ref.9, bf16[4096,1792]{1,0:T(8,128)(2,1)} %wu_ref.9), custom_call_target="tpu_custom_call" | custom-call | bytes 4194304 | tf_op jit(solution)/shard_map/bring/pallas_call | solution.py:61
  7.9 2.0 %copy-done = bf16[2,4096,256]{2,1,0:T(8,128)(2,1)} copy-done((bf16[2,4096,256]{2,1,0:T(8,128)(2,1)}, bf16[2,4096,256]{2,1,0:T(8,128)(2,1)S(1)}, u32[]{:S(2)}) %copy-start) | copy-done | bytes 4194328
  11.7 1.6 %collective-permute-start.2 = (bf16[32,4096]{1,0:T(8,128)(2,1)S(1)}, bf16[32,4096]{1,0:T(8,128)(2,1)S(1)}, u32[]{:S(2)}, u32[]{:S(2)}) collective-permute-start(bf16[32,4096]{1,0:T(8,128)(2,1)S(1)} %collective-permute-done.refs_1_), channel_id=1, source_target_pairs={{0,4},{1,5},{4,8},{5,9},{8,12},{9,13},{12,14},{13,15},{14,10},{15,... | collective-permute-start | bytes 786440 | tf_op jit(solution)/shard_map/ppermute | solution.py:458
  13.7 1.6 %collective-permute-start.6 = (bf16[32,4096]{1,0:T(8,128)(2,1)S(1)}, bf16[32,4096]{1,0:T(8,128)(2,1)S(1)}, u32[]{:S(2)}, u32[]{:S(2)}) collective-permute-start(bf16[32,4096]{1,0:T(8,128)(2,1)S(1)} %get-tuple-element.67.refs_0_), channel_id=1, source_target_pairs={{0,4},{1,5},{4,8},{5,9},{8,12},{9,13},{12,14},{13,15},{14,10},{15,... | collective-permute-start | bytes 786440 | tf_op jit(solution)/shard_map/ppermute | solution.py:458
  15.7 5.2 %collective-permute-done.2.refs_2_ = bf16[32,4096]{1,0:T(8,128)(2,1)S(1)} collective-permute-done((bf16[32,4096]{1,0:T(8,128)(2,1)S(1)}, bf16[32,4096]{1,0:T(8,128)(2,1)S(1)}, u32[]{:S(2)}, u32[]{:S(2)}) %collective-permute-start.2) | collective-permute-done | bytes 262176 | tf_op jit(solution)/shard_map/ppermute | solution.py:458
  20.9 1.6 %collective-permute-done.3.refs_7_ = bf16[32,4096]{1,0:T(8,128)(2,1)S(1)} collective-permute-done((bf16[32,4096]{1,0:T(8,128)(2,1)S(1)}, bf16[32,4096]{1,0:T(8,128)(2,1)S(1)}, u32[]{:S(2)}, u32[]{:S(2)}) %collective-permute-start.3) | collective-permute-done | bytes 262176 | tf_op jit(solution)/shard_map/ppermute | solution.py:461
  22.5 1.6 %collective-permute-start.4 = (bf16[32,4096]{1,0:T(8,128)(2,1)S(1)}, bf16[32,4096]{1,0:T(8,128)(2,1)S(1)}, u32[]{:S(2)}, u32[]{:S(2)}) collective-permute-start(bf16[32,4096]{1,0:T(8,128)(2,1)S(1)} %collective-permute-done.2.refs_2_), channel_id=1, source_target_pairs={{0,4},{1,5},{4,8},{5,9},{8,12},{9,13},{12,14},{13,15},{14,10},{15,... | collective-permute-start | bytes 786440 | tf_op jit(solution)/shard_map/ppermute | solution.py:458
  26.6 1.6 %collective-permute-done.7.refs_8_ = bf16[32,4096]{1,0:T(8,128)(2,1)S(1)} collective-permute-done((bf16[32,4096]{1,0:T(8,128)(2,1)S(1)}, bf16[32,4096]{1,0:T(8,128)(2,1)S(1)}, u32[]{:S(2)}, u32[]{:S(2)}) %collective-permute-start.7) | collective-permute-done | bytes 262176 | tf_op jit(solution)/shard_map/ppermute | solution.py:461
  28.1 1.6 %collective-permute-start.10 = (bf16[32,4096]{1,0:T(8,128)(2,1)S(1)}, bf16[32,4096]{1,0:T(8,128)(2,1)S(1)}, u32[]{:S(2)}, u32[]{:S(2)}) collective-permute-start(bf16[32,4096]{1,0:T(8,128)(2,1)S(1)} %collective-permute-done.6.refs_1_), channel_id=1, source_target_pairs={{0,4},{1,5},{4,8},{5,9},{8,12},{9,13},{12,14},{13,15},{14,10},{15,... | collective-permute-start | bytes 786440 | tf_op jit(solution)/shard_map/ppermute | solution.py:458
  32.2 1.6 %collective-permute-done.5.refs_6_ = bf16[32,4096]{1,0:T(8,128)(2,1)S(1)} collective-permute-done((bf16[32,4096]{1,0:T(8,128)(2,1)S(1)}, bf16[32,4096]{1,0:T(8,128)(2,1)S(1)}, u32[]{:S(2)}, u32[]{:S(2)}) %collective-permute-start.5) | collective-permute-done | bytes 262176 | tf_op jit(solution)/shard_map/ppermute | solution.py:461
  34.3 1.6 %collective-permute-start.8 = (bf16[16,4096]{1,0:T(8,128)(2,1)S(1)}, bf16[16,4096]{1,0:T(8,128)(2,1)S(1)}, u32[]{:S(2)}, u32[]{:S(2)}) collective-permute-start(bf16[16,4096]{1,0:T(8,128)(2,1)S(1)} %slice.12), channel_id=1, source_target_pairs={{0,4},{1,5},{4,8},{5,9},{8,12},{9,13},{12,14},{13,15},{14,10},{15,... | collective-permute-start | bytes 393224 | tf_op jit(solution)/shard_map/ppermute | solution.py:458
  39.7 1.6 %collective-permute-start.13 = (bf16[32,4096]{1,0:T(8,128)(2,1)S(1)}, bf16[32,4096]{1,0:T(8,128)(2,1)S(1)}, u32[]{:S(2)}, u32[]{:S(2)}) collective-permute-start(bf16[32,4096]{1,0:T(8,128)(2,1)S(1)} %collective-permute-done.10.refs_10_.rest_0_.refs_2_), channel_id=1, source_target_pairs={{0,4},{1,5},{4,8},{5,9},{8,12},{9,13},{12,14},{13,15},{14,10},{15,... | collective-permute-start | bytes 786440 | tf_op jit(solution)/shard_map/ppermute | solution.py:458
  41.8 2.1 %collective-permute-done.12.far_ref = bf16[256,4096]{1,0:T(8,128)(2,1)S(1)} collective-permute-done((bf16[256,4096]{1,0:T(8,128)(2,1)S(1)}, bf16[256,4096]{1,0:T(8,128)(2,1)S(1)}, u32[]{:S(2)}, u32[]{:S(2)}) %collective-permute-start.12) | collective-permute-done | bytes 2097184 | tf_op jit(solution)/shard_map/ppermute | solution.py:464
  43.9 5.6 %gate_up.3 = (f32[512,512]{1,0:T(8,128)S(1)}, f32[512,512]{1,0:T(8,128)S(1)}, bf16[2,4096,256]{2,1,0:T(8,128)(2,1)S(1)}) custom-call(bf16[256,4096]{1,0:T(8,128)(2,1)S(1)} %pack.1.near_ref, bf16[256,4096]{1,0:T(8,128)(2,1)S(1)} %collective-permute-done.12.far_ref, bf16[2,4096,256]{2,1,0:T(8,128)(2,1)S(1)} %copy-done.1, bf16[4096,1792]{1,0:T(8,128)(2,1)} %wg_ref.9, ...), custom_call_target="tpu_custom_call" | custom-call | flops 4294967296 | bytes 8388608 | tf_op jit(solution)/shard_map/gate_up/pallas_call | solution.py:216
  50.3 1.6 %collective-permute-start.15 = (bf16[16,4096]{1,0:T(8,128)(2,1)S(1)}, bf16[16,4096]{1,0:T(8,128)(2,1)S(1)}, u32[]{:S(2)}, u32[]{:S(2)}) collective-permute-start(bf16[16,4096]{1,0:T(8,128)(2,1)S(1)} %slice.14), channel_id=1, source_target_pairs={{0,4},{1,5},{4,8},{5,9},{8,12},{9,13},{12,14},{13,15},{14,10},{15,... | collective-permute-start | bytes 393224 | tf_op jit(solution)/shard_map/ppermute | solution.py:458
  51.9 8.1 %gate_up.4 = (f32[768,512]{1,0:T(8,128)S(1)}, f32[768,512]{1,0:T(8,128)S(1)}, bf16[2,4096,256]{2,1,0:T(8,128)(2,1)S(1)}) custom-call(bf16[256,4096]{1,0:T(8,128)(2,1)S(1)} %pack.1.near_ref, bf16[256,4096]{1,0:T(8,128)(2,1)S(1)} %collective-permute-done.12.far_ref, bf16[2,4096,256]{2,1,0:T(8,128)(2,1)S(1)} %get-tuple-element.78.head_ref, ...), custom_call_target="tpu_custom_call" | custom-call | flops 6442450944 | bytes 12582912 | tf_op jit(solution)/shard_map/gate_up/pallas_call | solution.py:216
  60.7 5.3 %gate_up.5 = (f32[512,512]{1,0:T(8,128)S(1)}, f32[512,512]{1,0:T(8,128)S(1)}, bf16[256,4096]{1,0:T(8,128)(2,1)S(1)}) custom-call(bf16[256,4096]{1,0:T(8,128)(2,1)S(1)} %pack.1.near_ref, bf16[256,4096]{1,0:T(8,128)(2,1)S(1)} %collective-permute-done.12.far_ref, bf16[2,4096,256]{2,1,0:T(8,128)(2,1)S(1)} %get-tuple-element.81.head_ref, ...), custom_call_target="tpu_custom_call" | custom-call | flops 4294967296 | bytes 8388608 | tf_op jit(solution)/shard_map/gate_up/pallas_call | solution.py:216
  66.0 28.8 %hidden_back.1 = (bf16[512,1792]{1,0:T(8,128)(2,1)S(1)}, bf16[512,1792]{1,0:T(8,128)(2,1)S(1)}, bf16[256,4096]{1,0:T(8,128)(2,1)S(1)}, bf16[256,4096]{1,0:T(8,128)(2,1)S(1)}) custom-call(s32[8]{0:T(128)S(1)} %fusion.3.refs_9_.spot_ref, bf16[4096,256]{1,0:T(8,128)(2,1)S(1)} %pack_turned.1.rest_0_.near_ref, ...), custom_call_target="tpu_custom_call" | custom-call | flops 22548578304 | bytes 44040192 | tf_op jit(solution)/shard_map/hidden_back/pallas_call | solution.py:333
  96.3 3.4 %fisher.5 = (bf16[4096,1792]{1,0:T(8,128)(2,1)}, bf16[4096,1792]{1,0:T(8,128)(2,1)}, f32[8,128]{1,0:T(8,128)S(1)}) custom-call(bf16[512,4096]{1,0:T(8,128)(2,1)S(1)} %arrange.1.x_ref, bf16[512,1792]{1,0:T(8,128)(2,1)S(1)} %get-tuple-element.86.gg_ref, bf16[512,1792]{1,0:T(8,128)(2,1)S(1)} %get-tuple-element.87.gu_ref), custom_call_target="tpu_custom_call" | custom-call | flops 1879048192 | bytes 3670016 | tf_op jit(solution)/shard_map/fisher/pallas_call | solution.py:431
  101.8 4.6 %fisher.6 = (bf16[4096,1792]{1,0:T(8,128)(2,1)}, bf16[4096,1792]{1,0:T(8,128)(2,1)}, f32[8,128]{1,0:T(8,128)S(1)}) custom-call(bf16[512,4096]{1,0:T(8,128)(2,1)S(1)} %arrange.1.x_ref, bf16[512,1792]{1,0:T(8,128)(2,1)S(1)} %get-tuple-element.86.gg_ref, bf16[512,1792]{1,0:T(8,128)(2,1)S(1)} %get-tuple-element.87.gu_ref, ...), custom_call_target="tpu_custom_call", output_to_operand_aliasing={{0}: (3, {}), {1}: (4, {})} | custom-call | flops 2818572288 | bytes 5505024 | tf_op jit(solution)/shard_map/fisher/pallas_call | solution.py:431
  108.6 5.8 %fisher.7 = (bf16[4096,1792]{1,0:T(8,128)(2,1)}, bf16[4096,1792]{1,0:T(8,128)(2,1)}, f32[8,128]{1,0:T(8,128)S(1)}) custom-call(bf16[512,4096]{1,0:T(8,128)(2,1)S(1)} %arrange.1.x_ref, bf16[512,1792]{1,0:T(8,128)(2,1)S(1)} %get-tuple-element.86.gg_ref, bf16[512,1792]{1,0:T(8,128)(2,1)S(1)} %get-tuple-element.87.gu_ref, ...), custom_call_target="tpu_custom_call", output_to_operand_aliasing={{0}: (3, {}), {1}: (4, {})} | custom-call | flops 3758096384 | bytes 7340032 | tf_op jit(solution)/shard_map/fisher/pallas_call | solution.py:431
  117.7 5.8 %fisher.8 = (bf16[4096,1792]{1,0:T(8,128)(2,1)}, bf16[4096,1792]{1,0:T(8,128)(2,1)}, f32[8,128]{1,0:T(8,128)S(1)}) custom-call(bf16[512,4096]{1,0:T(8,128)(2,1)S(1)} %arrange.1.x_ref, bf16[512,1792]{1,0:T(8,128)(2,1)S(1)} %get-tuple-element.86.gg_ref, bf16[512,1792]{1,0:T(8,128)(2,1)S(1)} %get-tuple-element.87.gu_ref, ...), custom_call_target="tpu_custom_call", output_to_operand_aliasing={{0}: (3, {}), {1}: (4, {})} | custom-call | flops 3758096384 | bytes 7340032 | tf_op jit(solution)/shard_map/fisher/pallas_call | solution.py:431
  125.8 4.6 %fisher.9 = (bf16[4096,1792]{1,0:T(8,128)(2,1)}, bf16[4096,1792]{1,0:T(8,128)(2,1)}, f32[8,128]{1,0:T(8,128)}) custom-call(bf16[512,4096]{1,0:T(8,128)(2,1)S(1)} %arrange.1.x_ref, bf16[512,1792]{1,0:T(8,128)(2,1)S(1)} %get-tuple-element.86.gg_ref, bf16[512,1792]{1,0:T(8,128)(2,1)S(1)} %get-tuple-element.87.gu_ref, ...), custom_call_target="tpu_custom_call", output_to_operand_aliasing={{0}: (3, {}), {1}: (4, {})} | custom-call | flops 2818572288 | bytes 5505024 | tf_op jit(solution)/shard_map/fisher/pallas_call | solution.py:431
  (69 shorter events, 29.1 us)
Async XLA Ops:
  0.6 9.5 %collective-permute-start = (bf16[32,4096]{1,0:T(8,128)(2,1)}, bf16[32,4096]{1,0:T(8,128)(2,1)S(1)}, u32[]{:S(2)}, u32[]{:S(2)}) collective-permute-start(bf16[32,4096]{1,0:T(8,128)(2,1)} %x_ref.1), channel_id=1, source_target_pairs={{0,4},{1,5},{4,8},{5,9},{8,12},{9,13},{12,14},{13,15},{14,10},{15,... | collective-permute-start | bytes 786440 | tf_op jit(solution)/shard_map/ppermute | solution.py:458
  3.7 8.0 %collective-permute-start.1 = (bf16[32,4096]{1,0:T(8,128)(2,1)}, bf16[32,4096]{1,0:T(8,128)(2,1)S(1)}, u32[]{:S(2)}, u32[]{:S(2)}) collective-permute-start(bf16[32,4096]{1,0:T(8,128)(2,1)} %x_ref.1), channel_id=1, source_target_pairs={{4,0},{5,1},{8,4},{9,5},{12,8},{13,9},{14,12},{15,13},{10,14},{11,... | collective-permute-start | bytes 786440 | tf_op jit(solution)/shard_map/ppermute | solution.py:461
  11.7 9.2 %collective-permute-start.2 = (bf16[32,4096]{1,0:T(8,128)(2,1)S(1)}, bf16[32,4096]{1,0:T(8,128)(2,1)S(1)}, u32[]{:S(2)}, u32[]{:S(2)}) collective-permute-start(bf16[32,4096]{1,0:T(8,128)(2,1)S(1)} %collective-permute-done.refs_1_), channel_id=1, source_target_pairs={{0,4},{1,5},{4,8},{5,9},{8,12},{9,13},{12,14},{13,15},{14,10},{15,... | collective-permute-start | bytes 786440 | tf_op jit(solution)/shard_map/ppermute | solution.py:458
  13.3 9.2 %collective-permute-start.3 = (bf16[32,4096]{1,0:T(8,128)(2,1)S(1)}, bf16[32,4096]{1,0:T(8,128)(2,1)S(1)}, u32[]{:S(2)}, u32[]{:S(2)}) collective-permute-start(bf16[32,4096]{1,0:T(8,128)(2,1)S(1)} %collective-permute-done.1.refs_8_), channel_id=1, source_target_pairs={{4,0},{5,1},{8,4},{9,5},{12,8},{13,9},{14,12},{15,13},{10,14},{11,... | collective-permute-start | bytes 786440 | tf_op jit(solution)/shard_map/ppermute | solution.py:461
  13.7 12.8 %collective-permute-start.6 = (bf16[32,4096]{1,0:T(8,128)(2,1)S(1)}, bf16[32,4096]{1,0:T(8,128)(2,1)S(1)}, u32[]{:S(2)}, u32[]{:S(2)}) collective-permute-start(bf16[32,4096]{1,0:T(8,128)(2,1)S(1)} %get-tuple-element.67.refs_0_), channel_id=1, source_target_pairs={{0,4},{1,5},{4,8},{5,9},{8,12},{9,13},{12,14},{13,15},{14,10},{15,... | collective-permute-start | bytes 786440 | tf_op jit(solution)/shard_map/ppermute | solution.py:458
  15.3 12.8 %collective-permute-start.7 = (bf16[32,4096]{1,0:T(8,128)(2,1)S(1)}, bf16[32,4096]{1,0:T(8,128)(2,1)S(1)}, u32[]{:S(2)}, u32[]{:S(2)}) collective-permute-start(bf16[32,4096]{1,0:T(8,128)(2,1)S(1)} %get-tuple-element.67.refs_0_), channel_id=1, source_target_pairs={{4,0},{5,1},{8,4},{9,5},{12,8},{13,9},{14,12},{15,13},{10,14},{11,... | collective-permute-start | bytes 786440 | tf_op jit(solution)/shard_map/ppermute | solution.py:461
  22.5 9.7 %collective-permute-start.4 = (bf16[32,4096]{1,0:T(8,128)(2,1)S(1)}, bf16[32,4096]{1,0:T(8,128)(2,1)S(1)}, u32[]{:S(2)}, u32[]{:S(2)}) collective-permute-start(bf16[32,4096]{1,0:T(8,128)(2,1)S(1)} %collective-permute-done.2.refs_2_), channel_id=1, source_target_pairs={{0,4},{1,5},{4,8},{5,9},{8,12},{9,13},{12,14},{13,15},{14,10},{15,... | collective-permute-start | bytes 786440 | tf_op jit(solution)/shard_map/ppermute | solution.py:458
  24.1 9.7 %collective-permute-start.5 = (bf16[32,4096]{1,0:T(8,128)(2,1)S(1)}, bf16[32,4096]{1,0:T(8,128)(2,1)S(1)}, u32[]{:S(2)}, u32[]{:S(2)}) collective-permute-start(bf16[32,4096]{1,0:T(8,128)(2,1)S(1)} %collective-permute-done.3.refs_7_), channel_id=1, source_target_pairs={{4,0},{5,1},{8,4},{9,5},{12,8},{13,9},{14,12},{15,13},{10,14},{11,... | collective-permute-start | bytes 786440 | tf_op jit(solution)/shard_map/ppermute | solution.py:461
  28.1 8.7 %collective-permute-start.10 = (bf16[32,4096]{1,0:T(8,128)(2,1)S(1)}, bf16[32,4096]{1,0:T(8,128)(2,1)S(1)}, u32[]{:S(2)}, u32[]{:S(2)}) collective-permute-start(bf16[32,4096]{1,0:T(8,128)(2,1)S(1)} %collective-permute-done.6.refs_1_), channel_id=1, source_target_pairs={{0,4},{1,5},{4,8},{5,9},{8,12},{9,13},{12,14},{13,15},{14,10},{15,... | collective-permute-start | bytes 786440 | tf_op jit(solution)/shard_map/ppermute | solution.py:458
  29.7 8.4 %collective-permute-start.11 = (bf16[32,4096]{1,0:T(8,128)(2,1)S(1)}, bf16[32,4096]{1,0:T(8,128)(2,1)S(1)}, u32[]{:S(2)}, u32[]{:S(2)}) collective-permute-start(bf16[32,4096]{1,0:T(8,128)(2,1)S(1)} %collective-permute-done.7.refs_8_), channel_id=1, source_target_pairs={{4,0},{5,1},{8,4},{9,5},{12,8},{13,9},{14,12},{15,13},{10,14},{11,... | collective-permute-start | bytes 786440 | tf_op jit(solution)/shard_map/ppermute | solution.py:461
  33.8 5.7 %collective-permute-start.9 = (bf16[16,4096]{1,0:T(8,128)(2,1)S(1)}, bf16[16,4096]{1,0:T(8,128)(2,1)S(1)}, u32[]{:S(2)}, u32[]{:S(2)}) collective-permute-start(bf16[16,4096]{1,0:T(8,128)(2,1)S(1)} %slice.13), channel_id=1, source_target_pairs={{4,0},{5,1},{8,4},{9,5},{12,8},{13,9},{14,12},{15,13},{10,14},{11,... | collective-permute-start | bytes 393224 | tf_op jit(solution)/shard_map/ppermute | solution.py:461
  34.3 5.2 %collective-permute-start.8 = (bf16[16,4096]{1,0:T(8,128)(2,1)S(1)}, bf16[16,4096]{1,0:T(8,128)(2,1)S(1)}, u32[]{:S(2)}, u32[]{:S(2)}) collective-permute-start(bf16[16,4096]{1,0:T(8,128)(2,1)S(1)} %slice.12), channel_id=1, source_target_pairs={{0,4},{1,5},{4,8},{5,9},{8,12},{9,13},{12,14},{13,15},{14,10},{15,... | collective-permute-start | bytes 393224 | tf_op jit(solution)/shard_map/ppermute | solution.py:458
  39.7 9.8 %collective-permute-start.13 = (bf16[32,4096]{1,0:T(8,128)(2,1)S(1)}, bf16[32,4096]{1,0:T(8,128)(2,1)S(1)}, u32[]{:S(2)}, u32[]{:S(2)}) collective-permute-start(bf16[32,4096]{1,0:T(8,128)(2,1)S(1)} %collective-permute-done.10.refs_10_.rest_0_.refs_2_), channel_id=1, source_target_pairs={{0,4},{1,5},{4,8},{5,9},{8,12},{9,13},{12,14},{13,15},{14,10},{15,... | collective-permute-start | bytes 786440 | tf_op jit(solution)/shard_map/ppermute | solution.py:458
  41.4 8.4 %collective-permute-start.14 = (bf16[32,4096]{1,0:T(8,128)(2,1)S(1)}, bf16[32,4096]{1,0:T(8,128)(2,1)S(1)}, u32[]{:S(2)}, u32[]{:S(2)}) collective-permute-start(bf16[32,4096]{1,0:T(8,128)(2,1)S(1)} %collective-permute-done.11.refs_11_.rest_1_.refs_7_), channel_id=1, source_target_pairs={{4,0},{5,1},{8,4},{9,5},{12,8},{13,9},{14,12},{15,13},{10,14},{11,... | collective-permute-start | bytes 786440 | tf_op jit(solution)/shard_map/ppermute | solution.py:461
  49.8 10.2 %collective-permute-start.16 = (bf16[16,4096]{1,0:T(8,128)(2,1)S(1)}, bf16[16,4096]{1,0:T(8,128)(2,1)S(1)}, u32[]{:S(2)}, u32[]{:S(2)}) collective-permute-start(bf16[16,4096]{1,0:T(8,128)(2,1)S(1)} %slice.15), channel_id=1, source_target_pairs={{4,0},{5,1},{8,4},{9,5},{12,8},{13,9},{14,12},{15,13},{10,14},{11,... | collective-permute-start | bytes 393224 | tf_op jit(solution)/shard_map/ppermute | solution.py:461
  50.3 9.7 %collective-permute-start.15 = (bf16[16,4096]{1,0:T(8,128)(2,1)S(1)}, bf16[16,4096]{1,0:T(8,128)(2,1)S(1)}, u32[]{:S(2)}, u32[]{:S(2)}) collective-permute-start(bf16[16,4096]{1,0:T(8,128)(2,1)S(1)} %slice.14), channel_id=1, source_target_pairs={{0,4},{1,5},{4,8},{5,9},{8,12},{9,13},{12,14},{13,15},{14,10},{15,... | collective-permute-start | bytes 393224 | tf_op jit(solution)/shard_map/ppermute | solution.py:458
  60.6 5.4 %collective-permute-start.17 = (bf16[4096,256]{1,0:T(8,128)(2,1)S(1)}, bf16[4096,256]{1,0:T(8,128)(2,1)S(1)}, u32[]{:S(2)}, u32[]{:S(2)}) collective-permute-start(bf16[4096,256]{1,0:T(8,128)(2,1)S(1)} %pack_turned.1.rest_0_.near_ref), channel_id=1, source_target_pairs={{0,1},{1,0},{2,3},{3,2},{4,5},{5,4},{6,7},{7,6},{8,9},{9,8},{10,11... | collective-permute-start | bytes 6291464 | tf_op jit(solution)/shard_map/ppermute | solution.py:464
  99.7 6.7 %collective-permute-start.19 = (bf16[16,4096]{1,0:T(8,128)(2,1)S(1)}, bf16[16,4096]{1,0:T(8,128)(2,1)S(1)}, u32[]{:S(2)}, u32[]{:S(2)}) collective-permute-start(bf16[16,4096]{1,0:T(8,128)(2,1)S(1)} %get-tuple-element.92.rest_2_), channel_id=1, source_target_pairs={{0,4},{1,5},{4,8},{5,9},{8,12},{9,13},{12,14},{13,15},{14,10},{15,... | collective-permute-start | bytes 393224 | tf_op jit(solution)/shard_map/ppermute | solution.py:458
  106.6 7.9 %collective-permute-start.21 = (bf16[32,4096]{1,0:T(8,128)(2,1)S(1)}, bf16[32,4096]{1,0:T(8,128)(2,1)S(1)}, u32[]{:S(2)}, u32[]{:S(2)}) collective-permute-start(bf16[32,4096]{1,0:T(8,128)(2,1)S(1)} %get-tuple-element.97.rest_2_), channel_id=1, source_target_pairs={{0,4},{1,5},{4,8},{5,9},{8,12},{9,13},{12,14},{13,15},{14,10},{15,... | collective-permute-start | bytes 786440 | tf_op jit(solution)/shard_map/ppermute | solution.py:458
  108.1 7.4 %collective-permute-start.22 = (bf16[32,4096]{1,0:T(8,128)(2,1)S(1)}, bf16[32,4096]{1,0:T(8,128)(2,1)S(1)}, u32[]{:S(2)}, u32[]{:S(2)}) collective-permute-start(bf16[32,4096]{1,0:T(8,128)(2,1)S(1)} %get-tuple-element.98.rest_3_), channel_id=1, source_target_pairs={{4,0},{5,1},{8,4},{9,5},{12,8},{13,9},{14,12},{15,13},{10,14},{11,... | collective-permute-start | bytes 786440 | tf_op jit(solution)/shard_map/ppermute | solution.py:461
  115.7 7.9 %collective-permute-start.23 = (bf16[32,4096]{1,0:T(8,128)(2,1)S(1)}, bf16[32,4096]{1,0:T(8,128)(2,1)S(1)}, u32[]{:S(2)}, u32[]{:S(2)}) collective-permute-start(bf16[32,4096]{1,0:T(8,128)(2,1)S(1)} %get-tuple-element.102.rest_2_), channel_id=1, source_target_pairs={{0,4},{1,5},{4,8},{5,9},{8,12},{9,13},{12,14},{13,15},{14,10},{15,... | collective-permute-start | bytes 786440 | tf_op jit(solution)/shard_map/ppermute | solution.py:458
  117.1 6.5 %collective-permute-start.24 = (bf16[32,4096]{1,0:T(8,128)(2,1)S(1)}, bf16[32,4096]{1,0:T(8,128)(2,1)S(1)}, u32[]{:S(2)}, u32[]{:S(2)}) collective-permute-start(bf16[32,4096]{1,0:T(8,128)(2,1)S(1)} %get-tuple-element.103.rest_3_), channel_id=1, source_target_pairs={{4,0},{5,1},{8,4},{9,5},{12,8},{13,9},{14,12},{15,13},{10,14},{11,... | collective-permute-start | bytes 786440 | tf_op jit(solution)/shard_map/ppermute | solution.py:461
  123.8 6.7 %collective-permute-start.25 = (bf16[32,4096]{1,0:T(8,128)(2,1)S(1)}, bf16[32,4096]{1,0:T(8,128)(2,1)S(1)}, u32[]{:S(2)}, u32[]{:S(2)}) collective-permute-start(bf16[32,4096]{1,0:T(8,128)(2,1)S(1)} %get-tuple-element.107.rest_2_), channel_id=1, source_target_pairs={{0,4},{1,5},{4,8},{5,9},{8,12},{9,13},{12,14},{13,15},{14,10},{15,... | collective-permute-start | bytes 786440 | tf_op jit(solution)/shard_map/ppermute | solution.py:458
  125.2 6.4 %collective-permute-start.26 = (bf16[32,4096]{1,0:T(8,128)(2,1)S(1)}, bf16[32,4096]{1,0:T(8,128)(2,1)S(1)}, u32[]{:S(2)}, u32[]{:S(2)}) collective-permute-start(bf16[32,4096]{1,0:T(8,128)(2,1)S(1)} %get-tuple-element.108.rest_3_), channel_id=1, source_target_pairs={{4,0},{5,1},{8,4},{9,5},{12,8},{13,9},{14,12},{15,13},{10,14},{11,... | collective-permute-start | bytes 786440 | tf_op jit(solution)/shard_map/ppermute | solution.py:461
  (9 other events, 79.6 us)

commit v15 on v14

--- a/solution.py
+++ b/solution.py
@@ -429,7 +429,7 @@
     width = gg.shape[1]
     block = pl.BlockSpec((step, width), lambda j: (first + j, 0))
     return pl.pallas_call(
-        functools.partial(fisher_kernel, tile(width, 256)),
+        functools.partial(fisher_kernel, tile(width, 896)),
         grid=(count,),
         in_specs=[pl.BlockSpec((rows, step), lambda j: (0, first + j))]
         + held_specs(2)

time: 133 us -> 134 us (level)
  Pallas kernels: 77.3 us -> 79.9 us
    pallas_call x5, Pallas kernels: 24.1 us -> 26.8 us  [fisher(): pl.pallas_call(functools.partial(fisher_kernel, tile(width, 896)), grid=(...]
  transfers between devices with their start and end apart: 27 -> 27, of which waited for: 15 -> 15; matrix products, arithmetic and copies ran while one was open for 1% -> 1% of each run, Pallas kernels for 35% -> 37%
where the time goes in v15:
time: 134 us
  Pallas kernels  79.9 us (60%)
  starting transfers between devices  26.4 us (20%)
  waiting for transfers between devices  20.8 us (16%)
  local copies, waits for them, and re-layouts  5.19 us (4%)
    pallas_call x1, Pallas kernels, back(): pl.pallas_call(functools.partial(back_kernel, step, 512, len(a)), in_spec...  28.8 us
    pallas_call x5, Pallas kernels, fisher(): pl.pallas_call(functools.partial(fisher_kernel, tile(width, 896)), grid=(...  26.8 us
    ppermute x12, starting transfers between devices, right(): return lax.ppermute(value, 'hid', to_right)  20.1 us
    pallas_call x3, Pallas kernels, gate_up(): pl.pallas_call(functools.partial(gate_up_kernel, first, step), in_specs=h...  19.1 us
    ppermute x12, waiting for transfers between devices, left(): return lax.ppermute(value, 'hid', to_left)  10.2 us
    ppermute x12, waiting for transfers between devices, right(): return lax.ppermute(value, 'hid', to_right)  8.49 us
    ppermute x12, starting transfers between devices, left(): return lax.ppermute(value, 'hid', to_left)  5.62 us
    unnamed x12, local copies, waits for them, and re-layouts  3.92 us
  transfers between devices with their start and end apart: 27, of which 15 were waited for; matrix products, arithmetic and copies ran while one was open for 1% of the time, Pallas kernels for 37%

profile of v15, /device:TPU:0, one launch (start us, length us, event | category | flops | bytes accessed | tf_op | source)
XLA Modules:
  0.0 133.9 jit_solution(8594550319528115938)
XLA Ops:
  0.6 3.1 %collective-permute-start = (bf16[32,4096]{1,0:T(8,128)(2,1)}, bf16[32,4096]{1,0:T(8,128)(2,1)S(1)}, u32[]{:S(2)}, u32[]{:S(2)}) collective-permute-start(bf16[32,4096]{1,0:T(8,128)(2,1)} %x_ref.1), channel_id=1, source_target_pairs={{0,4},{1,5},{4,8},{5,9},{8,12},{9,13},{12,14},{13,15},{14,10},{15,... | collective-permute-start | bytes 786440 | tf_op jit(solution)/shard_map/ppermute | solution.py:458
  5.6 2.3 %bring.1 = (bf16[32,4096]{1,0:T(8,128)(2,1)S(1)}, bf16[32,4096]{1,0:T(8,128)(2,1)S(1)}, bf16[2,4096,256]{2,1,0:T(8,128)(2,1)S(1)}) custom-call(bf16[32,4096]{1,0:T(8,128)(2,1)S(1)} %copy-done.3, bf16[32,4096]{1,0:T(8,128)(2,1)S(1)} %copy-done.2, bf16[4096,1792]{1,0:T(8,128)(2,1)} %wg_ref.9, bf16[4096,1792]{1,0:T(8,128)(2,1)} %wu_ref.9), custom_call_target="tpu_custom_call" | custom-call | bytes 4194304 | tf_op jit(solution)/shard_map/bring/pallas_call | solution.py:61
  7.9 2.0 %copy-done = bf16[2,4096,256]{2,1,0:T(8,128)(2,1)} copy-done((bf16[2,4096,256]{2,1,0:T(8,128)(2,1)}, bf16[2,4096,256]{2,1,0:T(8,128)(2,1)S(1)}, u32[]{:S(2)}) %copy-start) | copy-done | bytes 4194328
  11.7 1.6 %collective-permute-start.2 = (bf16[32,4096]{1,0:T(8,128)(2,1)S(1)}, bf16[32,4096]{1,0:T(8,128)(2,1)S(1)}, u32[]{:S(2)}, u32[]{:S(2)}) collective-permute-start(bf16[32,4096]{1,0:T(8,128)(2,1)S(1)} %collective-permute-done.refs_1_), channel_id=1, source_target_pairs={{0,4},{1,5},{4,8},{5,9},{8,12},{9,13},{12,14},{13,15},{14,10},{15,... | collective-permute-start | bytes 786440 | tf_op jit(solution)/shard_map/ppermute | solution.py:458
  13.7 1.6 %collective-permute-start.6 = (bf16[32,4096]{1,0:T(8,128)(2,1)S(1)}, bf16[32,4096]{1,0:T(8,128)(2,1)S(1)}, u32[]{:S(2)}, u32[]{:S(2)}) collective-permute-start(bf16[32,4096]{1,0:T(8,128)(2,1)S(1)} %get-tuple-element.67.refs_0_), channel_id=1, source_target_pairs={{0,4},{1,5},{4,8},{5,9},{8,12},{9,13},{12,14},{13,15},{14,10},{15,... | collective-permute-start | bytes 786440 | tf_op jit(solution)/shard_map/ppermute | solution.py:458
  15.7 5.2 %collective-permute-done.2.refs_2_ = bf16[32,4096]{1,0:T(8,128)(2,1)S(1)} collective-permute-done((bf16[32,4096]{1,0:T(8,128)(2,1)S(1)}, bf16[32,4096]{1,0:T(8,128)(2,1)S(1)}, u32[]{:S(2)}, u32[]{:S(2)}) %collective-permute-start.2) | collective-permute-done | bytes 262176 | tf_op jit(solution)/shard_map/ppermute | solution.py:458
  20.9 1.6 %collective-permute-done.3.refs_7_ = bf16[32,4096]{1,0:T(8,128)(2,1)S(1)} collective-permute-done((bf16[32,4096]{1,0:T(8,128)(2,1)S(1)}, bf16[32,4096]{1,0:T(8,128)(2,1)S(1)}, u32[]{:S(2)}, u32[]{:S(2)}) %collective-permute-start.3) | collective-permute-done | bytes 262176 | tf_op jit(solution)/shard_map/ppermute | solution.py:461
  22.5 1.6 %collective-permute-start.4 = (bf16[32,4096]{1,0:T(8,128)(2,1)S(1)}, bf16[32,4096]{1,0:T(8,128)(2,1)S(1)}, u32[]{:S(2)}, u32[]{:S(2)}) collective-permute-start(bf16[32,4096]{1,0:T(8,128)(2,1)S(1)} %collective-permute-done.2.refs_2_), channel_id=1, source_target_pairs={{0,4},{1,5},{4,8},{5,9},{8,12},{9,13},{12,14},{13,15},{14,10},{15,... | collective-permute-start | bytes 786440 | tf_op jit(solution)/shard_map/ppermute | solution.py:458
  26.6 1.6 %collective-permute-done.7.refs_8_ = bf16[32,4096]{1,0:T(8,128)(2,1)S(1)} collective-permute-done((bf16[32,4096]{1,0:T(8,128)(2,1)S(1)}, bf16[32,4096]{1,0:T(8,128)(2,1)S(1)}, u32[]{:S(2)}, u32[]{:S(2)}) %collective-permute-start.7) | collective-permute-done | bytes 262176 | tf_op jit(solution)/shard_map/ppermute | solution.py:461
  28.1 1.6 %collective-permute-start.10 = (bf16[32,4096]{1,0:T(8,128)(2,1)S(1)}, bf16[32,4096]{1,0:T(8,128)(2,1)S(1)}, u32[]{:S(2)}, u32[]{:S(2)}) collective-permute-start(bf16[32,4096]{1,0:T(8,128)(2,1)S(1)} %collective-permute-done.6.refs_1_), channel_id=1, source_target_pairs={{0,4},{1,5},{4,8},{5,9},{8,12},{9,13},{12,14},{13,15},{14,10},{15,... | collective-permute-start | bytes 786440 | tf_op jit(solution)/shard_map/ppermute | solution.py:458
  32.2 1.6 %collective-permute-done.5.refs_6_ = bf16[32,4096]{1,0:T(8,128)(2,1)S(1)} collective-permute-done((bf16[32,4096]{1,0:T(8,128)(2,1)S(1)}, bf16[32,4096]{1,0:T(8,128)(2,1)S(1)}, u32[]{:S(2)}, u32[]{:S(2)}) %collective-permute-start.5) | collective-permute-done | bytes 262176 | tf_op jit(solution)/shard_map/ppermute | solution.py:461
  34.3 1.6 %collective-permute-start.8 = (bf16[16,4096]{1,0:T(8,128)(2,1)S(1)}, bf16[16,4096]{1,0:T(8,128)(2,1)S(1)}, u32[]{:S(2)}, u32[]{:S(2)}) collective-permute-start(bf16[16,4096]{1,0:T(8,128)(2,1)S(1)} %slice.12), channel_id=1, source_target_pairs={{0,4},{1,5},{4,8},{5,9},{8,12},{9,13},{12,14},{13,15},{14,10},{15,... | collective-permute-start | bytes 393224 | tf_op jit(solution)/shard_map/ppermute | solution.py:458
  39.7 1.6 %collective-permute-start.13 = (bf16[32,4096]{1,0:T(8,128)(2,1)S(1)}, bf16[32,4096]{1,0:T(8,128)(2,1)S(1)}, u32[]{:S(2)}, u32[]{:S(2)}) collective-permute-start(bf16[32,4096]{1,0:T(8,128)(2,1)S(1)} %collective-permute-done.10.refs_10_.rest_0_.refs_2_), channel_id=1, source_target_pairs={{0,4},{1,5},{4,8},{5,9},{8,12},{9,13},{12,14},{13,15},{14,10},{15,... | collective-permute-start | bytes 786440 | tf_op jit(solution)/shard_map/ppermute | solution.py:458
  41.8 2.1 %collective-permute-done.12.far_ref = bf16[256,4096]{1,0:T(8,128)(2,1)S(1)} collective-permute-done((bf16[256,4096]{1,0:T(8,128)(2,1)S(1)}, bf16[256,4096]{1,0:T(8,128)(2,1)S(1)}, u32[]{:S(2)}, u32[]{:S(2)}) %collective-permute-start.12) | collective-permute-done | bytes 2097184 | tf_op jit(solution)/shard_map/ppermute | solution.py:464
  43.9 5.6 %gate_up.3 = (f32[512,512]{1,0:T(8,128)S(1)}, f32[512,512]{1,0:T(8,128)S(1)}, bf16[2,4096,256]{2,1,0:T(8,128)(2,1)S(1)}) custom-call(bf16[256,4096]{1,0:T(8,128)(2,1)S(1)} %pack.1.near_ref, bf16[256,4096]{1,0:T(8,128)(2,1)S(1)} %collective-permute-done.12.far_ref, bf16[2,4096,256]{2,1,0:T(8,128)(2,1)S(1)} %copy-done.1, bf16[4096,1792]{1,0:T(8,128)(2,1)} %wg_ref.9, ...), custom_call_target="tpu_custom_call" | custom-call | flops 4294967296 | bytes 8388608 | tf_op jit(solution)/shard_map/gate_up/pallas_call | solution.py:216
  50.3 1.6 %collective-permute-start.15 = (bf16[16,4096]{1,0:T(8,128)(2,1)S(1)}, bf16[16,4096]{1,0:T(8,128)(2,1)S(1)}, u32[]{:S(2)}, u32[]{:S(2)}) collective-permute-start(bf16[16,4096]{1,0:T(8,128)(2,1)S(1)} %slice.14), channel_id=1, source_target_pairs={{0,4},{1,5},{4,8},{5,9},{8,12},{9,13},{12,14},{13,15},{14,10},{15,... | collective-permute-start | bytes 393224 | tf_op jit(solution)/shard_map/ppermute | solution.py:458
  51.9 8.1 %gate_up.4 = (f32[768,512]{1,0:T(8,128)S(1)}, f32[768,512]{1,0:T(8,128)S(1)}, bf16[2,4096,256]{2,1,0:T(8,128)(2,1)S(1)}) custom-call(bf16[256,4096]{1,0:T(8,128)(2,1)S(1)} %pack.1.near_ref, bf16[256,4096]{1,0:T(8,128)(2,1)S(1)} %collective-permute-done.12.far_ref, bf16[2,4096,256]{2,1,0:T(8,128)(2,1)S(1)} %get-tuple-element.78.head_ref, ...), custom_call_target="tpu_custom_call" | custom-call | flops 6442450944 | bytes 12582912 | tf_op jit(solution)/shard_map/gate_up/pallas_call | solution.py:216
  60.7 5.3 %gate_up.5 = (f32[512,512]{1,0:T(8,128)S(1)}, f32[512,512]{1,0:T(8,128)S(1)}, bf16[256,4096]{1,0:T(8,128)(2,1)S(1)}) custom-call(bf16[256,4096]{1,0:T(8,128)(2,1)S(1)} %pack.1.near_ref, bf16[256,4096]{1,0:T(8,128)(2,1)S(1)} %collective-permute-done.12.far_ref, bf16[2,4096,256]{2,1,0:T(8,128)(2,1)S(1)} %get-tuple-element.81.head_ref, ...), custom_call_target="tpu_custom_call" | custom-call | flops 4294967296 | bytes 8388608 | tf_op jit(solution)/shard_map/gate_up/pallas_call | solution.py:216
  66.0 28.8 %hidden_back.1 = (bf16[512,1792]{1,0:T(8,128)(2,1)S(1)}, bf16[512,1792]{1,0:T(8,128)(2,1)S(1)}, bf16[256,4096]{1,0:T(8,128)(2,1)S(1)}, bf16[256,4096]{1,0:T(8,128)(2,1)S(1)}) custom-call(s32[8]{0:T(128)S(1)} %fusion.3.refs_9_.spot_ref, bf16[4096,256]{1,0:T(8,128)(2,1)S(1)} %pack_turned.1.rest_0_.near_ref, ...), custom_call_target="tpu_custom_call" | custom-call | flops 22548578304 | bytes 44040192 | tf_op jit(solution)/shard_map/hidden_back/pallas_call | solution.py:333
  96.3 3.7 %fisher.5 = (bf16[4096,1792]{1,0:T(8,128)(2,1)}, bf16[4096,1792]{1,0:T(8,128)(2,1)}, f32[8,128]{1,0:T(8,128)S(1)}) custom-call(bf16[512,4096]{1,0:T(8,128)(2,1)S(1)} %arrange.1.x_ref, bf16[512,1792]{1,0:T(8,128)(2,1)S(1)} %get-tuple-element.86.gg_ref, bf16[512,1792]{1,0:T(8,128)(2,1)S(1)} %get-tuple-element.87.gu_ref), custom_call_target="tpu_custom_call" | custom-call | flops 1879048192 | bytes 3670016 | tf_op jit(solution)/shard_map/fisher/pallas_call | solution.py:431
  102.1 5.1 %fisher.6 = (bf16[4096,1792]{1,0:T(8,128)(2,1)}, bf16[4096,1792]{1,0:T(8,128)(2,1)}, f32[8,128]{1,0:T(8,128)S(1)}) custom-call(bf16[512,4096]{1,0:T(8,128)(2,1)S(1)} %arrange.1.x_ref, bf16[512,1792]{1,0:T(8,128)(2,1)S(1)} %get-tuple-element.86.gg_ref, bf16[512,1792]{1,0:T(8,128)(2,1)S(1)} %get-tuple-element.87.gu_ref, ...), custom_call_target="tpu_custom_call", output_to_operand_aliasing={{0}: (3, {}), {1}: (4, {})} | custom-call | flops 2818572288 | bytes 5505024 | tf_op jit(solution)/shard_map/fisher/pallas_call | solution.py:431
  109.5 6.5 %fisher.7 = (bf16[4096,1792]{1,0:T(8,128)(2,1)}, bf16[4096,1792]{1,0:T(8,128)(2,1)}, f32[8,128]{1,0:T(8,128)S(1)}) custom-call(bf16[512,4096]{1,0:T(8,128)(2,1)S(1)} %arrange.1.x_ref, bf16[512,1792]{1,0:T(8,128)(2,1)S(1)} %get-tuple-element.86.gg_ref, bf16[512,1792]{1,0:T(8,128)(2,1)S(1)} %get-tuple-element.87.gu_ref, ...), custom_call_target="tpu_custom_call", output_to_operand_aliasing={{0}: (3, {}), {1}: (4, {})} | custom-call | flops 3758096384 | bytes 7340032 | tf_op jit(solution)/shard_map/fisher/pallas_call | solution.py:431
  118.6 6.5 %fisher.8 = (bf16[4096,1792]{1,0:T(8,128)(2,1)}, bf16[4096,1792]{1,0:T(8,128)(2,1)}, f32[8,128]{1,0:T(8,128)S(1)}) custom-call(bf16[512,4096]{1,0:T(8,128)(2,1)S(1)} %arrange.1.x_ref, bf16[512,1792]{1,0:T(8,128)(2,1)S(1)} %get-tuple-element.86.gg_ref, bf16[512,1792]{1,0:T(8,128)(2,1)S(1)} %get-tuple-element.87.gu_ref, ...), custom_call_target="tpu_custom_call", output_to_operand_aliasing={{0}: (3, {}), {1}: (4, {})} | custom-call | flops 3758096384 | bytes 7340032 | tf_op jit(solution)/shard_map/fisher/pallas_call | solution.py:431
  127.3 5.1 %fisher.9 = (bf16[4096,1792]{1,0:T(8,128)(2,1)}, bf16[4096,1792]{1,0:T(8,128)(2,1)}, f32[8,128]{1,0:T(8,128)}) custom-call(bf16[512,4096]{1,0:T(8,128)(2,1)S(1)} %arrange.1.x_ref, bf16[512,1792]{1,0:T(8,128)(2,1)S(1)} %get-tuple-element.86.gg_ref, bf16[512,1792]{1,0:T(8,128)(2,1)S(1)} %get-tuple-element.87.gu_ref, ...), custom_call_target="tpu_custom_call", output_to_operand_aliasing={{0}: (3, {}), {1}: (4, {})} | custom-call | flops 2818572288 | bytes 5505024 | tf_op jit(solution)/shard_map/fisher/pallas_call | solution.py:431
  (69 shorter events, 27.9 us)
Async XLA Ops:
  0.6 9.5 %collective-permute-start = (bf16[32,4096]{1,0:T(8,128)(2,1)}, bf16[32,4096]{1,0:T(8,128)(2,1)S(1)}, u32[]{:S(2)}, u32[]{:S(2)}) collective-permute-start(bf16[32,4096]{1,0:T(8,128)(2,1)} %x_ref.1), channel_id=1, source_target_pairs={{0,4},{1,5},{4,8},{5,9},{8,12},{9,13},{12,14},{13,15},{14,10},{15,... | collective-permute-start | bytes 786440 | tf_op jit(solution)/shard_map/ppermute | solution.py:458
  3.7 8.0 %collective-permute-start.1 = (bf16[32,4096]{1,0:T(8,128)(2,1)}, bf16[32,4096]{1,0:T(8,128)(2,1)S(1)}, u32[]{:S(2)}, u32[]{:S(2)}) collective-permute-start(bf16[32,4096]{1,0:T(8,128)(2,1)} %x_ref.1), channel_id=1, source_target_pairs={{4,0},{5,1},{8,4},{9,5},{12,8},{13,9},{14,12},{15,13},{10,14},{11,... | collective-permute-start | bytes 786440 | tf_op jit(solution)/shard_map/ppermute | solution.py:461
  11.7 9.2 %collective-permute-start.2 = (bf16[32,4096]{1,0:T(8,128)(2,1)S(1)}, bf16[32,4096]{1,0:T(8,128)(2,1)S(1)}, u32[]{:S(2)}, u32[]{:S(2)}) collective-permute-start(bf16[32,4096]{1,0:T(8,128)(2,1)S(1)} %collective-permute-done.refs_1_), channel_id=1, source_target_pairs={{0,4},{1,5},{4,8},{5,9},{8,12},{9,13},{12,14},{13,15},{14,10},{15,... | collective-permute-start | bytes 786440 | tf_op jit(solution)/shard_map/ppermute | solution.py:458
  13.3 9.2 %collective-permute-start.3 = (bf16[32,4096]{1,0:T(8,128)(2,1)S(1)}, bf16[32,4096]{1,0:T(8,128)(2,1)S(1)}, u32[]{:S(2)}, u32[]{:S(2)}) collective-permute-start(bf16[32,4096]{1,0:T(8,128)(2,1)S(1)} %collective-permute-done.1.refs_8_), channel_id=1, source_target_pairs={{4,0},{5,1},{8,4},{9,5},{12,8},{13,9},{14,12},{15,13},{10,14},{11,... | collective-permute-start | bytes 786440 | tf_op jit(solution)/shard_map/ppermute | solution.py:461
  13.7 12.8 %collective-permute-start.6 = (bf16[32,4096]{1,0:T(8,128)(2,1)S(1)}, bf16[32,4096]{1,0:T(8,128)(2,1)S(1)}, u32[]{:S(2)}, u32[]{:S(2)}) collective-permute-start(bf16[32,4096]{1,0:T(8,128)(2,1)S(1)} %get-tuple-element.67.refs_0_), channel_id=1, source_target_pairs={{0,4},{1,5},{4,8},{5,9},{8,12},{9,13},{12,14},{13,15},{14,10},{15,... | collective-permute-start | bytes 786440 | tf_op jit(solution)/shard_map/ppermute | solution.py:458
  15.3 12.8 %collective-permute-start.7 = (bf16[32,4096]{1,0:T(8,128)(2,1)S(1)}, bf16[32,4096]{1,0:T(8,128)(2,1)S(1)}, u32[]{:S(2)}, u32[]{:S(2)}) collective-permute-start(bf16[32,4096]{1,0:T(8,128)(2,1)S(1)} %get-tuple-element.67.refs_0_), channel_id=1, source_target_pairs={{4,0},{5,1},{8,4},{9,5},{12,8},{13,9},{14,12},{15,13},{10,14},{11,... | collective-permute-start | bytes 786440 | tf_op jit(solution)/shard_map/ppermute | solution.py:461
  22.5 9.7 %collective-permute-start.4 = (bf16[32,4096]{1,0:T(8,128)(2,1)S(1)}, bf16[32,4096]{1,0:T(8,128)(2,1)S(1)}, u32[]{:S(2)}, u32[]{:S(2)}) collective-permute-start(bf16[32,4096]{1,0:T(8,128)(2,1)S(1)} %collective-permute-done.2.refs_2_), channel_id=1, source_target_pairs={{0,4},{1,5},{4,8},{5,9},{8,12},{9,13},{12,14},{13,15},{14,10},{15,... | collective-permute-start | bytes 786440 | tf_op jit(solution)/shard_map/ppermute | solution.py:458
  24.1 9.7 %collective-permute-start.5 = (bf16[32,4096]{1,0:T(8,128)(2,1)S(1)}, bf16[32,4096]{1,0:T(8,128)(2,1)S(1)}, u32[]{:S(2)}, u32[]{:S(2)}) collective-permute-start(bf16[32,4096]{1,0:T(8,128)(2,1)S(1)} %collective-permute-done.3.refs_7_), channel_id=1, source_target_pairs={{4,0},{5,1},{8,4},{9,5},{12,8},{13,9},{14,12},{15,13},{10,14},{11,... | collective-permute-start | bytes 786440 | tf_op jit(solution)/shard_map/ppermute | solution.py:461
  28.1 8.7 %collective-permute-start.10 = (bf16[32,4096]{1,0:T(8,128)(2,1)S(1)}, bf16[32,4096]{1,0:T(8,128)(2,1)S(1)}, u32[]{:S(2)}, u32[]{:S(2)}) collective-permute-start(bf16[32,4096]{1,0:T(8,128)(2,1)S(1)} %collective-permute-done.6.refs_1_), channel_id=1, source_target_pairs={{0,4},{1,5},{4,8},{5,9},{8,12},{9,13},{12,14},{13,15},{14,10},{15,... | collective-permute-start | bytes 786440 | tf_op jit(solution)/shard_map/ppermute | solution.py:458
  29.7 8.4 %collective-permute-start.11 = (bf16[32,4096]{1,0:T(8,128)(2,1)S(1)}, bf16[32,4096]{1,0:T(8,128)(2,1)S(1)}, u32[]{:S(2)}, u32[]{:S(2)}) collective-permute-start(bf16[32,4096]{1,0:T(8,128)(2,1)S(1)} %collective-permute-done.7.refs_8_), channel_id=1, source_target_pairs={{4,0},{5,1},{8,4},{9,5},{12,8},{13,9},{14,12},{15,13},{10,14},{11,... | collective-permute-start | bytes 786440 | tf_op jit(solution)/shard_map/ppermute | solution.py:461
  33.8 5.7 %collective-permute-start.9 = (bf16[16,4096]{1,0:T(8,128)(2,1)S(1)}, bf16[16,4096]{1,0:T(8,128)(2,1)S(1)}, u32[]{:S(2)}, u32[]{:S(2)}) collective-permute-start(bf16[16,4096]{1,0:T(8,128)(2,1)S(1)} %slice.13), channel_id=1, source_target_pairs={{4,0},{5,1},{8,4},{9,5},{12,8},{13,9},{14,12},{15,13},{10,14},{11,... | collective-permute-start | bytes 393224 | tf_op jit(solution)/shard_map/ppermute | solution.py:461
  39.7 9.8 %collective-permute-start.13 = (bf16[32,4096]{1,0:T(8,128)(2,1)S(1)}, bf16[32,4096]{1,0:T(8,128)(2,1)S(1)}, u32[]{:S(2)}, u32[]{:S(2)}) collective-permute-start(bf16[32,4096]{1,0:T(8,128)(2,1)S(1)} %collective-permute-done.10.refs_10_.rest_0_.refs_2_), channel_id=1, source_target_pairs={{0,4},{1,5},{4,8},{5,9},{8,12},{9,13},{12,14},{13,15},{14,10},{15,... | collective-permute-start | bytes 786440 | tf_op jit(solution)/shard_map/ppermute | solution.py:458
  41.4 8.4 %collective-permute-start.14 = (bf16[32,4096]{1,0:T(8,128)(2,1)S(1)}, bf16[32,4096]{1,0:T(8,128)(2,1)S(1)}, u32[]{:S(2)}, u32[]{:S(2)}) collective-permute-start(bf16[32,4096]{1,0:T(8,128)(2,1)S(1)} %collective-permute-done.11.refs_11_.rest_1_.refs_7_), channel_id=1, source_target_pairs={{4,0},{5,1},{8,4},{9,5},{12,8},{13,9},{14,12},{15,13},{10,14},{11,... | collective-permute-start | bytes 786440 | tf_op jit(solution)/shard_map/ppermute | solution.py:461
  49.8 10.2 %collective-permute-start.16 = (bf16[16,4096]{1,0:T(8,128)(2,1)S(1)}, bf16[16,4096]{1,0:T(8,128)(2,1)S(1)}, u32[]{:S(2)}, u32[]{:S(2)}) collective-permute-start(bf16[16,4096]{1,0:T(8,128)(2,1)S(1)} %slice.15), channel_id=1, source_target_pairs={{4,0},{5,1},{8,4},{9,5},{12,8},{13,9},{14,12},{15,13},{10,14},{11,... | collective-permute-start | bytes 393224 | tf_op jit(solution)/shard_map/ppermute | solution.py:461
  50.3 9.7 %collective-permute-start.15 = (bf16[16,4096]{1,0:T(8,128)(2,1)S(1)}, bf16[16,4096]{1,0:T(8,128)(2,1)S(1)}, u32[]{:S(2)}, u32[]{:S(2)}) collective-permute-start(bf16[16,4096]{1,0:T(8,128)(2,1)S(1)} %slice.14), channel_id=1, source_target_pairs={{0,4},{1,5},{4,8},{5,9},{8,12},{9,13},{12,14},{13,15},{14,10},{15,... | collective-permute-start | bytes 393224 | tf_op jit(solution)/shard_map/ppermute | solution.py:458
  60.6 5.4 %collective-permute-start.17 = (bf16[4096,256]{1,0:T(8,128)(2,1)S(1)}, bf16[4096,256]{1,0:T(8,128)(2,1)S(1)}, u32[]{:S(2)}, u32[]{:S(2)}) collective-permute-start(bf16[4096,256]{1,0:T(8,128)(2,1)S(1)} %pack_turned.1.rest_0_.near_ref), channel_id=1, source_target_pairs={{0,1},{1,0},{2,3},{3,2},{4,5},{5,4},{6,7},{7,6},{8,9},{9,8},{10,11... | collective-permute-start | bytes 6291464 | tf_op jit(solution)/shard_map/ppermute | solution.py:464
  100.1 7.2 %collective-permute-start.19 = (bf16[16,4096]{1,0:T(8,128)(2,1)S(1)}, bf16[16,4096]{1,0:T(8,128)(2,1)S(1)}, u32[]{:S(2)}, u32[]{:S(2)}) collective-permute-start(bf16[16,4096]{1,0:T(8,128)(2,1)S(1)} %get-tuple-element.92.rest_2_), channel_id=1, source_target_pairs={{0,4},{1,5},{4,8},{5,9},{8,12},{9,13},{12,14},{13,15},{14,10},{15,... | collective-permute-start | bytes 393224 | tf_op jit(solution)/shard_map/ppermute | solution.py:458
  101.6 5.6 %collective-permute-start.20 = (bf16[16,4096]{1,0:T(8,128)(2,1)S(1)}, bf16[16,4096]{1,0:T(8,128)(2,1)S(1)}, u32[]{:S(2)}, u32[]{:S(2)}) collective-permute-start(bf16[16,4096]{1,0:T(8,128)(2,1)S(1)} %get-tuple-element.93.rest_3_), channel_id=1, source_target_pairs={{4,0},{5,1},{8,4},{9,5},{12,8},{13,9},{14,12},{15,13},{10,14},{11,... | collective-permute-start | bytes 393224 | tf_op jit(solution)/shard_map/ppermute | solution.py:461
  107.4 8.5 %collective-permute-start.21 = (bf16[32,4096]{1,0:T(8,128)(2,1)S(1)}, bf16[32,4096]{1,0:T(8,128)(2,1)S(1)}, u32[]{:S(2)}, u32[]{:S(2)}) collective-permute-start(bf16[32,4096]{1,0:T(8,128)(2,1)S(1)} %get-tuple-element.97.rest_2_), channel_id=1, source_target_pairs={{0,4},{1,5},{4,8},{5,9},{8,12},{9,13},{12,14},{13,15},{14,10},{15,... | collective-permute-start | bytes 786440 | tf_op jit(solution)/shard_map/ppermute | solution.py:458
  108.9 7.4 %collective-permute-start.22 = (bf16[32,4096]{1,0:T(8,128)(2,1)S(1)}, bf16[32,4096]{1,0:T(8,128)(2,1)S(1)}, u32[]{:S(2)}, u32[]{:S(2)}) collective-permute-start(bf16[32,4096]{1,0:T(8,128)(2,1)S(1)} %get-tuple-element.98.rest_3_), channel_id=1, source_target_pairs={{4,0},{5,1},{8,4},{9,5},{12,8},{13,9},{14,12},{15,13},{10,14},{11,... | collective-permute-start | bytes 786440 | tf_op jit(solution)/shard_map/ppermute | solution.py:461
  116.5 8.6 %collective-permute-start.23 = (bf16[32,4096]{1,0:T(8,128)(2,1)S(1)}, bf16[32,4096]{1,0:T(8,128)(2,1)S(1)}, u32[]{:S(2)}, u32[]{:S(2)}) collective-permute-start(bf16[32,4096]{1,0:T(8,128)(2,1)S(1)} %get-tuple-element.102.rest_2_), channel_id=1, source_target_pairs={{0,4},{1,5},{4,8},{5,9},{8,12},{9,13},{12,14},{13,15},{14,10},{15,... | collective-permute-start | bytes 786440 | tf_op jit(solution)/shard_map/ppermute | solution.py:458
  117.9 7.1 %collective-permute-start.24 = (bf16[32,4096]{1,0:T(8,128)(2,1)S(1)}, bf16[32,4096]{1,0:T(8,128)(2,1)S(1)}, u32[]{:S(2)}, u32[]{:S(2)}) collective-permute-start(bf16[32,4096]{1,0:T(8,128)(2,1)S(1)} %get-tuple-element.103.rest_3_), channel_id=1, source_target_pairs={{4,0},{5,1},{8,4},{9,5},{12,8},{13,9},{14,12},{15,13},{10,14},{11,... | collective-permute-start | bytes 786440 | tf_op jit(solution)/shard_map/ppermute | solution.py:461
  125.2 7.1 %collective-permute-start.25 = (bf16[32,4096]{1,0:T(8,128)(2,1)S(1)}, bf16[32,4096]{1,0:T(8,128)(2,1)S(1)}, u32[]{:S(2)}, u32[]{:S(2)}) collective-permute-start(bf16[32,4096]{1,0:T(8,128)(2,1)S(1)} %get-tuple-element.107.rest_2_), channel_id=1, source_target_pairs={{0,4},{1,5},{4,8},{5,9},{8,12},{9,13},{12,14},{13,15},{14,10},{15,... | collective-permute-start | bytes 786440 | tf_op jit(solution)/shard_map/ppermute | solution.py:458
  126.7 6.4 %collective-permute-start.26 = (bf16[32,4096]{1,0:T(8,128)(2,1)S(1)}, bf16[32,4096]{1,0:T(8,128)(2,1)S(1)}, u32[]{:S(2)}, u32[]{:S(2)}) collective-permute-start(bf16[32,4096]{1,0:T(8,128)(2,1)S(1)} %get-tuple-element.108.rest_3_), channel_id=1, source_target_pairs={{4,0},{5,1},{8,4},{9,5},{12,8},{13,9},{14,12},{15,13},{10,14},{11,... | collective-permute-start | bytes 786440 | tf_op jit(solution)/shard_map/ppermute | solution.py:461
  (9 other events, 80.0 us)
